TPU v7x, 32 devices: a whole 2x2x4 slice. The times are simulated.
32 devices in a mesh: dp: 16 (over z, x, core), tensor: 2 (over y).
Axes of the slice: x: 2, y: 2, z: 4, core: 2. Of those that a mesh axis runs over, the one named last changes fastest.
Arguments:
- layer_input: bfloat16 [23360, 1152], P(('dp', 'tensor')), may hold values from -6 to 6
- token_image: int32 [23360], P('dp'), may hold values from 0 to 2, as said below
- cotangent: bfloat16 [23360, 1152], P(('dp', 'tensor')), may hold values from -6 to 6
- ln1_gain: bfloat16 [1152], P('dp'), may hold values from 0.5 to 1.5
- ln1_bias: bfloat16 [1152], P('dp'), may hold values from -3 to 3
- w_qkv: bfloat16 [3, 1152, 1152], P(None, 'dp', 'tensor'), may hold values from -0.25 to 0.25
- qv_bias: bfloat16 [2, 1152], P(None, 'tensor'), may hold values from -3 to 3
- w_out: bfloat16 [1152, 1152], P('tensor', 'dp'), may hold values from -1 to 1
- out_bias: bfloat16 [1152], P('dp'), may hold values from -3 to 3
- ln2_gain: bfloat16 [1152], P('dp'), may hold values from 0.5 to 1.5
- ln2_bias: bfloat16 [1152], P('dp'), may hold values from -3 to 3
- w_fc1: bfloat16 [1152, 4304], P('dp', 'tensor'), may hold values from -0.1875 to 0.1875
- fc1_bias: bfloat16 [4304], P('tensor'), may hold values from -3 to 3
- w_fc2: bfloat16 [4304, 1152], P('tensor', 'dp'), may hold values from -0.09375 to 0.09375
- fc2_bias: bfloat16 [1152], P('dp'), may hold values from -3 to 3
Outputs:
- layer_output: bfloat16 [23360, 1152], P(('dp', 'tensor'))
- input_grad: float32 [23360, 1152], P(('dp', 'tensor'))
- ln1_gain_grad: float32 [1152], P('dp')
- ln1_bias_grad: float32 [1152], P('dp')
- w_qkv_grad: float32 [3, 1152, 1152], P(None, 'dp', 'tensor')
- qv_bias_grad: float32 [2, 1152], P(None, 'tensor')
- w_out_grad: float32 [1152, 1152], P('tensor', 'dp')
- out_bias_grad: float32 [1152], P('dp')
- ln2_gain_grad: float32 [1152], P('dp')
- ln2_bias_grad: float32 [1152], P('dp')
- w_fc1_grad: float32 [1152, 4304], P('dp', 'tensor')
- fc1_bias_grad: float32 [4304], P('tensor')
- w_fc2_grad: float32 [4304, 1152], P('tensor', 'dp')
- fc2_bias_grad: float32 [1152], P('dp')
Inputs may be any that keep to these rules, and one draw needn't show every extreme that they name: `token_image`: in each group of 1460 consecutive positions the values 0 to 1 appear in this order, 729 positions each; every other position holds 2 (padding), at places drawn from the seed.
All inputs are finite; a program needn't handle non-finite values.
Results may differ from a plain program's by a relative error of at most 0.012.
The roundings to bfloat16 on the way count: a program that leaves them out, or rounds other values in their place, can miss the bound.
Values may be sent and summed in bfloat16 or wider, within the bound.
No kernel may reach another device: no remote copies, remote signals or barrier semaphores. Data moves between devices by JAX's collectives and lax.ppermute only.
A program may use at most 256 MiB of HBM per device.

v0:
```python
import jax
import jax.numpy as jnp
from jax import lax
from jax.sharding import PartitionSpec as P

HEAD_DIM = 72
IMAGES = 2


layer_eps = 1e-06
gelu_scale = 0.7978845608028654


def gelu_tanh(values):
    return (
        0.5 * values * (1.0 + jnp.tanh(gelu_scale * (values + 0.044715 * values * values * values)))
    )


def norm_rows(values, gain, shift):
    centre = values - jnp.mean(values, axis=1, keepdims=True)
    spread = jnp.mean(centre * centre, axis=1, keepdims=True)
    return centre * lax.rsqrt(spread + layer_eps) * gain + shift


def contract_rows(left, right):
    return lax.dot_general(
        left, right, (((0,), (0,)), ((), ())), preferred_element_type=jnp.float32
    )


def contract_cols(left, right):
    return lax.dot_general(
        left, right, (((1,), (1,)), ((), ())), preferred_element_type=jnp.float32
    )


def split_heads(values, head_count):
    slot_count = values.shape[0]
    return values.reshape(slot_count, head_count, -1).transpose(1, 0, 2)


def join_heads(values):
    head_count, slot_count, head_size = values.shape
    return values.transpose(1, 0, 2).reshape(slot_count, head_count * head_size)


def block_rows(slot_count):
    half_rows = slot_count // 2
    return half_rows


def masked_scores(rows_query, head_keys, rows_ids, image_ids, score_scale):
    scores = contract_cols(rows_query, head_keys) * score_scale
    return jnp.where(rows_ids[:, None] == image_ids[None, :], scores, -1e30)


def heads_forward(query_heads, key_heads, value_heads, image_ids, score_scale):
    slot_count, head_size = (query_heads.shape[1], query_heads.shape[2])
    block_size = block_rows(slot_count)
    block_count = slot_count // block_size
    id_blocks = image_ids.reshape(block_count, block_size)

    def one_head(head_inputs):
        head_query, head_keys, head_values = head_inputs

        def one_block(block_inputs):
            rows_query, rows_ids = block_inputs
            scores = masked_scores(rows_query, head_keys, rows_ids, image_ids, score_scale)
            peak = jnp.max(scores, axis=1, keepdims=True)
            expo_rows = jnp.exp(scores - peak)
            row_total = jnp.sum(expo_rows, axis=1, keepdims=True)
            prob_rows = (expo_rows / row_total).astype(jnp.bfloat16)
            mixed = jnp.dot(prob_rows, head_values, preferred_element_type=jnp.float32)
            return (mixed.astype(jnp.bfloat16), peak[:, 0] + jnp.log(row_total[:, 0]))

        mixed, logsum = lax.map(
            one_block, (head_query.reshape(block_count, block_size, head_size), id_blocks)
        )
        return (mixed.reshape(slot_count, head_size), logsum.reshape(slot_count))

    return lax.map(one_head, (query_heads, key_heads, value_heads))


def heads_backward(query_heads, key_heads, value_heads, grad_heads, logsum, image_ids, score_scale):
    slot_count, head_size = (query_heads.shape[1], query_heads.shape[2])
    block_size = block_rows(slot_count)
    block_count = slot_count // block_size
    id_blocks = image_ids.reshape(block_count, block_size)

    def one_head(head_inputs):
        head_query, head_keys, head_values, head_grad, head_logsum = head_inputs

        def one_block(carried, block_inputs):
            key_sum, value_sum = carried
            rows_query, rows_grad, rows_logsum, rows_ids = block_inputs
            scores = masked_scores(rows_query, head_keys, rows_ids, image_ids, score_scale)
            prob_rows = jnp.exp(scores - rows_logsum[:, None])
            value_sum = value_sum + contract_rows(prob_rows.astype(jnp.bfloat16), rows_grad)
            grad_probs = contract_cols(rows_grad, head_values)
            centre = jnp.sum(grad_probs * prob_rows, axis=1, keepdims=True)
            grad_scores = (prob_rows * (grad_probs - centre)).astype(jnp.bfloat16)
            rows_dq = (
                jnp.dot(grad_scores, head_keys, preferred_element_type=jnp.float32) * score_scale
            ).astype(jnp.bfloat16)
            key_sum = key_sum + contract_rows(grad_scores, rows_query) * score_scale
            return ((key_sum, value_sum), rows_dq)

        zeros_init = jnp.zeros((slot_count, head_size), jnp.float32)
        block_inputs = (
            head_query.reshape(block_count, block_size, head_size),
            head_grad.reshape(block_count, block_size, head_size),
            head_logsum.reshape(block_count, block_size),
            id_blocks,
        )
        (key_sum, value_sum), query_grad = lax.scan(
            one_block, (zeros_init, zeros_init), block_inputs
        )
        return (
            query_grad.reshape(slot_count, head_size),
            key_sum.astype(jnp.bfloat16),
            value_sum.astype(jnp.bfloat16),
        )

    return lax.map(one_head, (query_heads, key_heads, value_heads, grad_heads, logsum))


def forward_pass(inputs, full_output):
    (
        layer_input,
        token_image,
        ln1_gain,
        ln1_bias,
        w_qkv,
        qv_bias,
        w_out,
        out_bias,
        ln2_gain,
        ln2_bias,
        w_fc1,
        fc1_bias,
        w_fc2,
        fc2_bias,
    ) = inputs
    head_count = w_qkv.shape[2] // HEAD_DIM
    score_scale = HEAD_DIM ** (-0.5)
    attn_params = (
        lax.all_gather(ln1_gain, "dp", axis=0, tiled=True),
        lax.all_gather(ln1_bias, "dp", axis=0, tiled=True),
        lax.all_gather(w_qkv, "dp", axis=1, tiled=True),
        lax.all_gather(w_out, "dp", axis=1, tiled=True),
        lax.all_gather(out_bias, "dp", axis=0, tiled=True),
    )
    mlp_params = (
        lax.all_gather(ln2_gain, "dp", axis=0, tiled=True),
        lax.all_gather(ln2_bias, "dp", axis=0, tiled=True),
        lax.all_gather(w_fc1, "dp", axis=0, tiled=True),
        lax.all_gather(w_fc2, "dp", axis=1, tiled=True),
        lax.all_gather(fc2_bias, "dp", axis=0, tiled=True),
    )
    input_rows = layer_input.astype(jnp.float32)
    normed = norm_rows(
        input_rows, attn_params[0].astype(jnp.float32), attn_params[1].astype(jnp.float32)
    )
    first_in = lax.all_gather(normed.astype(jnp.bfloat16), "tensor", axis=0, tiled=True)
    projected = jnp.einsum(
        "sd,cde->cse", first_in, attn_params[2], preferred_element_type=jnp.float32
    )
    bias_rows = qv_bias.astype(jnp.float32)
    query_heads = split_heads((projected[0] + bias_rows[0]).astype(jnp.bfloat16), head_count)
    key_heads = split_heads(projected[1].astype(jnp.bfloat16), head_count)
    value_heads = split_heads((projected[2] + bias_rows[1]).astype(jnp.bfloat16), head_count)
    mixed, logsum = heads_forward(query_heads, key_heads, value_heads, token_image, score_scale)
    attn_out = join_heads(mixed)
    resid = (
        input_rows
        + lax.psum_scatter(
            jnp.dot(attn_out, attn_params[3], preferred_element_type=jnp.float32),
            "tensor",
            scatter_dimension=0,
            tiled=True,
        )
        + attn_params[4].astype(jnp.float32)
    )
    normed_two = norm_rows(
        resid, mlp_params[0].astype(jnp.float32), mlp_params[1].astype(jnp.float32)
    )
    second_in = lax.all_gather(normed_two.astype(jnp.bfloat16), "tensor", axis=0, tiled=True)
    hidden = jnp.dot(
        second_in, mlp_params[2], preferred_element_type=jnp.float32
    ) + fc1_bias.astype(jnp.float32)
    active = gelu_tanh(hidden).astype(jnp.bfloat16)
    layer_output = None
    if full_output:
        summed = lax.psum_scatter(
            jnp.dot(active, mlp_params[3], preferred_element_type=jnp.float32).astype(jnp.bfloat16),
            "tensor",
            scatter_dimension=0,
            tiled=True,
        ).astype(jnp.float32)
        layer_output = (resid + summed + mlp_params[4].astype(jnp.float32)).astype(jnp.bfloat16)
    return (
        attn_params,
        mlp_params,
        input_rows,
        first_in,
        query_heads,
        key_heads,
        value_heads,
        logsum,
        attn_out,
        resid,
        second_in,
        hidden,
        active,
        layer_output,
    )


def shards(
    layer_input,
    token_image,
    cotangent,
    ln1_gain,
    ln1_bias,
    w_qkv,
    qv_bias,
    w_out,
    out_bias,
    ln2_gain,
    ln2_bias,
    w_fc1,
    fc1_bias,
    w_fc2,
    fc2_bias,
):
    inputs = (
        layer_input,
        token_image,
        ln1_gain,
        ln1_bias,
        w_qkv,
        qv_bias,
        w_out,
        out_bias,
        ln2_gain,
        ln2_bias,
        w_fc1,
        fc1_bias,
        w_fc2,
        fc2_bias,
    )
    first_pass = forward_pass(inputs, True)
    layer_output = first_pass[13]
    fenced = lax.optimization_barrier((layer_output, inputs))[1]
    saved = forward_pass(fenced, False)
    (
        attn_params,
        mlp_params,
        input_rows,
        first_in,
        query_heads,
        key_heads,
        value_heads,
        logsum,
        attn_out,
        resid,
        second_in,
        hidden,
        active,
        unused_output,
    ) = saved
    score_scale = HEAD_DIM ** (-0.5)
    row_count = layer_input.shape[0]
    tensor_at = lax.axis_index("tensor")
    image_rows = lax.dynamic_slice_in_dim(token_image, tensor_at * row_count, row_count)
    valid_mask = (image_rows < IMAGES).astype(jnp.float32)
    grad_rows = cotangent.astype(jnp.float32) * valid_mask[:, None]
    grad_low = grad_rows.astype(jnp.bfloat16)
    grad_all = lax.all_gather(grad_low, "tensor", axis=0, tiled=True)
    grad_active = contract_cols(grad_all, mlp_params[3])
    grad_hidden = jax.vjp(gelu_tanh, hidden)[1](grad_active)[0].astype(jnp.bfloat16)
    fc2_grad = contract_rows(active, grad_all)
    fc1_grad = contract_rows(second_in, grad_hidden)
    grad_normed_two = lax.psum_scatter(
        contract_cols(grad_hidden, mlp_params[2]), "tensor", scatter_dimension=0, tiled=True
    )
    norm_two_back = jax.vjp(
        norm_rows, resid, mlp_params[0].astype(jnp.float32), mlp_params[1].astype(jnp.float32)
    )[1]
    resid_part, ln2_gain_sum, ln2_bias_sum = norm_two_back(grad_normed_two)
    grad_resid = grad_rows + resid_part
    resid_low = grad_resid.astype(jnp.bfloat16)
    resid_all = lax.all_gather(resid_low, "tensor", axis=0, tiled=True)
    out_grad = contract_rows(attn_out, resid_all)
    grad_attn = contract_cols(resid_all, attn_params[3]).astype(jnp.bfloat16)
    head_count = query_heads.shape[0]
    grad_query, grad_keys, grad_values = heads_backward(
        query_heads,
        key_heads,
        value_heads,
        split_heads(grad_attn, head_count),
        logsum,
        token_image,
        score_scale,
    )
    grad_qkv = jnp.stack([join_heads(grad_query), join_heads(grad_keys), join_heads(grad_values)])
    qkv_grad = jnp.einsum("sd,cse->cde", first_in, grad_qkv, preferred_element_type=jnp.float32)
    grad_normed = lax.psum_scatter(
        jnp.einsum("cse,cde->sd", grad_qkv, attn_params[2], preferred_element_type=jnp.float32),
        "tensor",
        scatter_dimension=0,
        tiled=True,
    )
    norm_one_back = jax.vjp(
        norm_rows,
        input_rows,
        attn_params[0].astype(jnp.float32),
        attn_params[1].astype(jnp.float32),
    )[1]
    input_part, ln1_gain_sum, ln1_bias_sum = norm_one_back(grad_normed)
    input_grad = grad_resid + input_part
    qkv_piece, out_piece, fc1_piece, fc2_piece = (
        lax.psum_scatter(qkv_grad, "dp", scatter_dimension=1, tiled=True),
        lax.psum_scatter(out_grad, "dp", scatter_dimension=1, tiled=True),
        lax.psum_scatter(fc1_grad, "dp", scatter_dimension=0, tiled=True),
        lax.psum_scatter(fc2_grad, "dp", scatter_dimension=1, tiled=True),
    )
    full_width = layer_input.shape[1]
    head_width = qv_bias.shape[1]
    ff_width = fc1_bias.shape[0]
    row_sums = jnp.stack(
        [
            ln1_gain_sum,
            ln1_bias_sum,
            jnp.sum(resid_low.astype(jnp.float32), axis=0),
            ln2_gain_sum,
            ln2_bias_sum,
            jnp.sum(grad_rows, axis=0),
        ]
    )
    qv_sums = jnp.stack(
        [
            jnp.sum(grad_qkv[0].astype(jnp.float32), axis=0),
            jnp.sum(grad_qkv[2].astype(jnp.float32), axis=0),
        ]
    )
    qv_wide = lax.dynamic_update_slice_in_dim(
        jnp.zeros((2, full_width), jnp.float32), qv_sums, tensor_at * head_width, 1
    )
    fc1_sums = jnp.sum(grad_hidden.astype(jnp.float32), axis=0)
    fc1_wide = lax.dynamic_update_slice_in_dim(
        jnp.zeros((ff_width * lax.axis_size("tensor"),), jnp.float32),
        fc1_sums,
        tensor_at * ff_width,
        0,
    )
    row_total, qv_total, fc1_total = lax.psum((row_sums, qv_wide, fc1_wide), ("dp", "tensor"))
    dp_width = ln1_gain.shape[0]
    row_piece = lax.dynamic_slice_in_dim(row_total, lax.axis_index("dp") * dp_width, dp_width, 1)
    qv_piece = lax.dynamic_slice_in_dim(qv_total, tensor_at * head_width, head_width, 1)
    fc1_bias_piece = lax.dynamic_slice_in_dim(fc1_total, tensor_at * ff_width, ff_width, 0)
    return (
        layer_output,
        input_grad,
        row_piece[0],
        row_piece[1],
        qkv_piece,
        qv_piece,
        out_piece,
        row_piece[2],
        row_piece[3],
        row_piece[4],
        fc1_piece,
        fc1_bias_piece,
        fc2_piece,
        row_piece[5],
    )


def solution(mesh):
    in_specs = (
        P(("dp", "tensor"), None),
        P("dp"),
        P(("dp", "tensor"), None),
        P("dp"),
        P("dp"),
        P(None, "dp", "tensor"),
        P(None, "tensor"),
        P("tensor", "dp"),
        P("dp"),
        P("dp"),
        P("dp"),
        P("dp", "tensor"),
        P("tensor"),
        P("tensor", "dp"),
        P("dp"),
    )
    out_specs = (
        P(("dp", "tensor"), None),
        P(("dp", "tensor"), None),
        P("dp"),
        P("dp"),
        P(None, "dp", "tensor"),
        P(None, "tensor"),
        P("tensor", "dp"),
        P("dp"),
        P("dp"),
        P("dp"),
        P("dp", "tensor"),
        P("tensor"),
        P("tensor", "dp"),
        P("dp"),
    )
    return jax.shard_map(shards, mesh=mesh, in_specs=in_specs, out_specs=out_specs, check_vma=False)
```

profile of v0, /device:TPU:0, one launch (start us, length us, event | category | flops | bytes accessed | tf_op | source)
XLA Modules:
  0.0 2285.3 jit_solution(4382151977081165738)
XLA Ops:
  14.4 62.9 %all-reduce.27 = (bf16[1152]{0:T(1024)(128)(2,1)}, bf16[1152]{0:T(1024)(128)(2,1)}, bf16[1152]{0:T(1024)(128)(2,1)}, bf16[1152]{0:T(1024)(128)(2,1)S(1)}, bf16[1...) all-reduce(bf16[1152]{0:T(1024)(128)(2,1)S(1)} %dynamic-update-slice.4, ...), channel_id=1, replica_groups=mesh['dp'=16,'tensor'=2] {'dp'}, use_global_device_ids=true, to_apply=%add.4 | all-reduce | flops 6912 | bytes 27648
  86.2 42.0 %all-gather.37.cloned.1.call-done = bf16[2,730,1152]{2,1,0:T(8,128)(2,1)} async-done(((bf16[1,730,1152]{2,1,0:T(8,128)(2,1)}), bf16[2,730,1152]{2,1,0:T(8,128)(2,1)}) %all-gather.37.cloned.1.call-update) | async-done | bytes 3363856 | tf_op jit(solution)/shard_map/all_gather | solution.py:165
  130.8 51.3 %all-gather.21.cloned.1.call-done = bf16[3,1152,576]{2,1,0:T(8,128)(2,1)} async-done(((bf16[3,72,576]{2,1,0:T(8,128)(2,1)}), bf16[3,1152,576]{2,1,0:T(8,128)(2,1)}) %all-gather.21.cloned.1.call-update) | async-done | bytes 3981328 | tf_op jit(solution)/shard_map/all_gather | solution.py:150
  210.3 62.5 %while.74 = (s32[]{:T(128)}, bf16[8,1460,72]{1,2,0:T(8,128)(2,1)}, bf16[8,1460,72]{1,2,0:T(8,128)(2,1)S(1)}, bf16[8,1460,72]{2,1,0:T(8,128)(2,1)}, bf16[8,1460,7...) while((s32[]{:T(128)}, bf16[8,1460,72]{1,2,0:T(8,128)(2,1)}, ...), condition=%wide.region_7.8_spmd, body=%wide.region_2.7_spmd.sunk | while | flops 316593664 | bytes 17483044 | solution.py:82
  280.7 81.9 %fusion = f32[736,1152]{1,0:T(8,128)S(1)} fusion(f32[1460,1152]{1,0:T(8,128)} %fusion.114), kind=kCustom, calls=%all-reduce-scatter | all-reduce-scatter fusion | flops 1695745 | bytes 10119680
  385.2 45.6 %all-gather.39.cloned.1.call-done = bf16[2,730,1152]{2,1,0:T(8,128)(2,1)} async-done(((bf16[1,730,1152]{2,1,0:T(8,128)(2,1)}), bf16[2,730,1152]{2,1,0:T(8,128)(2,1)}) %all-gather.39.cloned.1.call-update) | async-done | bytes 3363856 | tf_op jit(solution)/shard_map/all_gather | solution.py:188
  435.1 52.6 %all-gather.25.cloned.1.call-done = bf16[1152,2152]{1,0:T(8,128)(2,1)} async-done(((bf16[72,2152]{1,0:T(8,128)(2,1)}), bf16[1152,2152]{1,0:T(8,128)(2,1)}) %all-gather.25.cloned.1.call-update) | async-done | bytes 4958224 | tf_op jit(solution)/shard_map/all_gather | solution.py:157
  487.7 55.5 %all-gather.27.cloned.1.call-done = bf16[2152,1152]{0,1:T(8,128)(2,1)} async-done(((bf16[2152,72]{0,1:T(8,128)(2,1)}), bf16[2152,1152]{0,1:T(8,128)(2,1)}) %all-gather.27.cloned.1.call-update) | async-done | bytes 4958224 | tf_op jit(solution)/shard_map/all_gather | solution.py:158
  543.2 23.4 %fusion.51 = bf16[1460,1152]{1,0:T(8,128)(2,1)} fusion(bf16[2152,1152]{0,1:T(8,128)(2,1)} %all-gather.27.cloned.1.call-done, bf16[1460,1152]{1,0:T(8,128)(2,1)} %reshape.293, bf16[1152,2152]{1,0:T(8,128)(2,1)} %all-gather.25.cloned.1.call-done, f32[2152]{0:T(1024)S(1)} %convert_element_type.177), kind=kOutput, calls=%fused_computation.89 | convolution fusion | flops 14511071232 | bytes 16652704 | tf_op jit(solution)/shard_map/dot_general | solution.py:196
  566.6 44.2 %fusion.1 = bf16[736,1152]{1,0:T(8,128)(2,1)S(1)} fusion(bf16[1460,1152]{1,0:T(8,128)(2,1)} %fusion.51), kind=kCustom, calls=%all-reduce-scatter.1 | all-reduce-scatter fusion | flops 1695745 | bytes 5060096
  630.3 57.7 %all-reduce.26 = (bf16[1152]{0:T(1024)(128)(2,1)S(1)}, bf16[1152]{0:T(1024)(128)(2,1)S(1)}, bf16[1152]{0:T(1024)(128)(2,1)}, bf16[1152]{0:T(1024)(128)(2,1)}, bf16[1152]{0:T(1024)(128)(2,1)}) all-reduce(bf16[1152]{0:T(1024)(128)(2,1)S(1)} %dynamic-update-slice.7, ...), channel_id=1, replica_groups=mesh['dp'=16,'tensor'=2] {'dp'}, use_global_device_ids=true, to_apply=%add.7 | all-reduce | flops 5760 | bytes 23040
  695.8 40.6 %all-gather.41.cloned.1.call-done = bf16[2,730,1152]{2,1,0:T(8,128)(2,1)} async-done(((bf16[1,730,1152]{2,1,0:T(8,128)(2,1)}), bf16[2,730,1152]{2,1,0:T(8,128)(2,1)}) %all-gather.41.cloned.1.call-update) | async-done | bytes 3363856 | tf_op jit(solution)/shard_map/all_gather | solution.py:165
  739.1 51.3 %all-gather.29.cloned.1.call-done = bf16[3,1152,576]{2,1,0:T(8,128)(2,1)} async-done(((bf16[3,72,576]{2,1,0:T(8,128)(2,1)}), bf16[3,1152,576]{2,1,0:T(8,128)(2,1)}) %all-gather.29.cloned.1.call-update) | async-done | bytes 3981328 | tf_op jit(solution)/shard_map/all_gather | solution.py:150
  819.4 207.3 %while.76 = (s32[]{:T(128)}, bf16[8,1460,72]{1,2,0:T(8,128)(2,1)}, f32[8,1460]{1,0:T(8,128)}, bf16[8,1460,72]{1,2,0:T(8,128)(2,1)}, bf16[8,1460,72]{2,1,0:T(8,12...) while((s32[]{:T(128)}, bf16[8,1460,72]{1,2,0:T(8,128)(2,1)}, ...), condition=%wide.region_19.20_spmd, body=%wide.region_14.19_spmd.sunk | while | flops 316594400 | bytes 35251300 | solution.py:82
  1035.7 83.2 %fusion.2 = f32[736,1152]{1,0:T(8,128)} fusion(f32[1460,1152]{1,0:T(8,128)} %fusion.115), kind=kCustom, calls=%all-reduce-scatter.2 | all-reduce-scatter fusion | flops 1695745 | bytes 10119680
  1144.5 43.2 %all-gather.43.cloned.1.call-done = bf16[2,730,1152]{2,1,0:T(8,128)(2,1)} async-done(((bf16[1,730,1152]{2,1,0:T(8,128)(2,1)}), bf16[2,730,1152]{2,1,0:T(8,128)(2,1)}) %all-gather.43.cloned.1.call-update) | async-done | bytes 3363856 | tf_op jit(solution)/shard_map/all_gather | solution.py:188
  1192.1 52.6 %all-gather.33.cloned.1.call-done = bf16[1152,2152]{1,0:T(8,128)(2,1)} async-done(((bf16[72,2152]{1,0:T(8,128)(2,1)}), bf16[1152,2152]{1,0:T(8,128)(2,1)}) %all-gather.33.cloned.1.call-update) | async-done | bytes 4958224 | tf_op jit(solution)/shard_map/all_gather | solution.py:157
  1259.7 40.6 %all-gather.35.cloned.1.call-done = bf16[2152,1152]{0,1:T(8,128)(2,1)} async-done(((bf16[2152,72]{0,1:T(8,128)(2,1)}), bf16[2152,1152]{0,1:T(8,128)(2,1)}) %all-gather.35.cloned.1.call-update) | async-done | bytes 4958224 | tf_op jit(solution)/shard_map/all_gather | solution.py:158
  1300.3 22.4 convert_reduce_fusion
  1336.4 81.8 %fusion.3 = f32[736,1152]{1,0:T(8,128)S(1)} fusion(f32[1460,1152]{1,0:T(8,128)} %fusion.116), kind=kCustom, calls=%all-reduce-scatter.3 | all-reduce-scatter fusion | flops 1695745 | bytes 10119680
  1443.1 47.2 %all-gather.47.cloned.1.call-done = bf16[2,730,1152]{2,1,0:T(8,128)(2,1)} async-done(((bf16[1,730,1152]{2,1,0:T(8,128)(2,1)}), bf16[2,730,1152]{2,1,0:T(8,128)(2,1)}) %all-gather.47.cloned.1.call-update) | async-done | bytes 3363856 | tf_op jit(solution)/shard_map/all_gather | solution.py:294
  1503.2 216.7 %while.78 = (s32[]{:T(128)}, bf16[8,1460,72]{1,2,0:T(8,128)(2,1)}, bf16[8,1460,72]{1,2,0:T(8,128)(2,1)}, bf16[8,1460,72]{1,2,0:T(8,128)(2,1)}, bf16[8,1460,72]{1...) while((s32[]{:T(128)}, bf16[8,1460,72]{1,2,0:T(8,128)(2,1)}, ...), condition=%wide.region_30.31_spmd, body=%wide.region_26.30_spmd.sunk | while | flops 778874112 | bytes 81266232 | solution.py:125
  1507.8 19.4 while.81
  1588.9 19.4 while.81
  1642.9 19.4 while.81
  1670.0 19.4 while.81
  1697.1 19.4 while.81
  1803.8 81.0 %fusion.4 = f32[736,1152]{1,0:T(8,128)S(1)} fusion(f32[1460,1152]{1,0:T(8,128)} %convolution_bitcast_fusion), kind=kCustom, calls=%all-reduce-scatter.4 | all-reduce-scatter fusion | flops 1695745 | bytes 10119680
  1909.8 43.0 %all-reduce.25 = (f32[6,1152]{1,0:T(8,128)S(1)}, f32[2,1152]{1,0:T(2,128)S(1)}, f32[4304]{0:T(1024)S(1)}) all-reduce(f32[6,1152]{1,0:T(8,128)S(1)} %stack.28, f32[2,1152]{1,0:T(2,128)S(1)} %dynamic_update_slice.40, f32[4304]{0:T(1024)S(1)} %copy-done.43), channel_id=1, replica_groups=mesh['dp'=16,'tensor'=2] {'dp','tensor'}, use_global_device_ids=true, to_apply=%region_40.41 | all-reduce | flops 13520 | bytes 108160 | tf_op jit(solution)/shard_map/psum | solution.py:358
  1970.5 67.7 %reduce-scatter.20.cloned.1.call-done = f32[576,72]{0,1:T(8,128)} async-done(((f32[576,1152]{0,1:T(8,128)}), f32[576,72]{0,1:T(8,128)}) %reduce-scatter.20.cloned.1.call-update) | async-done | bytes 165904
  2038.2 120.0 %reduce-scatter.22.cloned.1.call-done = f32[72,2152]{1,0:T(8,128)} async-done(((f32[1152,2152]{1,0:T(8,128)}), f32[72,2152]{1,0:T(8,128)}) %reduce-scatter.22.cloned.1.call-update) | async-done | bytes 619792
  2158.1 120.1 %reduce-scatter.24.cloned.1.call-done = f32[2152,72]{0,1:T(8,128)} async-done(((f32[2152,1152]{0,1:T(8,128)}), f32[2152,72]{0,1:T(8,128)}) %reduce-scatter.24.cloned.1.call-update) | async-done | bytes 619792
  (1265 shorter events, 1096.2 us)
Async XLA Ops:
  7.2 121.0 %all-gather.37.cloned.1.call-start = ((), (), s32[]{:S(2)}) async-start(), calls=%async_computation.11 | async-start | bytes 5087232 | tf_op jit(solution)/shard_map/all_gather | solution.py:165
  83.0 99.1 %all-gather.21.cloned.1.call-start = ((), (), s32[]{:S(2)}) async-start(), calls=%async_computation.3 | async-start | bytes 4700160 | tf_op jit(solution)/shard_map/all_gather | solution.py:150
  83.8 189.0 %all-gather.23.cloned.1.call-start = ((), (), s32[]{:S(2)}) async-start(), calls=%async_computation.4 | async-start | bytes 1566720 | tf_op jit(solution)/shard_map/all_gather | solution.py:151
  84.5 346.3 %all-gather.39.cloned.1.call-start = ((), (), s32[]{:S(2)}) async-start(), calls=%async_computation.12 | async-start | bytes 5087232 | tf_op jit(solution)/shard_map/all_gather | solution.py:188
  280.7 84.5 %copy-start.73 = (bf16[1152]{0:T(1024)(128)(2,1)S(1)}, bf16[1152]{0:T(1024)(128)(2,1)}, u32[]{:S(2)}) copy-start(bf16[1152]{0:T(1024)(128)(2,1)} %get-tuple-element.589) | copy-start | bytes 6916
  280.7 84.5 %copy-start.74 = (u32[32]{0:T(128)S(1)}, u32[32]{0:T(128)}, u32[]{:S(2)}) copy-start(u32[32]{0:T(128)} %constant.245) | copy-start | bytes 388
  280.7 85.7 %copy-start.72 = (bf16[1152]{0:T(1024)(128)(2,1)S(1)}, bf16[1152]{0:T(1024)(128)(2,1)}, u32[]{:S(2)}) copy-start(bf16[1152]{0:T(1024)(128)(2,1)} %get-tuple-element.588) | copy-start | bytes 6916
  280.7 85.8 %copy-start.71 = (bf16[1152]{0:T(1024)(128)(2,1)S(1)}, bf16[1152]{0:T(1024)(128)(2,1)}, u32[]{:S(2)}) copy-start(bf16[1152]{0:T(1024)(128)(2,1)} %get-tuple-element.587) | copy-start | bytes 6916
  362.7 4.1 collective-permute-start
  383.5 104.2 %all-gather.25.cloned.1.call-start = ((), (), s32[]{:S(2)}) async-start(), calls=%async_computation.5 | async-start | bytes 5326848 | tf_op jit(solution)/shard_map/all_gather | solution.py:157
  384.1 159.1 %all-gather.27.cloned.1.call-start = ((), (), s32[]{:S(2)}) async-start(), calls=%async_computation.6 | async-start | bytes 5326848 | tf_op jit(solution)/shard_map/all_gather | solution.py:158
  384.7 351.7 %all-gather.41.cloned.1.call-start = ((), (), s32[]{:S(2)}) async-start(), calls=%async_computation.13 | async-start | bytes 5087232 | tf_op jit(solution)/shard_map/all_gather | solution.py:165
  610.9 3.9 collective-permute-start.1
  690.5 99.9 %all-gather.29.cloned.1.call-start = ((), (), s32[]{:S(2)}) async-start(), calls=%async_computation.7 | async-start | bytes 4700160 | tf_op jit(solution)/shard_map/all_gather | solution.py:150
  691.3 335.4 %all-gather.31.cloned.1.call-start = ((), (), s32[]{:S(2)}) async-start(), calls=%async_computation.8 | async-start | bytes 1566720 | tf_op jit(solution)/shard_map/all_gather | solution.py:151
  692.0 449.8 %all-gather.45.cloned.1.call-start = ((), (), s32[]{:S(2)}) async-start(), calls=%async_computation.15 | async-start | bytes 5087232 | tf_op jit(solution)/shard_map/all_gather | solution.py:280
  694.3 493.4 %all-gather.43.cloned.1.call-start = ((), (), s32[]{:S(2)}) async-start(), calls=%async_computation.14 | async-start | bytes 5087232 | tf_op jit(solution)/shard_map/all_gather | solution.py:188
  1035.7 86.3 %copy-start.70 = (bf16[1152]{0:T(1024)(128)(2,1)S(1)}, bf16[1152]{0:T(1024)(128)(2,1)}, u32[]{:S(2)}) copy-start(bf16[1152]{0:T(1024)(128)(2,1)} %get-tuple-element.584) | copy-start | bytes 6916
  1035.7 86.4 %copy-start.69 = (bf16[1152]{0:T(1024)(128)(2,1)S(1)}, bf16[1152]{0:T(1024)(128)(2,1)}, u32[]{:S(2)}) copy-start(bf16[1152]{0:T(1024)(128)(2,1)} %get-tuple-element.586) | copy-start | bytes 6916
  1035.7 86.4 %copy-start.68 = (bf16[1152]{0:T(1024)(128)(2,1)S(1)}, bf16[1152]{0:T(1024)(128)(2,1)}, u32[]{:S(2)}) copy-start(bf16[1152]{0:T(1024)(128)(2,1)} %get-tuple-element.585) | copy-start | bytes 6916
  1119.7 4.0 collective-permute-start.2
  1140.4 104.3 %all-gather.33.cloned.1.call-start = ((), (), s32[]{:S(2)}) async-start(), calls=%async_computation.9 | async-start | bytes 5326848 | tf_op jit(solution)/shard_map/all_gather | solution.py:157
  1141.0 159.4 %all-gather.35.cloned.1.call-start = ((), (), s32[]{:S(2)}) async-start(), calls=%async_computation.10 | async-start | bytes 5326848 | tf_op jit(solution)/shard_map/all_gather | solution.py:158
  1141.7 348.6 %all-gather.47.cloned.1.call-start = ((), (), s32[]{:S(2)}) async-start(), calls=%async_computation.16 | async-start | bytes 5087232 | tf_op jit(solution)/shard_map/all_gather | solution.py:294
  1144.4 155.9 %copy-start.35 = (bf16[1460,1152]{1,0:T(8,128)(2,1)}, bf16[1460,1152]{1,0:T(8,128)(2,1)S(1)}, u32[]{:S(2)}) copy-start(bf16[1460,1152]{1,0:T(8,128)(2,1)S(1)} %reshape.299) | copy-start | bytes 10091524
  1420.0 4.3 collective-permute-start.3
  1443.0 525.4 %all-reduce.30.cloned.1.call-start = ((), (), s32[]{:S(2)}) async-start(), calls=%async_computation.17 | async-start | bytes 23592960
  1746.1 292.0 %reduce-scatter.20.cloned.1.call-start = ((), (), s32[]{:S(2)}) async-start(), calls=%async_computation.18 | async-start | bytes 3133440
  1753.4 404.7 %reduce-scatter.22.cloned.1.call-start = ((), (), s32[]{:S(2)}) async-start(), calls=%async_computation.19 | async-start | bytes 10653696
  1767.2 511.0 %reduce-scatter.24.cloned.1.call-start = ((), (), s32[]{:S(2)}) async-start(), calls=%async_computation.20 | async-start | bytes 10653696
  1803.8 84.4 %copy-start.64 = (f32[1,576]{1,0:T(1,128)S(1)}, f32[1,576]{1,0:T(1,128)}, u32[]{:S(2)}) copy-start(f32[1,576]{1,0:T(1,128)} %stack.29) | copy-start | bytes 6916
  1884.8 5.0 collective-permute-start.4
  (223 other events, 991.2 us)
Sparse Core Ops, SparseCore 0:
  83.2 44.9 all-gather.36
  130.4 51.7 all-gather.20
  184.3 37.8 all-gather.22
  383.7 47.0 all-gather.38
  432.8 54.9 all-gather.24
  489.7 53.4 all-gather.26
  690.6 45.7 all-gather.40
  738.6 51.7 all-gather.28
  792.6 37.8 all-gather.30
  831.8 46.5 all-gather.44
  1140.5 47.1 all-gather.42
  1189.7 54.9 all-gather.32
  1246.8 53.4 all-gather.34
  1443.1 47.1 all-gather.46
  1746.3 222.1 all-reduce.29
  1972.8 65.3 reduce-scatter.19
  2042.7 115.3 reduce-scatter.21
  2162.7 115.4 reduce-scatter.23
where the time goes:
time: 2300 us; the launch traced here: 2290 us
  waiting for transfers between devices  855 us (37%)
  blocking collectives  536 us (23%)
  matrix products  418 us (18%)
  local copies, waits for them, and re-layouts  335 us (15%)
  other arithmetic  105 us (5%)
    unnamed x7, blocking collectives  493 us
    unnamed x27, waiting for transfers between devices  332 us
    dot_general x67, matrix products, contract_cols(): lax.dot_general(left, right, (((1,), (1,)), ((), ())), preferred_element_...  125 us
    all_gather x2, waiting for transfers between devices, forward_pass(): lax.all_gather(w_fc1, 'dp', axis=0, tiled=True)  105 us
    all_gather x2, waiting for transfers between devices, forward_pass(): lax.all_gather(w_qkv, 'dp', axis=1, tiled=True)  103 us
    all_gather x2, waiting for transfers between devices, forward_pass(): lax.all_gather(w_fc2, 'dp', axis=1, tiled=True)  96.1 us
    unnamed x186, local copies, waits for them, and re-layouts  90.4 us
    all_gather x2, waiting for transfers between devices, forward_pass(): lax.all_gather(normed_two.astype(jnp.bfloat16), 'tensor', axis=0, tiled=T...  88.8 us
  transfers between devices with their start and end apart: 23, of which 20 were waited for; matrix products, arithmetic and copies ran while one was open for 26% of the time, Pallas kernels for 0%

commit v1 on v0

--- a/solution.py
+++ b/solution.py
@@ -1,9 +1,15 @@
+import functools
+
 import jax
 import jax.numpy as jnp
 from jax import lax
+from jax.experimental import pallas as pl
+from jax.experimental.pallas import tpu as pltpu
 from jax.sharding import PartitionSpec as P
 
 HEAD_DIM = 72
+LOG2E = 1.4426950408889634
+VMEM_BYTES = 60 * 1024 * 1024
 IMAGES = 2
 
 
@@ -378,6 +384,647 @@
     )
 
 
+def head_window(head, width):
+    start = head * HEAD_DIM
+    first = start // 128 * 128
+    last = min(first + 256, width)
+    return start - first, first, last
+
+
+def spare_lanes(offset):
+    if offset >= 2:
+        return 0, 1
+    return 126, 127
+
+
+def with_lanes(values, lane, offset, first_column, second_column):
+    one, two = spare_lanes(offset)
+    inside = (lane >= offset) & (lane < offset + HEAD_DIM)
+    kept = jnp.where(inside, values, 0)
+    kept = jnp.where(lane == one, first_column, kept)
+    return jnp.where(lane == two, second_column, kept)
+
+
+def only_head(values, lane, offset):
+    inside = (lane >= offset) & (lane < offset + HEAD_DIM)
+    return jnp.where(inside, values, 0)
+
+
+def row_columns(kind):
+    image = kind == 0
+    padding = (kind == 1) | (kind == 2)
+    low = jnp.bfloat16
+    image_query = jnp.where(image, 1.0, 0.0).astype(low)
+    other_query = jnp.where(image, 0.0, 1.0).astype(low)
+    image_key = jnp.where(image, 0.0, -1e30).astype(low)
+    padding_key = jnp.where(padding, 0.0, -1e30).astype(low)
+    return image_query, other_query, image_key, padding_key
+
+
+def dot_last(left, right):
+    return lax.dot_general(left, right, (((1,), (1,)), ((), ())), preferred_element_type=jnp.float32)
+
+
+def dot_first(left, right):
+    return lax.dot_general(left, right, (((0,), (0,)), ((), ())), preferred_element_type=jnp.float32)
+
+
+def forward_kernel(heads, width, block, kind_ref, block_kind_ref, qkv_ref, query_ref, out_ref, logsum_ref, keys_ref, values_ref, total_ref, log_ref):
+    step = pl.program_id(0)
+    scale = HEAD_DIM ** (-0.5) * LOG2E
+
+    @pl.when(step == 0)
+    def prepare():
+        keys_ref[:, :width] = qkv_ref[:, width : 2 * width]
+        values_ref[:, :width] = qkv_ref[:, 2 * width :]
+        if keys_ref.shape[1] > width:
+            blank = jnp.zeros((keys_ref.shape[0], keys_ref.shape[1] - width), keys_ref.dtype)
+            keys_ref[:, width:] = blank
+            values_ref[:, width:] = blank
+
+    rows = keys_ref.shape[0]
+    _, _, image_key, padding_key = row_columns(kind_ref[...])
+    image_query, other_query, _, _ = row_columns(block_kind_ref[...])
+    total_ref[...] = jnp.zeros_like(total_ref)
+    log_ref[...] = jnp.zeros_like(log_ref)
+    for head in range(heads):
+        offset, first, last = head_window(head, width)
+        lane = lax.broadcasted_iota(jnp.int32, (rows, last - first), 1)
+        lane_q = lax.broadcasted_iota(jnp.int32, (block, last - first), 1)
+        query = with_lanes(query_ref[:, first:last], lane_q, offset, image_query, other_query)
+        keys = with_lanes(keys_ref[:, first:last], lane, offset, image_key, padding_key)
+        values = only_head(values_ref[:, first:last], lane, offset)
+        scores = dot_last(query, keys)
+        peak = jnp.max(scores, axis=1, keepdims=True)
+        expo = jnp.exp2((scores - peak) * scale)
+        total = jnp.sum(expo, axis=1, keepdims=True)
+        mixed = jnp.dot(expo.astype(jnp.bfloat16), values, preferred_element_type=jnp.float32)
+        total_ref[:, first:last] += mixed * (1.0 / total)
+        logsum = peak * scale + jnp.log2(total)
+        lane_h = lax.broadcasted_iota(jnp.int32, log_ref.shape, 1)
+        log_ref[...] = jnp.where(lane_h == head, logsum, log_ref[...])
+    out_ref[...] = total_ref[...].astype(out_ref.dtype)
+    logsum_ref[...] = jnp.transpose(log_ref[...])[: logsum_ref.shape[0], :]
+
+
+def attention_forward(qkv, kind):
+    rows, three = qkv.shape
+    width = three // 3
+    heads = width // HEAD_DIM
+    block = 256
+    padded = -(-width // 128) * 128
+    return pl.pallas_call(
+        functools.partial(forward_kernel, heads, width, block),
+        grid=(rows // block,),
+        in_specs=[
+            pl.BlockSpec((rows, 1), lambda i: (0, 0)),
+            pl.BlockSpec((block, 1), lambda i: (i, 0)),
+            pl.BlockSpec((rows, three), lambda i: (0, 0)),
+            pl.BlockSpec((block, three), lambda i: (i, 0)),
+        ],
+        out_specs=[
+            pl.BlockSpec((block, width), lambda i: (i, 0)),
+            pl.BlockSpec((8, block), lambda i: (0, i)),
+        ],
+        out_shape=[
+            jax.ShapeDtypeStruct((rows, width), jnp.bfloat16),
+            jax.ShapeDtypeStruct((8, rows), jnp.float32),
+        ],
+        scratch_shapes=[
+            pltpu.VMEM((rows, padded), jnp.bfloat16),
+            pltpu.VMEM((rows, padded), jnp.bfloat16),
+            pltpu.VMEM((block, width), jnp.float32),
+            pltpu.VMEM((block, 128), jnp.float32),
+        ],
+        compiler_params=pltpu.CompilerParams(vmem_limit_bytes=VMEM_BYTES),
+        cost_estimate=pl.CostEstimate(flops=heads * 4 * rows * rows * 256, bytes_accessed=rows * three * 4, transcendentals=heads * rows * rows),
+        name="attn_fwd",
+    )(kind, kind, qkv, qkv)
+
+
+def backward_kernel(heads, width, block, kind_ref, block_kind_ref, qkv_ref, query_ref, grad_ref, logsum_ref, out_ref, keys_ref, values_ref, key_sum, value_sum, query_sum):
+    step = pl.program_id(0)
+    last_step = pl.num_programs(0) - 1
+    scale = HEAD_DIM ** (-0.5) * LOG2E
+    score_scale = HEAD_DIM ** (-0.5)
+
+    @pl.when(step == 0)
+    def prepare():
+        keys_ref[:, :width] = qkv_ref[:, width : 2 * width]
+        values_ref[:, :width] = qkv_ref[:, 2 * width :]
+        if keys_ref.shape[1] > width:
+            blank = jnp.zeros((keys_ref.shape[0], keys_ref.shape[1] - width), keys_ref.dtype)
+            keys_ref[:, width:] = blank
+            values_ref[:, width:] = blank
+        key_sum[...] = jnp.zeros_like(key_sum)
+        value_sum[...] = jnp.zeros_like(value_sum)
+
+    rows = keys_ref.shape[0]
+    _, _, image_key, padding_key = row_columns(kind_ref[...])
+    image_query, other_query, _, _ = row_columns(block_kind_ref[...])
+    query_sum[...] = jnp.zeros_like(query_sum)
+    for head in range(heads):
+        offset, first, last = head_window(head, width)
+        lane = lax.broadcasted_iota(jnp.int32, (rows, last - first), 1)
+        lane_q = lax.broadcasted_iota(jnp.int32, (block, last - first), 1)
+        query = only_head(query_ref[:, first:last], lane_q, offset)
+        query_biased = with_lanes(query, lane_q, offset, image_query, other_query)
+        keys = only_head(keys_ref[:, first:last], lane, offset)
+        keys_biased = with_lanes(keys, lane, offset, image_key, padding_key)
+        values = values_ref[:, first:last]
+        grad = only_head(grad_ref[:, first:last], lane_q, offset)
+        scores = dot_last(keys_biased, query_biased)
+        probs = jnp.exp2(scores * scale - logsum_ref[head : head + 1, :])
+        grad_probs = dot_last(values, grad)
+        weighted = probs * grad_probs
+        centre = jnp.sum(weighted, axis=0, keepdims=True)
+        grad_scores = (weighted - probs * centre).astype(jnp.bfloat16)
+        value_sum[:, first:last] += jnp.dot(probs.astype(jnp.bfloat16), grad, preferred_element_type=jnp.float32)
+        key_sum[:, first:last] += jnp.dot(grad_scores, query, preferred_element_type=jnp.float32)
+        query_sum[:, first:last] += dot_first(grad_scores, keys)
+    low = out_ref.dtype
+    out_ref[pl.ds(step * block, block), :width] = (query_sum[...] * score_scale).astype(low)
+
+    @pl.when(step == last_step)
+    def finish():
+        out_ref[:, width : 2 * width] = (key_sum[...] * score_scale).astype(low)
+        out_ref[:, 2 * width :] = value_sum[...].astype(low)
+
+
+def attention_backward(qkv, kind, grad, logsum):
+    rows, three = qkv.shape
+    width = three // 3
+    heads = width // HEAD_DIM
+    block = 256
+    padded = -(-width // 128) * 128
+    return pl.pallas_call(
+        functools.partial(backward_kernel, heads, width, block),
+        grid=(rows // block,),
+        in_specs=[
+            pl.BlockSpec((rows, 1), lambda i: (0, 0)),
+            pl.BlockSpec((block, 1), lambda i: (i, 0)),
+            pl.BlockSpec((rows, three), lambda i: (0, 0)),
+            pl.BlockSpec((block, three), lambda i: (i, 0)),
+            pl.BlockSpec((block, width), lambda i: (i, 0)),
+            pl.BlockSpec((8, block), lambda i: (0, i)),
+        ],
+        out_specs=pl.BlockSpec((rows, three), lambda i: (0, 0)),
+        out_shape=jax.ShapeDtypeStruct((rows, three), jnp.bfloat16),
+        scratch_shapes=[
+            pltpu.VMEM((rows, padded), jnp.bfloat16),
+            pltpu.VMEM((rows, padded), jnp.bfloat16),
+            pltpu.VMEM((rows, width), jnp.float32),
+            pltpu.VMEM((rows, width), jnp.float32),
+            pltpu.VMEM((block, width), jnp.float32),
+        ],
+        compiler_params=pltpu.CompilerParams(vmem_limit_bytes=VMEM_BYTES),
+        cost_estimate=pl.CostEstimate(flops=heads * 10 * rows * rows * 256, bytes_accessed=rows * three * 6, transcendentals=heads * rows * rows),
+        name="attn_bwd",
+    )(kind, kind, qkv, qkv, grad, logsum)
+
+
+PATCHES = 729
+AXES = ("dp", "tensor")
+
+
+def dual_kernel(spot_ref, left_one, left_two, right_one, right_two, near, *far):
+    step = pl.program_id(0)
+    side = spot_ref[0] ^ step
+    depth, _, high, rows = left_one.shape
+    total = None
+    for left, right in ((left_one, right_one), (left_two, right_two)):
+        strip = left[:, pl.ds(side, 1)].reshape(depth * high, rows)
+        product = jnp.dot(strip, right[...], preferred_element_type=jnp.float32)
+        total = product if total is None else total + product
+    total = total.astype(near.dtype).reshape(depth, high, -1)
+
+    @pl.when(step == 0)
+    def write_near():
+        near[...] = total
+
+    @pl.when(step == 1)
+    def write_far():
+        start = 0
+        for out in far:
+            out[...] = total[start : start + out.shape[0]]
+            start += out.shape[0]
+
+
+def dual_product(x_at, left_one, left_two, right_one, right_two, sizes):
+    depth, _, high, rows = left_one.shape
+    columns = right_one.shape[1]
+    left = pl.BlockSpec(left_one.shape, lambda i: (0, 0, 0, 0))
+    right = pl.BlockSpec((rows, columns), lambda i: (0, 0))
+    return pl.pallas_call(
+        dual_kernel,
+        grid=(2,),
+        in_specs=[pl.BlockSpec(memory_space=pltpu.SMEM), left, left, right, right],
+        out_specs=[pl.BlockSpec((size, high, columns), lambda i: (0, 0, 0)) for size in sizes],
+        out_shape=[jax.ShapeDtypeStruct((size, high, columns), jnp.bfloat16) for size in sizes],
+        compiler_params=pltpu.CompilerParams(vmem_limit_bytes=VMEM_BYTES),
+        cost_estimate=pl.CostEstimate(
+            flops=8 * depth * high * rows * columns,
+            bytes_accessed=4 * rows * (2 * depth * high + columns) + 4 * depth * high * columns,
+            transcendentals=0,
+        ),
+        name="weight_grad",
+    )(x_at, left_one, left_two, right_one, right_two)
+
+
+class Grid:
+    def __init__(self, depth):
+        self.depth = depth
+        dp_at = lax.axis_index("dp")
+        self.y = lax.axis_index("tensor")
+        self.c = dp_at % 2
+        self.x = dp_at // 2 % 2
+        self.z = dp_at // 4
+
+    def move(self, values, where):
+        pairs = []
+        for z in range(self.depth):
+            for x in range(2):
+                for c in range(2):
+                    for y in range(2):
+                        to_z, to_x, to_c, to_y = where(z, x, c, y)
+                        pairs.append(
+                            (
+                                ((z * 2 + x) * 2 + c) * 2 + y,
+                                ((to_z * 2 + to_x) * 2 + to_c) * 2 + to_y,
+                            )
+                        )
+        return lax.ppermute(values, AXES, pairs)
+
+    def over_x(self, values):
+        return self.move(values, lambda z, x, c, y: (z, 1 - x, c, y))
+
+    def over_y(self, values):
+        return self.move(values, lambda z, x, c, y: (z, x, c, 1 - y))
+
+    def over_core(self, values):
+        return self.move(values, lambda z, x, c, y: (z, x, 1 - c, y))
+
+    def along_z(self, values, hops):
+        return self.move(values, lambda z, x, c, y: ((z + hops) % self.depth, x, c, y))
+
+    def across_z(self, values, bit):
+        return self.move(values, lambda z, x, c, y: (z ^ bit, x, c, y))
+
+    def spread(self, block):
+        width = block.shape[1] // 2
+        mine = lax.dynamic_slice_in_dim(block, self.c * width, width, 1)
+        theirs = self.over_core(
+            lax.dynamic_slice_in_dim(block, (1 - self.c) * width, width, 1)
+        )
+        first = jnp.where(self.c == 0, mine, theirs)
+        second = jnp.where(self.c == 0, theirs, mine)
+        return jnp.concatenate([first, second])
+
+    def gather(self, block):
+        depth = self.depth
+        half = depth // 2
+        block = self.spread(block)[None]
+        came = [block] + [self.along_z(block, hops) for hops in range(1, depth)]
+        came = came[::-1]
+        own = lax.dynamic_slice_in_dim(
+            jnp.concatenate(came + came[:-1]), depth - 1 - self.z, depth
+        )
+        beside = self.over_x(own)
+        across = self.over_y(own)
+        corner = [self.over_y(beside[:half]), self.over_x(across[half:])]
+        groups = [(own, beside), (across, jnp.concatenate(corner))]
+        other = [
+            (self.over_core(own), self.over_core(beside)),
+            (
+                self.over_core(across),
+                jnp.concatenate([self.over_core(corner[0]), self.over_core(corner[1])]),
+            ),
+        ]
+        return [groups[0], other[0], groups[1], other[1]]
+
+    def assemble(self, group):
+        near, far = group
+        first = jnp.where(self.x == 0, near, far)
+        second = jnp.where(self.x == 0, far, near)
+        return jnp.stack([first, second], axis=1).reshape(-1, near.shape[-1])
+
+    def scatter(self, own, beside, across, corner):
+        depth = self.depth
+        half = depth // 2
+        low = jnp.bfloat16
+        wide = jnp.float32
+
+        def add(one, two):
+            return (one.astype(wide) + two.astype(wide)).astype(low)
+
+        corner_one = self.over_x(corner[0])
+        corner_two = self.over_y(corner[1])
+        beside = jnp.concatenate([beside[:half], add(beside[half:], corner_two)])
+        across = jnp.concatenate([add(across[:half], corner_one), across[half:]])
+        total = (
+            own.astype(wide)
+            + self.over_x(beside).astype(wide)
+            + self.over_y(across).astype(wide)
+        ).astype(low)
+        result = lax.dynamic_index_in_dim(total, self.z, 0, keepdims=False).astype(wide)
+        for hops in range(1, depth):
+            part = lax.dynamic_index_in_dim(total, (self.z + hops) % depth, 0, keepdims=False)
+            result = result + self.along_z(part, hops).astype(wide)
+        shard = result.shape[0] // 2
+        mine = lax.dynamic_slice_in_dim(result, self.c * shard, shard)
+        theirs = self.over_core(
+            lax.dynamic_slice_in_dim(result, (1 - self.c) * shard, shard)
+        )
+        first = jnp.where(self.c == 0, mine, theirs)
+        second = jnp.where(self.c == 0, theirs, mine)
+        return jnp.stack([first, second])
+
+    def reduce_all(self, values):
+        values = values + self.over_core(values)
+        values = values + self.over_x(values)
+        values = values + self.over_y(values)
+        bit = 1
+        while bit < self.depth:
+            values = values + self.across_z(values, bit)
+            bit *= 2
+        return values
+
+
+def norm_parts(values):
+    centre = values - jnp.mean(values, axis=1, keepdims=True)
+    spread = jnp.mean(centre * centre, axis=1, keepdims=True)
+    root = lax.rsqrt(spread + layer_eps)
+    return centre * root, root
+
+
+def norm_back(unit, root, gain, grad):
+    scaled = grad * gain
+    mean_one = jnp.mean(scaled, axis=1, keepdims=True)
+    mean_two = jnp.mean(scaled * unit, axis=1, keepdims=True)
+    return (
+        root * (scaled - mean_one - unit * mean_two),
+        jnp.sum(grad * unit, axis=0),
+        jnp.sum(grad, axis=0),
+    )
+
+
+def gelu_slope(values):
+    inner = jnp.tanh(gelu_scale * (values + 0.044715 * values * values * values))
+    slope = gelu_scale * (1.0 + 3.0 * 0.044715 * values * values)
+    return 0.5 * (1.0 + inner) + 0.5 * values * (1.0 - inner * inner) * slope
+
+
+def image_shards(
+    depth,
+    layer_input,
+    token_image,
+    cotangent,
+    ln1_gain,
+    ln1_bias,
+    w_qkv,
+    qv_bias,
+    w_out,
+    out_bias,
+    ln2_gain,
+    ln2_bias,
+    w_fc1,
+    fc1_bias,
+    w_fc2,
+    fc2_bias,
+):
+    low = jnp.bfloat16
+    wide = jnp.float32
+    grid = Grid(depth)
+    rows, full_width = layer_input.shape
+    shard = ln1_gain.shape[0]
+    head_width = qv_bias.shape[1]
+    ff_width = fc1_bias.shape[0]
+    padded = -(-(rows + 1) // 256) * 256
+
+    here = grid.y
+    mine = lax.dynamic_slice_in_dim(token_image, here * rows, rows)
+    theirs = lax.dynamic_slice_in_dim(token_image, (1 - here) * rows, rows)
+    places = lax.iota(jnp.int32, rows)
+    stray = mine == 1 - here
+    stray_here = jnp.any(stray)
+    stray_there = jnp.any(theirs == here)
+    blank = mine == IMAGES
+    first_blank = jnp.min(jnp.where(blank, places, rows - 1))
+    last_blank = jnp.max(jnp.where(blank, places, 0))
+    swap_at = jnp.where(stray_here, jnp.max(jnp.where(stray, places, 0)), first_blank)
+    swapped = stray_here | stray_there
+    blank_at = jnp.where(stray_here, swap_at, last_blank)
+
+    def one_row(values, at):
+        return lax.dynamic_slice_in_dim(values, at, 1)
+
+    sent = jnp.concatenate(
+        [one_row(layer_input, swap_at), one_row(cotangent, swap_at), one_row(layer_input, last_blank)]
+    )
+    came = grid.over_y(sent)
+    other_blank = jnp.where(stray_there, sent[0:1], came[2:3])
+    spread_rows = lax.broadcasted_iota(jnp.int32, (padded, 1), 0)
+    at_swap = (spread_rows == swap_at) & swapped
+
+    def stretch(values):
+        return jnp.pad(values, ((0, padded - rows), (0, 0)))
+
+    input_rows = jnp.where(at_swap, came[0:1], stretch(layer_input))
+    input_rows = jnp.where(spread_rows == rows, other_blank, input_rows)
+    grad_low = jnp.where(at_swap, came[1:2], stretch(cotangent))
+    grad_low = jnp.where(spread_rows == blank_at, 0, grad_low).astype(low)
+    kind = jnp.where(spread_rows > rows, 3, jnp.where(spread_rows == rows, 2, 0))
+    kind = jnp.where(spread_rows == blank_at, 1, kind)
+    input_rows, grad_low = lax.optimization_barrier((input_rows, grad_low))
+
+    quarter = head_width // 2
+    group_width = 4 * quarter
+    ff_padding = 2 * group_width - ff_width
+    vectors = jnp.stack([ln1_gain, ln1_bias, out_bias, ln2_gain, ln2_bias, fc2_bias])
+    vectors = lax.all_gather(vectors, "dp", axis=1, tiled=True).astype(wide)
+    gain_one, shift_one, out_shift, gain_two, shift_two, fc2_shift = [
+        vectors[i : i + 1] for i in range(6)
+    ]
+    biases = jnp.concatenate([qv_bias.reshape(-1), fc1_bias])
+    biases = jnp.pad(biases, (0, -biases.shape[0] % 128)).reshape(-1, 128)
+    other_biases = grid.over_y(biases).reshape(-1)
+
+    def ordered(first, second):
+        return jnp.where(grid.c == 0, first, second), jnp.where(grid.c == 0, second, first)
+
+    qv_groups, fc1_groups = [], []
+    for flat in (biases.reshape(-1), other_biases):
+        flat = flat.astype(wide)
+        pair = flat[: 2 * head_width].reshape(2, 2, quarter)
+        none = jnp.zeros((quarter,), wide)
+        qv_groups += ordered(
+            *[jnp.concatenate([pair[0, i], none, pair[1, i]]) for i in range(2)]
+        )
+        hidden_bias = flat[2 * head_width : 2 * head_width + ff_width]
+        hidden_bias = jnp.pad(hidden_bias, (0, ff_padding))
+        fc1_groups += ordered(hidden_bias[:group_width], hidden_bias[group_width:])
+
+    sources = [w_qkv[0], w_qkv[1], w_qkv[2], w_out.T]
+    first_block = jnp.concatenate(
+        [values[:, i * quarter : (i + 1) * quarter] for i in range(2) for values in sources],
+        axis=1,
+    )
+    second_block = jnp.pad(w_fc1, ((0, 0), (0, ff_padding)))
+    third_block = jnp.pad(w_fc2.T, ((0, 0), (0, ff_padding)))
+    attn_weights = [grid.assemble(group) for group in grid.gather(first_block)]
+    up_weights = [grid.assemble(group) for group in grid.gather(second_block)]
+    down_weights = [grid.assemble(group) for group in grid.gather(third_block)]
+
+    row_values = input_rows.astype(wide)
+    unit_one, root_one = norm_parts(row_values)
+    normed = (unit_one * gain_one + shift_one).astype(low)
+    resid = row_values + out_shift
+    qkv, mixed, logsums = [], [], []
+    groups = range(4)
+    inner = 3 * quarter
+    for side in groups:
+        projected = jnp.dot(normed, attn_weights[side][:, :inner], preferred_element_type=wide)
+        qkv.append((projected + qv_groups[side]).astype(low))
+        side_mixed, logsum = attention_forward(qkv[side], kind)
+        mixed.append(side_mixed)
+        logsums.append(logsum)
+    out_weights = [weights[:, inner:] for weights in attn_weights]
+    for side in groups:
+        resid = resid + contract_cols(mixed[side], out_weights[side])
+
+    unit_two, root_two = norm_parts(resid)
+    normed_two = (unit_two * gain_two + shift_two).astype(low)
+    hidden = [
+        jnp.dot(normed_two, up_weights[side], preferred_element_type=wide) + fc1_groups[side]
+        for side in groups
+    ]
+    active = [gelu_tanh(values).astype(low) for values in hidden]
+
+    def turned(values):
+        own = values.T.reshape(depth, 2, 2 * shard, padded)
+        return own, grid.over_core(own)
+
+    half = depth // 2
+    x_spot = grid.x.reshape(1)
+
+    def summed(left, sides):
+        given = grid.over_core(jnp.stack([sides[1], sides[3]]))
+        own, beside = dual_product(x_spot, *left, sides[0], given[0], (depth, depth))
+        across, corner_one, corner_two = dual_product(
+            x_spot, *left, sides[2], given[1], (depth, half, half)
+        )
+        return own, beside, across, (corner_one, corner_two)
+
+    fc2_piece = grid.scatter(*summed(turned(grad_low), active))
+
+    grad_hidden = []
+    for side in groups:
+        grad_active = jnp.dot(grad_low, down_weights[side], preferred_element_type=wide)
+        grad_hidden.append((grad_active * gelu_slope(hidden[side])).astype(low))
+    fc1_piece = grid.scatter(*summed(turned(normed_two), grad_hidden))
+    layer_rows = resid + fc2_shift
+    grad_normed_two = 0.0
+    for side in groups:
+        grad_normed_two = grad_normed_two + contract_cols(grad_hidden[side], up_weights[side])
+        layer_rows = layer_rows + contract_cols(active[side], down_weights[side])
+    layer_rows = layer_rows.astype(low)
+
+    resid_part, ln2_gain_sum, ln2_bias_sum = norm_back(
+        unit_two, root_two, gain_two, grad_normed_two
+    )
+    grad_resid = grad_low.astype(wide) + resid_part
+    resid_low = grad_resid.astype(low)
+    grad_qkv = []
+    for side in groups:
+        grad_attn = jnp.dot(resid_low, out_weights[side], preferred_element_type=wide).astype(low)
+        grad_qkv.append(attention_backward(qkv[side], kind, grad_attn, logsums[side]))
+    qkv_sums = summed(turned(normed), grad_qkv)
+    out_sums = summed(turned(resid_low), mixed)
+    joined = [
+        jnp.concatenate([one, two], axis=2)
+        for one, two in zip(qkv_sums[:3] + qkv_sums[3], out_sums[:3] + out_sums[3])
+    ]
+    attn_piece = grid.scatter(*joined[:3], joined[3:])
+    grad_normed = 0.0
+    for side in groups:
+        grad_normed = grad_normed + contract_cols(grad_qkv[side], attn_weights[side][:, :inner])
+    input_part, ln1_gain_sum, ln1_bias_sum = norm_back(unit_one, root_one, gain_one, grad_normed)
+    input_grad = grad_resid + input_part
+
+    returned = (
+        grid.over_y(one_row(layer_rows, swap_at)),
+        grid.over_y(one_row(input_grad, swap_at)),
+    )
+    layer_output = jnp.where(at_swap, returned[0], layer_rows)[:rows]
+    input_grad = jnp.where(at_swap, returned[1], input_grad)[:rows]
+
+    def column_sum(values):
+        return jnp.sum(values.astype(wide), axis=0)
+
+    def absolute(sums):
+        grouped = jnp.stack(sums).reshape(2, 2, -1)
+        grouped = jnp.where(here == 0, grouped, grouped[::-1])
+        return jnp.where(grid.c == 0, grouped, grouped[:, ::-1])
+
+    qkv_totals = absolute([column_sum(values) for values in grad_qkv])
+    qkv_totals = qkv_totals.reshape(2, 2, 3, quarter)[:, :, 0::2].transpose(0, 2, 1, 3)
+    fc1_totals = absolute([column_sum(values) for values in grad_hidden]).reshape(2, -1)
+    flat = jnp.concatenate(
+        [
+            ln1_gain_sum,
+            ln1_bias_sum,
+            column_sum(resid_low),
+            ln2_gain_sum,
+            ln2_bias_sum,
+            column_sum(grad_low),
+            qkv_totals.reshape(-1),
+            fc1_totals[:, :ff_width].reshape(-1),
+        ]
+    )
+    length = flat.shape[0]
+    lines = -(-length // 1024) * 8
+    flat = jnp.pad(flat, (0, lines * 128 - length)).reshape(lines, 128)
+    flat = grid.reduce_all(flat).reshape(-1)
+    row_total = flat[: 6 * full_width].reshape(6, full_width)
+    row_piece = lax.dynamic_slice_in_dim(row_total, lax.axis_index("dp") * shard, shard, 1)
+    start = 6 * full_width
+    qv_piece = lax.dynamic_slice_in_dim(flat, start + here * 2 * head_width, 2 * head_width)
+    start = start + 4 * head_width
+    fc1_bias_piece = lax.dynamic_slice_in_dim(flat, start + here * ff_width, ff_width)
+    heads_piece = attn_piece.reshape(2, shard, 4, quarter).transpose(2, 1, 0, 3)
+    heads_piece = heads_piece.reshape(4, shard, head_width)
+
+    def whole_columns(pair):
+        return jnp.concatenate([pair[0], pair[1][:, : group_width - ff_padding]], axis=1)
+
+    return (
+        layer_output,
+        input_grad,
+        row_piece[0],
+        row_piece[1],
+        heads_piece[:3],
+        qv_piece.reshape(2, head_width),
+        heads_piece[3].T,
+        row_piece[2],
+        row_piece[3],
+        row_piece[4],
+        whole_columns(fc1_piece),
+        fc1_bias_piece,
+        whole_columns(fc2_piece).T,
+        row_piece[5],
+    )
+
+
+def fits_images(mesh):
+    groups = mesh.shape["dp"] // 4
+    return (
+        mesh.shape["tensor"] == IMAGES
+        and mesh.shape["dp"] % 4 == 0
+        and groups >= 2
+        and groups & (groups - 1) == 0
+    )
+
+
 def solution(mesh):
     in_specs = (
         P(("dp", "tensor"), None),
@@ -412,4 +1059,11 @@
         P("tensor", "dp"),
         P("dp"),
     )
-    return jax.shard_map(shards, mesh=mesh, in_specs=in_specs, out_specs=out_specs, check_vma=False)
+
+    def body(*arrays):
+        slots = arrays[1].shape[0]
+        if fits_images(mesh) and slots == IMAGES * (PATCHES + 1):
+            return image_shards(mesh.shape["dp"] // 4, *arrays)
+        return shards(*arrays)
+
+    return jax.shard_map(body, mesh=mesh, in_specs=in_specs, out_specs=out_specs, check_vma=False)

time: 2300 us -> 842 us (0.37)
  waiting for transfers between devices: 855 us -> 226 us
  blocking collectives: 536 us -> 22.1 us
  matrix products: 418 us -> 115 us
  local copies, waits for them, and re-layouts: 335 us -> 106 us
  Pallas kernels: 0 us -> 153 us
  starting transfers between devices: 14.8 us -> 88.7 us
    all_gather x14 -> x0, waiting for transfers between devices: 523 us -> none  [the longest x2 105 us: forward_pass(): lax.all_gather(w_fc1, 'dp', axis=0, tiled=True)]
    unnamed x7 -> x0, blocking collectives: 493 us -> none
    unnamed x27 -> x0, waiting for transfers between devices: 332 us -> none
    dot_general x91 -> x16, matrix products: 292 us -> 57.6 us  [the longest x4 19.2 us: image_shards(): jnp.dot(grad_low, down_weights[side], preferred_element_type=wide)]
    ppermute x0 -> x80, waiting for transfers between devices: none -> 226 us  [move(): return lax.ppermute(values, AXES, pairs)]
    pallas_call x0 -> x16, Pallas kernels: none -> 153 us  [the longest x8 67.8 us: dual_product(): pl.pallas_call(dual_kernel, grid=(2,), in_specs=[pl.BlockSpec(memory_spac...]
    while x376 -> x0, local copies, waits for them, and re-layouts: 90 us -> none
    ppermute x0 -> x80, starting transfers between devices: none -> 88.7 us  [move(): return lax.ppermute(values, AXES, pairs)]
  transfers between devices with their start and end apart: 23 -> 80, of which waited for: 20 -> 24; matrix products, arithmetic and copies ran while one was open for 26% -> 27% of each run, Pallas kernels for 0% -> 17%
where the time goes in v1:
time: 842 us; the launch traced here: 830 us
  waiting for transfers between devices  226 us (27%)
  Pallas kernels  153 us (18%)
  matrix products  115 us (14%)
  other arithmetic  109 us (13%)
  local copies, waits for them, and re-layouts  106 us (13%)
  starting transfers between devices  88.7 us (11%)
  blocking collectives  22.1 us (3%)
  between operations  10.3 us (1%)
    ppermute x80, waiting for transfers between devices, move(): return lax.ppermute(values, AXES, pairs)  226 us
    ppermute x80, starting transfers between devices, move(): return lax.ppermute(values, AXES, pairs)  88.7 us
    pallas_call x8, Pallas kernels, dual_product(): pl.pallas_call(dual_kernel, grid=(2,), in_specs=[pl.BlockSpec(memory_spac...  67.8 us
    dot_general x16, matrix products, contract_cols(): lax.dot_general(left, right, (((1,), (1,)), ((), ())), preferred_element_...  57.7 us
    pallas_call x4, Pallas kernels, attention_backward(): pl.pallas_call(functools.partial(backward_kernel, heads, width, block), g...  53.6 us
    pallas_call x4, Pallas kernels, attention_forward(): pl.pallas_call(functools.partial(forward_kernel, heads, width, block), gr...  31.7 us
    another operation x24, other arithmetic, assemble(): return jnp.stack([first, second], axis=1).reshape(-1, near.shape[-1])  28.1 us
    all_gather x1, blocking collectives, image_shards(): vectors = lax.all_gather(vectors, 'dp', axis=1, tiled=True).astype(wide)  22.1 us
  transfers between devices with their start and end apart: 80, of which 24 were waited for; matrix products, arithmetic and copies ran while one was open for 27% of the time, Pallas kernels for 17%

profile of v1, /device:TPU:0, one launch (start us, length us, event | category | flops | bytes accessed | tf_op | source)
XLA Modules:
  0.0 830.5 jit_solution(8099487629422008504)
XLA Ops:
  22.9 22.1 %all-gather = bf16[16,72,6]{1,2,0:T(8,128)(2,1)S(1)} all-gather(bf16[1,72,6]{1,2,0:T(8,128)(2,1)S(1)} %bitcast.296), channel_id=1, replica_groups=mesh['dp'=16,'tensor'=2] {'dp'}, dimensions={0}, use_global_device_ids=true | all-gather | bytes 14688 | tf_op jit(solution)/shard_map/all_gather | solution.py:844
  66.9 13.0 %collective-permute-start.18 = (bf16[1,144,1152]{2,1,0:T(8,128)(2,1)S(1)}, bf16[1,144,1152]{2,1,0:T(8,128)(2,1)S(1)}, u32[]{:S(2)}, u32[]{:S(2)}) collective-permute-start(bf16[1,144,1152]{2,1,0:T(8,128)(2,1)S(1)} %maximum_bitcast_fusion.3), channel_id=1, source_target_pairs={{0,8},{1,9},{2,10},{3,11},{4,12},{5,13},{6,14},{7,15},{8,16},{9,17... | collective-permute-start | bytes 995336 | tf_op jit(solution)/shard_map/ppermute | solution.py:656
  79.9 20.7 %collective-permute-done.3 = bf16[1,144,1152]{2,1,0:T(8,128)(2,1)S(1)} collective-permute-done((bf16[1,144,1152]{2,1,0:T(8,128)(2,1)S(1)}, bf16[1,144,1152]{2,1,0:T(8,128)(2,1)S(1)}, u32[]{:S(2)}, u32[]{:S(2)}) %collective-permute-start.3) | collective-permute-done | bytes 331808 | tf_op jit(solution)/shard_map/ppermute | solution.py:656
  110.2 18.9 %collective-permute-done.17 = bf16[1,144,1152]{2,1,0:T(8,128)(2,1)S(1)} collective-permute-done((bf16[1,144,1152]{2,1,0:T(8,128)(2,1)S(1)}, bf16[1,144,1152]{2,1,0:T(8,128)(2,1)S(1)}, u32[]{:S(2)}, u32[]{:S(2)}) %collective-permute-start.17) | collective-permute-done | bytes 331808 | tf_op jit(solution)/shard_map/ppermute | solution.py:656
  132.3 10.5 %collective-permute-done.22 = bf16[1,144,1152]{2,1,0:T(8,128)(2,1)S(1)} collective-permute-done((bf16[1,144,1152]{2,1,0:T(8,128)(2,1)S(1)}, bf16[1,144,1152]{2,1,0:T(8,128)(2,1)S(1)}, u32[]{:S(2)}, u32[]{:S(2)}) %collective-permute-start.22) | collective-permute-done | bytes 331808 | tf_op jit(solution)/shard_map/ppermute | solution.py:656
  145.8 15.7 %collective-permute-done.5 = bf16[4,144,1152]{2,1,0:T(8,128)(2,1)} collective-permute-done((bf16[4,144,1152]{2,1,0:T(8,128)(2,1)}, bf16[4,144,1152]{2,1,0:T(8,128)(2,1)}, u32[]{:S(2)}, u32[]{:S(2)}) %collective-permute-start.5) | collective-permute-done | bytes 1327136 | tf_op jit(solution)/shard_map/ppermute | solution.py:656
  167.4 22.5 %collective-permute-done.19 = bf16[4,144,1152]{2,1,0:T(8,128)(2,1)S(1)} collective-permute-done((bf16[4,144,1152]{2,1,0:T(8,128)(2,1)}, bf16[4,144,1152]{2,1,0:T(8,128)(2,1)S(1)}, u32[]{:S(2)}, u32[]{:S(2)}) %collective-permute-start.19) | collective-permute-done | bytes 1327136 | tf_op jit(solution)/shard_map/ppermute | solution.py:656
  198.0 18.2 %collective-permute-done.24 = bf16[4,144,1152]{2,1,0:T(8,128)(2,1)S(1)} collective-permute-done((bf16[4,144,1152]{2,1,0:T(8,128)(2,1)}, bf16[4,144,1152]{2,1,0:T(8,128)(2,1)S(1)}, u32[]{:S(2)}, u32[]{:S(2)}) %collective-permute-start.24) | collective-permute-done | bytes 1327136 | tf_op jit(solution)/shard_map/ppermute | solution.py:656
  219.1 7.9 attn_fwd.4
  245.7 11.8 %collective-permute-done.30 = bf16[2,144,1152]{2,1,0:T(8,128)(2,1)} collective-permute-done((bf16[2,144,1152]{2,1,0:T(8,128)(2,1)S(1)}, bf16[2,144,1152]{2,1,0:T(8,128)(2,1)}, u32[]{:S(2)}, u32[]{:S(2)}) %collective-permute-start.30) | collective-permute-done | bytes 663584 | tf_op jit(solution)/shard_map/ppermute | solution.py:656
  259.8 10.8 %collective-permute-done.33 = bf16[2,144,1152]{2,1,0:T(8,128)(2,1)S(1)} collective-permute-done((bf16[2,144,1152]{2,1,0:T(8,128)(2,1)S(1)}, bf16[2,144,1152]{2,1,0:T(8,128)(2,1)S(1)}, u32[]{:S(2)}, u32[]{:S(2)}) %collective-permute-start.33) | collective-permute-done | bytes 663584 | tf_op jit(solution)/shard_map/ppermute | solution.py:656
  275.4 11.5 %collective-permute-done.34 = bf16[2,144,1152]{2,1,0:T(8,128)(2,1)} collective-permute-done((bf16[2,144,1152]{2,1,0:T(8,128)(2,1)S(1)}, bf16[2,144,1152]{2,1,0:T(8,128)(2,1)}, u32[]{:S(2)}, u32[]{:S(2)}) %collective-permute-start.34) | collective-permute-done | bytes 663584 | tf_op jit(solution)/shard_map/ppermute | solution.py:656
  297.2 7.9 attn_fwd.6
  326.5 7.8 attn_fwd.5
  341.6 8.2 attn_fwd.7
  431.1 13.3 %attn_bwd.4.right_one = bf16[768,864]{1,0:T(8,128)(2,1)} custom-call(s32[768,1]{1,0:T(8,128)} %select_select_fusion.2.kind_ref.block_kind_ref, s32[768,1]{1,0:T(8,128)} %select_select_fusion.2.kind_ref.block_kind_ref, bf16[768,864]{1,0:T(8,128)(2,1)} %add_convert_fusion.4.qkv_ref.query_ref, bf16[768,864]{1,0:T(8,128)(2,1)} %add_convert_fusion.4.qkv_ref.query_ref, ...), custom_call_target="tpu_custom_call" | custom-call | flops 6039797760 | bytes 3981312 | tf_op jit(solution)/shard_map/attn_bwd/pallas_call | solution.py:560
  476.2 13.2 %attn_bwd.5 = bf16[768,864]{1,0:T(8,128)(2,1)} custom-call(s32[768,1]{1,0:T(8,128)} %select_select_fusion.2.kind_ref.block_kind_ref, s32[768,1]{1,0:T(8,128)} %select_select_fusion.2.kind_ref.block_kind_ref, bf16[768,864]{1,0:T(8,128)(2,1)} %add_convert_fusion.3.qkv_ref.query_ref, bf16[768,864]{1,0:T(8,128)(2,1)} %add_convert_fusion.3.qkv_ref.query_ref, ...), custom_call_target="tpu_custom_call" | custom-call | flops 6039797760 | bytes 3981312 | tf_op jit(solution)/shard_map/attn_bwd/pallas_call | solution.py:560
  498.5 13.7 %attn_bwd.6.right_one = bf16[768,864]{1,0:T(8,128)(2,1)} custom-call(s32[768,1]{1,0:T(8,128)} %select_select_fusion.2.kind_ref.block_kind_ref, s32[768,1]{1,0:T(8,128)} %select_select_fusion.2.kind_ref.block_kind_ref, bf16[768,864]{1,0:T(8,128)(2,1)} %add_convert_fusion.2.qkv_ref.query_ref, bf16[768,864]{1,0:T(8,128)(2,1)} %add_convert_fusion.2.qkv_ref.query_ref, ...), custom_call_target="tpu_custom_call" | custom-call | flops 6039797760 | bytes 3981312 | tf_op jit(solution)/shard_map/attn_bwd/pallas_call | solution.py:560
  521.3 13.4 %attn_bwd.7 = bf16[768,864]{1,0:T(8,128)(2,1)} custom-call(s32[768,1]{1,0:T(8,128)} %select_select_fusion.2.kind_ref.block_kind_ref, s32[768,1]{1,0:T(8,128)} %select_select_fusion.2.kind_ref.block_kind_ref, bf16[768,864]{1,0:T(8,128)(2,1)} %add_convert_fusion.1.qkv_ref.query_ref, bf16[768,864]{1,0:T(8,128)(2,1)} %add_convert_fusion.1.qkv_ref.query_ref, ...), custom_call_target="tpu_custom_call" | custom-call | flops 6039797760 | bytes 3981312 | tf_op jit(solution)/shard_map/attn_bwd/pallas_call | solution.py:560
  617.5 8.6 %weight_grad.10 = (bf16[4,144,864]{2,1,0:T(8,128)(2,1)}, bf16[2,144,864]{2,1,0:T(8,128)(2,1)}, bf16[2,144,864]{2,1,0:T(8,128)(2,1)}) custom-call(s32[1]{0:T(128)} %bitcast.60.spot_ref, bf16[4,2,144,768]{3,2,1,0:T(8,128)(2,1)} %bitcast.62.left_one, bf16[4,2,144,768]{3,2,1,0:T(8,128)(2,1)} %collective-permute-done.48.left_two, ...), custom_call_target="tpu_custom_call" | custom-call | flops 3057647616 | bytes 8183808 | tf_op jit(solution)/shard_map/weight_grad/pallas_call | solution.py:618
  630.1 8.4 %weight_grad.8 = (bf16[4,144,864]{2,1,0:T(8,128)(2,1)}, bf16[4,144,864]{2,1,0:T(8,128)(2,1)}) custom-call(s32[1]{0:T(128)} %bitcast.60.spot_ref, bf16[4,2,144,768]{3,2,1,0:T(8,128)(2,1)} %bitcast.62.left_one, bf16[4,2,144,768]{3,2,1,0:T(8,128)(2,1)} %collective-permute-done.48.left_two, bf16[768,864]{1,0:T(8,128)(2,1)} %attn_bwd.4.right_one, ...), custom_call_target="tpu_custom_call" | custom-call | flops 3057647616 | bytes 8183808 | tf_op jit(solution)/shard_map/weight_grad/pallas_call | solution.py:618
  646.2 13.9 %collective-permute-done.52 = bf16[2,144,1152]{2,1,0:T(8,128)(2,1)S(1)} collective-permute-done((bf16[2,144,1152]{2,1,0:T(8,128)(2,1)S(1)}, bf16[2,144,1152]{2,1,0:T(8,128)(2,1)S(1)}, u32[]{:S(2)}, u32[]{:S(2)}) %collective-permute-start.52) | collective-permute-done | bytes 663584 | tf_op jit(solution)/shard_map/ppermute | solution.py:656
  667.4 10.0 %weight_grad.13 = (bf16[4,144,1152]{2,1,0:T(8,128)(2,1)}, bf16[2,144,1152]{2,1,0:T(8,128)(2,1)}, bf16[2,144,1152]{2,1,0:T(8,128)(2,1)}) custom-call(s32[1]{0:T(128)} %bitcast.60.spot_ref, bf16[4,2,144,768]{3,2,1,0:T(8,128)(2,1)} %bitcast.281, bf16[4,2,144,768]{3,2,1,0:T(8,128)(2,1)} %collective-permute-done.60.left_two, bf16[768,1152]{1,0:T(8,128)(2,1)} %copy-done.120, ...), custom_call_target="tpu_custom_call" | custom-call | flops 4076863488 | bytes 9732096 | tf_op jit(solution)/shard_map/weight_grad/pallas_call | solution.py:618
  679.3 9.8 %weight_grad.12 = (bf16[4,144,1152]{2,1,0:T(8,128)(2,1)}, bf16[4,144,1152]{2,1,0:T(8,128)(2,1)}) custom-call(s32[1]{0:T(128)} %bitcast.60.spot_ref, bf16[4,2,144,768]{3,2,1,0:T(8,128)(2,1)} %bitcast.282, bf16[4,2,144,768]{3,2,1,0:T(8,128)(2,1)} %collective-permute-done.60.left_two, bf16[768,1152]{1,0:T(8,128)(2,1)} %copy-done.118, ...), custom_call_target="tpu_custom_call" | custom-call | flops 4076863488 | bytes 9732096 | tf_op jit(solution)/shard_map/weight_grad/pallas_call | solution.py:618
  695.9 9.8 %weight_grad.15 = (bf16[4,144,1152]{2,1,0:T(8,128)(2,1)}, bf16[2,144,1152]{2,1,0:T(8,128)(2,1)}, bf16[2,144,1152]{2,1,0:T(8,128)(2,1)}) custom-call(s32[1]{0:T(128)} %bitcast.60.spot_ref, bf16[4,2,144,768]{3,2,1,0:T(8,128)(2,1)} %bitcast.94.left_one, bf16[4,2,144,768]{3,2,1,0:T(8,128)(2,1)} %collective-permute-done.70.left_two, ...), custom_call_target="tpu_custom_call" | custom-call | flops 4076863488 | bytes 9732096 | tf_op jit(solution)/shard_map/weight_grad/pallas_call | solution.py:618
  708.2 10.2 %weight_grad.14 = (bf16[4,144,1152]{2,1,0:T(8,128)(2,1)}, bf16[4,144,1152]{2,1,0:T(8,128)(2,1)}) custom-call(s32[1]{0:T(128)} %bitcast.60.spot_ref, bf16[4,2,144,768]{3,2,1,0:T(8,128)(2,1)} %bitcast.94.left_one, bf16[4,2,144,768]{3,2,1,0:T(8,128)(2,1)} %collective-permute-done.70.left_two, bf16[768,1152]{1,0:T(8,128)(2,1)} %get-tuple-element.195.right_one, ...), custom_call_target="tpu_custom_call" | custom-call | flops 4076863488 | bytes 9732096 | tf_op jit(solution)/shard_map/weight_grad/pallas_call | solution.py:618
  737.3 16.8 %collective-permute-done.57 = bf16[144,1152]{1,0:T(8,128)(2,1)S(1)} collective-permute-done((bf16[144,1152]{1,0:T(8,128)(2,1)S(1)}, bf16[144,1152]{1,0:T(8,128)(2,1)S(1)}, u32[]{:S(2)}, u32[]{:S(2)}) %collective-permute-start.57) | collective-permute-done | bytes 331808 | tf_op jit(solution)/shard_map/ppermute | solution.py:656
  774.2 8.8 %collective-permute-start.67 = (bf16[144,1152]{1,0:T(8,128)(2,1)S(1)}, bf16[144,1152]{1,0:T(8,128)(2,1)S(1)}, u32[]{:S(2)}, u32[]{:S(2)}) collective-permute-start(bf16[144,1152]{1,0:T(8,128)(2,1)S(1)} %get-tuple-element.145), channel_id=1, source_target_pairs={{0,16},{1,17},{2,18},{3,19},{4,20},{5,21},{6,22},{7,23},{8,24},{9,... | collective-permute-start | bytes 995336 | tf_op jit(solution)/shard_map/ppermute | solution.py:656
  783.0 7.5 collective-permute-done.75
  794.7 6.8 collective-permute-start.77
  801.5 16.6 %collective-permute-done.67 = bf16[144,1152]{1,0:T(8,128)(2,1)S(1)} collective-permute-done((bf16[144,1152]{1,0:T(8,128)(2,1)S(1)}, bf16[144,1152]{1,0:T(8,128)(2,1)S(1)}, u32[]{:S(2)}, u32[]{:S(2)}) %collective-permute-start.67) | collective-permute-done | bytes 331808 | tf_op jit(solution)/shard_map/ppermute | solution.py:656
  818.4 8.7 %collective-permute-done.77 = bf16[144,1152]{1,0:T(8,128)(2,1)S(1)} collective-permute-done((bf16[144,1152]{1,0:T(8,128)(2,1)S(1)}, bf16[144,1152]{1,0:T(8,128)(2,1)S(1)}, u32[]{:S(2)}, u32[]{:S(2)}) %collective-permute-start.77) | collective-permute-done | bytes 331808 | tf_op jit(solution)/shard_map/ppermute | solution.py:656
  (686 shorter events, 423.3 us)
Async XLA Ops:
  3.9 51.2 %collective-permute-start.1 = (bf16[72,1152]{1,0:T(8,128)(2,1)}, bf16[72,1152]{1,0:T(8,128)(2,1)}, u32[]{:S(2)}, u32[]{:S(2)}) collective-permute-start(bf16[72,1152]{1,0:T(8,128)(2,1)} %constant_dynamic-slice_fusion.9), channel_id=1, source_target_pairs={{0,2},{1,3},{2,0},{3,1},{4,6},{5,7},{6,4},{7,5},{8,10},{9,11},{10,... | collective-permute-start | bytes 497672 | tf_op jit(solution)/shard_map/ppermute | solution.py:656
  16.9 41.4 %collective-permute-start.15 = (bf16[72,1152]{1,0:T(8,128)(2,1)}, bf16[72,1152]{1,0:T(8,128)(2,1)}, u32[]{:S(2)}, u32[]{:S(2)}) collective-permute-start(bf16[72,1152]{1,0:T(8,128)(2,1)} %pad_dynamic-slice_fusion.2), channel_id=1, source_target_pairs={{0,2},{1,3},{2,0},{3,1},{4,6},{5,7},{6,4},{7,5},{8,10},{9,11},{10,... | collective-permute-start | bytes 497672 | tf_op jit(solution)/shard_map/ppermute | solution.py:656
  17.8 44.2 %collective-permute-start.20 = (bf16[72,1152]{1,0:T(8,128)(2,1)}, bf16[72,1152]{1,0:T(8,128)(2,1)}, u32[]{:S(2)}, u32[]{:S(2)}) collective-permute-start(bf16[72,1152]{1,0:T(8,128)(2,1)} %pad_dynamic-slice_fusion), channel_id=1, source_target_pairs={{0,2},{1,3},{2,0},{3,1},{4,6},{5,7},{6,4},{7,5},{8,10},{9,11},{10,... | collective-permute-start | bytes 497672 | tf_op jit(solution)/shard_map/ppermute | solution.py:656
  56.3 44.4 %collective-permute-start.3 = (bf16[1,144,1152]{2,1,0:T(8,128)(2,1)S(1)}, bf16[1,144,1152]{2,1,0:T(8,128)(2,1)S(1)}, u32[]{:S(2)}, u32[]{:S(2)}) collective-permute-start(bf16[1,144,1152]{2,1,0:T(8,128)(2,1)S(1)} %maximum_bitcast_fusion.2), channel_id=1, source_target_pairs={{0,16},{1,17},{2,18},{3,19},{4,20},{5,21},{6,22},{7,23},{8,24},{9,... | collective-permute-start | bytes 995336 | tf_op jit(solution)/shard_map/ppermute | solution.py:656
  56.5 44.2 %collective-permute-start.4 = (bf16[1,144,1152]{2,1,0:T(8,128)(2,1)S(1)}, bf16[1,144,1152]{2,1,0:T(8,128)(2,1)S(1)}, u32[]{:S(2)}, u32[]{:S(2)}) collective-permute-start(bf16[1,144,1152]{2,1,0:T(8,128)(2,1)S(1)} %maximum_bitcast_fusion.2), channel_id=1, source_target_pairs={{0,8},{1,9},{2,10},{3,11},{4,12},{5,13},{6,14},{7,15},{8,16},{9,17... | collective-permute-start | bytes 995336 | tf_op jit(solution)/shard_map/ppermute | solution.py:656
  59.6 45.1 %collective-permute-start.16 = (bf16[1,144,1152]{2,1,0:T(8,128)(2,1)S(1)}, bf16[1,144,1152]{2,1,0:T(8,128)(2,1)S(1)}, u32[]{:S(2)}, u32[]{:S(2)}) collective-permute-start(bf16[1,144,1152]{2,1,0:T(8,128)(2,1)S(1)} %maximum_bitcast_fusion.3), channel_id=1, source_target_pairs={{0,24},{1,25},{2,26},{3,27},{4,28},{5,29},{6,30},{7,31},{8,0},{9,1... | collective-permute-start | bytes 995336 | tf_op jit(solution)/shard_map/ppermute | solution.py:656
  62.0 67.1 %collective-permute-start.17 = (bf16[1,144,1152]{2,1,0:T(8,128)(2,1)S(1)}, bf16[1,144,1152]{2,1,0:T(8,128)(2,1)S(1)}, u32[]{:S(2)}, u32[]{:S(2)}) collective-permute-start(bf16[1,144,1152]{2,1,0:T(8,128)(2,1)S(1)} %maximum_bitcast_fusion.3), channel_id=1, source_target_pairs={{0,16},{1,17},{2,18},{3,19},{4,20},{5,21},{6,22},{7,23},{8,24},{9,... | collective-permute-start | bytes 995336 | tf_op jit(solution)/shard_map/ppermute | solution.py:656
  66.9 62.2 %collective-permute-start.18 = (bf16[1,144,1152]{2,1,0:T(8,128)(2,1)S(1)}, bf16[1,144,1152]{2,1,0:T(8,128)(2,1)S(1)}, u32[]{:S(2)}, u32[]{:S(2)}) collective-permute-start(bf16[1,144,1152]{2,1,0:T(8,128)(2,1)S(1)} %maximum_bitcast_fusion.3), channel_id=1, source_target_pairs={{0,8},{1,9},{2,10},{3,11},{4,12},{5,13},{6,14},{7,15},{8,16},{9,17... | collective-permute-start | bytes 995336 | tf_op jit(solution)/shard_map/ppermute | solution.py:656
  100.7 42.0 %collective-permute-start.22 = (bf16[1,144,1152]{2,1,0:T(8,128)(2,1)S(1)}, bf16[1,144,1152]{2,1,0:T(8,128)(2,1)S(1)}, u32[]{:S(2)}, u32[]{:S(2)}) collective-permute-start(bf16[1,144,1152]{2,1,0:T(8,128)(2,1)S(1)} %maximum_bitcast_fusion.4), channel_id=1, source_target_pairs={{0,16},{1,17},{2,18},{3,19},{4,20},{5,21},{6,22},{7,23},{8,24},{9,... | collective-permute-start | bytes 995336 | tf_op jit(solution)/shard_map/ppermute | solution.py:656
  129.2 175.9 %collective-permute-start.6 = (bf16[4,144,1152]{2,1,0:T(8,128)(2,1)}, bf16[4,144,1152]{2,1,0:T(8,128)(2,1)}, u32[]{:S(2)}, u32[]{:S(2)}) collective-permute-start(bf16[4,144,1152]{2,1,0:T(8,128)(2,1)} %constant_dynamic-slice_fusion.8), channel_id=1, source_target_pairs={{0,2},{1,3},{2,0},{3,1},{4,6},{5,7},{6,4},{7,5},{8,10},{9,11},{10,... | collective-permute-start | bytes 3981320 | tf_op jit(solution)/shard_map/ppermute | solution.py:656
  130.7 64.8 %collective-permute-start.8 = (bf16[4,144,1152]{2,1,0:T(8,128)(2,1)}, bf16[4,144,1152]{2,1,0:T(8,128)(2,1)}, u32[]{:S(2)}, u32[]{:S(2)}) collective-permute-start(bf16[4,144,1152]{2,1,0:T(8,128)(2,1)} %constant_dynamic-slice_fusion.8), channel_id=1, source_target_pairs={{0,1},{1,0},{2,3},{3,2},{4,5},{5,4},{6,7},{7,6},{8,9},{9,8},{10,11... | collective-permute-start | bytes 3981320 | tf_op jit(solution)/shard_map/ppermute | solution.py:656
  142.8 47.1 %collective-permute-start.19 = (bf16[4,144,1152]{2,1,0:T(8,128)(2,1)}, bf16[4,144,1152]{2,1,0:T(8,128)(2,1)S(1)}, u32[]{:S(2)}, u32[]{:S(2)}) collective-permute-start(bf16[4,144,1152]{2,1,0:T(8,128)(2,1)} %constant_dynamic-slice_fusion.7), channel_id=1, source_target_pairs={{0,4},{1,5},{2,6},{3,7},{4,0},{5,1},{6,2},{7,3},{8,12},{9,13},{10,... | collective-permute-start | bytes 3981320 | tf_op jit(solution)/shard_map/ppermute | solution.py:656
  142.8 89.6 %collective-permute-start.29 = (bf16[4,144,1152]{2,1,0:T(8,128)(2,1)}, bf16[4,144,1152]{2,1,0:T(8,128)(2,1)}, u32[]{:S(2)}, u32[]{:S(2)}) collective-permute-start(bf16[4,144,1152]{2,1,0:T(8,128)(2,1)} %constant_dynamic-slice_fusion.7), channel_id=1, source_target_pairs={{0,1},{1,0},{2,3},{3,2},{4,5},{5,4},{6,7},{7,6},{8,9},{9,8},{10,11... | collective-permute-start | bytes 3981320 | tf_op jit(solution)/shard_map/ppermute | solution.py:656
  161.5 54.7 %collective-permute-start.24 = (bf16[4,144,1152]{2,1,0:T(8,128)(2,1)}, bf16[4,144,1152]{2,1,0:T(8,128)(2,1)S(1)}, u32[]{:S(2)}, u32[]{:S(2)}) collective-permute-start(bf16[4,144,1152]{2,1,0:T(8,128)(2,1)} %constant_dynamic-slice_fusion.6), channel_id=1, source_target_pairs={{0,4},{1,5},{2,6},{3,7},{4,0},{5,1},{6,2},{7,3},{8,12},{9,13},{10,... | collective-permute-start | bytes 3981320 | tf_op jit(solution)/shard_map/ppermute | solution.py:656
  189.8 43.8 %collective-permute-start.32 = (bf16[4,144,1152]{2,1,0:T(8,128)(2,1)}, bf16[4,144,1152]{2,1,0:T(8,128)(2,1)}, u32[]{:S(2)}, u32[]{:S(2)}) collective-permute-start(bf16[4,144,1152]{2,1,0:T(8,128)(2,1)} %constant_dynamic-slice_fusion.6), channel_id=1, source_target_pairs={{0,1},{1,0},{2,3},{3,2},{4,5},{5,4},{6,7},{7,6},{8,9},{9,8},{10,11... | collective-permute-start | bytes 3981320 | tf_op jit(solution)/shard_map/ppermute | solution.py:656
  195.5 44.1 %collective-permute-start.9 = (bf16[2,144,1152]{2,1,0:T(8,128)(2,1)}, bf16[2,144,1152]{2,1,0:T(8,128)(2,1)}, u32[]{:S(2)}, u32[]{:S(2)}) collective-permute-start(bf16[2,144,1152]{2,1,0:T(8,128)(2,1)} %slice.382), channel_id=1, source_target_pairs={{0,1},{1,0},{2,3},{3,2},{4,5},{5,4},{6,7},{7,6},{8,9},{9,8},{10,11... | collective-permute-start | bytes 1990664 | tf_op jit(solution)/shard_map/ppermute | solution.py:656
  232.4 81.4 %collective-permute-start.27 = (bf16[4,144,1152]{2,1,0:T(8,128)(2,1)}, bf16[4,144,1152]{2,1,0:T(8,128)(2,1)}, u32[]{:S(2)}, u32[]{:S(2)}) collective-permute-start(bf16[4,144,1152]{2,1,0:T(8,128)(2,1)} %constant_dynamic-slice_fusion.6), channel_id=1, source_target_pairs={{0,2},{1,3},{2,0},{3,1},{4,6},{5,7},{6,4},{7,5},{8,10},{9,11},{10,... | collective-permute-start | bytes 3981320 | tf_op jit(solution)/shard_map/ppermute | solution.py:656
  233.7 84.0 %collective-permute-start.25 = (bf16[4,144,1152]{2,1,0:T(8,128)(2,1)}, bf16[4,144,1152]{2,1,0:T(8,128)(2,1)}, u32[]{:S(2)}, u32[]{:S(2)}) collective-permute-start(bf16[4,144,1152]{2,1,0:T(8,128)(2,1)} %constant_dynamic-slice_fusion.7), channel_id=1, source_target_pairs={{0,2},{1,3},{2,0},{3,1},{4,6},{5,7},{6,4},{7,5},{8,10},{9,11},{10,... | collective-permute-start | bytes 3981320 | tf_op jit(solution)/shard_map/ppermute | solution.py:656
  309.8 45.9 %collective-permute-start.38 = (bf16[4,144,1152]{2,1,0:T(8,128)(2,1)}, bf16[4,144,1152]{2,1,0:T(8,128)(2,1)}, u32[]{:S(2)}, u32[]{:S(2)}) collective-permute-start(bf16[4,144,1152]{2,1,0:T(8,128)(2,1)} %collective-permute-done.32), channel_id=1, source_target_pairs={{0,2},{1,3},{2,0},{3,1},{4,6},{5,7},{6,4},{7,5},{8,10},{9,11},{10,... | collective-permute-start | bytes 3981320 | tf_op jit(solution)/shard_map/ppermute | solution.py:656
  313.8 51.1 %collective-permute-start.35 = (bf16[4,144,1152]{2,1,0:T(8,128)(2,1)}, bf16[4,144,1152]{2,1,0:T(8,128)(2,1)}, u32[]{:S(2)}, u32[]{:S(2)}) collective-permute-start(bf16[4,144,1152]{2,1,0:T(8,128)(2,1)} %collective-permute-done.29), channel_id=1, source_target_pairs={{0,2},{1,3},{2,0},{3,1},{4,6},{5,7},{6,4},{7,5},{8,10},{9,11},{10,... | collective-permute-start | bytes 3981320 | tf_op jit(solution)/shard_map/ppermute | solution.py:656
  317.8 44.3 %collective-permute-start.36 = (bf16[2,144,1152]{2,1,0:T(8,128)(2,1)}, bf16[2,144,1152]{2,1,0:T(8,128)(2,1)}, u32[]{:S(2)}, u32[]{:S(2)}) collective-permute-start(bf16[2,144,1152]{2,1,0:T(8,128)(2,1)} %collective-permute-done.30), channel_id=1, source_target_pairs={{0,2},{1,3},{2,0},{3,1},{4,6},{5,7},{6,4},{7,5},{8,10},{9,11},{10,... | collective-permute-start | bytes 1990664 | tf_op jit(solution)/shard_map/ppermute | solution.py:656
  473.6 110.3 %collective-permute-start.41 = (bf16[1,1152]{1,0:T(2,128)(2,1)}, bf16[1,1152]{1,0:T(2,128)(2,1)S(1)}, u32[]{:S(2)}, u32[]{:S(2)}) collective-permute-start(bf16[1,1152]{1,0:T(2,128)(2,1)} %constant_dynamic-slice_fusion.5), channel_id=1, source_target_pairs={{0,1},{1,0},{2,3},{3,2},{4,5},{5,4},{6,7},{7,6},{8,9},{9,8},{10,11... | collective-permute-start | bytes 6920 | tf_op jit(solution)/shard_map/ppermute | solution.py:656
  552.3 50.3 %collective-permute-start.50 = (bf16[4,2,144,768]{3,2,1,0:T(8,128)(2,1)S(1)}, bf16[4,2,144,768]{3,2,1,0:T(8,128)(2,1)}, u32[]{:S(2)}, u32[]{:S(2)}) collective-permute-start(bf16[4,2,144,768]{3,2,1,0:T(8,128)(2,1)S(1)} %bitcast.235), channel_id=1, source_target_pairs={{0,2},{1,3},{2,0},{3,1},{4,6},{5,7},{6,4},{7,5},{8,10},{9,11},{10,... | collective-permute-start | bytes 5308424 | tf_op jit(solution)/shard_map/ppermute | solution.py:656
  561.1 52.5 %collective-permute-start.49 = (bf16[2,768,864]{1,2,0:T(8,128)(2,1)}, bf16[2,768,864]{1,2,0:T(8,128)(2,1)}, u32[]{:S(2)}, u32[]{:S(2)}) collective-permute-start(bf16[2,768,864]{1,2,0:T(8,128)(2,1)} %copy.128), channel_id=1, source_target_pairs={{0,2},{1,3},{2,0},{3,1},{4,6},{5,7},{6,4},{7,5},{8,10},{9,11},{10,... | collective-permute-start | bytes 7962632 | tf_op jit(solution)/shard_map/ppermute | solution.py:656
  596.5 99.4 %collective-permute-start.70 = (bf16[4,2,144,768]{3,2,1,0:T(8,128)(2,1)}, bf16[4,2,144,768]{3,2,1,0:T(8,128)(2,1)}, u32[]{:S(2)}, u32[]{:S(2)}) collective-permute-start(bf16[4,2,144,768]{3,2,1,0:T(8,128)(2,1)} %bitcast.94.left_one), channel_id=1, source_target_pairs={{0,2},{1,3},{2,0},{3,1},{4,6},{5,7},{6,4},{7,5},{8,10},{9,11},{10,... | collective-permute-start | bytes 5308424 | tf_op jit(solution)/shard_map/ppermute | solution.py:656
  598.6 63.5 %collective-permute-start.61 = (bf16[2,768,1152]{2,1,0:T(8,128)(2,1)}, bf16[2,768,1152]{2,1,0:T(8,128)(2,1)}, u32[]{:S(2)}, u32[]{:S(2)}) collective-permute-start(bf16[2,768,1152]{2,1,0:T(8,128)(2,1)} %pad_maximum_fusion), channel_id=1, source_target_pairs={{0,2},{1,3},{2,0},{3,1},{4,6},{5,7},{6,4},{7,5},{8,10},{9,11},{10,... | collective-permute-start | bytes 10616840 | tf_op jit(solution)/shard_map/ppermute | solution.py:656
  602.6 64.8 %collective-permute-start.60 = (bf16[4,2,144,768]{3,2,1,0:T(8,128)(2,1)}, bf16[4,2,144,768]{3,2,1,0:T(8,128)(2,1)}, u32[]{:S(2)}, u32[]{:S(2)}) collective-permute-start(bf16[4,2,144,768]{3,2,1,0:T(8,128)(2,1)} %bitcast.280), channel_id=1, source_target_pairs={{0,2},{1,3},{2,0},{3,1},{4,6},{5,7},{6,4},{7,5},{8,10},{9,11},{10,... | collective-permute-start | bytes 5308424 | tf_op jit(solution)/shard_map/ppermute | solution.py:656
  613.6 76.7 %collective-permute-start.71 = (bf16[2,768,1152]{2,1,0:T(8,128)(2,1)}, bf16[2,768,1152]{2,1,0:T(8,128)(2,1)}, u32[]{:S(2)}, u32[]{:S(2)}) collective-permute-start(bf16[2,768,1152]{2,1,0:T(8,128)(2,1)} %pad_maximum_fusion.1), channel_id=1, source_target_pairs={{0,2},{1,3},{2,0},{3,1},{4,6},{5,7},{6,4},{7,5},{8,10},{9,11},{10,... | collective-permute-start | bytes 10616840 | tf_op jit(solution)/shard_map/ppermute | solution.py:656
  660.1 64.5 %collective-permute-start.55 = (bf16[4,144,1152]{2,1,0:T(8,128)(2,1)}, bf16[4,144,1152]{2,1,0:T(8,128)(2,1)}, u32[]{:S(2)}, u32[]{:S(2)}) collective-permute-start(bf16[4,144,1152]{2,1,0:T(8,128)(2,1)} %fusion.67), channel_id=1, source_target_pairs={{0,1},{1,0},{2,3},{3,2},{4,5},{5,4},{6,7},{7,6},{8,9},{9,8},{10,11... | collective-permute-start | bytes 3981320 | tf_op jit(solution)/shard_map/ppermute | solution.py:656
  662.1 62.5 %collective-permute-start.53 = (bf16[4,144,1152]{2,1,0:T(8,128)(2,1)}, bf16[4,144,1152]{2,1,0:T(8,128)(2,1)}, u32[]{:S(2)}, u32[]{:S(2)}) collective-permute-start(bf16[4,144,1152]{2,1,0:T(8,128)(2,1)} %pad_maximum_fusion.15), channel_id=1, source_target_pairs={{0,4},{1,5},{2,6},{3,7},{4,0},{5,1},{6,2},{7,3},{8,12},{9,13},{10,... | collective-permute-start | bytes 3981320 | tf_op jit(solution)/shard_map/ppermute | solution.py:656
  720.4 45.7 %collective-permute-start.65 = (bf16[4,144,1152]{2,1,0:T(8,128)(2,1)S(1)}, bf16[4,144,1152]{2,1,0:T(8,128)(2,1)}, u32[]{:S(2)}, u32[]{:S(2)}) collective-permute-start(bf16[4,144,1152]{2,1,0:T(8,128)(2,1)S(1)} %pad_maximum_fusion.17), channel_id=1, source_target_pairs={{0,1},{1,0},{2,3},{3,2},{4,5},{5,4},{6,7},{7,6},{8,9},{9,8},{10,11... | collective-permute-start | bytes 3981320 | tf_op jit(solution)/shard_map/ppermute | solution.py:656
  774.2 43.9 %collective-permute-start.67 = (bf16[144,1152]{1,0:T(8,128)(2,1)S(1)}, bf16[144,1152]{1,0:T(8,128)(2,1)S(1)}, u32[]{:S(2)}, u32[]{:S(2)}) collective-permute-start(bf16[144,1152]{1,0:T(8,128)(2,1)S(1)} %get-tuple-element.145), channel_id=1, source_target_pairs={{0,16},{1,17},{2,18},{3,19},{4,20},{5,21},{6,22},{7,23},{8,24},{9,... | collective-permute-start | bytes 995336 | tf_op jit(solution)/shard_map/ppermute | solution.py:656
  (170 other events, 3033.7 us)

commit v2 on v0

--- a/solution.py
+++ b/solution.py
@@ -1,9 +1,15 @@
+import functools
+
 import jax
 import jax.numpy as jnp
 from jax import lax
+from jax.experimental import pallas as pl
+from jax.experimental.pallas import tpu as pltpu
 from jax.sharding import PartitionSpec as P
 
 HEAD_DIM = 72
+LOG2E = 1.4426950408889634
+VMEM_BYTES = 60 * 1024 * 1024
 IMAGES = 2
 
 
@@ -378,6 +384,1303 @@
     )
 
 
+def head_window(head, base, width):
+    start = base + head * HEAD_DIM
+    first = start // 128 * 128
+    last = min(-(-(start + HEAD_DIM) // 128) * 128, width)
+    return start - first, first, last
+
+
+def only_head(values, lane, offset):
+    inside = (lane >= offset) & (lane < offset + HEAD_DIM)
+    return jnp.where(inside, values, 0)
+
+
+def with_lanes(values, lane, offset, first_column, second_column):
+    one, two = (0, 1) if offset >= 2 else (126, 127)
+    values = jnp.where(lane == one, first_column, values)
+    return jnp.where(lane == two, second_column, values)
+
+
+def lane_index(rows, first, last):
+    return lax.broadcasted_iota(jnp.int32, (rows, last - first), 1)
+
+
+def row_columns(kind):
+    image = kind == 0
+    padding = (kind == 1) | (kind == 2)
+    low = jnp.bfloat16
+    image_query = jnp.where(image, 1.0, 0.0).astype(low)
+    other_query = jnp.where(image, 0.0, 1.0).astype(low)
+    image_key = jnp.where(image, 0.0, -1e30).astype(low)
+    padding_key = jnp.where(padding, 0.0, -1e30).astype(low)
+    return image_query, other_query, image_key, padding_key
+
+
+def dot_last(left, right):
+    return lax.dot_general(
+        left, right, (((1,), (1,)), ((), ())), preferred_element_type=jnp.float32
+    )
+
+
+def dot_first(left, right):
+    return lax.dot_general(
+        left, right, (((0,), (0,)), ((), ())), preferred_element_type=jnp.float32
+    )
+
+
+def split_rows(rows):
+    return [(start, min(start + 256, rows)) for start in range(0, rows, 256)]
+
+
+def heads_forward_kernel(places, heads, spot, kind_ref, x_ref, bias_ref, *refs):
+    count = sum(len(parts) for parts in places)
+    pieces = refs[:count]
+    qkv_ref, log_ref, own_ref, other_ref = refs[-10:-6]
+    weights, sems, keys_ref, values_ref, total_ref, logs_ref = refs[-6:]
+    step = pl.program_id(0)
+    start_then_wait(weight_copies(places, pieces, weights, sems, spot[0]), step)
+    scale = HEAD_DIM ** (-0.5) * LOG2E
+    rows = x_ref.shape[0]
+    part = heads * HEAD_DIM
+    inner = qkv_ref.shape[2]
+    width = keys_ref.shape[1]
+    base = width - part
+    projected = jnp.dot(
+        x_ref[...], strips(weights, step)[:, :inner], preferred_element_type=jnp.float32
+    )
+    qkv_ref[0] = (projected + bias_ref[0]).astype(jnp.bfloat16)
+    blank = jnp.zeros((rows, base), jnp.bfloat16)
+    keys_ref[:, :part] = qkv_ref[0, :, part : 2 * part]
+    keys_ref[:, part:] = blank
+    values_ref[:, :base] = blank
+    values_ref[:, base:] = qkv_ref[0, :, 2 * part : 3 * part]
+    image_query, other_query, image_key, padding_key = row_columns(kind_ref[...])
+    total_ref[...] = jnp.zeros_like(total_ref)
+    logs_ref[...] = jnp.zeros_like(logs_ref)
+    for head in range(heads):
+        offset, first, last = head_window(head, 0, width)
+        lane = lane_index(rows, first, last)
+        keys = with_lanes(
+            only_head(keys_ref[:, first:last], lane, offset), lane, offset, image_key, padding_key
+        )
+        query = with_lanes(
+            only_head(qkv_ref[0, :, first:last], lane, offset),
+            lane,
+            offset,
+            image_query,
+            other_query,
+        )
+        v_offset, v_first, v_last = head_window(head, base, width)
+        values = only_head(
+            values_ref[:, v_first:v_last], lane_index(rows, v_first, v_last), v_offset
+        )
+        for start, stop in split_rows(rows):
+            scores = dot_last(query[start:stop], keys)
+            peak = jnp.max(scores, axis=1, keepdims=True)
+            expo = jnp.exp2((scores - peak) * scale)
+            total = jnp.sum(expo, axis=1, keepdims=True)
+            mixed = jnp.dot(expo.astype(jnp.bfloat16), values, preferred_element_type=jnp.float32)
+            total_ref[start:stop, v_first:v_last] += mixed * (1.0 / total)
+            logsum = peak * scale + jnp.log2(total)
+            lane_h = lax.broadcasted_iota(jnp.int32, (stop - start, logs_ref.shape[1]), 1)
+            logs_ref[start:stop] = jnp.where(lane_h == head, logsum, logs_ref[start:stop])
+    log_ref[0] = jnp.transpose(logs_ref[...])[: log_ref.shape[1], :]
+
+    @pl.when(step == 0)
+    def write_own():
+        own_ref[...] = total_ref[...].astype(jnp.bfloat16)
+
+    @pl.when(step == 1)
+    def write_other():
+        other_ref[...] = total_ref[...].astype(jnp.bfloat16)
+
+
+def heads_forward_call(spot, kind, rows_in, biases, groups, waits=()):
+    rows, full = rows_in.shape
+    arrays, places = flatten(groups)
+    _, high, group_width = arrays[0].shape
+    depth = full // (2 * high)
+    count = len(groups)
+    part = group_width // 4
+    heads = part // HEAD_DIM
+    inner = -(-3 * part // 128) * 128
+    outer = -(-part // 128) * 128
+    side = pl.BlockSpec((rows, outer), lambda i: (0, 0))
+    return pl.pallas_call(
+        functools.partial(heads_forward_kernel, places, heads),
+        grid=(count,),
+        in_specs=[
+            smem_spec(),
+            pl.BlockSpec((rows, 1), lambda i: (0, 0)),
+            pl.BlockSpec((rows, full), lambda i: (0, 0)),
+            pl.BlockSpec((1, 1, inner), lambda i: (i, 0, 0)),
+        ]
+        + [any_spec()] * (len(arrays) + len(waits)),
+        out_specs=[
+            pl.BlockSpec((1, rows, inner), lambda i: (i, 0, 0)),
+            pl.BlockSpec((1, 8, rows), lambda i: (i, 0, 0)),
+            side,
+            side,
+        ],
+        out_shape=[
+            jax.ShapeDtypeStruct((count, rows, inner), jnp.bfloat16),
+            jax.ShapeDtypeStruct((count, 8, rows), jnp.float32),
+            jax.ShapeDtypeStruct((rows, outer), jnp.bfloat16),
+            jax.ShapeDtypeStruct((rows, outer), jnp.bfloat16),
+        ],
+        scratch_shapes=weight_scratch(places, depth, high, group_width)
+        + [
+            pltpu.VMEM((rows, outer), jnp.bfloat16),
+            pltpu.VMEM((rows, outer), jnp.bfloat16),
+            pltpu.VMEM((rows, outer), jnp.float32),
+            pltpu.VMEM((rows, 128), jnp.float32),
+        ],
+        compiler_params=limits(),
+        cost_estimate=cost(18),
+        name="heads_forward",
+    )(spot, kind, rows_in, biases, *arrays, *waits)
+
+
+def heads_backward_kernel(places, heads, spot, kind_ref, grad_ref, one_qkv, two_qkv, one_log, two_log, *refs):
+    count = sum(len(parts) for parts in places)
+    pieces = refs[:count]
+    out_ref, sum_ref = refs[-11:-9]
+    weights, sems, query_ref, keys_ref, values_ref, grads_ref, query_sum, key_sum, value_sum = refs[-9:]
+    step = pl.program_id(0)
+    width = keys_ref.shape[1]
+    first_lane = pieces[0].shape[2] - width
+    start_then_wait(weight_copies(places, pieces, weights, sems, spot[0], first_lane, width), step)
+    score_scale = HEAD_DIM ** (-0.5)
+    scale = score_scale * LOG2E
+    rows = grad_ref.shape[0]
+    part = heads * HEAD_DIM
+    base = width - part
+    blank = jnp.zeros((rows, base), jnp.bfloat16)
+
+    def load(qkv_ref):
+        query_ref[...] = qkv_ref[0, :, :width]
+        keys_ref[:, :part] = qkv_ref[0, :, part : 2 * part]
+        values_ref[:, base:] = qkv_ref[0, :, 2 * part : 3 * part]
+
+    @pl.when(step == 0)
+    def load_one():
+        load(one_qkv)
+
+    @pl.when(step == 1)
+    def load_two():
+        load(two_qkv)
+
+    keys_ref[:, part:] = blank
+    values_ref[:, :base] = blank
+    logs = jnp.where(step == 0, one_log[0], two_log[0])
+    grads_ref[...] = jnp.dot(
+        grad_ref[...], strips(weights, step), preferred_element_type=jnp.float32
+    ).astype(jnp.bfloat16)
+    image_query, other_query, image_key, padding_key = row_columns(kind_ref[...])
+    query_sum[...] = jnp.zeros_like(query_sum)
+    key_sum[...] = jnp.zeros_like(key_sum)
+    value_sum[...] = jnp.zeros_like(value_sum)
+    for head in range(heads):
+        offset, first, last = head_window(head, 0, width)
+        lane = lane_index(rows, first, last)
+        query = only_head(query_ref[:, first:last], lane, offset)
+        query_biased = with_lanes(query, lane, offset, image_query, other_query)
+        keys = only_head(keys_ref[:, first:last], lane, offset)
+        keys_biased = with_lanes(keys, lane, offset, image_key, padding_key)
+        v_offset, v_first, v_last = head_window(head, base, width)
+        values = values_ref[:, v_first:v_last]
+        grad = only_head(
+            grads_ref[:, v_first:v_last], lane_index(rows, v_first, v_last), v_offset
+        )
+        for start, stop in split_rows(rows):
+            scores = dot_last(keys_biased, query_biased[start:stop])
+            probs = jnp.exp2(scores * scale - logs[head : head + 1, start:stop])
+            grad_probs = dot_last(values, grad[start:stop])
+            weighted = probs * grad_probs
+            centre = jnp.sum(weighted, axis=0, keepdims=True)
+            grad_scores = (weighted - probs * centre).astype(jnp.bfloat16)
+            value_sum[:, v_first:v_last] += jnp.dot(
+                probs.astype(jnp.bfloat16), grad[start:stop], preferred_element_type=jnp.float32
+            )
+            key_sum[:, first:last] += jnp.dot(
+                grad_scores, query[start:stop], preferred_element_type=jnp.float32
+            )
+            query_sum[start:stop, first:last] += dot_first(grad_scores, keys)
+    low = jnp.bfloat16
+    out_ref[0, :, :part] = (query_sum[...] * score_scale).astype(low)[:, :part]
+    out_ref[0, :, part : 2 * part] = (key_sum[...] * score_scale).astype(low)[:, :part]
+    out_ref[0, :, 2 * part : 3 * part] = value_sum[...].astype(low)[:, base:]
+    tail = out_ref.shape[2] - 3 * part
+    if tail:
+        out_ref[0, :, 3 * part :] = jnp.zeros((rows, tail), low)
+    sum_ref[0] = jnp.sum(out_ref[0].astype(jnp.float32), axis=0, keepdims=True)
+
+
+def heads_backward_call(spot, kind, grad_rows, qkvs, logs, at, groups, waits=()):
+    rows, full = grad_rows.shape
+    arrays, places = flatten(groups)
+    _, high, group_width = arrays[0].shape
+    depth = full // (2 * high)
+    count = len(groups)
+    part = group_width // 4
+    heads = part // HEAD_DIM
+    inner = qkvs[0].shape[2]
+    outer = -(-part // 128) * 128
+    qkv_spec = pl.BlockSpec((1, rows, inner), lambda i: (at, 0, 0))
+    log_spec = pl.BlockSpec((1, 8, rows), lambda i: (at, 0, 0))
+    low = pltpu.VMEM((rows, outer), jnp.bfloat16)
+    wide = pltpu.VMEM((rows, outer), jnp.float32)
+    return pl.pallas_call(
+        functools.partial(heads_backward_kernel, places, heads),
+        grid=(count,),
+        in_specs=[
+            smem_spec(),
+            pl.BlockSpec((rows, 1), lambda i: (0, 0)),
+            pl.BlockSpec((rows, full), lambda i: (0, 0)),
+            qkv_spec,
+            qkv_spec,
+            log_spec,
+            log_spec,
+        ]
+        + [any_spec()] * (len(arrays) + len(waits)),
+        out_specs=[
+            pl.BlockSpec((1, rows, inner), lambda i: (i, 0, 0)),
+            pl.BlockSpec((1, 1, inner), lambda i: (i, 0, 0)),
+        ],
+        out_shape=[
+            jax.ShapeDtypeStruct((count, rows, inner), jnp.bfloat16),
+            jax.ShapeDtypeStruct((count, 1, inner), jnp.float32),
+        ],
+        scratch_shapes=weight_scratch(places, depth, high, outer)
+        + [low, low, low, low, wide, wide, wide],
+        compiler_params=limits(),
+        cost_estimate=cost(25),
+        name="heads_backward",
+    )(spot, kind, grad_rows, *qkvs, *logs, *arrays, *waits)
+
+
+def any_spec():
+    return pl.BlockSpec(memory_space=pl.ANY)
+
+
+def smem_spec():
+    return pl.BlockSpec(memory_space=pltpu.SMEM)
+
+
+def vmem_spec():
+    return pl.BlockSpec(memory_space=pltpu.VMEM)
+
+
+def limits():
+    return pltpu.CompilerParams(vmem_limit_bytes=VMEM_BYTES)
+
+
+def cost(micros):
+    return pl.CostEstimate(flops=0 * micros, bytes_accessed=0, transcendentals=0)
+
+
+def flatten(groups):
+    arrays = [piece for group in groups for piece, _, _ in group]
+    places = [[(at, x_off) for _, at, x_off in group] for group in groups]
+    return arrays, places
+
+
+def weight_copies(places, refs, weights, sems, x_at, first=0, width=None):
+    copies, at = [], 0
+    for group, parts in enumerate(places):
+        mine = []
+        for part, (start, x_off) in enumerate(parts):
+            source = refs[at]
+            at += 1
+            if width is not None:
+                source = source.at[:, :, pl.ds(first, width)]
+            target = weights.at[group, pl.ds(start, source.shape[0]), x_at ^ x_off]
+            mine.append(pltpu.make_async_copy(source, target, sems.at[group, part]))
+        copies.append(mine)
+    return copies
+
+
+def weight_scratch(places, depth, high, width):
+    count = len(places)
+    return [
+        pltpu.VMEM((count, depth, 2, high, width), jnp.bfloat16),
+        pltpu.SemaphoreType.DMA((count, max(len(parts) for parts in places))),
+    ]
+
+
+def start_then_wait(copies, step):
+    @pl.when(step == 0)
+    def begin():
+        for mine in copies:
+            for copy in mine:
+                copy.start()
+
+    for group, mine in enumerate(copies):
+
+        @pl.when(step == group)
+        def arrive(mine=mine):
+            for copy in mine:
+                copy.wait()
+
+
+def up_kernel(places, spot, x_ref, bias_ref, *refs):
+    count = sum(len(parts) for parts in places)
+    pieces = refs[:count]
+    active_ref, slope_ref, weights, sems = refs[-4:]
+    step = pl.program_id(0)
+    start_then_wait(weight_copies(places, pieces, weights, sems, spot[0]), step)
+    rows, full = x_ref.shape
+    width = weights.shape[-1]
+    tile = width // 3
+    for start in range(0, width, tile):
+        strip = weights[step, :, :, :, start : start + tile].reshape(full, tile)
+        hidden = jnp.dot(x_ref[...], strip, preferred_element_type=jnp.float32)
+        hidden = hidden + bias_ref[0, :, start : start + tile]
+        square = hidden * hidden
+        inner = jnp.tanh(hidden * (gelu_scale + gelu_scale * 0.044715 * square))
+        gate = 0.5 + 0.5 * inner
+        active_ref[0, :, start : start + tile] = (hidden * gate).astype(jnp.bfloat16)
+        grow = hidden * (gelu_scale + 3.0 * 0.044715 * gelu_scale * square)
+        slope = gate + grow * (0.5 - 0.5 * inner * inner)
+        slope_ref[0, :, start : start + tile] = slope.astype(jnp.bfloat16)
+
+
+def up_project(spot, rows_in, biases, groups, waits=()):
+    rows, full = rows_in.shape
+    arrays, places = flatten(groups)
+    _, high, width = arrays[0].shape
+    depth = full // (2 * high)
+    count = len(groups)
+    shape = jax.ShapeDtypeStruct((count, rows, width), jnp.bfloat16)
+    block = pl.BlockSpec((1, rows, width), lambda i: (i, 0, 0))
+    return pl.pallas_call(
+        functools.partial(up_kernel, places),
+        grid=(count,),
+        in_specs=[
+            smem_spec(),
+            pl.BlockSpec((rows, full), lambda i: (0, 0)),
+            pl.BlockSpec((1, 1, width), lambda i: (i, 0, 0)),
+        ]
+        + [any_spec()] * (len(arrays) + len(waits)),
+        out_specs=[block, block],
+        out_shape=[shape, shape],
+        scratch_shapes=weight_scratch(places, depth, high, width),
+        compiler_params=limits(),
+        cost_estimate=cost(14),
+        name="mlp_up",
+    )(spot, rows_in, biases, *arrays, *waits)
+
+
+def slope_kernel(places, spot, x_ref, slope_ref, *refs):
+    count = sum(len(parts) for parts in places)
+    pieces = refs[:count]
+    out_ref, sum_ref, weights, sems = refs[-4:]
+    step = pl.program_id(0)
+    start_then_wait(weight_copies(places, pieces, weights, sems, spot[0]), step)
+    rows, full = x_ref.shape
+    width = weights.shape[-1]
+    tile = width // 3
+    for start in range(0, width, tile):
+        strip = weights[step, :, :, :, start : start + tile].reshape(full, tile)
+        grad = jnp.dot(x_ref[...], strip, preferred_element_type=jnp.float32)
+        grad = grad * slope_ref[0, :, start : start + tile].astype(jnp.float32)
+        low = grad.astype(jnp.bfloat16)
+        out_ref[0, :, start : start + tile] = low
+        total = jnp.sum(low.astype(jnp.float32), axis=0, keepdims=True)
+        sum_ref[0, :, start : start + tile] = total
+
+
+def hidden_grad(spot, rows_in, slope, groups, waits=()):
+    rows, full = rows_in.shape
+    arrays, places = flatten(groups)
+    _, high, width = arrays[0].shape
+    depth = full // (2 * high)
+    count = len(groups)
+    block = pl.BlockSpec((1, rows, width), lambda i: (i, 0, 0))
+    return pl.pallas_call(
+        functools.partial(slope_kernel, places),
+        grid=(count,),
+        in_specs=[smem_spec(), pl.BlockSpec((rows, full), lambda i: (0, 0)), block]
+        + [any_spec()] * (len(arrays) + len(waits)),
+        out_specs=[block, pl.BlockSpec((1, 1, width), lambda i: (i, 0, 0))],
+        out_shape=[
+            jax.ShapeDtypeStruct((count, rows, width), jnp.bfloat16),
+            jax.ShapeDtypeStruct((count, 1, width), jnp.float32),
+        ],
+        scratch_shapes=weight_scratch(places, depth, high, width),
+        compiler_params=limits(),
+        cost_estimate=cost(12),
+        name="mlp_grad",
+    )(spot, rows_in, slope, *arrays, *waits)
+
+
+def accumulate(step, total, product):
+    @pl.when(step == 0)
+    def first():
+        total[...] = product
+
+    @pl.when(step > 0)
+    def later():
+        total[...] += product
+
+
+def by_rows(rows, block, body):
+    def one(i, carry):
+        body(pl.ds(pl.multiple_of(i * block, block), block))
+        return carry
+
+    lax.fori_loop(0, rows // block, one, 0)
+
+
+def unit_rows(values):
+    centre = values - jnp.mean(values, axis=1, keepdims=True)
+    spread = jnp.mean(centre * centre, axis=1, keepdims=True)
+    root = lax.rsqrt(spread + layer_eps)
+    return centre * root, root
+
+
+def norm_rows_back(values, gain, grad):
+    unit, root = unit_rows(values)
+    scaled = grad * gain
+    mean_one = jnp.mean(scaled, axis=1, keepdims=True)
+    mean_two = jnp.mean(scaled * unit, axis=1, keepdims=True)
+    part = root * (scaled - mean_one - unit * mean_two)
+    return part, jnp.sum(grad * unit, axis=0, keepdims=True), jnp.sum(grad, axis=0, keepdims=True)
+
+
+def strips(weights, step, parts=3):
+    _, depth, _, high, width = weights.shape
+    full = depth * 2 * high
+    return weights[step].reshape(full, width)
+
+
+def pick(step, refs):
+    half = refs[0].shape[0]
+    return lambda i: refs[i // half][i % half]
+
+
+def back_two_kernel(places, spot, later_ref, early_ref, resid_ref, grad_ref, gain_ref, *refs):
+    count = sum(len(parts) for parts in places)
+    pieces = refs[:count]
+    out_ref, low_ref, sum_ref, weights, sems, total = refs[-6:]
+    step = pl.program_id(0)
+    last = pl.num_programs(0) - 1
+    start_then_wait(weight_copies(places, pieces, weights, sems, spot[0]), step)
+    half = pl.num_programs(0) // 2
+
+    @pl.when(step < half)
+    def from_first():
+        accumulate(step, total, dot_last(later_ref[0], strips(weights, step)))
+
+    @pl.when(step >= half)
+    def from_second():
+        total[...] += dot_last(early_ref[0], strips(weights, step))
+
+    @pl.when(step == last)
+    def finish():
+        sum_ref[...] = jnp.zeros_like(sum_ref)
+
+        def block(span):
+            part, gain_sum, shift_sum = norm_rows_back(
+                resid_ref[span, :], gain_ref[...], total[span, :]
+            )
+            grad = grad_ref[span, :].astype(jnp.float32) + part
+            low = grad.astype(jnp.bfloat16)
+            out_ref[span, :] = grad
+            low_ref[span, :] = low
+            sum_ref[0:1, :] += gain_sum
+            sum_ref[1:2, :] += shift_sum
+            sum_ref[2:3, :] += jnp.sum(low.astype(jnp.float32), axis=0, keepdims=True)
+
+        by_rows(total.shape[0], 64, block)
+
+
+def two_stage_specs(count, rows, width):
+    half = count // 2
+    return [
+        pl.BlockSpec((1, rows, width), lambda i: (jnp.minimum(i, half - 1), 0, 0)),
+        pl.BlockSpec((1, rows, width), lambda i: (jnp.maximum(i - half, 0), 0, 0)),
+    ]
+
+
+def back_two(spot, first, second, resid, grad_low, gain, groups, waits=()):
+    rows, full = resid.shape
+    arrays, places = flatten(groups)
+    _, high, width = arrays[0].shape
+    depth = full // (2 * high)
+    count = len(groups)
+    whole = pl.BlockSpec((rows, full), lambda i: (0, 0))
+    return pl.pallas_call(
+        functools.partial(back_two_kernel, places),
+        grid=(count,),
+        in_specs=[smem_spec()]
+        + two_stage_specs(count, rows, width)
+        + [whole, whole, pl.BlockSpec((1, full), lambda i: (0, 0))]
+        + [any_spec()] * (len(arrays) + len(waits)),
+        out_specs=[whole, whole, pl.BlockSpec((8, full), lambda i: (0, 0))],
+        out_shape=[
+            jax.ShapeDtypeStruct((rows, full), jnp.float32),
+            jax.ShapeDtypeStruct((rows, full), jnp.bfloat16),
+            jax.ShapeDtypeStruct((8, full), jnp.float32),
+        ],
+        scratch_shapes=weight_scratch(places, depth, high, width)
+        + [pltpu.VMEM((rows, full), jnp.float32)],
+        compiler_params=limits(),
+        cost_estimate=cost(24),
+        name="norm_two_back",
+    )(spot, first, second, resid, grad_low, gain, *arrays, *waits)
+
+
+def back_one_kernel(places, spot, later_ref, early_ref, x_ref, grad_ref, gain_ref, *refs):
+    count = sum(len(parts) for parts in places)
+    pieces = refs[:count]
+    out_ref, sum_ref, weights, sems, total = refs[-5:]
+    step = pl.program_id(0)
+    last = pl.num_programs(0) - 1
+    inner = later_ref.shape[2]
+    start_then_wait(weight_copies(places, pieces, weights, sems, spot[0], 0, inner), step)
+    half = pl.num_programs(0) // 2
+
+    @pl.when(step < half)
+    def from_first():
+        accumulate(step, total, dot_last(later_ref[0], strips(weights, step)))
+
+    @pl.when(step >= half)
+    def from_second():
+        total[...] += dot_last(early_ref[0], strips(weights, step))
+
+    @pl.when(step == last)
+    def finish():
+        sum_ref[...] = jnp.zeros_like(sum_ref)
+
+        def block(span):
+            values = x_ref[span, :].astype(jnp.float32)
+            part, gain_sum, shift_sum = norm_rows_back(values, gain_ref[...], total[span, :])
+            out_ref[span, :] = grad_ref[span, :] + part
+            sum_ref[0:1, :] += gain_sum
+            sum_ref[1:2, :] += shift_sum
+
+        by_rows(total.shape[0], 64, block)
+
+
+def back_one(spot, first, second, rows_in, grad_resid, gain, groups, waits=()):
+    rows, full = rows_in.shape
+    arrays, places = flatten(groups)
+    _, high, _ = arrays[0].shape
+    width = first.shape[2]
+    depth = full // (2 * high)
+    count = len(groups)
+    whole = pl.BlockSpec((rows, full), lambda i: (0, 0))
+    return pl.pallas_call(
+        functools.partial(back_one_kernel, places),
+        grid=(count,),
+        in_specs=[smem_spec()]
+        + two_stage_specs(count, rows, width)
+        + [whole, whole, pl.BlockSpec((1, full), lambda i: (0, 0))]
+        + [any_spec()] * (len(arrays) + len(waits)),
+        out_specs=[whole, pl.BlockSpec((8, full), lambda i: (0, 0))],
+        out_shape=[
+            jax.ShapeDtypeStruct((rows, full), jnp.float32),
+            jax.ShapeDtypeStruct((8, full), jnp.float32),
+        ],
+        scratch_shapes=weight_scratch(places, depth, high, width)
+        + [pltpu.VMEM((rows, full), jnp.float32)],
+        compiler_params=limits(),
+        cost_estimate=cost(21),
+        name="norm_one_back",
+    )(spot, first, second, rows_in, grad_resid, gain, *arrays, *waits)
+
+
+def down_kernel(places, spot, later_ref, early_ref, resid_ref, shift_ref, *refs):
+    count = sum(len(parts) for parts in places)
+    pieces = refs[:count]
+    out_ref, weights, sems, total = refs[-4:]
+    step = pl.program_id(0)
+    last = pl.num_programs(0) - 1
+    start_then_wait(weight_copies(places, pieces, weights, sems, spot[0]), step)
+    half = pl.num_programs(0) // 2
+
+    @pl.when(step < half)
+    def from_first():
+        accumulate(step, total, dot_last(later_ref[0], strips(weights, step)))
+
+    @pl.when(step >= half)
+    def from_second():
+        total[...] += dot_last(early_ref[0], strips(weights, step))
+
+    @pl.when(step == last)
+    def finish():
+        def block(span):
+            values = resid_ref[span, :] + total[span, :] + shift_ref[...]
+            out_ref[span, :] = values.astype(out_ref.dtype)
+
+        by_rows(total.shape[0], 64, block)
+
+
+def down_project(spot, first, second, resid, shift, groups, waits=()):
+    rows, full = resid.shape
+    arrays, places = flatten(groups)
+    _, high, width = arrays[0].shape
+    depth = full // (2 * high)
+    count = len(groups)
+    whole = pl.BlockSpec((rows, full), lambda i: (0, 0))
+    return pl.pallas_call(
+        functools.partial(down_kernel, places),
+        grid=(count,),
+        in_specs=[smem_spec()]
+        + two_stage_specs(count, rows, width)
+        + [whole, pl.BlockSpec((1, full), lambda i: (0, 0))]
+        + [any_spec()] * (len(arrays) + len(waits)),
+        out_specs=whole,
+        out_shape=jax.ShapeDtypeStruct((rows, full), jnp.bfloat16),
+        scratch_shapes=weight_scratch(places, depth, high, width)
+        + [pltpu.VMEM((rows, full), jnp.float32)],
+        compiler_params=limits(),
+        cost_estimate=cost(18),
+        name="mlp_down",
+    )(spot, first, second, resid, shift, *arrays, *waits)
+
+
+def out_kernel(places, spot, one, two, three, four, x_ref, shift_ref, gain_ref, bias_ref, *refs):
+    count = sum(len(parts) for parts in places)
+    pieces = refs[:count]
+    resid_ref, normed_ref, weights, sems = refs[-4:]
+    outer = weights.shape[-1]
+    first = pieces[0].shape[-1] - outer
+    copies = weight_copies(places, pieces, weights, sems, spot[0], first, outer)
+    for mine in copies:
+        for copy in mine:
+            copy.start()
+    for group, mixed in enumerate((one, two, three, four)):
+        for copy in copies[group]:
+            copy.wait()
+        product = dot_last(mixed[...], strips(weights, group))
+        if group == 0:
+            resid_ref[...] = product
+        else:
+            resid_ref[...] += product
+
+    def block(span):
+        values = resid_ref[span, :] + x_ref[span, :].astype(jnp.float32) + shift_ref[...]
+        resid_ref[span, :] = values
+        unit, _ = unit_rows(values)
+        normed_ref[span, :] = (unit * gain_ref[...] + bias_ref[...]).astype(jnp.bfloat16)
+
+    by_rows(resid_ref.shape[0], 64, block)
+
+
+def out_project(spot, mixed, rows_in, shift, gain, bias, groups, waits=()):
+    rows, full = rows_in.shape
+    arrays, places = flatten(groups)
+    _, high, _ = arrays[0].shape
+    outer = mixed[0].shape[1]
+    depth = full // (2 * high)
+    return pl.pallas_call(
+        functools.partial(out_kernel, places),
+        in_specs=[smem_spec()] + [vmem_spec()] * 8 + [any_spec()] * (len(arrays) + len(waits)),
+        out_specs=[vmem_spec(), vmem_spec()],
+        out_shape=[
+            jax.ShapeDtypeStruct((rows, full), jnp.float32),
+            jax.ShapeDtypeStruct((rows, full), jnp.bfloat16),
+        ],
+        scratch_shapes=weight_scratch(places, depth, high, outer),
+        compiler_params=limits(),
+        cost_estimate=cost(13),
+        name="attn_out",
+    )(spot, *mixed, rows_in, shift, gain, bias, *arrays, *waits)
+
+
+def grad_kernel(pairs, waits, spot, *refs):
+    width_in = [4] * pairs
+    sources = refs[: sum(width_in)]
+    rest = refs[sum(width_in) + waits :]
+    own, beside, across, corner_one, corner_two = rest[:5]
+    holds = rest[5 : 5 + sum(width_in)]
+    stage, in_sems, out_sems = rest[-3:]
+    x_at = spot[0]
+    copies = [
+        pltpu.make_async_copy(source, hold, in_sems.at[i])
+        for i, (source, hold) in enumerate(zip(sources, holds))
+    ]
+    for copy in copies:
+        copy.start()
+    for copy in copies:
+        copy.wait()
+    _, depth, _, high, width = stage.shape
+    half = depth // 2
+    full = depth * 2 * high
+    out_copies = []
+    for side in range(2):
+        start = 0
+        total = None
+        for count in width_in:
+            held = holds[start : start + count]
+            start += count
+            product = dot_first(held[0][...], held[1][side])
+            product += dot_first(held[2][...], held[3][side])
+            if total is None:
+                total = product
+            else:
+                whole_tile = total.shape[1] + product.shape[1] - width
+                left = total.shape[1] - whole_tile
+                total = jnp.concatenate(
+                    [
+                        total[:, :left],
+                        total[:, left:] + product[:, :whole_tile],
+                        product[:, whole_tile:],
+                    ],
+                    axis=1,
+                )
+        stage[side] = total.astype(jnp.bfloat16).reshape(depth, 2, high, width)
+        near = stage.at[side, :, x_at]
+        far = stage.at[side, :, 1 - x_at]
+        if side == 0:
+            moves = [(near, own), (far, beside)]
+        else:
+            moves = [
+                (near, across),
+                (stage.at[side, pl.ds(0, half), 1 - x_at], corner_one),
+                (stage.at[side, pl.ds(half, half), 1 - x_at], corner_two),
+            ]
+        for source, target in moves:
+            copy = pltpu.make_async_copy(source, target, out_sems.at[len(out_copies)])
+            copy.start()
+            out_copies.append(copy)
+    for copy in out_copies:
+        copy.wait()
+
+
+def weight_grad(spot, pairs, depth, waits=()):
+    flat = [values for pair in pairs for both in pair for values in both]
+    full = flat[0].shape[1]
+    high = full // (2 * depth)
+    half = depth // 2
+    width = sum(pair[0][1].shape[2] for pair in pairs)
+    if len(pairs) > 1:
+        width = full
+    rows = flat[0].shape[0]
+    sizes = (depth, depth, depth, half, half)
+    return pl.pallas_call(
+        functools.partial(grad_kernel, len(pairs), len(waits)),
+        in_specs=[smem_spec()] + [any_spec()] * (len(flat) + len(waits)),
+        out_specs=[any_spec()] * 5,
+        out_shape=[jax.ShapeDtypeStruct((size, high, width), jnp.bfloat16) for size in sizes],
+        scratch_shapes=[pltpu.VMEM(values.shape, values.dtype) for values in flat]
+        + [
+            pltpu.VMEM((2, depth, 2, high, width), jnp.bfloat16),
+            pltpu.SemaphoreType.DMA((len(flat),)),
+            pltpu.SemaphoreType.DMA((5,)),
+        ],
+        compiler_params=limits(),
+        cost_estimate=cost(15),
+        name="weight_grad",
+    )(spot, *flat, *waits)
+
+
+def corner_kernel(beside_ref, across_ref, one_ref, two_ref, beside_out, across_out):
+    wide = jnp.float32
+    low = beside_out.dtype
+    beside_out[...] = (beside_ref[...].astype(wide) + two_ref[...].astype(wide)).astype(low)
+    across_out[...] = (across_ref[...].astype(wide) + one_ref[...].astype(wide)).astype(low)
+
+
+def add_corners(beside, across, corner_one, corner_two):
+    block = corner_one.shape
+    first = pl.BlockSpec(block, lambda i: (0, 0, 0))
+    second = pl.BlockSpec(block, lambda i: (1, 0, 0))
+    shape = jax.ShapeDtypeStruct(beside.shape, beside.dtype)
+    return pl.pallas_call(
+        corner_kernel,
+        grid=(1,),
+        in_specs=[second, first, first, first],
+        out_specs=[second, first],
+        out_shape=[shape, shape],
+        input_output_aliases={0: 0, 1: 1},
+        compiler_params=limits(),
+        name="add_corners",
+    )(beside, across, corner_one, corner_two)
+
+
+def square_kernel(own, one, two, out):
+    wide = jnp.float32
+    total = own[...].astype(wide) + one[...].astype(wide) + two[...].astype(wide)
+    out[...] = total.astype(out.dtype)
+
+
+def add_square(own, one, two):
+    depth, high, width = own.shape
+    block = pl.BlockSpec((1, high, width), lambda i: (i, 0, 0))
+    return pl.pallas_call(
+        square_kernel,
+        grid=(depth,),
+        in_specs=[block, block, block],
+        out_specs=block,
+        out_shape=jax.ShapeDtypeStruct(own.shape, own.dtype),
+        name="add_square",
+    )(own, one, two)
+
+
+PATCHES = 729
+AXES = ("dp", "tensor")
+
+
+def nothing(*refs):
+    del refs
+
+
+def fence(released, waited=()):
+    anywhere = pl.BlockSpec(memory_space=pl.ANY)
+    released, waited = list(released), list(waited)
+    return pl.pallas_call(
+        nothing,
+        in_specs=[anywhere] * (len(released) + len(waited)),
+        out_specs=[anywhere] * len(released),
+        out_shape=[jax.ShapeDtypeStruct(values.shape, values.dtype) for values in released],
+        input_output_aliases={i: i for i in range(len(released))},
+        name="fence",
+    )(*released, *waited)
+
+
+class Grid:
+    def __init__(self, depth):
+        self.depth = depth
+        dp_at = lax.axis_index("dp")
+        self.y = lax.axis_index("tensor")
+        self.c = dp_at % 2
+        self.x = dp_at // 2 % 2
+        self.z = dp_at // 4
+
+    def move(self, values, where):
+        pairs = []
+        for z in range(self.depth):
+            for x in range(2):
+                for c in range(2):
+                    for y in range(2):
+                        to_z, to_x, to_c, to_y = where(z, x, c, y)
+                        pairs.append(
+                            (
+                                ((z * 2 + x) * 2 + c) * 2 + y,
+                                ((to_z * 2 + to_x) * 2 + to_c) * 2 + to_y,
+                            )
+                        )
+        return lax.ppermute(values, AXES, pairs)
+
+    def over_x(self, values):
+        return self.move(values, lambda z, x, c, y: (z, 1 - x, c, y))
+
+    def over_y(self, values):
+        return self.move(values, lambda z, x, c, y: (z, x, c, 1 - y))
+
+    def over_core(self, values):
+        return self.move(values, lambda z, x, c, y: (z, x, 1 - c, y))
+
+    def along_z(self, values, hops):
+        return self.move(values, lambda z, x, c, y: ((z + hops) % self.depth, x, c, y))
+
+    def across_z(self, values, bit):
+        return self.move(values, lambda z, x, c, y: (z ^ bit, x, c, y))
+
+    def spread(self, block):
+        width = block.shape[1] // 2
+        mine = lax.dynamic_slice_in_dim(block, self.c * width, width, 1)
+        theirs = self.over_core(
+            lax.dynamic_slice_in_dim(block, (1 - self.c) * width, width, 1)
+        )
+        first = jnp.where(self.c == 0, mine, theirs)
+        second = jnp.where(self.c == 0, theirs, mine)
+        return jnp.concatenate([first, second])
+
+    def depth_groups(self):
+        return [
+            [(z * 2 + x) * 2 + c for z in range(self.depth)] for x in range(2) for c in range(2)
+        ]
+
+    def gather_depth(self, block):
+        return lax.all_gather(block, "dp", axis_index_groups=self.depth_groups())
+
+    def scatter_depth(self, total):
+        return lax.psum_scatter(total, "dp", axis_index_groups=self.depth_groups())
+
+    def scatter_core(self, result):
+        result = result.astype(jnp.float32)
+        shard = result.shape[0] // 2
+        mine = lax.dynamic_slice_in_dim(result, self.c * shard, shard)
+        theirs = self.over_core(
+            lax.dynamic_slice_in_dim(result, (1 - self.c) * shard, shard)
+        )
+        first = jnp.where(self.c == 0, mine, theirs)
+        second = jnp.where(self.c == 0, theirs, mine)
+        return jnp.stack([first, second])
+
+    def gather_small(self, values):
+        count, shard = values.shape
+        parts = jnp.zeros((self.depth, 2, 2, count, shard), values.dtype)
+        parts = lax.dynamic_update_slice(
+            parts, values[None, None, None], (self.z, self.x, self.c, 0, 0)
+        )
+        parts = parts + self.over_core(parts)
+        parts = parts + self.over_x(parts)
+        bit = 1
+        while bit < self.depth:
+            parts = parts + self.across_z(parts, bit)
+            bit *= 2
+        return parts.transpose(3, 0, 1, 2, 4).reshape(count, -1)
+
+
+def image_shards(
+    depth,
+    layer_input,
+    token_image,
+    cotangent,
+    ln1_gain,
+    ln1_bias,
+    w_qkv,
+    qv_bias,
+    w_out,
+    out_bias,
+    ln2_gain,
+    ln2_bias,
+    w_fc1,
+    fc1_bias,
+    w_fc2,
+    fc2_bias,
+):
+    low = jnp.bfloat16
+    wide = jnp.float32
+    grid = Grid(depth)
+    rows, full_width = layer_input.shape
+    shard = ln1_gain.shape[0]
+    head_width = qv_bias.shape[1]
+    ff_width = fc1_bias.shape[0]
+    padded = -(-(rows + 1) // 256) * 256
+
+    quarter = head_width // 2
+    group_width = 4 * quarter
+    ff_padding = 2 * group_width - ff_width
+    sources = [w_qkv[0], w_qkv[1], w_qkv[2], w_out.T]
+    first_block = jnp.concatenate(
+        [values[:, i * quarter : (i + 1) * quarter] for i in range(2) for values in sources],
+        axis=1,
+    )
+    second_block = jnp.pad(w_fc1, ((0, 0), (0, ff_padding)))
+    third_block = jnp.pad(w_fc2.T, ((0, 0), (0, ff_padding)))
+    half = depth // 2
+    blocks = [grid.spread(first_block), grid.spread(second_block), grid.spread(third_block)]
+    vectors = jnp.stack([ln1_gain, ln1_bias, out_bias, ln2_gain, ln2_bias, fc2_bias])
+    vectors = grid.gather_small(vectors).astype(wide)
+    (token_image, qv_bias) = fence([token_image, qv_bias], [blocks[0]])
+    own_one = grid.gather_depth(blocks[0])
+
+    here = grid.y
+    mine = lax.dynamic_slice_in_dim(token_image, here * rows, rows)
+    theirs = lax.dynamic_slice_in_dim(token_image, (1 - here) * rows, rows)
+    places = lax.iota(jnp.int32, rows)
+    stray = mine == 1 - here
+    stray_here = jnp.any(stray)
+    stray_there = jnp.any(theirs == here)
+    blank = mine == IMAGES
+    first_blank = jnp.min(jnp.where(blank, places, rows - 1))
+    last_blank = jnp.max(jnp.where(blank, places, 0))
+    swap_at = jnp.where(stray_here, jnp.max(jnp.where(stray, places, 0)), first_blank)
+    swapped = stray_here | stray_there
+    blank_at = jnp.where(stray_here, swap_at, last_blank)
+
+    def one_row(values, at):
+        return lax.dynamic_slice_in_dim(values, at, 1)
+
+    sent = jnp.concatenate(
+        [one_row(layer_input, swap_at), one_row(cotangent, swap_at), one_row(layer_input, last_blank)]
+    )
+    came = grid.over_y(sent)
+    other_blank = jnp.where(stray_there, sent[0:1], came[2:3])
+    spread_rows = lax.broadcasted_iota(jnp.int32, (padded, 1), 0)
+    at_swap = (spread_rows == swap_at) & swapped
+
+    def stretch(values):
+        return jnp.pad(values, ((0, padded - rows), (0, 0)))
+
+    input_rows = jnp.where(at_swap, came[0:1], stretch(layer_input))
+    input_rows = jnp.where(spread_rows == rows, other_blank, input_rows)
+    grad_low = jnp.where(at_swap, came[1:2], stretch(cotangent))
+    grad_low = jnp.where(spread_rows == blank_at, 0, grad_low).astype(low)
+    kind = jnp.where(spread_rows > rows, 3, jnp.where(spread_rows == rows, 2, 0))
+    kind = jnp.where(spread_rows == blank_at, 1, kind)
+    input_rows, grad_low = lax.optimization_barrier((input_rows, grad_low))
+
+    biases = jnp.concatenate([qv_bias.reshape(-1), fc1_bias])
+    biases = jnp.pad(biases, (0, -biases.shape[0] % 128)).reshape(-1, 128)
+    other_biases = grid.over_y(biases).reshape(-1)
+
+    def ordered(first, second):
+        return jnp.where(grid.c == 0, first, second), jnp.where(grid.c == 0, second, first)
+
+    spot = grid.x.reshape(1)
+    inner = -(-3 * quarter // 128) * 128
+    qv_groups, fc1_groups = [], []
+    for flat in (biases.reshape(-1), other_biases):
+        flat = flat.astype(wide)
+        pair = flat[: 2 * head_width].reshape(2, 2, quarter)
+        none = jnp.zeros((quarter,), wide)
+        rest = jnp.zeros((inner - 3 * quarter,), wide)
+        qv_groups += ordered(
+            *[jnp.concatenate([pair[0, i], none, pair[1, i], rest]) for i in range(2)]
+        )
+        hidden_bias = flat[2 * head_width : 2 * head_width + ff_width]
+        hidden_bias = jnp.pad(hidden_bias, (0, ff_padding))
+        fc1_groups += ordered(hidden_bias[:group_width], hidden_bias[group_width:])
+
+    def stacked(rows_of, picked):
+        return jnp.stack([rows_of[i] for i in picked])[:, None]
+
+    qv_stacks = [stacked(qv_groups, picked) for picked in ((0, 1), (2, 3))]
+    fc1_stacks = [stacked(fc1_groups, picked) for picked in ((1, 3), (0, 2))]
+
+    def sides_of(own):
+        return [grid.over_x(own), grid.over_y(own)]
+
+    def corners_of(beside, across):
+        return [grid.over_y(beside[:half]), grid.over_x(across[half:])]
+
+    def cores_of(*values):
+        return [grid.over_core(value) for value in values]
+
+    def near_groups(own, beside, there):
+        return [
+            [(own, 0, 0), (beside, 0, 1)],
+            [(there[0], 0, 0), (there[1], 0, 1)],
+        ]
+
+    def far_groups(across, corner, there):
+        return [
+            [(across, 0, 0), (corner[0], 0, 1), (corner[1], half, 1)],
+            [(there[0], 0, 0), (there[1], 0, 1), (there[2], half, 1)],
+        ]
+
+    own_one, vectors, input_rows, grad_low, kind, block_two, block_three, *stacks = fence(
+        [own_one, vectors, input_rows, grad_low, kind, blocks[1], blocks[2]]
+        + qv_stacks
+        + fc1_stacks
+    )
+    qv_stacks, fc1_stacks = stacks[:2], stacks[2:]
+    gain_one, shift_one, out_shift, gain_two, shift_two, fc2_shift = [
+        vectors[i : i + 1] for i in range(6)
+    ]
+    own_two = grid.gather_depth(block_two)
+    beside_one, across_one = sides_of(own_one)
+    unit_one, _ = unit_rows(input_rows.astype(wide))
+    normed = (unit_one * gain_one + shift_one).astype(low)
+    own_two, beside_one, across_one, normed, block_three, grad_there = fence(
+        [own_two, beside_one, across_one, normed, block_three, grid.over_core(grad_low)]
+    )
+    corner_one = corners_of(beside_one, across_one)
+    there = cores_of(own_one, beside_one)
+    across_there = grid.over_core(across_one)
+    sides_two = sides_of(own_two)
+    own_three = grid.gather_depth(block_three)
+    qkv, logs, mixed = [], [], []
+
+    def heads(stack, groups, waits):
+        results = heads_forward_call(spot, kind, normed, stack, groups, waits)
+        logs.append(results[1])
+        mixed.extend(results[2:])
+        return results[0]
+
+    attn_weights = near_groups(own_one, beside_one, there)
+    first_qkv = heads(qv_stacks[0], attn_weights, [])
+    *corner_one, across_there, first_qkv = fence(corner_one + [across_there, first_qkv])
+    there = [across_there] + cores_of(*corner_one)
+    attn_weights = attn_weights + far_groups(across_one, corner_one, there)
+    second_qkv = heads(qv_stacks[1], attn_weights[2:], [])
+    own_two_there = grid.over_core(own_two)
+    own_three, beside_two, across_two, own_two_there, second_qkv = fence(
+        [own_three] + sides_two + [own_two_there, second_qkv]
+    )
+    qkv = [first_qkv, second_qkv]
+    corner_two = corners_of(beside_two, across_two)
+    beside_there = grid.over_core(beside_two)
+    sides_three = sides_of(own_three)
+    resid, normed_two = out_project(
+        spot, mixed, input_rows, out_shift, gain_two, shift_two, attn_weights
+    )
+    *corner_two, normed_two, beside_there = fence(corner_two + [normed_two, beside_there])
+    up_weights = near_groups(own_two, beside_two, [own_two_there, beside_there])
+    there = cores_of(across_two, *corner_two)
+    up_weights = up_weights + far_groups(across_two, corner_two, there)
+    classes = ((1, 3), (0, 2))
+
+    def up(at, waits):
+        picked = [up_weights[i] for i in classes[at]]
+        return up_project(spot, normed_two, fc1_stacks[at], picked, waits)
+
+    other_active, other_slope = up(0, [])
+    beside_three, across_three, other_active = fence(sides_three + [other_active])
+    corner_three = corners_of(beside_three, across_three)
+    there = cores_of(own_three, beside_three)
+    across_there = grid.over_core(across_three)
+    active_there = grid.over_core(other_active)
+    own_active, own_slope = up(1, [other_active])
+    *corner_three, own_active = fence(corner_three + [own_active])
+    down_weights = near_groups(own_three, beside_three, there)
+    there = [across_there] + cores_of(*corner_three)
+    down_weights = down_weights + far_groups(across_three, corner_three, there)
+    fc2_sums = weight_grad(
+        spot, [((grad_low, own_active), (grad_there, active_there))], depth
+    )
+
+    def move_corners(sums):
+        return [grid.over_x(sums[3]), grid.over_y(sums[4])]
+
+    def back(at, slope, waits):
+        picked = [down_weights[i] for i in classes[at]]
+        return hidden_grad(spot, grad_low, slope, picked, waits)
+
+    moved = move_corners(fc2_sums)
+    other_hidden, other_fc1_sums = back(0, other_slope, [fc2_sums[0]])
+    *moved, other_hidden = fence(moved + [other_hidden])
+    beside, across = add_corners(fc2_sums[1], fc2_sums[2], *moved)
+    moved = [grid.over_x(beside), grid.over_y(across)]
+    hidden_there = grid.over_core(other_hidden)
+    own_hidden, own_fc1_sums = back(1, own_slope, [beside])
+    fc1_sums = weight_grad(
+        spot, [((normed_two, own_hidden), (grid.over_core(normed_two), hidden_there))], depth
+    )
+    *moved, near_sums, corner_a, corner_b = fence(moved + [fc1_sums[0], *fc1_sums[3:]])
+    fc2_piece = grid.scatter_depth(add_square(fc2_sums[0], *moved))
+    moved = [grid.over_x(corner_a), grid.over_y(corner_b)]
+    by_class = [up_weights[i] for i in classes[0] + classes[1]]
+    grad_resid, resid_low, sums_two = back_two(
+        spot,
+        other_hidden,
+        own_hidden,
+        resid,
+        grad_low,
+        gain_two,
+        by_class,
+        [near_sums],
+    )
+    *moved, resid_low = fence(moved + [resid_low])
+    beside, across = add_corners(fc1_sums[1], fc1_sums[2], *moved)
+    moved = [grid.over_x(beside), grid.over_y(across)]
+
+    def heads_back(at, waits):
+        return heads_backward_call(
+            spot, kind, resid_low, qkv, logs, at, [attn_weights[i] for i in classes[1 - at]], waits
+        )
+
+    other_qkv, other_qkv_sums = heads_back(1, [beside])
+    *moved, other_qkv, fc2_piece = fence(moved + [other_qkv, fc2_piece])
+    fc2_piece = grid.scatter_core(fc2_piece)
+    fc1_piece = grid.scatter_depth(add_square(near_sums, *moved))
+    qkv_there = grid.over_core(other_qkv)
+    own_qkv, own_qkv_sums = heads_back(0, [])
+    own_mixed = jnp.stack([mixed[0], mixed[2]])
+    other_mixed = jnp.stack([mixed[1], mixed[3]])
+    attn_sums = weight_grad(
+        spot,
+        [
+            ((normed, own_qkv), (grid.over_core(normed), qkv_there)),
+            ((resid_low, own_mixed), (grid.over_core(resid_low), grid.over_core(other_mixed))),
+        ],
+        depth,
+    )
+    near_sums, corner_a, corner_b = fence([attn_sums[0], *attn_sums[3:]])
+    moved = [grid.over_x(corner_a), grid.over_y(corner_b)]
+    by_class = [attn_weights[i] for i in classes[0] + classes[1]]
+    input_grad, sums_one = back_one(
+        spot, other_qkv, own_qkv, input_rows, grad_resid, gain_one, by_class, [near_sums]
+    )
+    *moved, sums_one, fc1_piece = fence(moved + [sums_one, fc1_piece])
+    beside, across = add_corners(attn_sums[1], attn_sums[2], *moved)
+    moved = [grid.over_x(beside), grid.over_y(across)]
+    fc1_piece = grid.scatter_core(fc1_piece)
+    by_class = [down_weights[i] for i in classes[0] + classes[1]]
+    layer_rows = down_project(
+        spot, other_active, own_active, resid, fc2_shift, by_class, [beside]
+    )
+
+    def column_sum(values):
+        return jnp.sum(values.astype(wide), axis=0)
+
+    def absolute(own_sums, other_sums):
+        grouped = jnp.concatenate([own_sums, other_sums], axis=1)
+        grouped = jnp.where(here == 0, grouped, grouped[::-1])
+        return jnp.where(grid.c == 0, grouped, grouped[:, ::-1])
+
+    qkv_totals = absolute(own_qkv_sums, other_qkv_sums)[:, :, : 3 * quarter]
+    qkv_totals = qkv_totals.reshape(2, 2, 3, quarter)[:, :, 0::2].transpose(0, 2, 1, 3)
+    fc1_totals = absolute(own_fc1_sums, other_fc1_sums).reshape(2, -1)
+    flat = jnp.concatenate(
+        [
+            sums_one[0],
+            sums_one[1],
+            sums_two[2],
+            sums_two[0],
+            sums_two[1],
+            column_sum(grad_low),
+            qkv_totals.reshape(-1),
+            fc1_totals[:, :ff_width].reshape(-1),
+        ]
+    )
+    length = flat.shape[0]
+    lines = -(-length // 1024) * 8
+    flat = jnp.pad(flat, (0, lines * 128 - length)).reshape(lines, 128)
+    flat = flat + grid.over_core(flat)
+    bit = 1
+    while bit < depth:
+        flat = flat + grid.across_z(flat, bit)
+        bit *= 2
+    *moved, flat = fence(moved + [flat], [layer_rows])
+    total = add_square(near_sums, *moved)
+    attn_piece = grid.scatter_depth(total)
+    flat = flat + grid.over_x(flat)
+    flat = flat + grid.over_y(flat)
+    flat = flat.reshape(-1)
+    swap_from = fence([one_row(layer_rows, swap_at), one_row(input_grad, swap_at)], [total])
+    returned = [grid.over_y(values) for values in swap_from]
+    layer_output = jnp.where(at_swap, returned[0], layer_rows)[:rows]
+    input_grad = jnp.where(at_swap, returned[1], input_grad)[:rows]
+    attn_piece = grid.scatter_core(attn_piece)
+    row_total = flat[: 6 * full_width].reshape(6, full_width)
+    row_piece = lax.dynamic_slice_in_dim(row_total, lax.axis_index("dp") * shard, shard, 1)
+    start = 6 * full_width
+    qv_piece = lax.dynamic_slice_in_dim(flat, start + here * 2 * head_width, 2 * head_width)
+    start = start + 4 * head_width
+    fc1_bias_piece = lax.dynamic_slice_in_dim(flat, start + here * ff_width, ff_width)
+    heads_piece = attn_piece.reshape(2, shard, 4, quarter).transpose(2, 1, 0, 3)
+    heads_piece = heads_piece.reshape(4, shard, head_width)
+
+    def whole_columns(pair):
+        return jnp.concatenate([pair[0], pair[1][:, : group_width - ff_padding]], axis=1)
+
+    return (
+        layer_output,
+        input_grad,
+        row_piece[0],
+        row_piece[1],
+        heads_piece[:3],
+        qv_piece.reshape(2, head_width),
+        heads_piece[3].T,
+        row_piece[2],
+        row_piece[3],
+        row_piece[4],
+        whole_columns(fc1_piece),
+        fc1_bias_piece,
+        whole_columns(fc2_piece).T,
+        row_piece[5],
+    )
+
+
+def fits_images(mesh):
+    groups = mesh.shape["dp"] // 4
+    return (
+        mesh.shape["tensor"] == IMAGES
+        and mesh.shape["dp"] % 4 == 0
+        and groups >= 2
+        and groups & (groups - 1) == 0
+    )
+
+
 def solution(mesh):
     in_specs = (
         P(("dp", "tensor"), None),
@@ -412,4 +1715,11 @@
         P("tensor", "dp"),
         P("dp"),
     )
-    return jax.shard_map(shards, mesh=mesh, in_specs=in_specs, out_specs=out_specs, check_vma=False)
+
+    def body(*arrays):
+        slots = arrays[1].shape[0]
+        if fits_images(mesh) and slots == IMAGES * (PATCHES + 1):
+            return image_shards(mesh.shape["dp"] // 4, *arrays)
+        return shards(*arrays)
+
+    return jax.shard_map(body, mesh=mesh, in_specs=in_specs, out_specs=out_specs, check_vma=False)

time: 2300 us -> 582 us (0.25)
  waiting for transfers between devices: 855 us -> 117 us
  blocking collectives: 536 us -> 0 us
  matrix products: 418 us -> 0 us
  Pallas kernels: 0 us -> 284 us
  local copies, waits for them, and re-layouts: 335 us -> 63.4 us
  other arithmetic: 105 us -> 37 us
  starting transfers between devices: 14.8 us -> 51.1 us
    all_gather x14 -> x3, waiting for transfers between devices: 523 us -> 12.5 us  [gather_depth(): return lax.all_gather(block, 'dp', axis_index_groups=self.depth_groups())]
    unnamed x7 -> x0, blocking collectives: 493 us -> none
    dot_general x158 -> x0, matrix products: 418 us -> none  [the longest x67 125 us: contract_cols(): lax.dot_general(left, right, (((1,), (1,)), ((), ())), preferred_element_...]
    unnamed x27 -> x6, waiting for transfers between devices: 332 us -> 0.1 us
    pallas_call x0 -> x37, Pallas kernels: none -> 284 us  [the longest x2 49.3 us: heads_backward_call(): pl.pallas_call(functools.partial(heads_backward_kernel, places, heads), g...]
    while x376 -> x0, local copies, waits for them, and re-layouts: 90 us -> none
    ppermute x0 -> x66, waiting for transfers between devices: none -> 89 us  [move(): return lax.ppermute(values, AXES, pairs)]
    unnamed x186 -> x126, local copies, waits for them, and re-layouts: 90.4 us -> 18 us
  transfers between devices with their start and end apart: 23 -> 72, of which waited for: 20 -> 27; matrix products, arithmetic and copies ran while one was open for 26% -> 13% of each run, Pallas kernels for 0% -> 48%
where the time goes in v2:
time: 582 us; the launch traced here: 575 us
  Pallas kernels  284 us (49%)
  waiting for transfers between devices  117 us (20%)
  local copies, waits for them, and re-layouts  63.4 us (11%)
  starting transfers between devices  51.1 us (9%)
  other arithmetic  37 us (6%)
  between operations  22.2 us (4%)
    ppermute x66, waiting for transfers between devices, move(): return lax.ppermute(values, AXES, pairs)  89 us
    ppermute x66, starting transfers between devices, move(): return lax.ppermute(values, AXES, pairs)  50.7 us
    pallas_call x2, Pallas kernels, heads_backward_call(): pl.pallas_call(functools.partial(heads_backward_kernel, places, heads), g...  49.3 us
    pallas_call x3, Pallas kernels, weight_grad(): pl.pallas_call(functools.partial(grad_kernel, len(pairs), len(waits)), in...  48.3 us
    pallas_call x2, Pallas kernels, heads_forward_call(): pl.pallas_call(functools.partial(heads_forward_kernel, places, heads), gr...  37.1 us
    pallas_call x2, Pallas kernels, up_project(): pl.pallas_call(functools.partial(up_kernel, places), grid=(count,), in_sp...  27.9 us
    pallas_call x1, Pallas kernels, back_two(): pl.pallas_call(functools.partial(back_two_kernel, places), grid=(count,),...  24.2 us
    pallas_call x2, Pallas kernels, hidden_grad(): pl.pallas_call(functools.partial(slope_kernel, places), grid=(count,), in...  23.4 us
  transfers between devices with their start and end apart: 72, of which 27 were waited for; matrix products, arithmetic and copies ran while one was open for 13% of the time, Pallas kernels for 48%

profile of v2, /device:TPU:0, one launch (start us, length us, event | category | flops | bytes accessed | tf_op | source)
XLA Modules:
  0.0 574.8 jit_solution(1659584390618262565)
XLA Ops:
  14.4 3.0 collective-permute-start.2
  23.4 3.1 collective-permute-start.4
  54.4 11.6 %all-gather.7.cloned.1.call-done = bf16[576,1152]{1,0:T(8,128)(2,1)} async-done(((bf16[144,1152]{1,0:T(8,128)(2,1)}), bf16[576,1152]{1,0:T(8,128)(2,1)}) %all-gather.7.cloned.1.call-update) | async-done | bytes 1327120 | tf_op jit(solution)/shard_map/all_gather | solution.py:1300
  74.2 23.7 %collective-permute-done.9.refs_1_ = bf16[4,144,1152]{2,1,0:T(8,128)(2,1)S(1)} collective-permute-done((bf16[4,144,1152]{2,1,0:T(8,128)(2,1)}, bf16[4,144,1152]{2,1,0:T(8,128)(2,1)S(1)}, u32[]{:S(2)}, u32[]{:S(2)}) %collective-permute-start.9) | collective-permute-done | bytes 1327136 | tf_op jit(solution)/shard_map/ppermute | solution.py:1267
  107.4 12.3 %collective-permute-done.15.refs_0_ = bf16[2,144,1152]{2,1,0:T(8,128)(2,1)} collective-permute-done((bf16[2,144,1152]{2,1,0:T(8,128)(2,1)}, bf16[2,144,1152]{2,1,0:T(8,128)(2,1)}, u32[]{:S(2)}, u32[]{:S(2)}) %collective-permute-start.15) | collective-permute-done | bytes 663584 | tf_op jit(solution)/shard_map/ppermute | solution.py:1267
  122.3 18.8 %heads_forward.2 = (bf16[2,768,896]{2,1,0:T(8,128)(2,1)}, f32[2,8,768]{2,1,0:T(8,128)}, bf16[768,384]{1,0:T(8,128)(2,1)}, bf16[768,384]{1,0:T(8,128)(2,1)}) custom-call(s32[1]{0:T(128)} %bitcast.4.spot, s32[768,1]{1,0:T(8,128)} %get-tuple-element.141.kind_ref, bf16[768,1152]{1,0:T(8,128)(2,1)} %get-tuple-element.142.x_ref.refs_0_, ...), custom_call_target="tpu_custom_call" | custom-call | tf_op jit(solution)/shard_map/heads_forward/pallas_call | solution.py:510
  146.3 18.3 %heads_forward.3 = (bf16[2,768,896]{2,1,0:T(8,128)(2,1)}, f32[2,8,768]{2,1,0:T(8,128)}, bf16[768,384]{1,0:T(8,128)(2,1)}, bf16[768,384]{1,0:T(8,128)(2,1)}) custom-call(s32[1]{0:T(128)} %bitcast.4.spot, s32[768,1]{1,0:T(8,128)} %get-tuple-element.141.kind_ref, bf16[768,1152]{1,0:T(8,128)(2,1)} %get-tuple-element.142.x_ref.refs_0_, ...), custom_call_target="tpu_custom_call" | custom-call | tf_op jit(solution)/shard_map/heads_forward/pallas_call | solution.py:510
  170.8 12.5 %collective-permute-done.24.refs_0_ = bf16[2,144,1152]{2,1,0:T(8,128)(2,1)S(1)} collective-permute-done((bf16[2,144,1152]{2,1,0:T(8,128)(2,1)S(1)}, bf16[2,144,1152]{2,1,0:T(8,128)(2,1)S(1)}, u32[]{:S(2)}, u32[]{:S(2)}) %collective-permute-start.24) | collective-permute-done | bytes 663584 | tf_op jit(solution)/shard_map/ppermute | solution.py:1267
  183.9 13.3 %attn_out.1 = (f32[768,1152]{1,0:T(8,128)}, bf16[768,1152]{1,0:T(8,128)(2,1)}) custom-call(s32[1]{0:T(128)} %bitcast.4.spot, bf16[768,384]{1,0:T(8,128)(2,1)} %get-tuple-element.155.one, bf16[768,384]{1,0:T(8,128)(2,1)} %get-tuple-element.156.two, bf16[768,384]{1,0:T(8,128)(2,1)} %get-tuple-element.157.three, bf16[768,384]{1,0:T(8,128)(2,1)} %get-tuple-element.158.four, ...), custom_call_target="tpu_custom_call" | custom-call | tf_op jit(solution)/shard_map/attn_out/pallas_call | solution.py:1079
  200.7 13.8 %mlp_up.2 = (bf16[2,768,1152]{2,1,0:T(8,128)(2,1)}, bf16[2,768,1152]{2,1,0:T(8,128)(2,1)}) custom-call(s32[1]{0:T(128)} %bitcast.4.spot, bf16[768,1152]{1,0:T(8,128)(2,1)} %get-tuple-element.160.x_ref.refs_0_, f32[2,1,1152]{2,1,0:T(1,128)} %get-tuple-element.161.bias_ref, bf16[4,144,1152]{2,1,0:T(8,128)(2,1)} %get-tuple-element.162.refs_0_, ...), custom_call_target="tpu_custom_call" | custom-call | tf_op jit(solution)/shard_map/mlp_up/pallas_call | solution.py:757
  221.9 12.8 %collective-permute-done.30.refs_0_ = bf16[2,144,1152]{2,1,0:T(8,128)(2,1)S(1)} collective-permute-done((bf16[2,144,1152]{2,1,0:T(8,128)(2,1)S(1)}, bf16[2,144,1152]{2,1,0:T(8,128)(2,1)S(1)}, u32[]{:S(2)}, u32[]{:S(2)}) %collective-permute-start.30) | collective-permute-done | bytes 663584 | tf_op jit(solution)/shard_map/ppermute | solution.py:1267
  234.6 14.1 %mlp_up.3 = (bf16[2,768,1152]{2,1,0:T(8,128)(2,1)}, bf16[2,768,1152]{2,1,0:T(8,128)(2,1)}) custom-call(s32[1]{0:T(128)} %bitcast.4.spot, bf16[768,1152]{1,0:T(8,128)(2,1)} %get-tuple-element.160.x_ref.refs_0_, f32[2,1,1152]{2,1,0:T(1,128)} %get-tuple-element.170.bias_ref, bf16[4,144,1152]{2,1,0:T(8,128)(2,1)} %get-tuple-element.140.refs_0_.refs_5_, ...), custom_call_target="tpu_custom_call" | custom-call | tf_op jit(solution)/shard_map/mlp_up/pallas_call | solution.py:757
  250.2 15.1 %weight_grad.3 = (bf16[4,144,1152]{2,1,0:T(8,128)(2,1)}, bf16[4,144,1152]{2,1,0:T(8,128)(2,1)}, bf16[4,144,1152]{2,1,0:T(8,128)(2,1)}, bf16[2,144,1152]{2,1,0:T(8,128)(2,1)}, bf16[2,144,1152]{2,1,0:T(8,128)(2,1)}) custom-call(s32[1]{0:T(128)} %bitcast.4.spot, bf16[768,1152]{1,0:T(8,128)(2,1)} %get-tuple-element.138.refs_0_.x_ref.grad_ref, ...), custom_call_target="tpu_custom_call" | custom-call | tf_op jit(solution)/shard_map/weight_grad/pallas_call | solution.py:1164
  269.4 11.9 %mlp_grad.2 = (bf16[2,768,1152]{2,1,0:T(8,128)(2,1)}, f32[2,1,1152]{2,1,0:T(1,128)}) custom-call(s32[1]{0:T(128)} %bitcast.4.spot, bf16[768,1152]{1,0:T(8,128)(2,1)} %get-tuple-element.138.refs_0_.x_ref.grad_ref, bf16[2,768,1152]{2,1,0:T(8,128)(2,1)} %get-tuple-element.181.slope_ref, bf16[4,144,1152]{2,1,0:T(8,128)(2,1)} %collective-permute-done.32.refs_0_, ...), custom_call_target="tpu_custom_call" | custom-call | tf_op jit(solution)/shard_map/mlp_grad/pallas_call | solution.py:801
  285.6 2.9 add_corners.3
  291.1 11.4 %mlp_grad.3 = (bf16[2,768,1152]{2,1,0:T(8,128)(2,1)}, f32[2,1,1152]{2,1,0:T(1,128)}) custom-call(s32[1]{0:T(128)} %bitcast.4.spot, bf16[768,1152]{1,0:T(8,128)(2,1)} %get-tuple-element.138.refs_0_.x_ref.grad_ref, bf16[2,768,1152]{2,1,0:T(8,128)(2,1)} %get-tuple-element.188.slope_ref, bf16[4,144,1152]{2,1,0:T(8,128)(2,1)} %get-tuple-element.152.refs_0_.refs_5_, ...), custom_call_target="tpu_custom_call" | custom-call | tf_op jit(solution)/shard_map/mlp_grad/pallas_call | solution.py:801
  302.5 15.1 %weight_grad.4 = (bf16[4,144,1152]{2,1,0:T(8,128)(2,1)}, bf16[4,144,1152]{2,1,0:T(8,128)(2,1)}, bf16[4,144,1152]{2,1,0:T(8,128)(2,1)}, bf16[2,144,1152]{2,1,0:T(8,128)(2,1)}, bf16[2,144,1152]{2,1,0:T(8,128)(2,1)}) custom-call(s32[1]{0:T(128)} %bitcast.4.spot, bf16[768,1152]{1,0:T(8,128)(2,1)} %get-tuple-element.160.x_ref.refs_0_, ...), custom_call_target="tpu_custom_call" | custom-call | tf_op jit(solution)/shard_map/weight_grad/pallas_call | solution.py:1164
  321.4 4.3 add_square.3
  328.5 24.2 %norm_two_back.1 = (f32[768,1152]{1,0:T(8,128)}, bf16[768,1152]{1,0:T(8,128)(2,1)}, f32[8,1152]{1,0:T(8,128)}) custom-call(s32[1]{0:T(128)} %bitcast.4.spot, bf16[2,768,1152]{2,1,0:T(8,128)(2,1)} %get-tuple-element.190.later_ref, bf16[2,768,1152]{2,1,0:T(8,128)(2,1)} %get-tuple-element.189.refs_1_.early_ref, f32[768,1152]{1,0:T(8,128)} %get-tuple-element.173.resid_ref, ...), custom_call_target="tpu_custom_call" | custom-call | tf_op jit(solution)/shard_map/norm_two_back/pallas_call | solution.py:914
  353.8 2.9 add_corners.4
  358.0 24.6 %heads_backward.3 = (bf16[2,768,896]{2,1,0:T(8,128)(2,1)}, f32[2,1,896]{2,1,0:T(1,128)}) custom-call(s32[1]{0:T(128)} %bitcast.4.spot, s32[768,1]{1,0:T(8,128)} %get-tuple-element.141.kind_ref, bf16[768,1152]{1,0:T(8,128)(2,1)} %get-tuple-element.198.grad_ref.refs_4_, bf16[2,768,896]{2,1,0:T(8,128)(2,1)} %get-tuple-element.199.one_qkv, ...), custom_call_target="tpu_custom_call" | custom-call | tf_op jit(solution)/shard_map/heads_backward/pallas_call | solution.py:634
  382.6 4.6 collective-permute-done.47.refs_0_
  395.3 4.2 add_square.4
  401.5 4.7 rev.15
  410.6 24.7 %heads_backward.2 = (bf16[2,768,896]{2,1,0:T(8,128)(2,1)}, f32[2,1,896]{2,1,0:T(1,128)}) custom-call(s32[1]{0:T(128)} %bitcast.4.spot, s32[768,1]{1,0:T(8,128)} %get-tuple-element.141.kind_ref, bf16[768,1152]{1,0:T(8,128)(2,1)} %get-tuple-element.198.grad_ref.refs_4_, bf16[2,768,896]{2,1,0:T(8,128)(2,1)} %get-tuple-element.199.one_qkv, ...), custom_call_target="tpu_custom_call" | custom-call | tf_op jit(solution)/shard_map/heads_backward/pallas_call | solution.py:634
  445.5 18.1 %weight_grad.5 = (bf16[4,144,1152]{2,1,0:T(8,128)(2,1)}, bf16[4,144,1152]{2,1,0:T(8,128)(2,1)}, bf16[4,144,1152]{2,1,0:T(8,128)(2,1)}, bf16[2,144,1152]{2,1,0:T(8,128)(2,1)}, bf16[2,144,1152]{2,1,0:T(8,128)(2,1)}) custom-call(s32[1]{0:T(128)} %bitcast.4.spot, bf16[768,1152]{1,0:T(8,128)(2,1)} %get-tuple-element.142.x_ref.refs_0_, ...), custom_call_target="tpu_custom_call" | custom-call | tf_op jit(solution)/shard_map/weight_grad/pallas_call | solution.py:1164
  467.1 20.6 %norm_one_back.1 = (f32[768,1152]{1,0:T(8,128)}, f32[8,1152]{1,0:T(8,128)}) custom-call(s32[1]{0:T(128)} %bitcast.4.spot, bf16[2,768,896]{2,1,0:T(8,128)(2,1)} %get-tuple-element.213.later_ref, bf16[2,768,896]{2,1,0:T(8,128)(2,1)} %get-tuple-element.203.refs_1_.early_ref, bf16[768,1152]{1,0:T(8,128)(2,1)} %get-tuple-element.135.x_ref, ...), custom_call_target="tpu_custom_call" | custom-call | tf_op jit(solution)/shard_map/norm_one_back/pallas_call | solution.py:975
  488.9 3.0 add_corners.5
  504.0 18.2 %mlp_down.1.refs_3_ = bf16[768,1152]{1,0:T(8,128)(2,1)} custom-call(s32[1]{0:T(128)} %bitcast.4.spot, bf16[2,768,1152]{2,1,0:T(8,128)(2,1)} %get-tuple-element.167.refs_5_.later_ref, bf16[2,768,1152]{2,1,0:T(8,128)(2,1)} %get-tuple-element.172.refs_1_.early_ref, f32[768,1152]{1,0:T(8,128)} %get-tuple-element.173.resid_ref, ...), custom_call_target="tpu_custom_call" | custom-call | tf_op jit(solution)/shard_map/mlp_down/pallas_call | solution.py:1028
  526.2 4.5 add_square.5.refs_2_
  540.3 4.0 slice_select_fusion
  545.8 15.3 %reduce-scatter.8.cloned.1.call-done = bf16[1,144,1152]{2,1,0:T(8,128)(2,1)} async-done(((bf16[4,144,1152]{2,1,0:T(8,128)(2,1)}), bf16[1,144,1152]{2,1,0:T(8,128)(2,1)}) %reduce-scatter.8.cloned.1.call-update) | async-done | bytes 331792 | tf_op jit(solution)/shard_map/reduce_scatter | solution.py:1303
  (419 shorter events, 160.8 us)
Async XLA Ops:
  7.2 58.8 %all-gather.7.cloned.1.call-start = ((), (), s32[]{:S(2)}) async-start(), calls=%async_computation.6 | async-start | bytes 1658880 | tf_op jit(solution)/shard_map/all_gather | solution.py:1300
  31.0 69.1 %all-gather.9.cloned.1.call-start = ((), (), s32[]{:S(2)}) async-start(), calls=%async_computation.7 | async-start | bytes 1658880 | tf_op jit(solution)/shard_map/all_gather | solution.py:1300
  66.0 98.7 %all-gather.11.cloned.1.call-start = ((), (), s32[]{:S(2)}) async-start(), calls=%async_computation.8 | async-start | bytes 1658880 | tf_op jit(solution)/shard_map/all_gather | solution.py:1300
  66.1 33.1 %collective-permute-start.11 = (bf16[768,1152]{1,0:T(8,128)(2,1)}, bf16[768,1152]{1,0:T(8,128)(2,1)}, u32[]{:S(2)}, u32[]{:S(2)}) collective-permute-start(bf16[768,1152]{1,0:T(8,128)(2,1)} %get-tuple-element.138.refs_0_.x_ref.grad_ref), channel_id=1, source_target_pairs={{0,2},{1,3},{2,0},{3,1},{4,6},{5,7},{6,4},{7,5},{8,10},{9,11},{10,... | collective-permute-start | bytes 5308424 | tf_op jit(solution)/shard_map/ppermute | solution.py:1267
  66.1 31.8 %collective-permute-start.9 = (bf16[4,144,1152]{2,1,0:T(8,128)(2,1)}, bf16[4,144,1152]{2,1,0:T(8,128)(2,1)S(1)}, u32[]{:S(2)}, u32[]{:S(2)}) collective-permute-start(bf16[4,144,1152]{2,1,0:T(8,128)(2,1)} %get-tuple-element.134.refs_0_.refs_5_), channel_id=1, source_target_pairs={{0,4},{1,5},{2,6},{3,7},{4,0},{5,1},{6,2},{7,3},{8,12},{9,13},{10,... | collective-permute-start | bytes 3981320 | tf_op jit(solution)/shard_map/ppermute | solution.py:1267
  67.7 31.5 %collective-permute-start.10 = (bf16[4,144,1152]{2,1,0:T(8,128)(2,1)}, bf16[4,144,1152]{2,1,0:T(8,128)(2,1)}, u32[]{:S(2)}, u32[]{:S(2)}) collective-permute-start(bf16[4,144,1152]{2,1,0:T(8,128)(2,1)} %get-tuple-element.134.refs_0_.refs_5_), channel_id=1, source_target_pairs={{0,1},{1,0},{2,3},{3,2},{4,5},{5,4},{6,7},{7,6},{8,9},{9,8},{10,11... | collective-permute-start | bytes 3981320 | tf_op jit(solution)/shard_map/ppermute | solution.py:1267
  69.1 37.7 %collective-permute-start.18 = (bf16[4,144,1152]{2,1,0:T(8,128)(2,1)}, bf16[4,144,1152]{2,1,0:T(8,128)(2,1)}, u32[]{:S(2)}, u32[]{:S(2)}) collective-permute-start(bf16[4,144,1152]{2,1,0:T(8,128)(2,1)} %get-tuple-element.134.refs_0_.refs_5_), channel_id=1, source_target_pairs={{0,2},{1,3},{2,0},{3,1},{4,6},{5,7},{6,4},{7,5},{8,10},{9,11},{10,... | collective-permute-start | bytes 3981320 | tf_op jit(solution)/shard_map/ppermute | solution.py:1267
  100.1 41.0 %collective-permute-start.17 = (bf16[4,144,1152]{2,1,0:T(8,128)(2,1)}, bf16[4,144,1152]{2,1,0:T(8,128)(2,1)S(1)}, u32[]{:S(2)}, u32[]{:S(2)}) collective-permute-start(bf16[4,144,1152]{2,1,0:T(8,128)(2,1)} %get-tuple-element.144.refs_0_.refs_4_.refs_2_.refs_7_), channel_id=1, source_target_pairs={{0,2},{1,3},{2,0},{3,1},{4,6},{5,7},{6,4},{7,5},{8,10},{9,11},{10,... | collective-permute-start | bytes 3981320 | tf_op jit(solution)/shard_map/ppermute | solution.py:1267
  104.1 283.6 %reduce-scatter.4.cloned.1.call-start = ((), (), s32[]{:S(2)}) async-start(), calls=%async_computation.3 | async-start | bytes 1658880 | tf_op jit(solution)/shard_map/reduce_scatter | solution.py:1303
  105.3 35.8 %collective-permute-start.16 = (bf16[2,144,1152]{2,1,0:T(8,128)(2,1)S(1)}, bf16[2,144,1152]{2,1,0:T(8,128)(2,1)}, u32[]{:S(2)}, u32[]{:S(2)}) collective-permute-start(bf16[2,144,1152]{2,1,0:T(8,128)(2,1)S(1)} %slice.236), channel_id=1, source_target_pairs={{0,4},{1,5},{2,6},{3,7},{4,0},{5,1},{6,2},{7,3},{8,12},{9,13},{10,... | collective-permute-start | bytes 1990664 | tf_op jit(solution)/shard_map/ppermute | solution.py:1267
  106.9 57.8 %collective-permute-start.12 = (bf16[4,144,1152]{2,1,0:T(8,128)(2,1)}, bf16[4,144,1152]{2,1,0:T(8,128)(2,1)}, u32[]{:S(2)}, u32[]{:S(2)}) collective-permute-start(bf16[4,144,1152]{2,1,0:T(8,128)(2,1)} %get-tuple-element.140.refs_0_.refs_5_), channel_id=1, source_target_pairs={{0,4},{1,5},{2,6},{3,7},{4,0},{5,1},{6,2},{7,3},{8,12},{9,13},{10,... | collective-permute-start | bytes 3981320 | tf_op jit(solution)/shard_map/ppermute | solution.py:1267
  119.8 44.9 %collective-permute-start.13 = (bf16[4,144,1152]{2,1,0:T(8,128)(2,1)}, bf16[4,144,1152]{2,1,0:T(8,128)(2,1)}, u32[]{:S(2)}, u32[]{:S(2)}) collective-permute-start(bf16[4,144,1152]{2,1,0:T(8,128)(2,1)} %get-tuple-element.140.refs_0_.refs_5_), channel_id=1, source_target_pairs={{0,1},{1,0},{2,3},{3,2},{4,5},{5,4},{6,7},{7,6},{8,9},{9,8},{10,11... | collective-permute-start | bytes 3981320 | tf_op jit(solution)/shard_map/ppermute | solution.py:1267
  121.2 43.4 %collective-permute-start.14 = (bf16[4,144,1152]{2,1,0:T(8,128)(2,1)}, bf16[4,144,1152]{2,1,0:T(8,128)(2,1)}, u32[]{:S(2)}, u32[]{:S(2)}) collective-permute-start(bf16[4,144,1152]{2,1,0:T(8,128)(2,1)} %get-tuple-element.140.refs_0_.refs_5_), channel_id=1, source_target_pairs={{0,2},{1,3},{2,0},{3,1},{4,6},{5,7},{6,4},{7,5},{8,10},{9,11},{10,... | collective-permute-start | bytes 3981320 | tf_op jit(solution)/shard_map/ppermute | solution.py:1267
  164.7 32.5 %collective-permute-start.26 = (bf16[4,144,1152]{2,1,0:T(8,128)(2,1)}, bf16[4,144,1152]{2,1,0:T(8,128)(2,1)}, u32[]{:S(2)}, u32[]{:S(2)}) collective-permute-start(bf16[4,144,1152]{2,1,0:T(8,128)(2,1)} %get-tuple-element.153.refs_1_.refs_6_), channel_id=1, source_target_pairs={{0,2},{1,3},{2,0},{3,1},{4,6},{5,7},{6,4},{7,5},{8,10},{9,11},{10,... | collective-permute-start | bytes 3981320 | tf_op jit(solution)/shard_map/ppermute | solution.py:1267
  170.2 44.3 %collective-permute-start.22 = (bf16[4,144,1152]{2,1,0:T(8,128)(2,1)}, bf16[4,144,1152]{2,1,0:T(8,128)(2,1)S(1)}, u32[]{:S(2)}, u32[]{:S(2)}) collective-permute-start(bf16[4,144,1152]{2,1,0:T(8,128)(2,1)} %get-tuple-element.152.refs_0_.refs_5_), channel_id=1, source_target_pairs={{0,4},{1,5},{2,6},{3,7},{4,0},{5,1},{6,2},{7,3},{8,12},{9,13},{10,... | collective-permute-start | bytes 3981320 | tf_op jit(solution)/shard_map/ppermute | solution.py:1267
  183.3 31.2 %collective-permute-start.23 = (bf16[4,144,1152]{2,1,0:T(8,128)(2,1)}, bf16[4,144,1152]{2,1,0:T(8,128)(2,1)S(1)}, u32[]{:S(2)}, u32[]{:S(2)}) collective-permute-start(bf16[4,144,1152]{2,1,0:T(8,128)(2,1)} %get-tuple-element.152.refs_0_.refs_5_), channel_id=1, source_target_pairs={{0,1},{1,0},{2,3},{3,2},{4,5},{5,4},{6,7},{7,6},{8,9},{9,8},{10,11... | collective-permute-start | bytes 3981320 | tf_op jit(solution)/shard_map/ppermute | solution.py:1267
  216.1 34.1 %collective-permute-start.37 = (bf16[2,768,1152]{2,1,0:T(8,128)(2,1)}, bf16[2,768,1152]{2,1,0:T(8,128)(2,1)}, u32[]{:S(2)}, u32[]{:S(2)}) collective-permute-start(bf16[2,768,1152]{2,1,0:T(8,128)(2,1)} %get-tuple-element.167.refs_5_.later_ref), channel_id=1, source_target_pairs={{0,2},{1,3},{2,0},{3,1},{4,6},{5,7},{6,4},{7,5},{8,10},{9,11},{10,... | collective-permute-start | bytes 10616840 | tf_op jit(solution)/shard_map/ppermute | solution.py:1267
  219.0 46.3 %collective-permute-start.32 = (bf16[4,144,1152]{2,1,0:T(8,128)(2,1)}, bf16[4,144,1152]{2,1,0:T(8,128)(2,1)}, u32[]{:S(2)}, u32[]{:S(2)}) collective-permute-start(bf16[4,144,1152]{2,1,0:T(8,128)(2,1)} %get-tuple-element.152.refs_0_.refs_5_), channel_id=1, source_target_pairs={{0,2},{1,3},{2,0},{3,1},{4,6},{5,7},{6,4},{7,5},{8,10},{9,11},{10,... | collective-permute-start | bytes 3981320 | tf_op jit(solution)/shard_map/ppermute | solution.py:1267
  219.0 47.8 %collective-permute-start.33 = (bf16[4,144,1152]{2,1,0:T(8,128)(2,1)}, bf16[4,144,1152]{2,1,0:T(8,128)(2,1)}, u32[]{:S(2)}, u32[]{:S(2)}) collective-permute-start(bf16[4,144,1152]{2,1,0:T(8,128)(2,1)} %get-tuple-element.168.refs_1_.refs_6_), channel_id=1, source_target_pairs={{0,2},{1,3},{2,0},{3,1},{4,6},{5,7},{6,4},{7,5},{8,10},{9,11},{10,... | collective-permute-start | bytes 3981320 | tf_op jit(solution)/shard_map/ppermute | solution.py:1267
  234.6 33.7 %collective-permute-start.34 = (bf16[4,144,1152]{2,1,0:T(8,128)(2,1)S(1)}, bf16[4,144,1152]{2,1,0:T(8,128)(2,1)}, u32[]{:S(2)}, u32[]{:S(2)}) collective-permute-start(bf16[4,144,1152]{2,1,0:T(8,128)(2,1)S(1)} %copy-done.10), channel_id=1, source_target_pairs={{0,2},{1,3},{2,0},{3,1},{4,6},{5,7},{6,4},{7,5},{8,10},{9,11},{10,... | collective-permute-start | bytes 3981320 | tf_op jit(solution)/shard_map/ppermute | solution.py:1267
  288.6 31.8 %collective-permute-start.40 = (bf16[4,144,1152]{2,1,0:T(8,128)(2,1)}, bf16[4,144,1152]{2,1,0:T(8,128)(2,1)S(1)}, u32[]{:S(2)}, u32[]{:S(2)}) collective-permute-start(bf16[4,144,1152]{2,1,0:T(8,128)(2,1)} %get-tuple-element.186.refs_5_), channel_id=1, source_target_pairs={{0,4},{1,5},{2,6},{3,7},{4,0},{5,1},{6,2},{7,3},{8,12},{9,13},{10,... | collective-permute-start | bytes 3981320 | tf_op jit(solution)/shard_map/ppermute | solution.py:1267
  289.6 31.6 %collective-permute-start.41 = (bf16[4,144,1152]{2,1,0:T(8,128)(2,1)}, bf16[4,144,1152]{2,1,0:T(8,128)(2,1)}, u32[]{:S(2)}, u32[]{:S(2)}) collective-permute-start(bf16[4,144,1152]{2,1,0:T(8,128)(2,1)} %get-tuple-element.187), channel_id=1, source_target_pairs={{0,1},{1,0},{2,3},{3,2},{4,5},{5,4},{6,7},{7,6},{8,9},{9,8},{10,11... | collective-permute-start | bytes 3981320 | tf_op jit(solution)/shard_map/ppermute | solution.py:1267
  325.6 162.1 %reduce-scatter.6.cloned.1.call-start = ((), (), s32[]{:S(2)}) async-start(), calls=%async_computation.4 | async-start | bytes 1658880 | tf_op jit(solution)/shard_map/reduce_scatter | solution.py:1303
  356.7 30.5 %collective-permute-start.47 = (bf16[4,144,1152]{2,1,0:T(8,128)(2,1)}, bf16[4,144,1152]{2,1,0:T(8,128)(2,1)S(1)}, u32[]{:S(2)}, u32[]{:S(2)}) collective-permute-start(bf16[4,144,1152]{2,1,0:T(8,128)(2,1)} %get-tuple-element.208.refs_5_), channel_id=1, source_target_pairs={{0,4},{1,5},{2,6},{3,7},{4,0},{5,1},{6,2},{7,3},{8,12},{9,13},{10,... | collective-permute-start | bytes 3981320 | tf_op jit(solution)/shard_map/ppermute | solution.py:1267
  388.8 56.6 %collective-permute-start.49 = (bf16[2,768,896]{2,1,0:T(8,128)(2,1)}, bf16[2,768,896]{2,1,0:T(8,128)(2,1)}, u32[]{:S(2)}, u32[]{:S(2)}) collective-permute-start(bf16[2,768,896]{2,1,0:T(8,128)(2,1)} %get-tuple-element.213.later_ref), channel_id=1, source_target_pairs={{0,2},{1,3},{2,0},{3,1},{4,6},{5,7},{6,4},{7,5},{8,10},{9,11},{10,... | collective-permute-start | bytes 8257544 | tf_op jit(solution)/shard_map/ppermute | solution.py:1267
  391.2 54.2 %collective-permute-start.46 = (bf16[768,1152]{1,0:T(8,128)(2,1)S(1)}, bf16[768,1152]{1,0:T(8,128)(2,1)}, u32[]{:S(2)}, u32[]{:S(2)}) collective-permute-start(bf16[768,1152]{1,0:T(8,128)(2,1)S(1)} %copy-done.2), channel_id=1, source_target_pairs={{0,2},{1,3},{2,0},{3,1},{4,6},{5,7},{6,4},{7,5},{8,10},{9,11},{10,... | collective-permute-start | bytes 5308424 | tf_op jit(solution)/shard_map/ppermute | solution.py:1267
  393.6 51.8 %collective-permute-start.51 = (bf16[2,768,384]{2,1,0:T(8,128)(2,1)}, bf16[2,768,384]{2,1,0:T(8,128)(2,1)}, u32[]{:S(2)}, u32[]{:S(2)}) collective-permute-start(bf16[2,768,384]{2,1,0:T(8,128)(2,1)} %pad_maximum_fusion.1), channel_id=1, source_target_pairs={{0,2},{1,3},{2,0},{3,1},{4,6},{5,7},{6,4},{7,5},{8,10},{9,11},{10,... | collective-permute-start | bytes 3538952 | tf_op jit(solution)/shard_map/ppermute | solution.py:1267
  399.5 161.6 %reduce-scatter.8.cloned.1.call-start = ((), (), s32[]{:S(2)}) async-start(), calls=%async_computation.5 | async-start | bytes 1658880 | tf_op jit(solution)/shard_map/reduce_scatter | solution.py:1303
  400.3 45.1 %collective-permute-start.50 = (bf16[768,1152]{1,0:T(8,128)(2,1)S(1)}, bf16[768,1152]{1,0:T(8,128)(2,1)}, u32[]{:S(2)}, u32[]{:S(2)}) collective-permute-start(bf16[768,1152]{1,0:T(8,128)(2,1)S(1)} %copy-done.5), channel_id=1, source_target_pairs={{0,2},{1,3},{2,0},{3,1},{4,6},{5,7},{6,4},{7,5},{8,10},{9,11},{10,... | collective-permute-start | bytes 5308424 | tf_op jit(solution)/shard_map/ppermute | solution.py:1267
  491.8 32.2 %collective-permute-start.54 = (bf16[4,144,1152]{2,1,0:T(8,128)(2,1)}, bf16[4,144,1152]{2,1,0:T(8,128)(2,1)S(1)}, u32[]{:S(2)}, u32[]{:S(2)}) collective-permute-start(bf16[4,144,1152]{2,1,0:T(8,128)(2,1)} %get-tuple-element.228.refs_10_), channel_id=1, source_target_pairs={{0,4},{1,5},{2,6},{3,7},{4,0},{5,1},{6,2},{7,3},{8,12},{9,13},{10,... | collective-permute-start | bytes 3981320 | tf_op jit(solution)/shard_map/ppermute | solution.py:1267
  493.0 31.9 %collective-permute-start.55 = (bf16[4,144,1152]{2,1,0:T(8,128)(2,1)}, bf16[4,144,1152]{2,1,0:T(8,128)(2,1)S(1)}, u32[]{:S(2)}, u32[]{:S(2)}) collective-permute-start(bf16[4,144,1152]{2,1,0:T(8,128)(2,1)} %get-tuple-element.230), channel_id=1, source_target_pairs={{0,1},{1,0},{2,3},{3,2},{4,5},{5,4},{6,7},{7,6},{8,9},{9,8},{10,11... | collective-permute-start | bytes 3981320 | tf_op jit(solution)/shard_map/ppermute | solution.py:1267
  498.5 32.8 %collective-permute-start.64 = (f32[72,1152]{1,0:T(8,128)}, f32[72,1152]{1,0:T(8,128)S(1)}, u32[]{:S(2)}, u32[]{:S(2)}) collective-permute-start(f32[72,1152]{1,0:T(8,128)} %constant_dynamic-slice_fusion.1), channel_id=1, source_target_pairs={{0,2},{1,3},{2,0},{3,1},{4,6},{5,7},{6,4},{7,5},{8,10},{9,11},{10,... | collective-permute-start | bytes 995336 | tf_op jit(solution)/shard_map/ppermute | solution.py:1267
  (98 other events, 877.4 us)
Sparse Core Ops, SparseCore 0:
  31.2 34.7 all-gather.6
  68.1 31.9 all-gather.8
  104.2 31.0 all-gather.10
  325.8 30.1 reduce-scatter.3
  399.7 29.3 reduce-scatter.5
  530.8 30.3 reduce-scatter.7

commit v3 on v0

--- a/solution.py
+++ b/solution.py
@@ -1,6 +1,10 @@
+import functools
+
 import jax
 import jax.numpy as jnp
 from jax import lax
+from jax.experimental import pallas as pl
+from jax.experimental.pallas import tpu as pltpu
 from jax.sharding import PartitionSpec as P
 
 HEAD_DIM = 72
@@ -378,6 +382,1489 @@
     )
 
 
+LOG2E = 1.4426950408889634
+VMEM_BYTES = 60 * 1024 * 1024
+
+
+def head_window(head, base, width):
+    start = base + head * HEAD_DIM
+    first = start // 128 * 128
+    last = min(-(-(start + HEAD_DIM) // 128) * 128, width)
+    return start - first, first, last
+
+
+def only_head(values, lane, offset):
+    inside = (lane >= offset) & (lane < offset + HEAD_DIM)
+    return jnp.where(inside, values, 0)
+
+
+def with_lanes(values, lane, offset, first_column, second_column):
+    one, two = (0, 1) if offset >= 2 else (126, 127)
+    values = jnp.where(lane == one, first_column, values)
+    return jnp.where(lane == two, second_column, values)
+
+
+def lane_index(rows, first, last):
+    return lax.broadcasted_iota(jnp.int32, (rows, last - first), 1)
+
+
+def row_columns(kind):
+    image = kind == 0
+    padding = (kind == 1) | (kind == 2)
+    low = jnp.bfloat16
+    image_query = jnp.where(image, 1.0, 0.0).astype(low)
+    other_query = jnp.where(image, 0.0, 1.0).astype(low)
+    image_key = jnp.where(image, 0.0, -1e30).astype(low)
+    padding_key = jnp.where(padding, 0.0, -1e30).astype(low)
+    return image_query, other_query, image_key, padding_key
+
+
+def dot_last(left, right):
+    return lax.dot_general(
+        left, right, (((1,), (1,)), ((), ())), preferred_element_type=jnp.float32
+    )
+
+
+def dot_first(left, right):
+    return lax.dot_general(
+        left, right, (((0,), (0,)), ((), ())), preferred_element_type=jnp.float32
+    )
+
+
+def heads_forward_kernel(places, heads, waits, spot, kind_ref, x_any, bias_ref, *refs):
+    count = sum(len(parts) for parts in places)
+    pieces = refs[:count]
+    qkv_any, probs_any, *mixed_any = refs[count + waits : count + waits + 4]
+    x_ref, qkv_ref, probs_ref, keys_ref, values_ref, total_ref, mixed_ref = refs[-12:-5]
+    in_sems, out_sems, probs_sems, weights, sems = refs[-5:]
+    scale = HEAD_DIM ** (-0.5) * LOG2E
+    rows = x_ref.shape[0]
+    part = heads * HEAD_DIM
+    inner = qkv_ref.shape[2]
+    width = keys_ref.shape[1]
+    base = width - part
+    groups = len(places)
+    slots = probs_ref.shape[0]
+    copies = weight_copies(places, pieces, weights, sems, spot[0])
+    x_copy = pltpu.make_async_copy(x_any, x_ref, in_sems.at[0])
+    begin([x_copy] + copies[0])
+    arrive([x_copy] + copies[0])
+    image_query, other_query, image_key, padding_key = row_columns(kind_ref[...])
+    blank = jnp.zeros((rows, base), jnp.bfloat16)
+    sent, writes = [], []
+    for group in range(groups):
+        if group + 1 < groups:
+            begin(copies[group + 1])
+        if group:
+            arrive(copies[group])
+        projected = jnp.dot(
+            x_ref[...], strips(weights, group)[:, :inner], preferred_element_type=jnp.float32
+        )
+        qkv_ref[group] = (projected + bias_ref[group]).astype(jnp.bfloat16)
+        copy = pltpu.make_async_copy(qkv_ref.at[group], qkv_any.at[group], out_sems.at[group])
+        copy.start()
+        sent.append(copy)
+        keys_ref[:, :part] = qkv_ref[group, :, part : 2 * part]
+        keys_ref[:, part:] = blank
+        values_ref[:, :base] = blank
+        values_ref[:, base:] = qkv_ref[group, :, 2 * part : 3 * part]
+        total_ref[...] = jnp.zeros_like(total_ref)
+        for head in range(heads):
+            offset, first, last = head_window(head, 0, width)
+            lane = lane_index(rows, first, last)
+            keys = with_lanes(
+                only_head(keys_ref[:, first:last], lane, offset),
+                lane,
+                offset,
+                image_key,
+                padding_key,
+            )
+            query = with_lanes(
+                only_head(qkv_ref[group, :, first:last], lane, offset),
+                lane,
+                offset,
+                image_query,
+                other_query,
+            )
+            v_offset, v_first, v_last = head_window(head, base, width)
+            values = only_head(
+                values_ref[:, v_first:v_last], lane_index(rows, v_first, v_last), v_offset
+            )
+            at = group * heads + head
+            slot = at % slots
+            if at >= slots:
+                writes[at - slots].wait()
+            for tile in row_tiles(rows, 384):
+                scores = dot_last(query[tile], keys)
+                peak = jnp.max(scores, axis=1, keepdims=True)
+                expo = jnp.exp2((scores - peak) * scale)
+                total = jnp.sum(expo, axis=1, keepdims=True)
+                probs = (expo * (1.0 / total)).astype(jnp.bfloat16)
+                probs_ref[slot, tile, :] = probs
+                total_ref[tile, v_first:v_last] += jnp.dot(
+                    probs, values, preferred_element_type=jnp.float32
+                )
+            copy = pltpu.make_async_copy(
+                probs_ref.at[slot], probs_any.at[group, head], probs_sems.at[slot]
+            )
+            copy.start()
+            writes.append(copy)
+        mixed_ref[group] = total_ref[...].astype(jnp.bfloat16)
+        copy = pltpu.make_async_copy(
+            mixed_ref.at[group], mixed_any[group], out_sems.at[groups + group]
+        )
+        copy.start()
+        sent.append(copy)
+    arrive(sent + writes[-slots:])
+
+
+def heads_forward_call(spot, kind, rows_in, biases, groups, waits=()):
+    rows, full = rows_in.shape
+    arrays, places = flatten(groups)
+    _, high, group_width = arrays[0].shape
+    depth = full // (2 * high)
+    count = len(groups)
+    part = group_width // 4
+    heads = part // HEAD_DIM
+    inner = -(-3 * part // 128) * 128
+    outer = -(-part // 128) * 128
+    slots = min(8, count * heads)
+    return call(
+        functools.partial(heads_forward_kernel, places, heads, len(waits)),
+        "heads_forward",
+        [spot, kind, rows_in, biases, *arrays],
+        [smem_spec(), vmem_spec(), any_spec(), vmem_spec()] + [any_spec()] * len(arrays),
+        [
+            (any_spec(), (count, rows, inner), jnp.bfloat16),
+            (any_spec(), (count, heads, rows, rows), jnp.bfloat16),
+            (any_spec(), (rows, outer), jnp.bfloat16),
+            (any_spec(), (rows, outer), jnp.bfloat16),
+        ],
+        [
+            low_scratch(rows, full),
+            low_scratch(count, rows, inner),
+            low_scratch(slots, rows, rows),
+            low_scratch(rows, outer),
+            low_scratch(rows, outer),
+            wide_scratch(rows, outer),
+            low_scratch(count, rows, outer),
+            copy_sems(1),
+            copy_sems(2 * count),
+            copy_sems(slots),
+        ]
+        + weight_scratch(places, depth, high, group_width),
+        waits,
+    )
+
+
+def heads_backward_kernel(places, heads, picks, waits, spot, grad_any, qkv_any, probs_any, *refs):
+    count = sum(len(parts) for parts in places)
+    groups = len(places)
+    mixed_any = refs[:groups]
+    pieces = refs[groups : groups + count]
+    first_out = groups + count + waits
+    outs_any = refs[first_out : first_out + groups]
+    sum_ref = refs[first_out + groups]
+    grad_ref, qkv_ref, probs_ref, mixed_ref, out_ref, keys_ref, values_ref, grads_ref = refs[-16:-8]
+    query_sum, key_sum, value_sum, in_sems, probs_sems, out_sems, weights, sems = refs[-8:]
+    width = keys_ref.shape[1]
+    first_lane = pieces[0].shape[2] - width
+    loads = weight_copies(places, pieces, weights, sems, spot[0], first_lane, width)
+    grad_copy = pltpu.make_async_copy(grad_any, grad_ref, in_sems.at[2 * groups])
+    slots = probs_ref.shape[0]
+    seconds, reads = [], []
+    for group in range(groups):
+        seconds.append(
+            [
+                pltpu.make_async_copy(
+                    qkv_any.at[picks[group]], qkv_ref.at[group], in_sems.at[2 * group]
+                ),
+                pltpu.make_async_copy(
+                    mixed_any[group], mixed_ref.at[group], in_sems.at[2 * group + 1]
+                ),
+            ]
+        )
+        for head in range(heads):
+            slot = len(reads) % slots
+            reads.append(
+                pltpu.make_async_copy(
+                    probs_any.at[picks[group], head], probs_ref.at[slot], probs_sems.at[slot]
+                )
+            )
+    begin([grad_copy] + loads[0])
+    begin(seconds[0])
+    begin(reads[:2])
+    score_scale = HEAD_DIM ** (-0.5)
+    rows = grad_ref.shape[0]
+    part = heads * HEAD_DIM
+    base = width - part
+    low = jnp.bfloat16
+    blank = jnp.zeros((rows, base), low)
+    sent = []
+    started = 2
+    for group in range(groups):
+        arrive(([grad_copy] if group == 0 else []) + loads[group])
+        grads_ref[...] = jnp.dot(
+            grad_ref[...], strips(weights, group), preferred_element_type=jnp.float32
+        ).astype(low)
+        arrive(seconds[group])
+        if group + 1 < groups:
+            begin(loads[group + 1] + seconds[group + 1])
+        keys_ref[:, :part] = qkv_ref[group, :, part : 2 * part]
+        keys_ref[:, part:] = blank
+        values_ref[:, :base] = blank
+        values_ref[:, base:] = qkv_ref[group, :, 2 * part : 3 * part]
+        query_sum[...] = jnp.zeros_like(query_sum)
+        key_sum[...] = jnp.zeros_like(key_sum)
+        value_sum[...] = jnp.zeros_like(value_sum)
+        weighted = grads_ref[...].astype(jnp.float32) * mixed_ref[group].astype(jnp.float32)
+        for head in range(heads):
+            at = group * heads + head
+            offset, first, last = head_window(head, 0, width)
+            lane = lane_index(rows, first, last)
+            query = only_head(qkv_ref[group, :, first:last], lane, offset)
+            keys = only_head(keys_ref[:, first:last], lane, offset)
+            v_offset, v_first, v_last = head_window(head, base, width)
+            v_lane = lane_index(rows, v_first, v_last)
+            values = values_ref[:, v_first:v_last]
+            grad = only_head(grads_ref[:, v_first:v_last], v_lane, v_offset)
+            centre = jnp.sum(
+                only_head(weighted[:, v_first:v_last], v_lane, v_offset), axis=1, keepdims=True
+            )
+            while started < len(reads) and started - at < slots:
+                reads[started].start()
+                started += 1
+            reads[at].wait()
+            probs = probs_ref[at % slots]
+            grad_probs = dot_last(grad, values)
+            grad_scores = (probs.astype(jnp.float32) * (grad_probs - centre)).astype(low)
+            value_sum[:, v_first:v_last] += dot_first(probs, grad)
+            key_sum[:, first:last] += dot_first(grad_scores, query)
+            query_sum[:, first:last] += jnp.dot(
+                grad_scores, keys, preferred_element_type=jnp.float32
+            )
+        out_ref[group, :, :part] = (query_sum[...] * score_scale).astype(low)[:, :part]
+        out_ref[group, :, part : 2 * part] = (key_sum[...] * score_scale).astype(low)[:, :part]
+        out_ref[group, :, 2 * part : 3 * part] = value_sum[...].astype(low)[:, base:]
+        tail = out_ref.shape[2] - 3 * part
+        if tail:
+            out_ref[group, :, 3 * part :] = jnp.zeros((rows, tail), low)
+        copy = pltpu.make_async_copy(out_ref.at[group], outs_any[group], out_sems.at[group])
+        copy.start()
+        sent.append(copy)
+        sum_ref[group] = jnp.sum(out_ref[group].astype(jnp.float32), axis=0, keepdims=True)
+    arrive(sent)
+
+
+def heads_backward_call(spot, grad_rows, qkv, probs, mixed, groups, picks, waits=()):
+    rows, full = grad_rows.shape
+    arrays, places = flatten(groups)
+    _, high, group_width = arrays[0].shape
+    depth = full // (2 * high)
+    part = group_width // 4
+    heads = part // HEAD_DIM
+    inner = qkv.shape[2]
+    outer = mixed[0].shape[1]
+    count = len(groups)
+    slots = min(count * heads, 6)
+    return call(
+        functools.partial(heads_backward_kernel, places, heads, picks, len(waits)),
+        "heads_backward",
+        [spot, grad_rows, qkv, probs, *mixed, *arrays],
+        [smem_spec()] + [any_spec()] * (3 + count + len(arrays)),
+        [(any_spec(), (rows, inner), jnp.bfloat16)] * count
+        + [(vmem_spec(), (count, 1, inner), jnp.float32)],
+        [
+            low_scratch(rows, full),
+            low_scratch(count, rows, inner),
+            low_scratch(slots, rows, rows),
+            low_scratch(count, rows, outer),
+            low_scratch(count, rows, inner),
+            low_scratch(rows, outer),
+            low_scratch(rows, outer),
+            low_scratch(rows, outer),
+            wide_scratch(rows, outer),
+            wide_scratch(rows, outer),
+            wide_scratch(rows, outer),
+            copy_sems(2 * count + 1),
+            copy_sems(slots),
+            copy_sems(count),
+        ]
+        + weight_scratch(places, depth, high, outer),
+        waits,
+    )
+
+
+def any_spec():
+    return pl.BlockSpec(memory_space=pl.ANY)
+
+
+def smem_spec():
+    return pl.BlockSpec(memory_space=pltpu.SMEM)
+
+
+def vmem_spec():
+    return pl.BlockSpec(memory_space=pltpu.VMEM)
+
+
+def limits():
+    return pltpu.CompilerParams(vmem_limit_bytes=VMEM_BYTES)
+
+
+def low_scratch(*shape):
+    return pltpu.VMEM(shape, jnp.bfloat16)
+
+
+def wide_scratch(*shape):
+    return pltpu.VMEM(shape, jnp.float32)
+
+
+def copy_sems(*shape):
+    return pltpu.SemaphoreType.DMA(shape)
+
+
+def begin(copies):
+    for copy in copies:
+        copy.start()
+
+
+def arrive(copies):
+    for copy in copies:
+        copy.wait()
+
+
+def call(kernel, name, operands, specs, outs, scratch, waits=()):
+    no_cost = pl.CostEstimate(flops=0, bytes_accessed=0, transcendentals=0)
+    out_specs = [spec for spec, _, _ in outs]
+    return pl.pallas_call(
+        kernel,
+        in_specs=list(specs) + [any_spec()] * len(waits),
+        out_specs=out_specs,
+        out_shape=[jax.ShapeDtypeStruct(shape, kind) for _, shape, kind in outs],
+        scratch_shapes=scratch,
+        compiler_params=limits(),
+        cost_estimate=no_cost,
+        name=name,
+    )(*operands, *waits)
+
+
+def flatten(groups):
+    arrays = [piece for group in groups for piece, _, _ in group]
+    places = [[(at, x_off) for _, at, x_off in group] for group in groups]
+    return arrays, places
+
+
+def weight_copies(places, refs, weights, sems, x_at, first=0, width=None):
+    copies, at = [], 0
+    for group, parts in enumerate(places):
+        mine = []
+        for part, (start, x_off) in enumerate(parts):
+            source = refs[at]
+            at += 1
+            if width is not None:
+                source = source.at[:, :, pl.ds(first, width)]
+            target = weights.at[group, pl.ds(start, source.shape[0]), x_at ^ x_off]
+            mine.append(pltpu.make_async_copy(source, target, sems.at[group, part]))
+        copies.append(mine)
+    return copies
+
+
+def weight_scratch(places, depth, high, width):
+    count = len(places)
+    return [
+        pltpu.VMEM((count, depth, 2, high, width), jnp.bfloat16),
+        copy_sems(count, max(len(parts) for parts in places)),
+    ]
+
+
+def strips(weights, at):
+    _, depth, _, high, width = weights.shape
+    return weights[at].reshape(depth * 2 * high, width)
+
+
+def row_tiles(rows, size):
+    return [slice(start, min(start + size, rows)) for start in range(0, rows, size)]
+
+
+def out_copies(pairs, sems):
+    return [
+        pltpu.make_async_copy(source, target, sems.at[i])
+        for i, (source, target) in enumerate(pairs)
+    ]
+
+
+def up_kernel(places, waits, spot, x_any, bias_ref, *refs):
+    count = sum(len(parts) for parts in places)
+    pieces = refs[:count]
+    active_any, slope_any = refs[count + waits : count + waits + 2]
+    x_ref, active_ref, slope_ref, x_sem, out_sems, weights, sems = refs[-7:]
+    rows = x_ref.shape[0]
+    groups = len(places)
+    copies = weight_copies(places, pieces, weights, sems, spot[0])
+    x_copy = pltpu.make_async_copy(x_any, x_ref, x_sem.at[0])
+    begin([x_copy] + copies[0])
+    arrive([x_copy] + copies[0])
+    sent = []
+    for group in range(groups):
+        if group + 1 < groups:
+            begin(copies[group + 1])
+        if group:
+            arrive(copies[group])
+        whole = strips(weights, group)
+        for tile in row_tiles(rows, 128):
+            hidden = jnp.dot(x_ref[tile, :], whole, preferred_element_type=jnp.float32)
+            hidden = hidden + bias_ref[group]
+            square = hidden * hidden
+            inner = jnp.tanh(hidden * (gelu_scale + gelu_scale * 0.044715 * square))
+            gate = 0.5 + 0.5 * inner
+            active_ref[group, tile, :] = (hidden * gate).astype(jnp.bfloat16)
+            grow = hidden * (gelu_scale + 3.0 * 0.044715 * gelu_scale * square)
+            slope = gate + grow * (0.5 - 0.5 * inner * inner)
+            slope_ref[group, tile, :] = slope.astype(jnp.bfloat16)
+        for half, tile in enumerate(row_tiles(rows, rows // 2)):
+            span = pl.ds(tile.start, rows // 2)
+            for at, (source, target) in enumerate(
+                ((active_ref, active_any), (slope_ref, slope_any))
+            ):
+                copy = pltpu.make_async_copy(
+                    source.at[group, span], target.at[group, span], out_sems.at[group, half, at]
+                )
+                copy.start()
+                sent.append(copy)
+    arrive(sent)
+
+
+def up_project(spot, rows_in, biases, groups, waits=()):
+    rows, full = rows_in.shape
+    arrays, places = flatten(groups)
+    _, high, width = arrays[0].shape
+    depth = full // (2 * high)
+    count = len(groups)
+    shape = (count, rows, width)
+    return call(
+        functools.partial(up_kernel, places, len(waits)),
+        "mlp_up",
+        [spot, rows_in, biases, *arrays],
+        [smem_spec(), any_spec(), vmem_spec()] + [any_spec()] * len(arrays),
+        [(any_spec(), shape, jnp.bfloat16)] * 2,
+        [
+            low_scratch(rows, full),
+            low_scratch(*shape),
+            low_scratch(*shape),
+            copy_sems(1),
+            copy_sems(count, 2, 2),
+        ]
+        + weight_scratch(places, depth, high, width),
+        waits,
+    )
+
+
+def slope_kernel(places, waits, spot, x_any, slope_any, *refs):
+    count = sum(len(parts) for parts in places)
+    pieces = refs[:count]
+    out_any, sum_ref = refs[count + waits : count + waits + 2]
+    x_ref, slope_ref, out_ref, in_sems, out_sems, weights, sems = refs[-7:]
+    rows = x_ref.shape[0]
+    groups = len(places)
+    copies = weight_copies(places, pieces, weights, sems, spot[0])
+    x_copy = pltpu.make_async_copy(x_any, x_ref, in_sems.at[groups])
+    for group, mine in enumerate(copies):
+        mine.append(
+            pltpu.make_async_copy(slope_any.at[group], slope_ref.at[group], in_sems.at[group])
+        )
+    begin([x_copy] + copies[0])
+    arrive([x_copy] + copies[0])
+    sent = []
+    for group in range(groups):
+        if group + 1 < groups:
+            begin(copies[group + 1])
+        if group:
+            arrive(copies[group])
+        whole = strips(weights, group)
+        total = jnp.zeros((1, weights.shape[-1]), jnp.float32)
+        for tile in row_tiles(rows, 256):
+            grad = jnp.dot(x_ref[tile, :], whole, preferred_element_type=jnp.float32)
+            low = (grad * slope_ref[group, tile, :].astype(jnp.float32)).astype(jnp.bfloat16)
+            out_ref[group, tile, :] = low
+            total += jnp.sum(low.astype(jnp.float32), axis=0, keepdims=True)
+        sum_ref[group] = total
+        for half, tile in enumerate(row_tiles(rows, rows // 2)):
+            span = pl.ds(tile.start, rows // 2)
+            copy = pltpu.make_async_copy(
+                out_ref.at[group, span], out_any.at[group, span], out_sems.at[group, half]
+            )
+            copy.start()
+            sent.append(copy)
+    arrive(sent)
+
+
+def hidden_grad(spot, rows_in, slope, groups, waits=()):
+    rows, full = rows_in.shape
+    arrays, places = flatten(groups)
+    _, high, width = arrays[0].shape
+    depth = full // (2 * high)
+    count = len(groups)
+    shape = (count, rows, width)
+    return call(
+        functools.partial(slope_kernel, places, len(waits)),
+        "mlp_grad",
+        [spot, rows_in, slope, *arrays],
+        [smem_spec(), any_spec(), any_spec()] + [any_spec()] * len(arrays),
+        [
+            (any_spec(), shape, jnp.bfloat16),
+            (vmem_spec(), (count, 1, width), jnp.float32),
+        ],
+        [
+            low_scratch(rows, full),
+            low_scratch(*shape),
+            low_scratch(*shape),
+            copy_sems(count + 1),
+            copy_sems(count, 2),
+        ]
+        + weight_scratch(places, depth, high, width),
+        waits,
+    )
+
+
+def unit_rows(values):
+    centre = values - jnp.mean(values, axis=1, keepdims=True)
+    spread = jnp.mean(centre * centre, axis=1, keepdims=True)
+    root = lax.rsqrt(spread + layer_eps)
+    return centre * root, root
+
+
+def norm_rows_back(values, gain, grad):
+    unit, root = unit_rows(values)
+    scaled = grad * gain
+    mean_one = jnp.mean(scaled, axis=1, keepdims=True)
+    mean_two = jnp.mean(scaled * unit, axis=1, keepdims=True)
+    part = root * (scaled - mean_one - unit * mean_two)
+    return part, jnp.sum(grad * unit, axis=0, keepdims=True), jnp.sum(grad, axis=0, keepdims=True)
+
+
+def back_kernel(places, sources, waits, keep_low, spot, *refs):
+    count = sum(len(parts) for parts in places)
+    grads_any = refs[:sources]
+    base_any, grad_any, gain_ref = refs[sources : sources + 3]
+    pieces = refs[sources + 3 : sources + 3 + count]
+    outs = 3 if keep_low else 2
+    first_out = sources + 3 + count + waits
+    out_any, *low_any, sum_ref = refs[first_out : first_out + outs]
+    grads_ref, base_ref, grad_ref, total, in_sems, out_sems, weights, sems = refs[
+        first_out + outs : first_out + outs + 8
+    ]
+    rows = total.shape[0]
+    groups = len(places)
+    width = weights.shape[-1]
+    copies = weight_copies(places, pieces, weights, sems, spot[0], 0, width)
+    at = 0
+    for source in grads_any:
+        parts = [source] if len(source.shape) == 2 else [source.at[i] for i in range(source.shape[0])]
+        for part in parts:
+            copies[at].append(pltpu.make_async_copy(part, grads_ref.at[at], in_sems.at[at]))
+            at += 1
+    late = [
+        pltpu.make_async_copy(base_any, base_ref, in_sems.at[groups]),
+        pltpu.make_async_copy(grad_any, grad_ref, in_sems.at[groups + 1]),
+    ]
+    begin(copies[0])
+    for group in range(groups):
+        if group + 1 < groups:
+            begin(copies[group + 1])
+        else:
+            begin(late)
+        arrive(copies[group])
+        whole = strips(weights, group)
+        if group == 0:
+            total[...] = dot_last(grads_ref[group], whole)
+        elif group + 1 < groups:
+            total[...] += dot_last(grads_ref[group], whole)
+        else:
+            products = [
+                (tile, dot_last(grads_ref[group, tile, :], whole)) for tile in row_tiles(rows, 256)
+            ]
+    arrive(late)
+    sums = [jnp.zeros((1, total.shape[1]), jnp.float32) for _ in range(3)]
+    sent = []
+    for tile, product in products:
+        for small in range(tile.start, tile.stop, 128):
+            span = slice(small, small + 128)
+            inside = slice(small - tile.start, small - tile.start + 128)
+            part, gain_sum, shift_sum = norm_rows_back(
+                base_ref[span, :].astype(jnp.float32),
+                gain_ref[...],
+                total[span, :] + product[inside],
+            )
+            grad = grad_ref[span, :].astype(jnp.float32) + part
+            total[span, :] = grad
+            sums[0] += gain_sum
+            sums[1] += shift_sum
+            if keep_low:
+                low = grad.astype(jnp.bfloat16)
+                grads_ref[0, span, :] = low
+                sums[2] += jnp.sum(low.astype(jnp.float32), axis=0, keepdims=True)
+        long = pl.ds(tile.start, tile.stop - tile.start)
+        pairs = [(total.at[long], out_any.at[long])]
+        if keep_low:
+            pairs.append((grads_ref.at[0, long], low_any[0].at[long]))
+        for source, target in pairs:
+            copy = pltpu.make_async_copy(source, target, out_sems.at[len(sent)])
+            copy.start()
+            sent.append(copy)
+    sum_ref[...] = jnp.concatenate(sums + [jnp.zeros((5, total.shape[1]), jnp.float32)])
+    arrive(sent)
+
+
+def norm_back(name, spot, grads, base, grad, gain, groups, keep_low, waits=()):
+    rows, full = base.shape
+    arrays, places = flatten(groups)
+    _, high, _ = arrays[0].shape
+    width = grads[0].shape[-1]
+    depth = full // (2 * high)
+    outs = [(any_spec(), (rows, full), jnp.float32)]
+    if keep_low:
+        outs.append((any_spec(), (rows, full), jnp.bfloat16))
+    outs.append((vmem_spec(), (8, full), jnp.float32))
+    return call(
+        functools.partial(back_kernel, places, len(grads), len(waits), keep_low),
+        name,
+        [spot, *grads, base, grad, gain, *arrays],
+        [smem_spec()] + [any_spec()] * (len(grads) + 2) + [vmem_spec()] + [any_spec()] * len(arrays),
+        outs,
+        [
+            low_scratch(len(groups), rows, width),
+            pltpu.VMEM(base.shape, base.dtype),
+            pltpu.VMEM(grad.shape, grad.dtype),
+            wide_scratch(rows, full),
+            copy_sems(len(groups) + 2),
+            copy_sems(2 * -(-rows // 256)),
+        ]
+        + weight_scratch(places, depth, high, width),
+        waits,
+    )
+
+
+def down_kernel(places, waits, spot, later_any, early_any, resid_any, shift_ref, *refs):
+    count = sum(len(parts) for parts in places)
+    pieces = refs[:count]
+    out_any = refs[count + waits]
+    active_ref, resid_ref, total, out_ref, in_sems, out_sems, weights, sems = refs[-8:]
+    rows = total.shape[0]
+    groups = len(places)
+    copies = weight_copies(places, pieces, weights, sems, spot[0])
+    half = groups // 2
+    for group in range(groups):
+        source = later_any.at[group] if group < half else early_any.at[group - half]
+        copies[group].append(
+            pltpu.make_async_copy(source, active_ref.at[group], in_sems.at[group])
+        )
+    late = [pltpu.make_async_copy(resid_any, resid_ref, in_sems.at[groups])]
+    begin(copies[0])
+    for group in range(groups):
+        begin(copies[group + 1] if group + 1 < groups else late)
+        arrive(copies[group])
+        product = dot_last(active_ref[group], strips(weights, group))
+        if group == 0:
+            total[...] = product
+        else:
+            total[...] += product
+    arrive(late)
+    out_ref[...] = (total[...] + resid_ref[...] + shift_ref[...]).astype(out_ref.dtype)
+    copy = pltpu.make_async_copy(out_ref, out_any, out_sems.at[0])
+    copy.start()
+    copy.wait()
+
+
+def down_project(spot, first, second, resid, shift, groups, waits=()):
+    rows, full = resid.shape
+    arrays, places = flatten(groups)
+    _, high, width = arrays[0].shape
+    depth = full // (2 * high)
+    return call(
+        functools.partial(down_kernel, places, len(waits)),
+        "mlp_down",
+        [spot, first, second, resid, shift, *arrays],
+        [smem_spec()] + [any_spec()] * 3 + [vmem_spec()] + [any_spec()] * len(arrays),
+        [(any_spec(), (rows, full), jnp.bfloat16)],
+        [
+            low_scratch(len(groups), rows, width),
+            wide_scratch(rows, full),
+            wide_scratch(rows, full),
+            low_scratch(rows, full),
+            copy_sems(len(groups) + 1),
+            copy_sems(1),
+        ]
+        + weight_scratch(places, depth, high, width),
+        waits,
+    )[0]
+
+
+def out_kernel(places, waits, spot, one, two, three, four, x_any, shift_ref, gain_ref, bias_ref, *refs):
+    count = sum(len(parts) for parts in places)
+    pieces = refs[:count]
+    resid_any, normed_any = refs[count + waits : count + waits + 2]
+    mixed_ref, x_ref, resid_ref, normed_ref, in_sems, out_sems, weights, sems = refs[-8:]
+    rows = x_ref.shape[0]
+    outer = weights.shape[-1]
+    first = pieces[0].shape[-1] - outer
+    copies = weight_copies(places, pieces, weights, sems, spot[0], first, outer)
+    for group, mixed in enumerate((one, two, three, four)):
+        copies[group].append(
+            pltpu.make_async_copy(mixed, mixed_ref.at[group], in_sems.at[group])
+        )
+    late = [pltpu.make_async_copy(x_any, x_ref, in_sems.at[4])]
+    for mine in copies:
+        begin(mine)
+    begin(late)
+    for group in range(4):
+        arrive(copies[group])
+        if group < 3:
+            product = dot_last(mixed_ref[group], strips(weights, group))
+            if group == 0:
+                resid_ref[...] = product
+            else:
+                resid_ref[...] += product
+    arrive(late)
+    whole = strips(weights, 3)
+    products = [(tile, dot_last(mixed_ref[3, tile, :], whole)) for tile in row_tiles(rows, 256)]
+    sent = []
+    for tile, product in products:
+        for small in range(tile.start, tile.stop, 128):
+            span = slice(small, small + 128)
+            inside = slice(small - tile.start, small - tile.start + 128)
+            values = resid_ref[span, :] + product[inside] + x_ref[span, :].astype(jnp.float32)
+            values = values + shift_ref[...]
+            resid_ref[span, :] = values
+            unit, _ = unit_rows(values)
+            normed_ref[span, :] = (unit * gain_ref[...] + bias_ref[...]).astype(jnp.bfloat16)
+        long = pl.ds(tile.start, tile.stop - tile.start)
+        for source, target in ((resid_ref, resid_any), (normed_ref, normed_any)):
+            copy = pltpu.make_async_copy(source.at[long], target.at[long], out_sems.at[len(sent)])
+            copy.start()
+            sent.append(copy)
+    arrive(sent)
+
+
+def out_project(spot, mixed, rows_in, shift, gain, bias, groups, waits=()):
+    rows, full = rows_in.shape
+    arrays, places = flatten(groups)
+    _, high, _ = arrays[0].shape
+    outer = mixed[0].shape[1]
+    depth = full // (2 * high)
+    return call(
+        functools.partial(out_kernel, places, len(waits)),
+        "attn_out",
+        [spot, *mixed, rows_in, shift, gain, bias, *arrays],
+        [smem_spec()] + [any_spec()] * 5 + [vmem_spec()] * 3 + [any_spec()] * len(arrays),
+        [
+            (any_spec(), (rows, full), jnp.float32),
+            (any_spec(), (rows, full), jnp.bfloat16),
+        ],
+        [
+            low_scratch(4, rows, outer),
+            low_scratch(rows, full),
+            wide_scratch(rows, full),
+            low_scratch(rows, full),
+            copy_sems(5),
+            copy_sems(2 * -(-rows // 256)),
+        ]
+        + weight_scratch(places, depth, high, outer),
+        waits,
+    )
+
+
+def grad_kernel(sides, extra, waits, spot, *refs):
+    inputs = 4 + (4 if extra else 0)
+    sources = refs[:inputs]
+    outs_at = inputs + waits
+    count = sum(2 + side for side in sides)
+    outs = list(refs[outs_at : outs_at + count])
+    holds = refs[outs_at + count : outs_at + count + inputs]
+    stage, in_sems, out_sems = refs[-3:]
+    x_at = spot[0]
+    def load(source, hold, at):
+        return pltpu.make_async_copy(source, hold, in_sems.at[at])
+
+    count = len(sides)
+    first_x = load(sources[0], holds[0], 0)
+    second_x = load(sources[2], holds[2], 1)
+    firsts = [load(sources[1].at[i], holds[1].at[i], 2 + 2 * i) for i in range(count)]
+    seconds = [load(sources[3].at[i], holds[3].at[i], 3 + 2 * i) for i in range(count)]
+    extras = [load(sources[j], holds[j], 2 * count + j - 2) for j in range(4, inputs)]
+    _, depth, _, high, width = stage.shape
+    half = depth // 2
+    begin([first_x, firsts[0]])
+    arrive([first_x, firsts[0]])
+    begin([second_x, seconds[0]])
+    begin(extras)
+    sent = []
+    starts = []
+    for side in sides:
+        starts.append(sum(2 + before for before in sides[: len(starts)]))
+    for i, side in enumerate(sides):
+        if i:
+            arrive([firsts[i], seconds[i]])
+        for part in range(2):
+            cut = slice(part * half * 2 * high, (part + 1) * half * 2 * high)
+            span = pl.ds(part * half, half)
+            product = dot_first(holds[0][:, cut], holds[1][i])
+            if i == 0 and part == 0:
+                arrive([second_x, seconds[0]])
+                for later in range(1, count):
+                    begin([firsts[later], seconds[later]])
+            product += dot_first(holds[2][:, cut], holds[3][i])
+            if extra:
+                if i == 0 and part == 0:
+                    arrive(extras)
+                other = dot_first(holds[4][:, cut], holds[5][...])
+                other += dot_first(holds[6][:, cut], holds[7][...])
+                both = product.shape[1] + other.shape[1] - width
+                left = product.shape[1] - both
+                product = jnp.concatenate(
+                    [product[:, :left], product[:, left:] + other[:, :both], other[:, both:]],
+                    axis=1,
+                )
+            stage[i, part * half : (part + 1) * half] = product.astype(jnp.bfloat16).reshape(
+                half, 2, high, width
+            )
+            near_out = outs[starts[i]].at[span]
+            if side == 0:
+                far_out = outs[starts[i] + 1].at[span]
+            else:
+                far_out = outs[starts[i] + 1 + part]
+            for source, target in (
+                (stage.at[i, span, x_at], near_out),
+                (stage.at[i, span, 1 - x_at], far_out),
+            ):
+                copy = pltpu.make_async_copy(source, target, out_sems.at[len(sent)])
+                copy.start()
+                sent.append(copy)
+    arrive(sent)
+
+
+def weight_grad(spot, left, right, depth, sides=(0, 1), extra=(), waits=()):
+    rows, full = left[0].shape
+    high = full // (2 * depth)
+    half = depth // 2
+    count = len(sides)
+    rights = [values.reshape(count, rows, -1) for values in right]
+    width = full if extra else rights[0].shape[2]
+    operands = [left[0], rights[0], left[1], rights[1], *extra]
+    shapes = []
+    for side in sides:
+        shapes += [depth, depth] if side == 0 else [depth, half, half]
+    outs = [(any_spec(), (size, high, width), jnp.bfloat16) for size in shapes]
+    return call(
+        functools.partial(grad_kernel, sides, bool(extra), len(waits)),
+        "weight_grad",
+        [spot, *operands],
+        [smem_spec()] + [any_spec()] * len(operands),
+        outs,
+        [pltpu.VMEM(values.shape, values.dtype) for values in operands]
+        + [
+            low_scratch(count, depth, 2, high, width),
+            copy_sems(2 + 2 * count + 4),
+            copy_sems(4 * count),
+        ],
+        waits,
+    )
+
+
+def corner_kernel(beside_ref, across_ref, one_ref, two_ref, beside_out, across_out):
+    wide = jnp.float32
+    low = beside_out.dtype
+    beside_out[...] = (beside_ref[...].astype(wide) + two_ref[...].astype(wide)).astype(low)
+    across_out[...] = (across_ref[...].astype(wide) + one_ref[...].astype(wide)).astype(low)
+
+
+def add_corners(beside, across, corner_one, corner_two):
+    block = corner_one.shape
+    first = pl.BlockSpec(block, lambda i: (0, 0, 0))
+    second = pl.BlockSpec(block, lambda i: (1, 0, 0))
+    shape = jax.ShapeDtypeStruct(beside.shape, beside.dtype)
+    return pl.pallas_call(
+        corner_kernel,
+        grid=(1,),
+        in_specs=[second, first, first, first],
+        out_specs=[second, first],
+        out_shape=[shape, shape],
+        input_output_aliases={0: 0, 1: 1},
+        compiler_params=limits(),
+        name="add_corners",
+    )(beside, across, corner_one, corner_two)
+
+
+def one_corner_kernel(base_ref, part_ref, out_ref):
+    total = base_ref[...].astype(jnp.float32) + part_ref[...].astype(jnp.float32)
+    out_ref[...] = total.astype(out_ref.dtype)
+
+
+def add_corner(base, part, half):
+    block = part.shape
+    spec = pl.BlockSpec(block, lambda i: (half, 0, 0))
+    return pl.pallas_call(
+        one_corner_kernel,
+        grid=(1,),
+        in_specs=[spec, pl.BlockSpec(block, lambda i: (0, 0, 0))],
+        out_specs=spec,
+        out_shape=jax.ShapeDtypeStruct(base.shape, base.dtype),
+        input_output_aliases={0: 0},
+        compiler_params=limits(),
+        name="add_corner",
+    )(base, part)
+
+
+def square_kernel(own, one, two, out):
+    wide = jnp.float32
+    total = own[...].astype(wide) + one[...].astype(wide) + two[...].astype(wide)
+    out[...] = total.astype(out.dtype)
+
+
+def add_square(own, one, two):
+    depth, high, width = own.shape
+    block = pl.BlockSpec((depth // 2, high, width), lambda i: (i, 0, 0))
+    return pl.pallas_call(
+        square_kernel,
+        grid=(2,),
+        in_specs=[block, block, block],
+        out_specs=block,
+        out_shape=jax.ShapeDtypeStruct(own.shape, own.dtype),
+        compiler_params=limits(),
+        name="add_square",
+    )(own, one, two)
+
+
+def halves_kernel(first_ref, second_ref, first_out, second_out):
+    first_out[...] = first_ref[...]
+    second_out[...] = second_ref[...]
+
+
+def take_halves(first, second):
+    half = (first.shape[0] // 2,) + first.shape[1:]
+    front = pl.BlockSpec(half, lambda i: (0, 0, 0))
+    back = pl.BlockSpec(half, lambda i: (1, 0, 0))
+    shape = jax.ShapeDtypeStruct(half, first.dtype)
+    return pl.pallas_call(
+        halves_kernel,
+        grid=(1,),
+        in_specs=[front, back],
+        out_specs=[front, front],
+        out_shape=[shape, shape],
+        compiler_params=limits(),
+        name="take_halves",
+    )(first, second)
+
+
+PATCHES = 729
+AXES = ("dp", "tensor")
+
+
+def nothing(*refs):
+    del refs
+
+
+def fence(released, waited=()):
+    anywhere = pl.BlockSpec(memory_space=pl.ANY)
+    released, waited = list(released), list(waited)
+    return pl.pallas_call(
+        nothing,
+        in_specs=[anywhere] * (len(released) + len(waited)),
+        out_specs=[anywhere] * len(released),
+        out_shape=[jax.ShapeDtypeStruct(values.shape, values.dtype) for values in released],
+        input_output_aliases={i: i for i in range(len(released))},
+        name="fence",
+    )(*released, *waited)
+
+
+class Grid:
+    def __init__(self, depth):
+        self.depth = depth
+        dp_at = lax.axis_index("dp")
+        self.y = lax.axis_index("tensor")
+        self.c = dp_at % 2
+        self.x = dp_at // 2 % 2
+        self.z = dp_at // 4
+
+    def move(self, values, where):
+        pairs = []
+        for z in range(self.depth):
+            for x in range(2):
+                for c in range(2):
+                    for y in range(2):
+                        to_z, to_x, to_c, to_y = where(z, x, c, y)
+                        pairs.append(
+                            (
+                                ((z * 2 + x) * 2 + c) * 2 + y,
+                                ((to_z * 2 + to_x) * 2 + to_c) * 2 + to_y,
+                            )
+                        )
+        return lax.ppermute(values, AXES, pairs)
+
+    def over_x(self, values):
+        return self.move(values, lambda z, x, c, y: (z, 1 - x, c, y))
+
+    def over_y(self, values):
+        return self.move(values, lambda z, x, c, y: (z, x, c, 1 - y))
+
+    def over_core(self, values):
+        return self.move(values, lambda z, x, c, y: (z, x, 1 - c, y))
+
+    def along_z(self, values, hops):
+        return self.move(values, lambda z, x, c, y: ((z + hops) % self.depth, x, c, y))
+
+    def across_z(self, values, bit):
+        return self.move(values, lambda z, x, c, y: (z ^ bit, x, c, y))
+
+    def spread(self, block):
+        width = block.shape[1] // 2
+        mine = lax.dynamic_slice_in_dim(block, self.c * width, width, 1)
+        theirs = self.over_core(
+            lax.dynamic_slice_in_dim(block, (1 - self.c) * width, width, 1)
+        )
+        first = jnp.where(self.c == 0, mine, theirs)
+        second = jnp.where(self.c == 0, theirs, mine)
+        return jnp.concatenate([first, second])
+
+    def depth_groups(self):
+        return [
+            [(z * 2 + x) * 2 + c for z in range(self.depth)] for x in range(2) for c in range(2)
+        ]
+
+    def gather_depth(self, block):
+        return lax.all_gather(block, "dp", axis_index_groups=self.depth_groups())
+
+    def scatter_depth(self, total):
+        return lax.psum_scatter(total, "dp", axis_index_groups=self.depth_groups())
+
+    def scatter_core(self, result):
+        result = result.astype(jnp.float32)
+        shard = result.shape[0] // 2
+        mine = lax.dynamic_slice_in_dim(result, self.c * shard, shard)
+        theirs = self.over_core(
+            lax.dynamic_slice_in_dim(result, (1 - self.c) * shard, shard)
+        )
+        first = jnp.where(self.c == 0, mine, theirs)
+        second = jnp.where(self.c == 0, theirs, mine)
+        return jnp.stack([first, second])
+
+    def gather_small(self, values):
+        count, shard = values.shape
+        parts = jnp.zeros((self.depth, 2, 2, count, shard), values.dtype)
+        parts = lax.dynamic_update_slice(
+            parts, values[None, None, None], (self.z, self.x, self.c, 0, 0)
+        )
+        parts = parts + self.over_core(parts)
+        parts = parts + self.over_x(parts)
+        bit = 1
+        while bit < self.depth:
+            parts = parts + self.across_z(parts, bit)
+            bit *= 2
+        return parts.transpose(3, 0, 1, 2, 4).reshape(count, -1)
+
+
+def image_shards(
+    depth,
+    layer_input,
+    token_image,
+    cotangent,
+    ln1_gain,
+    ln1_bias,
+    w_qkv,
+    qv_bias,
+    w_out,
+    out_bias,
+    ln2_gain,
+    ln2_bias,
+    w_fc1,
+    fc1_bias,
+    w_fc2,
+    fc2_bias,
+):
+    low = jnp.bfloat16
+    wide = jnp.float32
+    grid = Grid(depth)
+    rows, full_width = layer_input.shape
+    shard = ln1_gain.shape[0]
+    head_width = qv_bias.shape[1]
+    ff_width = fc1_bias.shape[0]
+    padded = -(-(rows + 1) // 256) * 256
+
+    quarter = head_width // 2
+    group_width = 4 * quarter
+    ff_padding = 2 * group_width - ff_width
+    sources = [w_qkv[0], w_qkv[1], w_qkv[2], w_out.T]
+    first_block = jnp.concatenate(
+        [values[:, i * quarter : (i + 1) * quarter] for i in range(2) for values in sources],
+        axis=1,
+    )
+    second_block = jnp.pad(w_fc1, ((0, 0), (0, ff_padding)))
+    third_block = jnp.pad(w_fc2.T, ((0, 0), (0, ff_padding)))
+    half = depth // 2
+    blocks = [grid.spread(first_block), grid.spread(second_block), grid.spread(third_block)]
+    vectors = jnp.stack([ln1_gain, ln1_bias, out_bias, ln2_gain, ln2_bias, fc2_bias])
+    (vectors,) = fence([vectors], [blocks[0]])
+    vectors = grid.gather_small(vectors).astype(wide)
+    own_one = grid.gather_depth(blocks[0])
+
+    here = grid.y
+    mine = lax.dynamic_slice_in_dim(token_image, here * rows, rows)
+    theirs = lax.dynamic_slice_in_dim(token_image, (1 - here) * rows, rows)
+    mine, theirs = fence([mine, theirs], [blocks[0]])
+    places = lax.iota(jnp.int32, rows)
+    stray = mine == 1 - here
+    stray_here = jnp.any(stray)
+    stray_there = jnp.any(theirs == here)
+    blank = mine == IMAGES
+    first_blank = jnp.min(jnp.where(blank, places, rows - 1))
+    last_blank = jnp.max(jnp.where(blank, places, 0))
+    swap_at = jnp.where(stray_here, jnp.max(jnp.where(stray, places, 0)), first_blank)
+    swapped = stray_here | stray_there
+    blank_at = jnp.where(stray_here, swap_at, last_blank)
+
+    def one_row(values, at):
+        return lax.dynamic_slice_in_dim(values, at, 1)
+
+    sent = jnp.concatenate(
+        [one_row(layer_input, swap_at), one_row(cotangent, swap_at), one_row(layer_input, last_blank)]
+    )
+    came = grid.over_y(sent)
+    other_blank = jnp.where(stray_there, sent[0:1], came[2:3])
+    spread_rows = lax.broadcasted_iota(jnp.int32, (padded, 1), 0)
+    at_swap = (spread_rows == swap_at) & swapped
+
+    def stretch(values):
+        return jnp.pad(values, ((0, padded - rows), (0, 0)))
+
+    input_rows = jnp.where(at_swap, came[0:1], stretch(layer_input))
+    input_rows = jnp.where(spread_rows == rows, other_blank, input_rows)
+    grad_low = jnp.where(at_swap, came[1:2], stretch(cotangent))
+    grad_low = jnp.where(spread_rows == blank_at, 0, grad_low).astype(low)
+    kind = jnp.where(spread_rows > rows, 3, jnp.where(spread_rows == rows, 2, 0))
+    kind = jnp.where(spread_rows == blank_at, 1, kind)
+    input_rows, grad_low = lax.optimization_barrier((input_rows, grad_low))
+
+    biases = jnp.concatenate([qv_bias.reshape(-1), fc1_bias])
+    biases = jnp.pad(biases, (0, -biases.shape[0] % 128)).reshape(-1, 128)
+    (biases,) = fence([biases], [blocks[0]])
+    other_biases = grid.over_y(biases).reshape(-1)
+
+    def ordered(first, second):
+        return jnp.where(grid.c == 0, first, second), jnp.where(grid.c == 0, second, first)
+
+    spot = grid.x.reshape(1)
+    inner = -(-3 * quarter // 128) * 128
+    qv_groups, fc1_groups = [], []
+    for flat in (biases.reshape(-1), other_biases):
+        flat = flat.astype(wide)
+        pair = flat[: 2 * head_width].reshape(2, 2, quarter)
+        none = jnp.zeros((quarter,), wide)
+        rest = jnp.zeros((inner - 3 * quarter,), wide)
+        qv_groups += ordered(
+            *[jnp.concatenate([pair[0, i], none, pair[1, i], rest]) for i in range(2)]
+        )
+        hidden_bias = flat[2 * head_width : 2 * head_width + ff_width]
+        hidden_bias = jnp.pad(hidden_bias, (0, ff_padding))
+        fc1_groups += ordered(hidden_bias[:group_width], hidden_bias[group_width:])
+
+    def stacked(rows_of, picked):
+        return jnp.stack([rows_of[i] for i in picked])[:, None]
+
+    qv_stacks = [stacked(qv_groups, picked) for picked in ((0, 1), (2, 3))]
+    fc1_stacks = [stacked(fc1_groups, picked) for picked in ((1, 3), (0, 2))]
+
+    def sides_of(own):
+        return [grid.over_x(own), grid.over_y(own)]
+
+    def corners_of(beside, across):
+        first, second = take_halves(beside, across)
+        return [grid.over_y(first), grid.over_x(second)]
+
+    def cores_of(*values):
+        return [grid.over_core(value) for value in values]
+
+    def near_groups(own, beside, there):
+        return [
+            [(own, 0, 0), (beside, 0, 1)],
+            [(there[0], 0, 0), (there[1], 0, 1)],
+        ]
+
+    def far_groups(across, corner, there):
+        return [
+            [(across, 0, 0), (corner[0], 0, 1), (corner[1], half, 1)],
+            [(there[0], 0, 0), (there[1], 0, 1), (there[2], half, 1)],
+        ]
+
+    own_one, vectors, input_rows, grad_low, kind, block_two, block_three, *stacks = fence(
+        [own_one, vectors, input_rows, grad_low, kind, blocks[1], blocks[2]]
+        + qv_stacks
+        + fc1_stacks
+    )
+    qv_stacks, fc1_stacks = stacks[:2], stacks[2:]
+    gain_one, shift_one, out_shift, gain_two, shift_two, fc2_shift = [
+        vectors[i : i + 1] for i in range(6)
+    ]
+    own_two = grid.gather_depth(block_two)
+    beside_one, across_one = sides_of(own_one)
+    unit_one, _ = unit_rows(input_rows.astype(wide))
+    normed = (unit_one * gain_one + shift_one).astype(low)
+    own_two, beside_one, across_one, normed, block_three, grad_there = fence(
+        [own_two, beside_one, across_one, normed, block_three, grid.over_core(grad_low)]
+    )
+    corner_one = corners_of(beside_one, across_one)
+    there = cores_of(own_one, beside_one)
+    own_two_there = grid.over_core(own_two)
+    across_there = grid.over_core(across_one)
+    sides_two = sides_of(own_two)
+    own_three = grid.gather_depth(block_three)
+
+    def heads(stack, groups, waits=()):
+        return heads_forward_call(spot, kind, normed, stack, groups, waits)
+
+    attn_weights = near_groups(own_one, beside_one, there)
+    first_qkv, first_probs, *mixed = heads(qv_stacks[0], attn_weights, [own_two_there])
+    *corner_one, across_there, first_qkv = fence(corner_one + [across_there, first_qkv])
+    there = [across_there] + cores_of(*corner_one)
+    attn_weights = attn_weights + far_groups(across_one, corner_one, there)
+    second_qkv, second_probs, *more = heads(qv_stacks[1], attn_weights[2:])
+    mixed = mixed + more
+    own_three, beside_two, across_two, second_qkv = fence(
+        [own_three] + sides_two + [second_qkv]
+    )
+    corner_two = corners_of(beside_two, across_two)
+    sides_three = sides_of(own_three)
+    beside_there, across_there = cores_of(beside_two, across_two)
+    own_three_there = grid.over_core(own_three)
+    resid, normed_two = out_project(
+        spot,
+        mixed,
+        input_rows,
+        out_shift,
+        gain_two,
+        shift_two,
+        attn_weights,
+        [beside_there, across_there, own_three_there],
+    )
+    *corner_two, normed_two = fence(corner_two + [normed_two])
+    up_weights = near_groups(own_two, beside_two, [own_two_there, beside_there])
+    there = [across_there] + cores_of(*corner_two)
+    up_weights = up_weights + far_groups(across_two, corner_two, there)
+    classes = ((1, 3), (0, 2))
+
+    def up(at, waits):
+        picked = [up_weights[i] for i in classes[at]]
+        return up_project(spot, normed_two, fc1_stacks[at], picked, waits)
+
+    other_active, other_slope = up(0, [])
+    beside_three, across_three, other_active = fence(sides_three + [other_active])
+    corner_three = corners_of(beside_three, across_three)
+    beside_there = grid.over_core(beside_three)
+    across_there = grid.over_core(across_three)
+    active_there = grid.over_core(other_active)
+    own_active, own_slope = up(1, [other_active])
+    *corner_three, own_active, active_there = fence(corner_three + [own_active, active_there])
+    down_weights = near_groups(own_three, beside_three, [own_three_there, beside_there])
+    there = [across_there] + cores_of(*corner_three)
+    down_weights = down_weights + far_groups(across_three, corner_three, there)
+    fc2_sums = weight_grad(spot, (grad_low, grad_there), (own_active, active_there), depth)
+
+    def move_corners(sums):
+        return [grid.over_x(sums[3]), grid.over_y(sums[4])]
+
+    def back(at, slope, waits):
+        picked = [down_weights[i] for i in classes[at]]
+        return hidden_grad(spot, grad_low, slope, picked, waits)
+
+    moved = move_corners(fc2_sums)
+    other_hidden, other_fc1_sums = back(0, other_slope, [fc2_sums[0]])
+    hidden_there = grid.over_core(other_hidden)
+    normed_two_there = grid.over_core(normed_two)
+    own_hidden, own_fc1_sums = back(1, own_slope, [other_hidden])
+    *moved, own_hidden, hidden_there, normed_two_there = fence(
+        moved + [own_hidden, hidden_there, normed_two_there]
+    )
+    beside, across = add_corners(fc2_sums[1], fc2_sums[2], *moved)
+    moved = [grid.over_x(beside), grid.over_y(across)]
+    fc1_sums = weight_grad(
+        spot, (normed_two, normed_two_there), (own_hidden, hidden_there), depth, waits=[beside]
+    )
+    normed_there = grid.over_core(normed)
+    by_class = [up_weights[i] for i in classes[0] + classes[1]]
+    grad_resid, resid_low, sums_two = norm_back(
+        "norm_two_back",
+        spot,
+        [other_hidden, own_hidden],
+        resid,
+        grad_low,
+        gain_two,
+        by_class,
+        True,
+        [fc1_sums[0], normed_there],
+    )
+    *moved, resid_low, corner_a, corner_b = fence(moved + [resid_low, *fc1_sums[3:]])
+    fc2_piece = grid.scatter_depth(add_square(fc2_sums[0], *moved))
+    moved = [grid.over_x(corner_a), grid.over_y(corner_b)]
+    resid_there = grid.over_core(resid_low)
+
+    def heads_back(qkv, probs, side, waits):
+        order = [1 + 2 * side, 2 * side]
+        return heads_backward_call(
+            spot,
+            resid_low,
+            qkv,
+            probs,
+            [mixed[i] for i in order],
+            [attn_weights[i] for i in order],
+            (1, 0),
+            waits,
+        )
+
+    far_other, far_own, far_sums = heads_back(second_qkv, second_probs, 1, [])
+    *moved, far_other = fence(moved + [far_other])
+    far_there = grid.over_core(far_other)
+    beside, across = add_corners(fc1_sums[1], fc1_sums[2], *moved)
+    moved = [grid.over_x(beside), grid.over_y(across)]
+    far_mixed = grid.over_core(mixed[3])
+    near_other, near_own, near_sums_qkv = heads_back(first_qkv, first_probs, 0, [beside])
+    near_other, far_there, far_mixed, resid_there, fc2_piece = fence(
+        [near_other, far_there, far_mixed, resid_there, fc2_piece]
+    )
+    near_there = grid.over_core(near_other)
+    near_mixed = grid.over_core(mixed[1])
+
+    def attn_grad(side, own_part, there_part, own_mixed, there_mixed, waits):
+        return weight_grad(
+            spot,
+            (normed, normed_there),
+            (own_part, there_part),
+            depth,
+            (side,),
+            (resid_low, own_mixed, resid_there, there_mixed),
+            waits,
+        )
+
+    far_across, corner_a, corner_b = attn_grad(1, far_own, far_there, mixed[2], far_mixed, [])
+    *moved, corner_a, corner_b = fence(moved + [corner_a, corner_b])
+    fc1_piece = grid.scatter_depth(add_square(fc1_sums[0], *moved))
+    moved = [grid.over_x(corner_a), grid.over_y(corner_b)]
+    near_sums, beside = attn_grad(0, near_own, near_there, mixed[0], near_mixed, [far_across])
+    *moved, beside = fence(moved + [beside])
+    beside, across = add_corners(beside, far_across, *moved)
+    moved = [grid.over_x(beside), grid.over_y(across)]
+    by_class = [down_weights[i] for i in classes[0] + classes[1]]
+    layer_rows = down_project(
+        spot, other_active, own_active, resid, fc2_shift, by_class, [beside]
+    )
+    by_class = [attn_weights[i] for i in (1, 3, 0, 2)]
+    input_grad, sums_one = norm_back(
+        "norm_one_back",
+        spot,
+        [near_other, far_other, near_own, far_own],
+        input_rows,
+        grad_resid,
+        gain_one,
+        by_class,
+        False,
+        [layer_rows],
+    )
+
+    def column_sum(values):
+        return jnp.sum(values.astype(wide), axis=0)
+
+    def absolute(near_other, near_own, far_other, far_own):
+        near = ordered(near_own, near_other)
+        far = ordered(far_own, far_other)
+        return [
+            (jnp.where(here == 0, one, two), jnp.where(here == 0, two, one))
+            for one, two in zip(near, far)
+        ]
+
+    qkv_totals = absolute(near_sums_qkv[0], near_sums_qkv[1], far_sums[0], far_sums[1])
+    query_and_value = [
+        qkv_totals[half_at][side][0, at : at + quarter]
+        for side in range(2)
+        for at in (0, 2 * quarter)
+        for half_at in range(2)
+    ]
+    fc1_totals = absolute(
+        other_fc1_sums[0], own_fc1_sums[0], other_fc1_sums[1], own_fc1_sums[1]
+    )
+    fc1_rows = []
+    for side in range(2):
+        fc1_rows += [fc1_totals[0][side][0], fc1_totals[1][side][0, : ff_width - group_width]]
+    flat = jnp.concatenate(
+        [
+            sums_one[0],
+            sums_one[1],
+            sums_two[2],
+            sums_two[0],
+            sums_two[1],
+            column_sum(grad_low),
+            *query_and_value,
+            *fc1_rows,
+        ]
+    )
+    length = flat.shape[0]
+    lines = -(-length // 1024) * 8
+    flat = jnp.pad(flat, (0, lines * 128 - length)).reshape(lines, 128)
+    *moved, flat, fc1_piece = fence(moved + [flat, fc1_piece])
+    total = add_square(near_sums, *moved)
+    attn_piece = grid.scatter_depth(total)
+    (flat, fc1_piece, fc2_piece) = fence([flat, fc1_piece, fc2_piece], [total])
+    flat = flat + grid.over_core(flat)
+    flat = flat + grid.over_x(flat)
+    flat = flat + grid.over_y(flat)
+    bit = 1
+    while bit < depth:
+        flat = flat + grid.across_z(flat, bit)
+        bit *= 2
+    flat = flat.reshape(-1)
+    fc1_piece = grid.scatter_core(fc1_piece)
+    fc2_piece = grid.scatter_core(fc2_piece)
+    swap_from = fence([one_row(layer_rows, swap_at), one_row(input_grad, swap_at)], [total])
+    returned = [grid.over_y(values) for values in swap_from]
+    layer_output = jnp.where(at_swap, returned[0], layer_rows)[:rows]
+    input_grad = jnp.where(at_swap, returned[1], input_grad)[:rows]
+    attn_piece = grid.scatter_core(attn_piece)
+    row_total = flat[: 6 * full_width].reshape(6, full_width)
+    row_piece = lax.dynamic_slice_in_dim(row_total, lax.axis_index("dp") * shard, shard, 1)
+    start = 6 * full_width
+    qv_piece = lax.dynamic_slice_in_dim(flat, start + here * 2 * head_width, 2 * head_width)
+    start = start + 4 * head_width
+    fc1_bias_piece = lax.dynamic_slice_in_dim(flat, start + here * ff_width, ff_width)
+    heads_piece = attn_piece.reshape(2, shard, 4, quarter).transpose(2, 1, 0, 3)
+    heads_piece = heads_piece.reshape(4, shard, head_width)
+
+    def whole_columns(pair):
+        return jnp.concatenate([pair[0], pair[1][:, : group_width - ff_padding]], axis=1)
+
+    return (
+        layer_output,
+        input_grad,
+        row_piece[0],
+        row_piece[1],
+        heads_piece[:3],
+        qv_piece.reshape(2, head_width),
+        heads_piece[3].T,
+        row_piece[2],
+        row_piece[3],
+        row_piece[4],
+        whole_columns(fc1_piece),
+        fc1_bias_piece,
+        whole_columns(fc2_piece).T,
+        row_piece[5],
+    )
+
+
+def fits_images(mesh):
+    groups = mesh.shape["dp"] // 4
+    return (
+        mesh.shape["tensor"] == IMAGES
+        and mesh.shape["dp"] % 4 == 0
+        and groups >= 2
+        and groups & (groups - 1) == 0
+    )
+
+
 def solution(mesh):
     in_specs = (
         P(("dp", "tensor"), None),
@@ -412,4 +1899,11 @@
         P("tensor", "dp"),
         P("dp"),
     )
-    return jax.shard_map(shards, mesh=mesh, in_specs=in_specs, out_specs=out_specs, check_vma=False)
+
+    def body(*arrays):
+        slots = arrays[1].shape[0]
+        if fits_images(mesh) and slots == IMAGES * (PATCHES + 1):
+            return image_shards(mesh.shape["dp"] // 4, *arrays)
+        return shards(*arrays)
+
+    return jax.shard_map(body, mesh=mesh, in_specs=in_specs, out_specs=out_specs, check_vma=False)

time: 2300 us -> 494 us (0.21)
  waiting for transfers between devices: 855 us -> 84.8 us
  blocking collectives: 536 us -> 0 us
  matrix products: 418 us -> 0 us
  local copies, waits for them, and re-layouts: 335 us -> 35.9 us
  Pallas kernels: 0 us -> 264 us
  other arithmetic: 105 us -> 33.7 us
  starting transfers between devices: 14.8 us -> 47.6 us
    all_gather x14 -> x3, waiting for transfers between devices: 523 us -> 0.14 us  [gather_depth(): return lax.all_gather(block, 'dp', axis_index_groups=self.depth_groups())]
    unnamed x7 -> x0, blocking collectives: 493 us -> none
    dot_general x158 -> x0, matrix products: 418 us -> none  [the longest x67 125 us: contract_cols(): lax.dot_general(left, right, (((1,), (1,)), ((), ())), preferred_element_...]
    unnamed x27 -> x6, waiting for transfers between devices: 332 us -> 0.1 us
    pallas_call x0 -> x44, Pallas kernels: none -> 264 us  [the longest x16 238 us: call(): pl.pallas_call(kernel, in_specs=list(specs) + [any_spec()] * len(waits),...]
    while x376 -> x0, local copies, waits for them, and re-layouts: 90 us -> none
    ppermute x0 -> x68, waiting for transfers between devices: none -> 84.1 us  [move(): return lax.ppermute(values, AXES, pairs)]
    unnamed x186 -> x92, local copies, waits for them, and re-layouts: 90.4 us -> 10.5 us
  transfers between devices with their start and end apart: 23 -> 74, of which waited for: 20 -> 28; matrix products, arithmetic and copies ran while one was open for 26% -> 10% of each run, Pallas kernels for 0% -> 51%
where the time goes in v3:
time: 494 us; the launch traced here: 488 us
  Pallas kernels  264 us (53%)
  waiting for transfers between devices  84.8 us (17%)
  starting transfers between devices  47.6 us (10%)
  local copies, waits for them, and re-layouts  35.9 us (7%)
  other arithmetic  33.7 us (7%)
  between operations  22 us (4%)
    pallas_call x16, Pallas kernels, call(): pl.pallas_call(kernel, in_specs=list(specs) + [any_spec()] * len(waits),...  238 us
    ppermute x68, waiting for transfers between devices, move(): return lax.ppermute(values, AXES, pairs)  84.1 us
    ppermute x68, starting transfers between devices, move(): return lax.ppermute(values, AXES, pairs)  47 us
    unnamed x92, local copies, waits for them, and re-layouts  10.5 us
    pallas_call x3, Pallas kernels, add_square(): pl.pallas_call(square_kernel, grid=(2,), in_specs=[block, block, block],...  10 us
  transfers between devices with their start and end apart: 74, of which 28 were waited for; matrix products, arithmetic and copies ran while one was open for 10% of the time, Pallas kernels for 51%

profile of v3, /device:TPU:0, one launch (start us, length us, event | category | flops | bytes accessed | tf_op | source)
XLA Modules:
  0.0 487.9 jit_solution(4162578507372888725)
XLA Ops:
  47.3 4.7 collective-permute-done.3
  52.9 3.4 select_select_fusion
  66.0 23.7 %collective-permute-done.9.refs_1_ = bf16[4,144,1152]{2,1,0:T(8,128)(2,1)S(1)} collective-permute-done((bf16[4,144,1152]{2,1,0:T(8,128)(2,1)}, bf16[4,144,1152]{2,1,0:T(8,128)(2,1)S(1)}, u32[]{:S(2)}, u32[]{:S(2)}) %collective-permute-start.9) | collective-permute-done | bytes 1327136 | tf_op jit(solution)/shard_map/ppermute | solution.py:1401
  99.8 16.8 %heads_forward.2 = (bf16[2,768,896]{2,1,0:T(8,128)(2,1)}, bf16[2,4,768,768]{3,2,1,0:T(8,128)(2,1)}, bf16[768,384]{1,0:T(8,128)(2,1)}, bf16[768,384]{1,0:T(8,128)(2,1)}) custom-call(s32[1]{0:T(128)} %bitcast.4.spot, s32[768,1]{1,0:T(8,128)} %get-tuple-element.155.kind_ref, bf16[768,1152]{1,0:T(8,128)(2,1)} %get-tuple-element.156.x_any.refs_0_, ...), custom_call_target="tpu_custom_call" | custom-call | tf_op jit(solution)/shard_map/heads_forward/pallas_call | solution.py:739
  121.9 17.3 %heads_forward.3 = (bf16[2,768,896]{2,1,0:T(8,128)(2,1)}, bf16[2,4,768,768]{3,2,1,0:T(8,128)(2,1)}, bf16[768,384]{1,0:T(8,128)(2,1)}, bf16[768,384]{1,0:T(8,128)(2,1)}) custom-call(s32[1]{0:T(128)} %bitcast.4.spot, s32[768,1]{1,0:T(8,128)} %get-tuple-element.155.kind_ref, bf16[768,1152]{1,0:T(8,128)(2,1)} %get-tuple-element.156.x_any.refs_0_, ...), custom_call_target="tpu_custom_call" | custom-call | tf_op jit(solution)/shard_map/heads_forward/pallas_call | solution.py:739
  149.9 9.4 %attn_out.1 = (f32[768,1152]{1,0:T(8,128)}, bf16[768,1152]{1,0:T(8,128)(2,1)}) custom-call(s32[1]{0:T(128)} %bitcast.4.spot, bf16[768,384]{1,0:T(8,128)(2,1)} %get-tuple-element.173.one.refs_1_.refs_5_, bf16[768,384]{1,0:T(8,128)(2,1)} %get-tuple-element.174.two.refs_0_, bf16[768,384]{1,0:T(8,128)(2,1)} %get-tuple-element.175.three.refs_1_.refs_5_, ...), custom_call_target="tpu_custom_call" | custom-call | tf_op jit(solution)/shard_map/attn_out/pallas_call | solution.py:739
  159.3 4.2 collective-permute-done.24.refs_0_
  164.9 2.7 collective-permute-done.29.refs_3_.refs_8_
  168.5 11.2 %mlp_up.2 = (bf16[2,768,1152]{2,1,0:T(8,128)(2,1)}, bf16[2,768,1152]{2,1,0:T(8,128)(2,1)}) custom-call(s32[1]{0:T(128)} %bitcast.4.spot, bf16[768,1152]{1,0:T(8,128)(2,1)} %get-tuple-element.178.x_any.refs_0_, f32[2,1,1152]{2,1,0:T(1,128)} %get-tuple-element.179.bias_ref, bf16[4,144,1152]{2,1,0:T(8,128)(2,1)} %collective-permute-done.19.refs_4_.refs_0_.refs_5_, ...), custom_call_target="tpu_custom_call" | custom-call | tf_op jit(solution)/shard_map/mlp_up/pallas_call | solution.py:739
  179.7 12.1 %collective-permute-done.22.refs_0_ = bf16[4,144,1152]{2,1,0:T(8,128)(2,1)S(1)} collective-permute-done((bf16[4,144,1152]{2,1,0:T(8,128)(2,1)}, bf16[4,144,1152]{2,1,0:T(8,128)(2,1)S(1)}, u32[]{:S(2)}, u32[]{:S(2)}) %collective-permute-start.22) | collective-permute-done | bytes 1327136 | tf_op jit(solution)/shard_map/ppermute | solution.py:1401
  199.4 11.4 %mlp_up.3 = (bf16[2,768,1152]{2,1,0:T(8,128)(2,1)}, bf16[2,768,1152]{2,1,0:T(8,128)(2,1)}) custom-call(s32[1]{0:T(128)} %bitcast.4.spot, bf16[768,1152]{1,0:T(8,128)(2,1)} %get-tuple-element.178.x_any.refs_0_, f32[2,1,1152]{2,1,0:T(1,128)} %get-tuple-element.188.bias_ref, bf16[4,144,1152]{2,1,0:T(8,128)(2,1)} %get-tuple-element.154.refs_0_.refs_10_, ...), custom_call_target="tpu_custom_call" | custom-call | tf_op jit(solution)/shard_map/mlp_up/pallas_call | solution.py:739
  215.2 15.2 %weight_grad.4 = (bf16[4,144,1152]{2,1,0:T(8,128)(2,1)}, bf16[4,144,1152]{2,1,0:T(8,128)(2,1)}, bf16[4,144,1152]{2,1,0:T(8,128)(2,1)}, bf16[2,144,1152]{2,1,0:T(8,128)(2,1)}, bf16[2,144,1152]{2,1,0:T(8,128)(2,1)}) custom-call(s32[1]{0:T(128)} %bitcast.4.spot, bf16[768,1152]{1,0:T(8,128)(2,1)} %get-tuple-element.152.refs_0_.x_any.refs_3_, ...), custom_call_target="tpu_custom_call" | custom-call | tf_op jit(solution)/shard_map/weight_grad/pallas_call | solution.py:739
  231.3 10.3 %mlp_grad.2 = (bf16[2,768,1152]{2,1,0:T(8,128)(2,1)}, f32[2,1,1152]{2,1,0:T(1,128)}) custom-call(s32[1]{0:T(128)} %bitcast.4.spot, bf16[768,1152]{1,0:T(8,128)(2,1)} %get-tuple-element.152.refs_0_.x_any.refs_3_, bf16[2,768,1152]{2,1,0:T(8,128)(2,1)} %get-tuple-element.199.slope_any, bf16[4,144,1152]{2,1,0:T(8,128)(2,1)} %collective-permute-done.28.refs_12_.refs_0_, ...), custom_call_target="tpu_custom_call" | custom-call | tf_op jit(solution)/shard_map/mlp_grad/pallas_call | solution.py:739
  244.7 10.1 %mlp_grad.3 = (bf16[2,768,1152]{2,1,0:T(8,128)(2,1)}, f32[2,1,1152]{2,1,0:T(1,128)}) custom-call(s32[1]{0:T(128)} %bitcast.4.spot, bf16[768,1152]{1,0:T(8,128)(2,1)} %get-tuple-element.152.refs_0_.x_any.refs_3_, bf16[2,768,1152]{2,1,0:T(8,128)(2,1)} %get-tuple-element.198.slope_any, bf16[4,144,1152]{2,1,0:T(8,128)(2,1)} %get-tuple-element.168.refs_0_.refs_5_, ...), custom_call_target="tpu_custom_call" | custom-call | tf_op jit(solution)/shard_map/mlp_grad/pallas_call | solution.py:739
  254.8 4.5 collective-permute-done.38.refs_0_
  260.6 2.9 add_corners.3
  265.1 15.0 %weight_grad.5 = (bf16[4,144,1152]{2,1,0:T(8,128)(2,1)}, bf16[4,144,1152]{2,1,0:T(8,128)(2,1)}, bf16[4,144,1152]{2,1,0:T(8,128)(2,1)}, bf16[2,144,1152]{2,1,0:T(8,128)(2,1)}, bf16[2,144,1152]{2,1,0:T(8,128)(2,1)}) custom-call(s32[1]{0:T(128)} %bitcast.4.spot, bf16[768,1152]{1,0:T(8,128)(2,1)} %get-tuple-element.178.x_any.refs_0_, ...), custom_call_target="tpu_custom_call" | custom-call | tf_op jit(solution)/shard_map/weight_grad/pallas_call | solution.py:739
  280.1 21.8 %norm_two_back.1 = (f32[768,1152]{1,0:T(8,128)}, bf16[768,1152]{1,0:T(8,128)(2,1)}, f32[8,1152]{1,0:T(8,128)}) custom-call(s32[1]{0:T(128)} %bitcast.4.spot, bf16[2,768,1152]{2,1,0:T(8,128)(2,1)} %get-tuple-element.201.refs_5_.refs_0_, bf16[2,768,1152]{2,1,0:T(8,128)(2,1)} %get-tuple-element.203.refs_1_, f32[768,1152]{1,0:T(8,128)} %get-tuple-element.191.refs_2_.resid_any, ...), custom_call_target="tpu_custom_call" | custom-call | tf_op jit(solution)/shard_map/norm_two_back/pallas_call | solution.py:739
  302.9 3.3 add_square.3
  308.8 21.0 %heads_backward.2 = (bf16[768,896]{1,0:T(8,128)(2,1)}, bf16[768,896]{1,0:T(8,128)(2,1)}, f32[2,1,896]{2,1,0:T(1,128)}) custom-call(s32[1]{0:T(128)} %bitcast.4.spot, bf16[768,1152]{1,0:T(8,128)(2,1)} %get-tuple-element.220.grad_any.refs_4_, bf16[2,768,896]{2,1,0:T(8,128)(2,1)} %get-tuple-element.221.qkv_any, ...), custom_call_target="tpu_custom_call" | custom-call | tf_op jit(solution)/shard_map/heads_backward/pallas_call | solution.py:739
  330.4 2.9 add_corners.4
  335.0 21.2 %heads_backward.3 = (bf16[768,896]{1,0:T(8,128)(2,1)}, bf16[768,896]{1,0:T(8,128)(2,1)}, f32[2,1,896]{2,1,0:T(1,128)}) custom-call(s32[1]{0:T(128)} %bitcast.4.spot, bf16[768,1152]{1,0:T(8,128)(2,1)} %get-tuple-element.220.grad_any.refs_4_, bf16[2,768,896]{2,1,0:T(8,128)(2,1)} %get-tuple-element.229.qkv_any, ...), custom_call_target="tpu_custom_call" | custom-call | tf_op jit(solution)/shard_map/heads_backward/pallas_call | solution.py:739
  357.9 11.2 %weight_grad.6 = (bf16[4,144,1152]{2,1,0:T(8,128)(2,1)}, bf16[2,144,1152]{2,1,0:T(8,128)(2,1)}, bf16[2,144,1152]{2,1,0:T(8,128)(2,1)}) custom-call(s32[1]{0:T(128)} %bitcast.4.spot, bf16[768,1152]{1,0:T(8,128)(2,1)} %get-tuple-element.156.x_any.refs_0_, bf16[1,768,896]{2,1,0:T(8,128)(2,1)} %bitcast.109, ...), custom_call_target="tpu_custom_call" | custom-call | tf_op jit(solution)/shard_map/weight_grad/pallas_call | solution.py:739
  369.1 3.3 add_square.4
  377.4 11.1 %weight_grad.7 = (bf16[4,144,1152]{2,1,0:T(8,128)(2,1)}, bf16[4,144,1152]{2,1,0:T(8,128)(2,1)}) custom-call(s32[1]{0:T(128)} %bitcast.4.spot, bf16[768,1152]{1,0:T(8,128)(2,1)} %get-tuple-element.156.x_any.refs_0_, bf16[1,768,896]{2,1,0:T(8,128)(2,1)} %bitcast.108, bf16[768,1152]{1,0:T(8,128)(2,1)} %collective-permute-done.44.refs_16_.refs_2_, ...), custom_call_target="tpu_custom_call" | custom-call | tf_op jit(solution)/shard_map/weight_grad/pallas_call | solution.py:739
  391.7 3.0 add_corners.5
  397.7 17.6 %mlp_down.1.refs_17_ = bf16[768,1152]{1,0:T(8,128)(2,1)} custom-call(s32[1]{0:T(128)} %bitcast.4.spot, bf16[2,768,1152]{2,1,0:T(8,128)(2,1)} %get-tuple-element.183.refs_5_.later_any, bf16[2,768,1152]{2,1,0:T(8,128)(2,1)} %get-tuple-element.190.refs_1_.early_any, f32[768,1152]{1,0:T(8,128)} %get-tuple-element.191.refs_2_.resid_any, ...), custom_call_target="tpu_custom_call" | custom-call | tf_op jit(solution)/shard_map/mlp_down/pallas_call | solution.py:739
  415.2 17.0 %norm_one_back.1 = (f32[768,1152]{1,0:T(8,128)}, f32[8,1152]{1,0:T(8,128)}) custom-call(s32[1]{0:T(128)} %bitcast.4.spot, bf16[768,896]{1,0:T(8,128)(2,1)} %get-tuple-element.243.refs_0_, bf16[768,896]{1,0:T(8,128)(2,1)} %get-tuple-element.232.refs_1_, bf16[768,896]{1,0:T(8,128)(2,1)} %get-tuple-element.242.refs_2_, ...), custom_call_target="tpu_custom_call" | custom-call | tf_op jit(solution)/shard_map/norm_one_back/pallas_call | solution.py:739
  435.5 3.4 add_square.5.refs_2_.refs_3_
  455.9 3.6 collective-permute-done.63
  460.3 4.0 slice_select_fusion
  464.3 5.3 %collective-permute-done.64 = f32[112,128]{1,0:T(8,128)S(1)} collective-permute-done((f32[112,128]{1,0:T(8,128)S(1)}, f32[112,128]{1,0:T(8,128)S(1)}, u32[]{:S(2)}, u32[]{:S(2)}) %collective-permute-start.64) | collective-permute-done | bytes 57376 | tf_op jit(solution)/shard_map/ppermute | solution.py:1401
  (383 shorter events, 141.2 us)
Async XLA Ops:
  7.2 50.6 %all-gather.7.cloned.1.call-start = ((), (), s32[]{:S(2)}) async-start(), calls=%async_computation.6 | async-start | bytes 1658880 | tf_op jit(solution)/shard_map/all_gather | solution.py:1434
  11.8 24.1 %collective-permute-start.7 = (bf16[72,1152]{1,0:T(8,128)(2,1)}, bf16[72,1152]{1,0:T(8,128)(2,1)}, u32[]{:S(2)}, u32[]{:S(2)}) collective-permute-start(bf16[72,1152]{1,0:T(8,128)(2,1)} %pad_dynamic-slice_fusion), channel_id=1, source_target_pairs={{0,2},{1,3},{2,0},{3,1},{4,6},{5,7},{6,4},{7,5},{8,10},{9,11},{10,... | collective-permute-start | bytes 497672 | tf_op jit(solution)/shard_map/ppermute | solution.py:1401
  13.7 22.3 %collective-permute-start.6 = (bf16[72,1152]{1,0:T(8,128)(2,1)}, bf16[72,1152]{1,0:T(8,128)(2,1)}, u32[]{:S(2)}, u32[]{:S(2)}) collective-permute-start(bf16[72,1152]{1,0:T(8,128)(2,1)} %pad_dynamic-slice_fusion.2), channel_id=1, source_target_pairs={{0,2},{1,3},{2,0},{3,1},{4,6},{5,7},{6,4},{7,5},{8,10},{9,11},{10,... | collective-permute-start | bytes 497672 | tf_op jit(solution)/shard_map/ppermute | solution.py:1401
  18.7 72.4 %all-gather.9.cloned.1.call-start = ((), (), s32[]{:S(2)}) async-start(), calls=%async_computation.7 | async-start | bytes 1658880 | tf_op jit(solution)/shard_map/all_gather | solution.py:1434
  57.9 83.7 %all-gather.11.cloned.1.call-start = ((), (), s32[]{:S(2)}) async-start(), calls=%async_computation.8 | async-start | bytes 1658880 | tf_op jit(solution)/shard_map/all_gather | solution.py:1434
  57.9 33.1 %collective-permute-start.11 = (bf16[768,1152]{1,0:T(8,128)(2,1)}, bf16[768,1152]{1,0:T(8,128)(2,1)}, u32[]{:S(2)}, u32[]{:S(2)}) collective-permute-start(bf16[768,1152]{1,0:T(8,128)(2,1)} %get-tuple-element.152.refs_0_.x_any.refs_3_), channel_id=1, source_target_pairs={{0,2},{1,3},{2,0},{3,1},{4,6},{5,7},{6,4},{7,5},{8,10},{9,11},{10,... | collective-permute-start | bytes 5308424 | tf_op jit(solution)/shard_map/ppermute | solution.py:1401
  58.0 31.8 %collective-permute-start.9 = (bf16[4,144,1152]{2,1,0:T(8,128)(2,1)}, bf16[4,144,1152]{2,1,0:T(8,128)(2,1)S(1)}, u32[]{:S(2)}, u32[]{:S(2)}) collective-permute-start(bf16[4,144,1152]{2,1,0:T(8,128)(2,1)} %get-tuple-element.148.refs_0_.refs_4_.refs_12_), channel_id=1, source_target_pairs={{0,4},{1,5},{2,6},{3,7},{4,0},{5,1},{6,2},{7,3},{8,12},{9,13},{10,... | collective-permute-start | bytes 3981320 | tf_op jit(solution)/shard_map/ppermute | solution.py:1401
  59.5 31.5 %collective-permute-start.10 = (bf16[4,144,1152]{2,1,0:T(8,128)(2,1)}, bf16[4,144,1152]{2,1,0:T(8,128)(2,1)}, u32[]{:S(2)}, u32[]{:S(2)}) collective-permute-start(bf16[4,144,1152]{2,1,0:T(8,128)(2,1)} %get-tuple-element.148.refs_0_.refs_4_.refs_12_), channel_id=1, source_target_pairs={{0,1},{1,0},{2,3},{3,2},{4,5},{5,4},{6,7},{7,6},{8,9},{9,8},{10,11... | collective-permute-start | bytes 3981320 | tf_op jit(solution)/shard_map/ppermute | solution.py:1401
  61.0 34.9 %collective-permute-start.17 = (bf16[4,144,1152]{2,1,0:T(8,128)(2,1)}, bf16[4,144,1152]{2,1,0:T(8,128)(2,1)}, u32[]{:S(2)}, u32[]{:S(2)}) collective-permute-start(bf16[4,144,1152]{2,1,0:T(8,128)(2,1)} %get-tuple-element.148.refs_0_.refs_4_.refs_12_), channel_id=1, source_target_pairs={{0,2},{1,3},{2,0},{3,1},{4,6},{5,7},{6,4},{7,5},{8,10},{9,11},{10,... | collective-permute-start | bytes 3981320 | tf_op jit(solution)/shard_map/ppermute | solution.py:1401
  91.7 25.0 %collective-permute-start.16 = (bf16[4,144,1152]{2,1,0:T(8,128)(2,1)}, bf16[4,144,1152]{2,1,0:T(8,128)(2,1)S(1)}, u32[]{:S(2)}, u32[]{:S(2)}) collective-permute-start(bf16[4,144,1152]{2,1,0:T(8,128)(2,1)} %get-tuple-element.158.second_ref.refs_0_.refs_4_.refs_5_.refs_14_), channel_id=1, source_target_pairs={{0,2},{1,3},{2,0},{3,1},{4,6},{5,7},{6,4},{7,5},{8,10},{9,11},{10,... | collective-permute-start | bytes 3981320 | tf_op jit(solution)/shard_map/ppermute | solution.py:1401
  91.7 264.5 %reduce-scatter.4.cloned.1.call-start = ((), (), s32[]{:S(2)}) async-start(), calls=%async_computation.3 | async-start | bytes 1658880 | tf_op jit(solution)/shard_map/reduce_scatter | solution.py:1437
  94.5 22.2 %collective-permute-start.14 = (bf16[2,144,1152]{2,1,0:T(8,128)(2,1)}, bf16[2,144,1152]{2,1,0:T(8,128)(2,1)}, u32[]{:S(2)}, u32[]{:S(2)}) collective-permute-start(bf16[2,144,1152]{2,1,0:T(8,128)(2,1)} %get-tuple-element.160), channel_id=1, source_target_pairs={{0,1},{1,0},{2,3},{3,2},{4,5},{5,4},{6,7},{7,6},{8,9},{9,8},{10,11... | collective-permute-start | bytes 1990664 | tf_op jit(solution)/shard_map/ppermute | solution.py:1401
  97.4 44.2 %collective-permute-start.12 = (bf16[4,144,1152]{2,1,0:T(8,128)(2,1)}, bf16[4,144,1152]{2,1,0:T(8,128)(2,1)S(1)}, u32[]{:S(2)}, u32[]{:S(2)}) collective-permute-start(bf16[4,144,1152]{2,1,0:T(8,128)(2,1)} %get-tuple-element.154.refs_0_.refs_10_), channel_id=1, source_target_pairs={{0,4},{1,5},{2,6},{3,7},{4,0},{5,1},{6,2},{7,3},{8,12},{9,13},{10,... | collective-permute-start | bytes 3981320 | tf_op jit(solution)/shard_map/ppermute | solution.py:1401
  98.4 43.2 %collective-permute-start.13 = (bf16[4,144,1152]{2,1,0:T(8,128)(2,1)}, bf16[4,144,1152]{2,1,0:T(8,128)(2,1)}, u32[]{:S(2)}, u32[]{:S(2)}) collective-permute-start(bf16[4,144,1152]{2,1,0:T(8,128)(2,1)} %get-tuple-element.154.refs_0_.refs_10_), channel_id=1, source_target_pairs={{0,1},{1,0},{2,3},{3,2},{4,5},{5,4},{6,7},{7,6},{8,9},{9,8},{10,11... | collective-permute-start | bytes 3981320 | tf_op jit(solution)/shard_map/ppermute | solution.py:1401
  147.6 44.2 %collective-permute-start.22 = (bf16[4,144,1152]{2,1,0:T(8,128)(2,1)}, bf16[4,144,1152]{2,1,0:T(8,128)(2,1)S(1)}, u32[]{:S(2)}, u32[]{:S(2)}) collective-permute-start(bf16[4,144,1152]{2,1,0:T(8,128)(2,1)} %get-tuple-element.168.refs_0_.refs_5_), channel_id=1, source_target_pairs={{0,4},{1,5},{2,6},{3,7},{4,0},{5,1},{6,2},{7,3},{8,12},{9,13},{10,... | collective-permute-start | bytes 3981320 | tf_op jit(solution)/shard_map/ppermute | solution.py:1401
  148.2 43.7 %collective-permute-start.23 = (bf16[4,144,1152]{2,1,0:T(8,128)(2,1)}, bf16[4,144,1152]{2,1,0:T(8,128)(2,1)S(1)}, u32[]{:S(2)}, u32[]{:S(2)}) collective-permute-start(bf16[4,144,1152]{2,1,0:T(8,128)(2,1)} %get-tuple-element.168.refs_0_.refs_5_), channel_id=1, source_target_pairs={{0,1},{1,0},{2,3},{3,2},{4,5},{5,4},{6,7},{7,6},{8,9},{9,8},{10,11... | collective-permute-start | bytes 3981320 | tf_op jit(solution)/shard_map/ppermute | solution.py:1401
  198.9 31.5 %collective-permute-start.34 = (bf16[4,144,1152]{2,1,0:T(8,128)(2,1)S(1)}, bf16[4,144,1152]{2,1,0:T(8,128)(2,1)}, u32[]{:S(2)}, u32[]{:S(2)}) collective-permute-start(bf16[4,144,1152]{2,1,0:T(8,128)(2,1)S(1)} %copy-done.9), channel_id=1, source_target_pairs={{0,2},{1,3},{2,0},{3,1},{4,6},{5,7},{6,4},{7,5},{8,10},{9,11},{10,... | collective-permute-start | bytes 3981320 | tf_op jit(solution)/shard_map/ppermute | solution.py:1401
  198.9 31.5 %collective-permute-start.35 = (bf16[4,144,1152]{2,1,0:T(8,128)(2,1)S(1)}, bf16[4,144,1152]{2,1,0:T(8,128)(2,1)}, u32[]{:S(2)}, u32[]{:S(2)}) collective-permute-start(bf16[4,144,1152]{2,1,0:T(8,128)(2,1)S(1)} %copy-done.11), channel_id=1, source_target_pairs={{0,2},{1,3},{2,0},{3,1},{4,6},{5,7},{6,4},{7,5},{8,10},{9,11},{10,... | collective-permute-start | bytes 3981320 | tf_op jit(solution)/shard_map/ppermute | solution.py:1401
  244.6 35.4 %collective-permute-start.44 = (bf16[768,1152]{1,0:T(8,128)(2,1)S(1)}, bf16[768,1152]{1,0:T(8,128)(2,1)}, u32[]{:S(2)}, u32[]{:S(2)}) collective-permute-start(bf16[768,1152]{1,0:T(8,128)(2,1)S(1)} %copy-done.2), channel_id=1, source_target_pairs={{0,2},{1,3},{2,0},{3,1},{4,6},{5,7},{6,4},{7,5},{8,10},{9,11},{10,... | collective-permute-start | bytes 5308424 | tf_op jit(solution)/shard_map/ppermute | solution.py:1401
  263.5 38.4 %collective-permute-start.42 = (bf16[4,144,1152]{2,1,0:T(8,128)(2,1)}, bf16[4,144,1152]{2,1,0:T(8,128)(2,1)S(1)}, u32[]{:S(2)}, u32[]{:S(2)}) collective-permute-start(bf16[4,144,1152]{2,1,0:T(8,128)(2,1)} %get-tuple-element.210.refs_4_), channel_id=1, source_target_pairs={{0,4},{1,5},{2,6},{3,7},{4,0},{5,1},{6,2},{7,3},{8,12},{9,13},{10,... | collective-permute-start | bytes 3981320 | tf_op jit(solution)/shard_map/ppermute | solution.py:1401
  264.0 37.8 %collective-permute-start.43 = (bf16[4,144,1152]{2,1,0:T(8,128)(2,1)}, bf16[4,144,1152]{2,1,0:T(8,128)(2,1)}, u32[]{:S(2)}, u32[]{:S(2)}) collective-permute-start(bf16[4,144,1152]{2,1,0:T(8,128)(2,1)} %get-tuple-element.213), channel_id=1, source_target_pairs={{0,1},{1,0},{2,3},{3,2},{4,5},{5,4},{6,7},{7,6},{8,9},{9,8},{10,11... | collective-permute-start | bytes 3981320 | tf_op jit(solution)/shard_map/ppermute | solution.py:1401
  306.3 128.2 %reduce-scatter.6.cloned.1.call-start = ((), (), s32[]{:S(2)}) async-start(), calls=%async_computation.4 | async-start | bytes 1658880 | tf_op jit(solution)/shard_map/reduce_scatter | solution.py:1437
  306.3 23.5 %collective-permute-start.45 = (bf16[2,144,1152]{2,1,0:T(8,128)(2,1)}, bf16[2,144,1152]{2,1,0:T(8,128)(2,1)}, u32[]{:S(2)}, u32[]{:S(2)}) collective-permute-start(bf16[2,144,1152]{2,1,0:T(8,128)(2,1)} %get-tuple-element.218), channel_id=1, source_target_pairs={{0,4},{1,5},{2,6},{3,7},{4,0},{5,1},{6,2},{7,3},{8,12},{9,13},{10,... | collective-permute-start | bytes 1990664 | tf_op jit(solution)/shard_map/ppermute | solution.py:1401
  308.8 47.3 %collective-permute-start.51 = (bf16[768,1152]{1,0:T(8,128)(2,1)S(1)}, bf16[768,1152]{1,0:T(8,128)(2,1)S(1)}, u32[]{:S(2)}, u32[]{:S(2)}) collective-permute-start(bf16[768,1152]{1,0:T(8,128)(2,1)S(1)} %copy-done.4), channel_id=1, source_target_pairs={{0,2},{1,3},{2,0},{3,1},{4,6},{5,7},{6,4},{7,5},{8,10},{9,11},{10,... | collective-permute-start | bytes 5308424 | tf_op jit(solution)/shard_map/ppermute | solution.py:1401
  329.9 26.3 %collective-permute-start.49 = (bf16[768,896]{1,0:T(8,128)(2,1)}, bf16[768,896]{1,0:T(8,128)(2,1)}, u32[]{:S(2)}, u32[]{:S(2)}) collective-permute-start(bf16[768,896]{1,0:T(8,128)(2,1)} %get-tuple-element.232.refs_1_), channel_id=1, source_target_pairs={{0,2},{1,3},{2,0},{3,1},{4,6},{5,7},{6,4},{7,5},{8,10},{9,11},{10,... | collective-permute-start | bytes 4128776 | tf_op jit(solution)/shard_map/ppermute | solution.py:1401
  333.4 35.7 %collective-permute-start.47 = (bf16[4,144,1152]{2,1,0:T(8,128)(2,1)}, bf16[4,144,1152]{2,1,0:T(8,128)(2,1)}, u32[]{:S(2)}, u32[]{:S(2)}) collective-permute-start(bf16[4,144,1152]{2,1,0:T(8,128)(2,1)} %get-tuple-element.226.refs_6_), channel_id=1, source_target_pairs={{0,4},{1,5},{2,6},{3,7},{4,0},{5,1},{6,2},{7,3},{8,12},{9,13},{10,... | collective-permute-start | bytes 3981320 | tf_op jit(solution)/shard_map/ppermute | solution.py:1401
  333.9 35.2 %collective-permute-start.48 = (bf16[4,144,1152]{2,1,0:T(8,128)(2,1)}, bf16[4,144,1152]{2,1,0:T(8,128)(2,1)}, u32[]{:S(2)}, u32[]{:S(2)}) collective-permute-start(bf16[4,144,1152]{2,1,0:T(8,128)(2,1)} %get-tuple-element.227), channel_id=1, source_target_pairs={{0,1},{1,0},{2,3},{3,2},{4,5},{5,4},{6,7},{7,6},{8,9},{9,8},{10,11... | collective-permute-start | bytes 3981320 | tf_op jit(solution)/shard_map/ppermute | solution.py:1401
  372.4 101.7 %reduce-scatter.8.cloned.1.call-start = ((), (), s32[]{:S(2)}) async-start(), calls=%async_computation.5 | async-start | bytes 1658880 | tf_op jit(solution)/shard_map/reduce_scatter | solution.py:1437
  394.7 39.8 %collective-permute-start.56 = (bf16[4,144,1152]{2,1,0:T(8,128)(2,1)}, bf16[4,144,1152]{2,1,0:T(8,128)(2,1)S(1)}, u32[]{:S(2)}, u32[]{:S(2)}) collective-permute-start(bf16[4,144,1152]{2,1,0:T(8,128)(2,1)} %get-tuple-element.249.refs_10_), channel_id=1, source_target_pairs={{0,4},{1,5},{2,6},{3,7},{4,0},{5,1},{6,2},{7,3},{8,12},{9,13},{10,... | collective-permute-start | bytes 3981320 | tf_op jit(solution)/shard_map/ppermute | solution.py:1401
  395.2 39.2 %collective-permute-start.57 = (bf16[4,144,1152]{2,1,0:T(8,128)(2,1)}, bf16[4,144,1152]{2,1,0:T(8,128)(2,1)}, u32[]{:S(2)}, u32[]{:S(2)}) collective-permute-start(bf16[4,144,1152]{2,1,0:T(8,128)(2,1)} %get-tuple-element.253), channel_id=1, source_target_pairs={{0,1},{1,0},{2,3},{3,2},{4,5},{5,4},{6,7},{7,6},{8,9},{9,8},{10,11... | collective-permute-start | bytes 3981320 | tf_op jit(solution)/shard_map/ppermute | solution.py:1401
  444.9 26.8 %collective-permute-start.66 = (f32[72,1152]{1,0:T(8,128)}, f32[72,1152]{1,0:T(8,128)}, u32[]{:S(2)}, u32[]{:S(2)}) collective-permute-start(f32[72,1152]{1,0:T(8,128)} %constant_dynamic-slice_fusion.1), channel_id=1, source_target_pairs={{0,2},{1,3},{2,0},{3,1},{4,6},{5,7},{6,4},{7,5},{8,10},{9,11},{10,... | collective-permute-start | bytes 995336 | tf_op jit(solution)/shard_map/ppermute | solution.py:1401
  448.7 24.0 %collective-permute-start.67 = (f32[72,1152]{1,0:T(8,128)}, f32[72,1152]{1,0:T(8,128)S(1)}, u32[]{:S(2)}, u32[]{:S(2)}) collective-permute-start(f32[72,1152]{1,0:T(8,128)} %constant_dynamic-slice_fusion), channel_id=1, source_target_pairs={{0,2},{1,3},{2,0},{3,1},{4,6},{5,7},{6,4},{7,5},{8,10},{9,11},{10,... | collective-permute-start | bytes 995336 | tf_op jit(solution)/shard_map/ppermute | solution.py:1401
  (88 other events, 711.9 us)
Sparse Core Ops, SparseCore 0:
  18.9 35.0 all-gather.6
  58.0 33.1 all-gather.8
  92.7 32.0 all-gather.10
  306.4 30.9 reduce-scatter.3
  372.6 31.0 reduce-scatter.5
  440.5 33.5 reduce-scatter.7

commit v4 on v3

--- a/solution.py
+++ b/solution.py
@@ -521,7 +521,7 @@
 def heads_forward_call(spot, kind, rows_in, biases, groups, waits=()):
     rows, full = rows_in.shape
     arrays, places = flatten(groups)
-    _, high, group_width = arrays[0].shape
+    high, group_width = arrays[0].shape[-2:]
     depth = full // (2 * high)
     count = len(groups)
     part = group_width // 4
@@ -568,7 +568,7 @@
     grad_ref, qkv_ref, probs_ref, mixed_ref, out_ref, keys_ref, values_ref, grads_ref = refs[-16:-8]
     query_sum, key_sum, value_sum, in_sems, probs_sems, out_sems, weights, sems = refs[-8:]
     width = keys_ref.shape[1]
-    first_lane = pieces[0].shape[2] - width
+    first_lane = pieces[0].shape[-1] - width
     loads = weight_copies(places, pieces, weights, sems, spot[0], first_lane, width)
     grad_copy = pltpu.make_async_copy(grad_any, grad_ref, in_sems.at[2 * groups])
     slots = probs_ref.shape[0]
@@ -659,7 +659,7 @@
 def heads_backward_call(spot, grad_rows, qkv, probs, mixed, groups, picks, waits=()):
     rows, full = grad_rows.shape
     arrays, places = flatten(groups)
-    _, high, group_width = arrays[0].shape
+    high, group_width = arrays[0].shape[-2:]
     depth = full // (2 * high)
     part = group_width // 4
     heads = part // HEAD_DIM
@@ -734,7 +734,7 @@
 
 
 def call(kernel, name, operands, specs, outs, scratch, waits=()):
-    no_cost = pl.CostEstimate(flops=0, bytes_accessed=0, transcendentals=0)
+    no_cost = pl.CostEstimate(flops=1024, bytes_accessed=1024, transcendentals=0)
     out_specs = [spec for spec, _, _ in outs]
     return pl.pallas_call(
         kernel,
@@ -749,8 +749,8 @@
 
 
 def flatten(groups):
-    arrays = [piece for group in groups for piece, _, _ in group]
-    places = [[(at, x_off) for _, at, x_off in group] for group in groups]
+    arrays = [part[0] for group in groups for part in group]
+    places = [[part[1:] for part in group] for group in groups]
     return arrays, places
 
 
@@ -758,8 +758,8 @@
     copies, at = [], 0
     for group, parts in enumerate(places):
         mine = []
-        for part, (start, x_off) in enumerate(parts):
-            source = refs[at]
+        for part, (start, x_off, *pick) in enumerate(parts):
+            source = refs[at].at[:, pick[0]] if pick else refs[at]
             at += 1
             if width is not None:
                 source = source.at[:, :, pl.ds(first, width)]
@@ -837,7 +837,7 @@
 def up_project(spot, rows_in, biases, groups, waits=()):
     rows, full = rows_in.shape
     arrays, places = flatten(groups)
-    _, high, width = arrays[0].shape
+    high, width = arrays[0].shape[-2:]
     depth = full // (2 * high)
     count = len(groups)
     shape = (count, rows, width)
@@ -859,73 +859,6 @@
     )
 
 
-def slope_kernel(places, waits, spot, x_any, slope_any, *refs):
-    count = sum(len(parts) for parts in places)
-    pieces = refs[:count]
-    out_any, sum_ref = refs[count + waits : count + waits + 2]
-    x_ref, slope_ref, out_ref, in_sems, out_sems, weights, sems = refs[-7:]
-    rows = x_ref.shape[0]
-    groups = len(places)
-    copies = weight_copies(places, pieces, weights, sems, spot[0])
-    x_copy = pltpu.make_async_copy(x_any, x_ref, in_sems.at[groups])
-    for group, mine in enumerate(copies):
-        mine.append(
-            pltpu.make_async_copy(slope_any.at[group], slope_ref.at[group], in_sems.at[group])
-        )
-    begin([x_copy] + copies[0])
-    arrive([x_copy] + copies[0])
-    sent = []
-    for group in range(groups):
-        if group + 1 < groups:
-            begin(copies[group + 1])
-        if group:
-            arrive(copies[group])
-        whole = strips(weights, group)
-        total = jnp.zeros((1, weights.shape[-1]), jnp.float32)
-        for tile in row_tiles(rows, 256):
-            grad = jnp.dot(x_ref[tile, :], whole, preferred_element_type=jnp.float32)
-            low = (grad * slope_ref[group, tile, :].astype(jnp.float32)).astype(jnp.bfloat16)
-            out_ref[group, tile, :] = low
-            total += jnp.sum(low.astype(jnp.float32), axis=0, keepdims=True)
-        sum_ref[group] = total
-        for half, tile in enumerate(row_tiles(rows, rows // 2)):
-            span = pl.ds(tile.start, rows // 2)
-            copy = pltpu.make_async_copy(
-                out_ref.at[group, span], out_any.at[group, span], out_sems.at[group, half]
-            )
-            copy.start()
-            sent.append(copy)
-    arrive(sent)
-
-
-def hidden_grad(spot, rows_in, slope, groups, waits=()):
-    rows, full = rows_in.shape
-    arrays, places = flatten(groups)
-    _, high, width = arrays[0].shape
-    depth = full // (2 * high)
-    count = len(groups)
-    shape = (count, rows, width)
-    return call(
-        functools.partial(slope_kernel, places, len(waits)),
-        "mlp_grad",
-        [spot, rows_in, slope, *arrays],
-        [smem_spec(), any_spec(), any_spec()] + [any_spec()] * len(arrays),
-        [
-            (any_spec(), shape, jnp.bfloat16),
-            (vmem_spec(), (count, 1, width), jnp.float32),
-        ],
-        [
-            low_scratch(rows, full),
-            low_scratch(*shape),
-            low_scratch(*shape),
-            copy_sems(count + 1),
-            copy_sems(count, 2),
-        ]
-        + weight_scratch(places, depth, high, width),
-        waits,
-    )
-
-
 def unit_rows(values):
     centre = values - jnp.mean(values, axis=1, keepdims=True)
     spread = jnp.mean(centre * centre, axis=1, keepdims=True)
@@ -942,17 +875,165 @@
     return part, jnp.sum(grad * unit, axis=0, keepdims=True), jnp.sum(grad, axis=0, keepdims=True)
 
 
-def back_kernel(places, sources, waits, keep_low, spot, *refs):
+def mlp_back_kernel(down_places, up_places, waits, spot, x_any, one_any, two_any, resid_any, gain_ref, *refs):
+    count = [sum(len(parts) for parts in places) for places in (down_places, up_places)]
+    down_pieces = refs[: count[0]]
+    up_pieces = refs[count[0] : count[0] + count[1]]
+    at = count[0] + count[1] + waits
+    one_out, two_out, low_any, sum_ref, hidden_sums = refs[at : at + 5]
+    x_ref, slope_ref, hidden_ref, resid_ref, total, low_ref, in_sems, hidden_sems, out_sems = refs[
+        at + 5 : at + 14
+    ]
+    down_weights, down_sems, up_weights, up_sems = refs[at + 14 :]
+    rows = x_ref.shape[0]
+    groups = len(down_places)
+    half = groups // 2
+    slots = down_weights.shape[0]
+
+    def slotted(places, pieces, weights, sems):
+        copies, first = [], 0
+        for group, parts in enumerate(places):
+            mine = pieces[first : first + len(parts)]
+            first += len(parts)
+            slot = group % slots
+            copies += weight_copies(
+                [parts],
+                mine,
+                weights.at[pl.ds(slot, 1)],
+                sems.at[pl.ds(slot, 1)],
+                spot[0],
+            )
+        return copies
+
+    downs = slotted(down_places, down_pieces, down_weights, down_sems)
+    ups = slotted(up_places, up_pieces, up_weights, up_sems)
+    for group in range(groups):
+        source = one_any.at[group] if group < half else two_any.at[group - half]
+        slot = group % slots
+        downs[group].append(
+            pltpu.make_async_copy(source, slope_ref.at[slot], in_sems.at[2 + slot])
+        )
+    x_copy = pltpu.make_async_copy(x_any, x_ref, in_sems.at[0])
+    late = pltpu.make_async_copy(resid_any, resid_ref, in_sems.at[1])
+    begin([x_copy] + downs[0])
+    arrive([x_copy] + downs[0])
+    sent = []
+    for group in range(groups):
+        slot = group % slots
+        begin(ups[group])
+        whole = strips(down_weights, slot)
+        column_total = jnp.zeros((1, total.shape[1]), jnp.float32)
+        if group >= slots:
+            sent[group - slots].wait()
+        for tile in row_tiles(rows, 256):
+            grad = jnp.dot(x_ref[tile, :], whole, preferred_element_type=jnp.float32)
+            low = (grad * slope_ref[slot, tile, :].astype(jnp.float32)).astype(jnp.bfloat16)
+            hidden_ref[slot, tile, :] = low
+            column_total += jnp.sum(low.astype(jnp.float32), axis=0, keepdims=True)
+        hidden_sums[group] = column_total
+        target = one_out.at[group] if group < half else two_out.at[group - half]
+        copy = pltpu.make_async_copy(hidden_ref.at[slot], target, hidden_sems.at[slot])
+        copy.start()
+        sent.append(copy)
+        arrive(ups[group])
+        if group + 1 < groups:
+            begin(downs[group + 1])
+        else:
+            begin([late])
+        whole = strips(up_weights, slot)
+        if group == 0:
+            total[...] = dot_last(hidden_ref[slot], whole)
+        elif group + 1 < groups:
+            total[...] += dot_last(hidden_ref[slot], whole)
+        else:
+            products = [
+                (tile, dot_last(hidden_ref[slot, tile, :], whole)) for tile in row_tiles(rows, 256)
+            ]
+        if group + 1 < groups:
+            arrive(downs[group + 1])
+    arrive([late])
+    sums = [jnp.zeros((1, total.shape[1]), jnp.float32) for _ in range(3)]
+    low_sent = []
+    for tile, product in products:
+        for small in range(tile.start, tile.stop, 128):
+            span = slice(small, small + 128)
+            inside = slice(small - tile.start, small - tile.start + 128)
+            part, gain_sum, shift_sum = norm_rows_back(
+                resid_ref[span, :].astype(jnp.float32),
+                gain_ref[...],
+                total[span, :] + product[inside],
+            )
+            low = (x_ref[span, :].astype(jnp.float32) + part).astype(jnp.bfloat16)
+            low_ref[span, :] = low
+            sums[0] += gain_sum
+            sums[1] += shift_sum
+            sums[2] += jnp.sum(low.astype(jnp.float32), axis=0, keepdims=True)
+        long = pl.ds(tile.start, tile.stop - tile.start)
+        copy = pltpu.make_async_copy(
+            low_ref.at[long], low_any.at[long], out_sems.at[len(low_sent)]
+        )
+        copy.start()
+        low_sent.append(copy)
+    sum_ref[...] = jnp.concatenate(sums + [jnp.zeros((5, total.shape[1]), jnp.float32)])
+    arrive(sent[-slots:] + low_sent)
+
+
+def mlp_back(spot, grad_low, first_slope, second_slope, resid, gain, downs, ups, waits=()):
+    rows, full = grad_low.shape
+    down_arrays, down_places = flatten(downs)
+    up_arrays, up_places = flatten(ups)
+    high, width = up_arrays[0].shape[-2:]
+    depth = full // (2 * high)
+    count = len(downs)
+    slots = 2
+    shape = (count // 2, rows, width)
+
+    def slot_scratch(places):
+        return [
+            pltpu.VMEM((slots, depth, 2, high, width), jnp.bfloat16),
+            copy_sems(slots, max(len(parts) for parts in places)),
+        ]
+
+    return call(
+        functools.partial(mlp_back_kernel, down_places, up_places, len(waits)),
+        "mlp_back",
+        [spot, grad_low, first_slope, second_slope, resid, gain, *down_arrays, *up_arrays],
+        [smem_spec()]
+        + [any_spec()] * 4
+        + [vmem_spec()]
+        + [any_spec()] * (len(down_arrays) + len(up_arrays)),
+        [
+            (any_spec(), shape, jnp.bfloat16),
+            (any_spec(), shape, jnp.bfloat16),
+            (any_spec(), (rows, full), jnp.bfloat16),
+            (vmem_spec(), (8, full), jnp.float32),
+            (vmem_spec(), (count, 1, width), jnp.float32),
+        ],
+        [
+            low_scratch(rows, full),
+            low_scratch(slots, rows, width),
+            low_scratch(slots, rows, width),
+            pltpu.VMEM(resid.shape, resid.dtype),
+            wide_scratch(rows, full),
+            low_scratch(rows, full),
+            copy_sems(2 + slots),
+            copy_sems(slots),
+            copy_sems(-(-rows // 256)),
+        ]
+        + slot_scratch(down_places)
+        + slot_scratch(up_places),
+        waits,
+    )
+
+
+def back_kernel(places, sources, waits, spot, *refs):
     count = sum(len(parts) for parts in places)
     grads_any = refs[:sources]
     base_any, grad_any, gain_ref = refs[sources : sources + 3]
     pieces = refs[sources + 3 : sources + 3 + count]
-    outs = 3 if keep_low else 2
     first_out = sources + 3 + count + waits
-    out_any, *low_any, sum_ref = refs[first_out : first_out + outs]
-    grads_ref, base_ref, grad_ref, total, in_sems, out_sems, weights, sems = refs[
-        first_out + outs : first_out + outs + 8
-    ]
+    out_any, sum_ref = refs[first_out : first_out + 2]
+    grads_ref, base_ref, grad_ref, total, in_sems, out_sems, weights, sems = refs[first_out + 2 :]
     rows = total.shape[0]
     groups = len(places)
     width = weights.shape[-1]
@@ -969,11 +1050,8 @@
     ]
     begin(copies[0])
     for group in range(groups):
-        if group + 1 < groups:
-            begin(copies[group + 1])
-        else:
-            begin(late)
         arrive(copies[group])
+        begin(copies[group + 1] if group + 1 < groups else late)
         whole = strips(weights, group)
         if group == 0:
             total[...] = dot_last(grads_ref[group], whole)
@@ -984,7 +1062,7 @@
                 (tile, dot_last(grads_ref[group, tile, :], whole)) for tile in row_tiles(rows, 256)
             ]
     arrive(late)
-    sums = [jnp.zeros((1, total.shape[1]), jnp.float32) for _ in range(3)]
+    sums = [jnp.zeros((1, total.shape[1]), jnp.float32) for _ in range(2)]
     sent = []
     for tile, product in products:
         for small in range(tile.start, tile.stop, 128):
@@ -999,35 +1077,27 @@
             total[span, :] = grad
             sums[0] += gain_sum
             sums[1] += shift_sum
-            if keep_low:
-                low = grad.astype(jnp.bfloat16)
-                grads_ref[0, span, :] = low
-                sums[2] += jnp.sum(low.astype(jnp.float32), axis=0, keepdims=True)
         long = pl.ds(tile.start, tile.stop - tile.start)
-        pairs = [(total.at[long], out_any.at[long])]
-        if keep_low:
-            pairs.append((grads_ref.at[0, long], low_any[0].at[long]))
-        for source, target in pairs:
-            copy = pltpu.make_async_copy(source, target, out_sems.at[len(sent)])
-            copy.start()
-            sent.append(copy)
-    sum_ref[...] = jnp.concatenate(sums + [jnp.zeros((5, total.shape[1]), jnp.float32)])
+        copy = pltpu.make_async_copy(total.at[long], out_any.at[long], out_sems.at[len(sent)])
+        copy.start()
+        sent.append(copy)
+    sum_ref[...] = jnp.concatenate(sums + [jnp.zeros((6, total.shape[1]), jnp.float32)])
     arrive(sent)
 
 
-def norm_back(name, spot, grads, base, grad, gain, groups, keep_low, waits=()):
+def norm_back(spot, grads, base, grad, gain, groups, waits=()):
     rows, full = base.shape
     arrays, places = flatten(groups)
-    _, high, _ = arrays[0].shape
+    high, _ = arrays[0].shape[-2:]
     width = grads[0].shape[-1]
     depth = full // (2 * high)
-    outs = [(any_spec(), (rows, full), jnp.float32)]
-    if keep_low:
-        outs.append((any_spec(), (rows, full), jnp.bfloat16))
-    outs.append((vmem_spec(), (8, full), jnp.float32))
+    outs = [
+        (any_spec(), (rows, full), jnp.float32),
+        (vmem_spec(), (8, full), jnp.float32),
+    ]
     return call(
-        functools.partial(back_kernel, places, len(grads), len(waits), keep_low),
-        name,
+        functools.partial(back_kernel, places, len(grads), len(waits)),
+        "norm_one_back",
         [spot, *grads, base, grad, gain, *arrays],
         [smem_spec()] + [any_spec()] * (len(grads) + 2) + [vmem_spec()] + [any_spec()] * len(arrays),
         outs,
@@ -1037,7 +1107,7 @@
             pltpu.VMEM(grad.shape, grad.dtype),
             wide_scratch(rows, full),
             copy_sems(len(groups) + 2),
-            copy_sems(2 * -(-rows // 256)),
+            copy_sems(-(-rows // 256)),
         ]
         + weight_scratch(places, depth, high, width),
         waits,
@@ -1060,25 +1130,35 @@
         )
     late = [pltpu.make_async_copy(resid_any, resid_ref, in_sems.at[groups])]
     begin(copies[0])
-    for group in range(groups):
-        begin(copies[group + 1] if group + 1 < groups else late)
+    for group in range(groups - 1):
         arrive(copies[group])
+        begin(copies[group + 1])
+        if group + 2 == groups:
+            begin(late)
         product = dot_last(active_ref[group], strips(weights, group))
         if group == 0:
             total[...] = product
         else:
             total[...] += product
-    arrive(late)
-    out_ref[...] = (total[...] + resid_ref[...] + shift_ref[...]).astype(out_ref.dtype)
-    copy = pltpu.make_async_copy(out_ref, out_any, out_sems.at[0])
-    copy.start()
-    copy.wait()
+    arrive(copies[-1] + late)
+    whole = strips(weights, groups - 1)
+    sent = []
+    for tile in row_tiles(rows, 256):
+        product = dot_last(active_ref[groups - 1, tile, :], whole)
+        product = product + total[tile, :] + shift_ref[...]
+        product = product + resid_ref[tile, :].astype(jnp.float32)
+        out_ref[tile, :] = product.astype(out_ref.dtype)
+        long = pl.ds(tile.start, tile.stop - tile.start)
+        copy = pltpu.make_async_copy(out_ref.at[long], out_any.at[long], out_sems.at[len(sent)])
+        copy.start()
+        sent.append(copy)
+    arrive(sent)
 
 
 def down_project(spot, first, second, resid, shift, groups, waits=()):
     rows, full = resid.shape
     arrays, places = flatten(groups)
-    _, high, width = arrays[0].shape
+    high, width = arrays[0].shape[-2:]
     depth = full // (2 * high)
     return call(
         functools.partial(down_kernel, places, len(waits)),
@@ -1088,11 +1168,11 @@
         [(any_spec(), (rows, full), jnp.bfloat16)],
         [
             low_scratch(len(groups), rows, width),
-            wide_scratch(rows, full),
+            pltpu.VMEM(resid.shape, resid.dtype),
             wide_scratch(rows, full),
             low_scratch(rows, full),
             copy_sems(len(groups) + 1),
-            copy_sems(1),
+            copy_sems(-(-rows // 256)),
         ]
         + weight_scratch(places, depth, high, width),
         waits,
@@ -1103,7 +1183,7 @@
     count = sum(len(parts) for parts in places)
     pieces = refs[:count]
     resid_any, normed_any = refs[count + waits : count + waits + 2]
-    mixed_ref, x_ref, resid_ref, normed_ref, in_sems, out_sems, weights, sems = refs[-8:]
+    mixed_ref, x_ref, resid_ref, low_ref, normed_ref, in_sems, out_sems, weights, sems = refs[-9:]
     rows = x_ref.shape[0]
     outer = weights.shape[-1]
     first = pieces[0].shape[-1] - outer
@@ -1134,11 +1214,11 @@
             inside = slice(small - tile.start, small - tile.start + 128)
             values = resid_ref[span, :] + product[inside] + x_ref[span, :].astype(jnp.float32)
             values = values + shift_ref[...]
-            resid_ref[span, :] = values
+            low_ref[span, :] = values.astype(jnp.bfloat16)
             unit, _ = unit_rows(values)
             normed_ref[span, :] = (unit * gain_ref[...] + bias_ref[...]).astype(jnp.bfloat16)
         long = pl.ds(tile.start, tile.stop - tile.start)
-        for source, target in ((resid_ref, resid_any), (normed_ref, normed_any)):
+        for source, target in ((low_ref, resid_any), (normed_ref, normed_any)):
             copy = pltpu.make_async_copy(source.at[long], target.at[long], out_sems.at[len(sent)])
             copy.start()
             sent.append(copy)
@@ -1148,7 +1228,7 @@
 def out_project(spot, mixed, rows_in, shift, gain, bias, groups, waits=()):
     rows, full = rows_in.shape
     arrays, places = flatten(groups)
-    _, high, _ = arrays[0].shape
+    high, _ = arrays[0].shape[-2:]
     outer = mixed[0].shape[1]
     depth = full // (2 * high)
     return call(
@@ -1157,7 +1237,7 @@
         [spot, *mixed, rows_in, shift, gain, bias, *arrays],
         [smem_spec()] + [any_spec()] * 5 + [vmem_spec()] * 3 + [any_spec()] * len(arrays),
         [
-            (any_spec(), (rows, full), jnp.float32),
+            (any_spec(), (rows, full), jnp.bfloat16),
             (any_spec(), (rows, full), jnp.bfloat16),
         ],
         [
@@ -1165,6 +1245,7 @@
             low_scratch(rows, full),
             wide_scratch(rows, full),
             low_scratch(rows, full),
+            low_scratch(rows, full),
             copy_sems(5),
             copy_sems(2 * -(-rows // 256)),
         ]
@@ -1177,7 +1258,7 @@
     inputs = 4 + (4 if extra else 0)
     sources = refs[:inputs]
     outs_at = inputs + waits
-    count = sum(2 + side for side in sides)
+    count = sum(3 + side // 2 for side in sides)
     outs = list(refs[outs_at : outs_at + count])
     holds = refs[outs_at + count : outs_at + count + inputs]
     stage, in_sems, out_sems = refs[-3:]
@@ -1200,7 +1281,7 @@
     sent = []
     starts = []
     for side in sides:
-        starts.append(sum(2 + before for before in sides[: len(starts)]))
+        starts.append(sum(3 + before // 2 for before in sides[: len(starts)]))
     for i, side in enumerate(sides):
         if i:
             arrive([firsts[i], seconds[i]])
@@ -1227,11 +1308,12 @@
             stage[i, part * half : (part + 1) * half] = product.astype(jnp.bfloat16).reshape(
                 half, 2, high, width
             )
-            near_out = outs[starts[i]].at[span]
             if side == 0:
-                far_out = outs[starts[i] + 1].at[span]
+                near_out = outs[starts[i]].at[span]
+                far_out = outs[starts[i] + 1 + part]
             else:
-                far_out = outs[starts[i] + 1 + part]
+                near_out = outs[starts[i] + part]
+                far_out = outs[starts[i] + 2 + part]
             for source, target in (
                 (stage.at[i, span, x_at], near_out),
                 (stage.at[i, span, 1 - x_at], far_out),
@@ -1242,7 +1324,7 @@
     arrive(sent)
 
 
-def weight_grad(spot, left, right, depth, sides=(0, 1), extra=(), waits=()):
+def weight_grad(spot, left, right, depth, sides=(0, 2), extra=(), waits=()):
     rows, full = left[0].shape
     high = full // (2 * depth)
     half = depth // 2
@@ -1252,7 +1334,7 @@
     operands = [left[0], rights[0], left[1], rights[1], *extra]
     shapes = []
     for side in sides:
-        shapes += [depth, depth] if side == 0 else [depth, half, half]
+        shapes += [depth, half, half] if side == 0 else [half] * 4
     outs = [(any_spec(), (size, high, width), jnp.bfloat16) for size in shapes]
     return call(
         functools.partial(grad_kernel, sides, bool(extra), len(waits)),
@@ -1270,68 +1352,43 @@
     )
 
 
-def corner_kernel(beside_ref, across_ref, one_ref, two_ref, beside_out, across_out):
+def pair_kernel(one_ref, two_ref, three_ref, four_ref, first_out, second_out):
     wide = jnp.float32
-    low = beside_out.dtype
-    beside_out[...] = (beside_ref[...].astype(wide) + two_ref[...].astype(wide)).astype(low)
-    across_out[...] = (across_ref[...].astype(wide) + one_ref[...].astype(wide)).astype(low)
-
-
-def add_corners(beside, across, corner_one, corner_two):
-    block = corner_one.shape
-    first = pl.BlockSpec(block, lambda i: (0, 0, 0))
-    second = pl.BlockSpec(block, lambda i: (1, 0, 0))
-    shape = jax.ShapeDtypeStruct(beside.shape, beside.dtype)
+    low = first_out.dtype
+    first_out[...] = (one_ref[...].astype(wide) + two_ref[...].astype(wide)).astype(low)
+    second_out[...] = (three_ref[...].astype(wide) + four_ref[...].astype(wide)).astype(low)
+
+
+def add_pairs(one, two, three, four):
+    shape = jax.ShapeDtypeStruct(one.shape, one.dtype)
     return pl.pallas_call(
-        corner_kernel,
-        grid=(1,),
-        in_specs=[second, first, first, first],
-        out_specs=[second, first],
+        pair_kernel,
+        in_specs=[vmem_spec()] * 4,
+        out_specs=[vmem_spec()] * 2,
         out_shape=[shape, shape],
-        input_output_aliases={0: 0, 1: 1},
         compiler_params=limits(),
-        name="add_corners",
-    )(beside, across, corner_one, corner_two)
-
-
-def one_corner_kernel(base_ref, part_ref, out_ref):
-    total = base_ref[...].astype(jnp.float32) + part_ref[...].astype(jnp.float32)
-    out_ref[...] = total.astype(out_ref.dtype)
-
-
-def add_corner(base, part, half):
-    block = part.shape
-    spec = pl.BlockSpec(block, lambda i: (half, 0, 0))
-    return pl.pallas_call(
-        one_corner_kernel,
-        grid=(1,),
-        in_specs=[spec, pl.BlockSpec(block, lambda i: (0, 0, 0))],
-        out_specs=spec,
-        out_shape=jax.ShapeDtypeStruct(base.shape, base.dtype),
-        input_output_aliases={0: 0},
-        compiler_params=limits(),
-        name="add_corner",
-    )(base, part)
-
-
-def square_kernel(own, one, two, out):
+        name="add_pairs",
+    )(one, two, three, four)
+
+
+def square_kernel(own, one_lo, one_hi, two_lo, two_hi, out):
     wide = jnp.float32
-    total = own[...].astype(wide) + one[...].astype(wide) + two[...].astype(wide)
-    out[...] = total.astype(out.dtype)
-
-
-def add_square(own, one, two):
-    depth, high, width = own.shape
-    block = pl.BlockSpec((depth // 2, high, width), lambda i: (i, 0, 0))
+    half = one_lo.shape[0]
+    for part, (one, two) in enumerate(((one_lo, two_lo), (one_hi, two_hi))):
+        span = slice(part * half, (part + 1) * half)
+        total = own[span].astype(wide) + one[...].astype(wide) + two[...].astype(wide)
+        out[span] = total.astype(out.dtype)
+
+
+def add_square(own, *parts):
     return pl.pallas_call(
         square_kernel,
-        grid=(2,),
-        in_specs=[block, block, block],
-        out_specs=block,
+        in_specs=[vmem_spec()] * 5,
+        out_specs=vmem_spec(),
         out_shape=jax.ShapeDtypeStruct(own.shape, own.dtype),
         compiler_params=limits(),
         name="add_square",
-    )(own, one, two)
+    )(own, *parts)
 
 
 def halves_kernel(first_ref, second_ref, first_out, second_out):
@@ -1405,6 +1462,9 @@
 
     def over_y(self, values):
         return self.move(values, lambda z, x, c, y: (z, x, c, 1 - y))
+
+    def over_both(self, values):
+        return self.move(values, lambda z, x, c, y: (z, 1 - x, c, 1 - y))
 
     def over_core(self, values):
         return self.move(values, lambda z, x, c, y: (z, x, 1 - c, y))
@@ -1503,7 +1563,7 @@
     blocks = [grid.spread(first_block), grid.spread(second_block), grid.spread(third_block)]
     vectors = jnp.stack([ln1_gain, ln1_bias, out_bias, ln2_gain, ln2_bias, fc2_bias])
     (vectors,) = fence([vectors], [blocks[0]])
-    vectors = grid.gather_small(vectors).astype(wide)
+    vectors = grid.gather_small(vectors)
     own_one = grid.gather_depth(blocks[0])
 
     here = grid.y
@@ -1528,6 +1588,23 @@
         [one_row(layer_input, swap_at), one_row(cotangent, swap_at), one_row(layer_input, last_blank)]
     )
     came = grid.over_y(sent)
+    biases = jnp.concatenate([qv_bias.reshape(-1), fc1_bias])
+    biases = jnp.pad(biases, (0, -biases.shape[0] % 128)).reshape(-1, 128)
+    (biases,) = fence([biases], [blocks[0]])
+    other_biases = grid.over_y(biases)
+
+    def sides_of(own):
+        return [grid.over_x(own), grid.over_y(own)]
+
+    beside_three, across_three = sides_of(blocks[2])
+    quad = [blocks[2], beside_three, across_three, grid.over_both(blocks[2])]
+    (block_two,) = fence([blocks[1]], [vectors, came])
+    own_two = grid.gather_depth(block_two)
+    own_one, vectors, came, other_biases, *quad = fence(
+        [own_one, vectors, came, other_biases] + quad
+    )
+    vectors = vectors.astype(wide)
+    other_biases = other_biases.reshape(-1)
     other_blank = jnp.where(stray_there, sent[0:1], came[2:3])
     spread_rows = lax.broadcasted_iota(jnp.int32, (padded, 1), 0)
     at_swap = (spread_rows == swap_at) & swapped
@@ -1542,11 +1619,6 @@
     kind = jnp.where(spread_rows > rows, 3, jnp.where(spread_rows == rows, 2, 0))
     kind = jnp.where(spread_rows == blank_at, 1, kind)
     input_rows, grad_low = lax.optimization_barrier((input_rows, grad_low))
-
-    biases = jnp.concatenate([qv_bias.reshape(-1), fc1_bias])
-    biases = jnp.pad(biases, (0, -biases.shape[0] % 128)).reshape(-1, 128)
-    (biases,) = fence([biases], [blocks[0]])
-    other_biases = grid.over_y(biases).reshape(-1)
 
     def ordered(first, second):
         return jnp.where(grid.c == 0, first, second), jnp.where(grid.c == 0, second, first)
@@ -1572,9 +1644,6 @@
     qv_stacks = [stacked(qv_groups, picked) for picked in ((0, 1), (2, 3))]
     fc1_stacks = [stacked(fc1_groups, picked) for picked in ((1, 3), (0, 2))]
 
-    def sides_of(own):
-        return [grid.over_x(own), grid.over_y(own)]
-
     def corners_of(beside, across):
         first, second = take_halves(beside, across)
         return [grid.over_y(first), grid.over_x(second)]
@@ -1594,28 +1663,25 @@
             [(there[0], 0, 0), (there[1], 0, 1), (there[2], half, 1)],
         ]
 
-    own_one, vectors, input_rows, grad_low, kind, block_two, block_three, *stacks = fence(
-        [own_one, vectors, input_rows, grad_low, kind, blocks[1], blocks[2]]
-        + qv_stacks
-        + fc1_stacks
-    )
-    qv_stacks, fc1_stacks = stacks[:2], stacks[2:]
+    quad = jnp.stack(quad)
     gain_one, shift_one, out_shift, gain_two, shift_two, fc2_shift = [
         vectors[i : i + 1] for i in range(6)
     ]
-    own_two = grid.gather_depth(block_two)
     beside_one, across_one = sides_of(own_one)
     unit_one, _ = unit_rows(input_rows.astype(wide))
     normed = (unit_one * gain_one + shift_one).astype(low)
-    own_two, beside_one, across_one, normed, block_three, grad_there = fence(
-        [own_two, beside_one, across_one, normed, block_three, grid.over_core(grad_low)]
-    )
+    own_two, beside_one, across_one, normed, quad, grad_there, kind, *stacks = fence(
+        [own_two, beside_one, across_one, normed, quad, grid.over_core(grad_low), kind]
+        + qv_stacks
+        + fc1_stacks
+    )
+    qv_stacks, fc1_stacks = stacks[:2], stacks[2:]
     corner_one = corners_of(beside_one, across_one)
     there = cores_of(own_one, beside_one)
     own_two_there = grid.over_core(own_two)
     across_there = grid.over_core(across_one)
     sides_two = sides_of(own_two)
-    own_three = grid.gather_depth(block_three)
+    quads = grid.gather_depth(quad)
 
     def heads(stack, groups, waits=()):
         return heads_forward_call(spot, kind, normed, stack, groups, waits)
@@ -1627,13 +1693,9 @@
     attn_weights = attn_weights + far_groups(across_one, corner_one, there)
     second_qkv, second_probs, *more = heads(qv_stacks[1], attn_weights[2:])
     mixed = mixed + more
-    own_three, beside_two, across_two, second_qkv = fence(
-        [own_three] + sides_two + [second_qkv]
-    )
+    beside_two, across_two, second_qkv = fence(sides_two + [second_qkv])
     corner_two = corners_of(beside_two, across_two)
-    sides_three = sides_of(own_three)
     beside_there, across_there = cores_of(beside_two, across_two)
-    own_three_there = grid.over_core(own_three)
     resid, normed_two = out_project(
         spot,
         mixed,
@@ -1642,9 +1704,10 @@
         gain_two,
         shift_two,
         attn_weights,
-        [beside_there, across_there, own_three_there],
-    )
-    *corner_two, normed_two = fence(corner_two + [normed_two])
+        [beside_there, across_there],
+    )
+    normed_there = grid.over_core(normed)
+    *corner_two, normed_two, normed_there = fence(corner_two + [normed_two, normed_there])
     up_weights = near_groups(own_two, beside_two, [own_two_there, beside_there])
     there = [across_there] + cores_of(*corner_two)
     up_weights = up_weights + far_groups(across_two, corner_two, there)
@@ -1655,54 +1718,55 @@
         return up_project(spot, normed_two, fc1_stacks[at], picked, waits)
 
     other_active, other_slope = up(0, [])
-    beside_three, across_three, other_active = fence(sides_three + [other_active])
-    corner_three = corners_of(beside_three, across_three)
-    beside_there = grid.over_core(beside_three)
-    across_there = grid.over_core(across_three)
+    (other_active,) = fence([other_active])
     active_there = grid.over_core(other_active)
     own_active, own_slope = up(1, [other_active])
-    *corner_three, own_active, active_there = fence(corner_three + [own_active, active_there])
-    down_weights = near_groups(own_three, beside_three, [own_three_there, beside_there])
-    there = [across_there] + cores_of(*corner_three)
-    down_weights = down_weights + far_groups(across_three, corner_three, there)
+    normed_two_there = grid.over_core(normed_two)
+    near_mixed, far_mixed = grid.over_core(mixed[1]), grid.over_core(mixed[3])
+    own_active, active_there, normed_two_there, near_mixed, far_mixed = fence(
+        [own_active, active_there, normed_two_there, near_mixed, far_mixed]
+    )
     fc2_sums = weight_grad(spot, (grad_low, grad_there), (own_active, active_there), depth)
-
-    def move_corners(sums):
-        return [grid.over_x(sums[3]), grid.over_y(sums[4])]
-
-    def back(at, slope, waits):
-        picked = [down_weights[i] for i in classes[at]]
-        return hidden_grad(spot, grad_low, slope, picked, waits)
-
-    moved = move_corners(fc2_sums)
-    other_hidden, other_fc1_sums = back(0, other_slope, [fc2_sums[0]])
+    fc2_near, quads = fence([fc2_sums[0], quads])
+    quads_there = grid.over_core(quads)
+    down_weights = [
+        [(source, 0, 0, at), (source, 0, 1, at + 1)]
+        for at in (0, 2)
+        for source in (quads, quads_there)
+    ]
+
+    def move_first(sums):
+        _, beside_lo, _, _, across_hi, corner_lo, corner_hi = sums
+        return [
+            grid.over_x(corner_lo),
+            grid.over_y(corner_hi),
+            grid.over_x(beside_lo),
+            grid.over_y(across_hi),
+        ]
+
+    def move_second(sums, corner_lo, corner_hi):
+        beside_hi, across_lo = add_pairs(sums[2], corner_hi, sums[3], corner_lo)
+        return [grid.over_x(beside_hi), grid.over_y(across_lo)]
+
+    def join(own, first, second):
+        return add_square(own, first[0], second[0], second[1], first[1])
+
+    fc2_moved = move_first(fc2_sums)
+    order = (0, 2, 1, 3)
+    own_hidden, other_hidden, resid_low, sums_two, fc1_bias_sums = mlp_back(
+        spot,
+        grad_low,
+        own_slope,
+        other_slope,
+        resid,
+        gain_two,
+        [down_weights[i] for i in order],
+        [up_weights[i] for i in order],
+        [fc2_near],
+    )
+    resid_low, other_hidden, *fc2_moved = fence([resid_low, other_hidden] + fc2_moved)
+    fc2_second = move_second(fc2_sums, *fc2_moved[:2])
     hidden_there = grid.over_core(other_hidden)
-    normed_two_there = grid.over_core(normed_two)
-    own_hidden, own_fc1_sums = back(1, own_slope, [other_hidden])
-    *moved, own_hidden, hidden_there, normed_two_there = fence(
-        moved + [own_hidden, hidden_there, normed_two_there]
-    )
-    beside, across = add_corners(fc2_sums[1], fc2_sums[2], *moved)
-    moved = [grid.over_x(beside), grid.over_y(across)]
-    fc1_sums = weight_grad(
-        spot, (normed_two, normed_two_there), (own_hidden, hidden_there), depth, waits=[beside]
-    )
-    normed_there = grid.over_core(normed)
-    by_class = [up_weights[i] for i in classes[0] + classes[1]]
-    grad_resid, resid_low, sums_two = norm_back(
-        "norm_two_back",
-        spot,
-        [other_hidden, own_hidden],
-        resid,
-        grad_low,
-        gain_two,
-        by_class,
-        True,
-        [fc1_sums[0], normed_there],
-    )
-    *moved, resid_low, corner_a, corner_b = fence(moved + [resid_low, *fc1_sums[3:]])
-    fc2_piece = grid.scatter_depth(add_square(fc2_sums[0], *moved))
-    moved = [grid.over_x(corner_a), grid.over_y(corner_b)]
     resid_there = grid.over_core(resid_low)
 
     def heads_back(qkv, probs, side, waits):
@@ -1719,17 +1783,21 @@
         )
 
     far_other, far_own, far_sums = heads_back(second_qkv, second_probs, 1, [])
-    *moved, far_other = fence(moved + [far_other])
+    *fc2_second, far_other, hidden_there, resid_there = fence(
+        fc2_second + [far_other, hidden_there, resid_there]
+    )
     far_there = grid.over_core(far_other)
-    beside, across = add_corners(fc1_sums[1], fc1_sums[2], *moved)
-    moved = [grid.over_x(beside), grid.over_y(across)]
-    far_mixed = grid.over_core(mixed[3])
-    near_other, near_own, near_sums_qkv = heads_back(first_qkv, first_probs, 0, [beside])
-    near_other, far_there, far_mixed, resid_there, fc2_piece = fence(
-        [near_other, far_there, far_mixed, resid_there, fc2_piece]
-    )
+    fc2_total = join(fc2_near, fc2_moved[2:], fc2_second)
+    fc1_sums = weight_grad(
+        spot, (normed_two, normed_two_there), (own_hidden, hidden_there), depth, waits=[fc2_total]
+    )
+    far_there, fc2_total, fc1_near = fence([far_there, fc2_total, fc1_sums[0]])
+    fc2_piece = grid.scatter_depth(fc2_total)
+    fc1_moved = move_first(fc1_sums)
+    near_other, near_own, near_sums_qkv = heads_back(first_qkv, first_probs, 0, [fc1_near])
+    near_other, *fc1_moved = fence([near_other] + fc1_moved)
+    fc1_second = move_second(fc1_sums, *fc1_moved[:2])
     near_there = grid.over_core(near_other)
-    near_mixed = grid.over_core(mixed[1])
 
     def attn_grad(side, own_part, there_part, own_mixed, there_mixed, waits):
         return weight_grad(
@@ -1742,29 +1810,41 @@
             waits,
         )
 
-    far_across, corner_a, corner_b = attn_grad(1, far_own, far_there, mixed[2], far_mixed, [])
-    *moved, corner_a, corner_b = fence(moved + [corner_a, corner_b])
-    fc1_piece = grid.scatter_depth(add_square(fc1_sums[0], *moved))
-    moved = [grid.over_x(corner_a), grid.over_y(corner_b)]
-    near_sums, beside = attn_grad(0, near_own, near_there, mixed[0], near_mixed, [far_across])
-    *moved, beside = fence(moved + [beside])
-    beside, across = add_corners(beside, far_across, *moved)
-    moved = [grid.over_x(beside), grid.over_y(across)]
+    across_lo, across_hi, corner_lo, corner_hi = attn_grad(
+        2, far_own, far_there, mixed[2], far_mixed, [near_other]
+    )
+    across_lo, across_hi, corner_lo, corner_hi, near_there = fence(
+        [across_lo, across_hi, corner_lo, corner_hi, near_there]
+    )
+    corners = [grid.over_x(corner_lo), grid.over_y(corner_hi)]
+    attn_first = grid.over_y(across_hi)
+    near_sums, beside_lo, beside_hi = attn_grad(
+        0, near_own, near_there, mixed[0], near_mixed, [across_lo]
+    )
+    *fc1_second, beside_lo, beside_hi, fc2_piece = fence(
+        fc1_second + [beside_lo, beside_hi, fc2_piece]
+    )
+    beside_first = grid.over_x(beside_lo)
+    fc1_total = join(fc1_near, fc1_moved[2:], fc1_second)
     by_class = [down_weights[i] for i in classes[0] + classes[1]]
     layer_rows = down_project(
-        spot, other_active, own_active, resid, fc2_shift, by_class, [beside]
-    )
+        spot, other_active, own_active, resid, fc2_shift, by_class, [fc1_total]
+    )
+    *corners, attn_first, beside_first, fc1_total = fence(
+        corners + [attn_first, beside_first, fc1_total], [layer_rows]
+    )
+    fc1_piece = grid.scatter_depth(fc1_total)
+    beside_hi, across_lo = add_pairs(beside_hi, corners[1], across_lo, corners[0])
+    moved = [grid.over_x(beside_hi), grid.over_y(across_lo)]
     by_class = [attn_weights[i] for i in (1, 3, 0, 2)]
     input_grad, sums_one = norm_back(
-        "norm_one_back",
         spot,
         [near_other, far_other, near_own, far_own],
         input_rows,
-        grad_resid,
+        resid_low,
         gain_one,
         by_class,
-        False,
-        [layer_rows],
+        [beside_hi],
     )
 
     def column_sum(values):
@@ -1785,9 +1865,7 @@
         for at in (0, 2 * quarter)
         for half_at in range(2)
     ]
-    fc1_totals = absolute(
-        other_fc1_sums[0], own_fc1_sums[0], other_fc1_sums[1], own_fc1_sums[1]
-    )
+    fc1_totals = absolute(*[fc1_bias_sums[i] for i in (2, 0, 3, 1)])
     fc1_rows = []
     for side in range(2):
         fc1_rows += [fc1_totals[0][side][0], fc1_totals[1][side][0, : ff_width - group_width]]
@@ -1807,7 +1885,7 @@
     lines = -(-length // 1024) * 8
     flat = jnp.pad(flat, (0, lines * 128 - length)).reshape(lines, 128)
     *moved, flat, fc1_piece = fence(moved + [flat, fc1_piece])
-    total = add_square(near_sums, *moved)
+    total = join(near_sums, [beside_first, attn_first], moved)
     attn_piece = grid.scatter_depth(total)
     (flat, fc1_piece, fc2_piece) = fence([flat, fc1_piece, fc2_piece], [total])
     flat = flat + grid.over_core(flat)

time: 494 us -> 478 us (0.968)
  waiting for transfers between devices: 84.8 us -> 69.6 us
  Pallas kernels: 264 us -> 251 us
  starting transfers between devices: 47.6 us -> 55.2 us
  local copies, waits for them, and re-layouts: 35.9 us -> 40.9 us
    ppermute x68 -> x69, waiting for transfers between devices: 84.1 us -> 49.6 us  [move(): return lax.ppermute(values, AXES, pairs)]
    all_gather x3, waiting for transfers between devices: 0.14 us -> 15.2 us  [gather_depth(): return lax.all_gather(block, 'dp', axis_index_groups=self.depth_groups())]
    pallas_call x16 -> x14, Pallas kernels: 238 us -> 227 us  [call(): pl.pallas_call(kernel, in_specs=list(specs) + [any_spec()] * len(waits),...]
    ppermute x68 -> x69, starting transfers between devices: 47 us -> 54 us  [move(): return lax.ppermute(values, AXES, pairs)]
    unnamed x92 -> x122, local copies, waits for them, and re-layouts: 10.5 us -> 17 us
  transfers between devices with their start and end apart: 74 -> 75, of which waited for: 28 -> 23; matrix products, arithmetic and copies ran while one was open for 10% -> 10% of each run, Pallas kernels for 51% -> 53%
where the time goes in v4:
time: 478 us; the launch traced here: 470 us
  Pallas kernels  251 us (53%)
  waiting for transfers between devices  69.6 us (15%)
  starting transfers between devices  55.2 us (12%)
  local copies, waits for them, and re-layouts  40.9 us (9%)
  other arithmetic  31.1 us (7%)
  between operations  22.3 us (5%)
    pallas_call x14, Pallas kernels, call(): pl.pallas_call(kernel, in_specs=list(specs) + [any_spec()] * len(waits),...  227 us
    ppermute x69, starting transfers between devices, move(): return lax.ppermute(values, AXES, pairs)  54 us
    ppermute x69, waiting for transfers between devices, move(): return lax.ppermute(values, AXES, pairs)  49.6 us
    unnamed x122, local copies, waits for them, and re-layouts  17 us
    all_gather x3, waiting for transfers between devices, gather_depth(): return lax.all_gather(block, 'dp', axis_index_groups=self.depth_groups())  15.2 us
    pallas_call x3, Pallas kernels, add_square(): pl.pallas_call(square_kernel, in_specs=[vmem_spec()] * 5, out_specs=vmem_...  11 us
  transfers between devices with their start and end apart: 75, of which 23 were waited for; matrix products, arithmetic and copies ran while one was open for 10% of the time, Pallas kernels for 53%

profile of v4, /device:TPU:0, one launch (start us, length us, event | category | flops | bytes accessed | tf_op | source)
XLA Modules:
  0.0 470.5 jit_solution(9916059848718729454)
XLA Ops:
  36.1 3.9 collective-permute-done.3
  43.1 3.1 collective-permute-done.4
  47.9 5.9 %collective-permute-done.5 = bf16[4,2,2,6,72]{4,3,2,1,0:T(8,128)(2,1)S(1)} collective-permute-done((bf16[4,2,2,6,72]{4,3,2,1,0:T(8,128)(2,1)S(1)}, bf16[4,2,2,6,72]{4,3,2,1,0:T(8,128)(2,1)S(1)}, u32[]{:S(2)}, u32[]{:S(2)}) %collective-permute-start.5) | collective-permute-done | bytes 13856 | tf_op jit(solution)/shard_map/ppermute | solution.py:1458
  65.6 2.9 select_select_fusion
  76.7 15.1 %all-gather.7.cloned.1.call-done = bf16[576,1152]{1,0:T(8,128)(2,1)} async-done(((bf16[144,1152]{1,0:T(8,128)(2,1)}), bf16[576,1152]{1,0:T(8,128)(2,1)}) %all-gather.7.cloned.1.call-update) | async-done | bytes 1327120 | tf_op jit(solution)/shard_map/all_gather | solution.py:1494
  101.3 17.2 %heads_forward.2 = (bf16[2,768,896]{2,1,0:T(8,128)(2,1)}, bf16[2,4,768,768]{3,2,1,0:T(8,128)(2,1)}, bf16[768,384]{1,0:T(8,128)(2,1)}, bf16[768,384]{1,0:T(8,128)(2,1)}) custom-call(s32[1]{0:T(128)} %bitcast.4.spot, s32[768,1]{1,0:T(8,128)} %get-tuple-element.169.kind_ref, bf16[768,1152]{1,0:T(8,128)(2,1)} %get-tuple-element.170.x_any.refs_0_, ...), custom_call_target="tpu_custom_call" | custom-call | flops 1024 | bytes 1024 | tf_op jit(solution)/shard_map/heads_forward/pallas_call | solution.py:739
  123.0 17.1 %heads_forward.3 = (bf16[2,768,896]{2,1,0:T(8,128)(2,1)}, bf16[2,4,768,768]{3,2,1,0:T(8,128)(2,1)}, bf16[768,384]{1,0:T(8,128)(2,1)}, bf16[768,384]{1,0:T(8,128)(2,1)}) custom-call(s32[1]{0:T(128)} %bitcast.4.spot, s32[768,1]{1,0:T(8,128)} %get-tuple-element.169.kind_ref, bf16[768,1152]{1,0:T(8,128)(2,1)} %get-tuple-element.170.x_any.refs_0_, ...), custom_call_target="tpu_custom_call" | custom-call | flops 1024 | bytes 1024 | tf_op jit(solution)/shard_map/heads_forward/pallas_call | solution.py:739
  140.1 3.3 collective-permute-done.15.refs_0_
  149.0 9.7 %attn_out.1 = (bf16[768,1152]{1,0:T(8,128)(2,1)}, bf16[768,1152]{1,0:T(8,128)(2,1)}) custom-call(s32[1]{0:T(128)} %bitcast.4.spot, bf16[768,384]{1,0:T(8,128)(2,1)} %get-tuple-element.186.one.refs_1_.refs_5_, bf16[768,384]{1,0:T(8,128)(2,1)} %get-tuple-element.187.two.refs_0_, bf16[768,384]{1,0:T(8,128)(2,1)} %get-tuple-element.188.three.refs_1_.refs_5_, ...), custom_call_target="tpu_custom_call" | custom-call | flops 1024 | bytes 1024 | tf_op jit(solution)/shard_map/attn_out/pallas_call | solution.py:739
  158.7 4.8 %collective-permute-done.25.refs_0_ = bf16[2,144,1152]{2,1,0:T(8,128)(2,1)} collective-permute-done((bf16[2,144,1152]{2,1,0:T(8,128)(2,1)}, bf16[2,144,1152]{2,1,0:T(8,128)(2,1)}, u32[]{:S(2)}, u32[]{:S(2)}) %collective-permute-start.25) | collective-permute-done | bytes 663584 | tf_op jit(solution)/shard_map/ppermute | solution.py:1458
  168.0 11.3 %mlp_up.2 = (bf16[2,768,1152]{2,1,0:T(8,128)(2,1)}, bf16[2,768,1152]{2,1,0:T(8,128)(2,1)}) custom-call(s32[1]{0:T(128)} %bitcast.4.spot, bf16[768,1152]{1,0:T(8,128)(2,1)} %get-tuple-element.191.x_any.refs_0_, f32[2,1,1152]{2,1,0:T(1,128)} %get-tuple-element.192.bias_ref, bf16[4,144,1152]{2,1,0:T(8,128)(2,1)} %collective-permute-done.22.refs_4_.refs_0_.refs_13_, ...), custom_call_target="tpu_custom_call" | custom-call | flops 1024 | bytes 1024 | tf_op jit(solution)/shard_map/mlp_up/pallas_call | solution.py:739
  181.4 11.3 %mlp_up.3 = (bf16[2,768,1152]{2,1,0:T(8,128)(2,1)}, bf16[2,768,1152]{2,1,0:T(8,128)(2,1)}) custom-call(s32[1]{0:T(128)} %bitcast.4.spot, bf16[768,1152]{1,0:T(8,128)(2,1)} %get-tuple-element.191.x_any.refs_0_, f32[2,1,1152]{2,1,0:T(1,128)} %get-tuple-element.196.bias_ref, bf16[4,144,1152]{2,1,0:T(8,128)(2,1)} %get-tuple-element.168.refs_0_.refs_8_, ...), custom_call_target="tpu_custom_call" | custom-call | flops 1024 | bytes 1024 | tf_op jit(solution)/shard_map/mlp_up/pallas_call | solution.py:739
  194.0 14.8 %weight_grad.4 = (bf16[4,144,1152]{2,1,0:T(8,128)(2,1)}, bf16[2,144,1152]{2,1,0:T(8,128)(2,1)}, bf16[2,144,1152]{2,1,0:T(8,128)(2,1)}, bf16[2,144,1152]{2,1,0:T(...) custom-call(s32[1]{0:T(128)} %bitcast.4.spot, ...), custom_call_target="tpu_custom_call" | custom-call | flops 1024 | bytes 1024 | tf_op jit(solution)/shard_map/weight_grad/pallas_call | solution.py:739
  213.6 4.4 collective-permute-done.36.refs_4_.refs_5_.refs_6_.refs_7_.refs_0_.refs_1_.refs_2_.refs_3_
  218.1 33.1 %mlp_back.1 = (bf16[2,768,1152]{2,1,0:T(8,128)(2,1)}, bf16[2,768,1152]{2,1,0:T(8,128)(2,1)}, bf16[768,1152]{1,0:T(8,128)(2,1)}, f32[8,1152]{1,0:T(8,128)}, f32[4,1,1152]{2,1,0:T(1,128)}) custom-call(s32[1]{0:T(128)} %bitcast.4.spot, bf16[768,1152]{1,0:T(8,128)(2,1)} %copy-done.4, bf16[2,768,1152]{2,1,0:T(8,128)(2,1)} %get-tuple-element.206.one_any, ...), custom_call_target="tpu_custom_call" | custom-call | flops 1024 | bytes 1024 | tf_op jit(solution)/shard_map/mlp_back/pallas_call | solution.py:739
  253.2 2.9 add_pairs.3
  259.0 21.2 %heads_backward.2 = (bf16[768,896]{1,0:T(8,128)(2,1)}, bf16[768,896]{1,0:T(8,128)(2,1)}, f32[2,1,896]{2,1,0:T(1,128)}) custom-call(s32[1]{0:T(128)} %bitcast.4.spot, bf16[768,1152]{1,0:T(8,128)(2,1)} %get-tuple-element.220.grad_any.refs_4_.refs_5_, bf16[2,768,896]{2,1,0:T(8,128)(2,1)} %get-tuple-element.221.qkv_any, ...), custom_call_target="tpu_custom_call" | custom-call | flops 1024 | bytes 1024 | tf_op jit(solution)/shard_map/heads_backward/pallas_call | solution.py:739
  281.9 3.7 add_square.3.refs_4_.refs_1_
  285.5 14.8 %weight_grad.5 = (bf16[4,144,1152]{2,1,0:T(8,128)(2,1)}, bf16[2,144,1152]{2,1,0:T(8,128)(2,1)}, bf16[2,144,1152]{2,1,0:T(8,128)(2,1)}, bf16[2,144,1152]{2,1,0:T(...) custom-call(s32[1]{0:T(128)} %bitcast.4.spot, ...), custom_call_target="tpu_custom_call" | custom-call | flops 1024 | bytes 1024 | tf_op jit(solution)/shard_map/weight_grad/pallas_call | solution.py:739
  306.1 20.9 %heads_backward.3 = (bf16[768,896]{1,0:T(8,128)(2,1)}, bf16[768,896]{1,0:T(8,128)(2,1)}, f32[2,1,896]{2,1,0:T(1,128)}) custom-call(s32[1]{0:T(128)} %bitcast.4.spot, bf16[768,1152]{1,0:T(8,128)(2,1)} %get-tuple-element.220.grad_any.refs_4_.refs_5_, bf16[2,768,896]{2,1,0:T(8,128)(2,1)} %get-tuple-element.235.qkv_any, ...), custom_call_target="tpu_custom_call" | custom-call | flops 1024 | bytes 1024 | tf_op jit(solution)/shard_map/heads_backward/pallas_call | solution.py:739
  327.1 6.7 %collective-permute-done.48.refs_3_ = bf16[2,144,1152]{2,1,0:T(8,128)(2,1)S(1)} collective-permute-done((bf16[2,144,1152]{2,1,0:T(8,128)(2,1)}, bf16[2,144,1152]{2,1,0:T(8,128)(2,1)S(1)}, u32[]{:S(2)}, u32[]{:S(2)}) %collective-permute-start.48) | collective-permute-done | bytes 663584 | tf_op jit(solution)/shard_map/ppermute | solution.py:1458
  334.9 2.9 add_pairs.4
  339.9 10.9 %weight_grad.6 = (bf16[2,144,1152]{2,1,0:T(8,128)(2,1)}, bf16[2,144,1152]{2,1,0:T(8,128)(2,1)}, bf16[2,144,1152]{2,1,0:T(8,128)(2,1)}, bf16[2,144,1152]{2,1,0:T(8,128)(2,1)}) custom-call(s32[1]{0:T(128)} %bitcast.4.spot, bf16[768,1152]{1,0:T(8,128)(2,1)} %get-tuple-element.170.x_any.refs_0_, bf16[1,768,896]{2,1,0:T(8,128)(2,1)} %bitcast.115, ...), custom_call_target="tpu_custom_call" | custom-call | flops 1024 | bytes 1024 | tf_op jit(solution)/shard_map/weight_grad/pallas_call | solution.py:739
  354.5 11.2 %weight_grad.7 = (bf16[4,144,1152]{2,1,0:T(8,128)(2,1)}, bf16[2,144,1152]{2,1,0:T(8,128)(2,1)}, bf16[2,144,1152]{2,1,0:T(8,128)(2,1)}) custom-call(s32[1]{0:T(128)} %bitcast.4.spot, bf16[768,1152]{1,0:T(8,128)(2,1)} %get-tuple-element.170.x_any.refs_0_, bf16[1,768,896]{2,1,0:T(8,128)(2,1)} %bitcast.116, bf16[768,1152]{1,0:T(8,128)(2,1)} %get-tuple-element.250.refs_2_, ...), custom_call_target="tpu_custom_call" | custom-call | flops 1024 | bytes 1024 | tf_op jit(solution)/shard_map/weight_grad/pallas_call | solution.py:739
  367.3 3.7 add_square.4.refs_8_.refs_4_
  371.0 16.3 %mlp_down.1.refs_5_ = bf16[768,1152]{1,0:T(8,128)(2,1)} custom-call(s32[1]{0:T(128)} %bitcast.4.spot, bf16[2,768,1152]{2,1,0:T(8,128)(2,1)} %fence.31.refs_5_.later_any, bf16[2,768,1152]{2,1,0:T(8,128)(2,1)} %get-tuple-element.198.refs_1_.early_any, bf16[768,1152]{1,0:T(8,128)(2,1)} %get-tuple-element.199.resid_any, f32[1,1152]{1,0:T(1,128)} %get-tuple-element.358.shift_ref, ...), custom_call_target="tpu_custom_call" | custom-call | flops 1024 | bytes 1024 | tf_op jit(solution)/shard_map/mlp_down/pallas_call | solution.py:739
  391.7 3.1 add_pairs.5
  397.4 16.9 %norm_one_back.1 = (f32[768,1152]{1,0:T(8,128)}, f32[8,1152]{1,0:T(8,128)}) custom-call(s32[1]{0:T(128)} %bitcast.4.spot, bf16[768,896]{1,0:T(8,128)(2,1)} %get-tuple-element.255.refs_8_.refs_0_, bf16[768,896]{1,0:T(8,128)(2,1)} %get-tuple-element.225.refs_1_, bf16[768,896]{1,0:T(8,128)(2,1)} %get-tuple-element.249.refs_2_, ...), custom_call_target="tpu_custom_call" | custom-call | flops 1024 | bytes 1024 | tf_op jit(solution)/shard_map/norm_one_back/pallas_call | solution.py:739
  418.5 3.7 add_square.5.refs_2_.refs_3_
  437.4 4.7 %collective-permute-done.64 = f32[112,128]{1,0:T(8,128)S(1)} collective-permute-done((f32[112,128]{1,0:T(8,128)S(1)}, f32[112,128]{1,0:T(8,128)S(1)}, u32[]{:S(2)}, u32[]{:S(2)}) %collective-permute-start.64) | collective-permute-done | bytes 57376 | tf_op jit(solution)/shard_map/ppermute | solution.py:1458
  442.2 4.0 slice_select_fusion
  446.3 4.5 collective-permute-done.65
  (420 shorter events, 138.0 us)
Async XLA Ops:
  7.2 51.0 %all-gather.9.cloned.1.call-start = ((), (), s32[]{:S(2)}) async-start(), calls=%async_computation.7 | async-start | bytes 1658880 | tf_op jit(solution)/shard_map/all_gather | solution.py:1494
  19.6 72.3 %all-gather.7.cloned.1.call-start = ((), (), s32[]{:S(2)}) async-start(), calls=%async_computation.6 | async-start | bytes 1658880 | tf_op jit(solution)/shard_map/all_gather | solution.py:1494
  19.9 38.2 %collective-permute-start.10 = (bf16[144,1152]{1,0:T(8,128)(2,1)S(1)}, bf16[144,1152]{1,0:T(8,128)(2,1)S(1)}, u32[]{:S(2)}, u32[]{:S(2)}) collective-permute-start(bf16[144,1152]{1,0:T(8,128)(2,1)S(1)} %pad_maximum_fusion.4.refs_4_), channel_id=1, source_target_pairs={{0,1},{1,0},{2,3},{3,2},{4,5},{5,4},{6,7},{7,6},{8,9},{9,8},{10,11... | collective-permute-start | bytes 995336 | tf_op jit(solution)/shard_map/ppermute | solution.py:1458
  22.5 35.6 %collective-permute-start.11 = (bf16[144,1152]{1,0:T(8,128)(2,1)S(1)}, bf16[144,1152]{1,0:T(8,128)(2,1)S(1)}, u32[]{:S(2)}, u32[]{:S(2)}) collective-permute-start(bf16[144,1152]{1,0:T(8,128)(2,1)S(1)} %pad_maximum_fusion.4.refs_4_), channel_id=1, source_target_pairs={{0,5},{1,4},{2,7},{3,6},{4,1},{5,0},{6,3},{7,2},{8,13},{9,12},{10,... | collective-permute-start | bytes 995336 | tf_op jit(solution)/shard_map/ppermute | solution.py:1458
  23.9 34.2 %collective-permute-start.9 = (bf16[144,1152]{1,0:T(8,128)(2,1)S(1)}, bf16[144,1152]{1,0:T(8,128)(2,1)S(1)}, u32[]{:S(2)}, u32[]{:S(2)}) collective-permute-start(bf16[144,1152]{1,0:T(8,128)(2,1)S(1)} %pad_maximum_fusion.4.refs_4_), channel_id=1, source_target_pairs={{0,4},{1,5},{2,6},{3,7},{4,0},{5,1},{6,2},{7,3},{8,12},{9,13},{10,... | collective-permute-start | bytes 995336 | tf_op jit(solution)/shard_map/ppermute | solution.py:1458
  24.0 34.1 %collective-permute-start.7 = (bf16[26,128]{1,0:T(8,128)(2,1)}, bf16[26,128]{1,0:T(8,128)(2,1)S(1)}, u32[]{:S(2)}, u32[]{:S(2)}) collective-permute-start(bf16[26,128]{1,0:T(8,128)(2,1)} %fence.25), channel_id=1, source_target_pairs={{0,1},{1,0},{2,3},{3,2},{4,5},{5,4},{6,7},{7,6},{8,9},{9,8},{10,11... | collective-permute-start | bytes 19976 | tf_op jit(solution)/shard_map/ppermute | solution.py:1458
  58.0 150.8 %all-gather.11.cloned.1.call-start = ((), (), s32[]{:S(2)}) async-start(), calls=%async_computation.8 | async-start | bytes 6635520 | tf_op jit(solution)/shard_map/all_gather | solution.py:1494
  60.4 31.4 %collective-permute-start.12 = (bf16[4,144,1152]{2,1,0:T(8,128)(2,1)}, bf16[4,144,1152]{2,1,0:T(8,128)(2,1)S(1)}, u32[]{:S(2)}, u32[]{:S(2)}) collective-permute-start(bf16[4,144,1152]{2,1,0:T(8,128)(2,1)} %get-tuple-element.158.refs_0_.refs_4_.refs_12_), channel_id=1, source_target_pairs={{0,4},{1,5},{2,6},{3,7},{4,0},{5,1},{6,2},{7,3},{8,12},{9,13},{10,... | collective-permute-start | bytes 3981320 | tf_op jit(solution)/shard_map/ppermute | solution.py:1458
  62.3 29.6 %collective-permute-start.13 = (bf16[4,144,1152]{2,1,0:T(8,128)(2,1)}, bf16[4,144,1152]{2,1,0:T(8,128)(2,1)}, u32[]{:S(2)}, u32[]{:S(2)}) collective-permute-start(bf16[4,144,1152]{2,1,0:T(8,128)(2,1)} %get-tuple-element.158.refs_0_.refs_4_.refs_12_), channel_id=1, source_target_pairs={{0,1},{1,0},{2,3},{3,2},{4,5},{5,4},{6,7},{7,6},{8,9},{9,8},{10,11... | collective-permute-start | bytes 3981320 | tf_op jit(solution)/shard_map/ppermute | solution.py:1458
  64.0 33.7 %collective-permute-start.20 = (bf16[4,144,1152]{2,1,0:T(8,128)(2,1)}, bf16[4,144,1152]{2,1,0:T(8,128)(2,1)}, u32[]{:S(2)}, u32[]{:S(2)}) collective-permute-start(bf16[4,144,1152]{2,1,0:T(8,128)(2,1)} %get-tuple-element.158.refs_0_.refs_4_.refs_12_), channel_id=1, source_target_pairs={{0,2},{1,3},{2,0},{3,1},{4,6},{5,7},{6,4},{7,5},{8,10},{9,11},{10,... | collective-permute-start | bytes 3981320 | tf_op jit(solution)/shard_map/ppermute | solution.py:1458
  93.5 272.3 %reduce-scatter.4.cloned.1.call-start = ((), (), s32[]{:S(2)}) async-start(), calls=%async_computation.3 | async-start | bytes 1658880 | tf_op jit(solution)/shard_map/reduce_scatter | solution.py:1497
  93.7 24.8 %collective-permute-start.19 = (bf16[4,144,1152]{2,1,0:T(8,128)(2,1)}, bf16[4,144,1152]{2,1,0:T(8,128)(2,1)S(1)}, u32[]{:S(2)}, u32[]{:S(2)}) collective-permute-start(bf16[4,144,1152]{2,1,0:T(8,128)(2,1)} %get-tuple-element.172.second_ref.refs_0_.refs_4_.refs_5_.refs_14_), channel_id=1, source_target_pairs={{0,2},{1,3},{2,0},{3,1},{4,6},{5,7},{6,4},{7,5},{8,10},{9,11},{10,... | collective-permute-start | bytes 3981320 | tf_op jit(solution)/shard_map/ppermute | solution.py:1458
  99.1 44.3 %collective-permute-start.15 = (bf16[4,144,1152]{2,1,0:T(8,128)(2,1)}, bf16[4,144,1152]{2,1,0:T(8,128)(2,1)}, u32[]{:S(2)}, u32[]{:S(2)}) collective-permute-start(bf16[4,144,1152]{2,1,0:T(8,128)(2,1)} %get-tuple-element.168.refs_0_.refs_8_), channel_id=1, source_target_pairs={{0,4},{1,5},{2,6},{3,7},{4,0},{5,1},{6,2},{7,3},{8,12},{9,13},{10,... | collective-permute-start | bytes 3981320 | tf_op jit(solution)/shard_map/ppermute | solution.py:1458
  99.8 43.7 %collective-permute-start.16 = (bf16[4,144,1152]{2,1,0:T(8,128)(2,1)}, bf16[4,144,1152]{2,1,0:T(8,128)(2,1)}, u32[]{:S(2)}, u32[]{:S(2)}) collective-permute-start(bf16[4,144,1152]{2,1,0:T(8,128)(2,1)} %get-tuple-element.168.refs_0_.refs_8_), channel_id=1, source_target_pairs={{0,1},{1,0},{2,3},{3,2},{4,5},{5,4},{6,7},{7,6},{8,9},{9,8},{10,11... | collective-permute-start | bytes 3981320 | tf_op jit(solution)/shard_map/ppermute | solution.py:1458
  121.1 37.7 %collective-permute-start.29 = (bf16[768,1152]{1,0:T(8,128)(2,1)S(1)}, bf16[768,1152]{1,0:T(8,128)(2,1)S(1)}, u32[]{:S(2)}, u32[]{:S(2)}) collective-permute-start(bf16[768,1152]{1,0:T(8,128)(2,1)S(1)} %copy-done.1), channel_id=1, source_target_pairs={{0,2},{1,3},{2,0},{3,1},{4,6},{5,7},{6,4},{7,5},{8,10},{9,11},{10,... | collective-permute-start | bytes 5308424 | tf_op jit(solution)/shard_map/ppermute | solution.py:1458
  209.3 41.8 %collective-permute-start.37 = (bf16[2,144,1152]{2,1,0:T(8,128)(2,1)}, bf16[2,144,1152]{2,1,0:T(8,128)(2,1)S(1)}, u32[]{:S(2)}, u32[]{:S(2)}) collective-permute-start(bf16[2,144,1152]{2,1,0:T(8,128)(2,1)} %get-tuple-element.211), channel_id=1, source_target_pairs={{0,4},{1,5},{2,6},{3,7},{4,0},{5,1},{6,2},{7,3},{8,12},{9,13},{10,... | collective-permute-start | bytes 1990664 | tf_op jit(solution)/shard_map/ppermute | solution.py:1458
  211.0 40.1 %collective-permute-start.38 = (bf16[2,144,1152]{2,1,0:T(8,128)(2,1)}, bf16[2,144,1152]{2,1,0:T(8,128)(2,1)S(1)}, u32[]{:S(2)}, u32[]{:S(2)}) collective-permute-start(bf16[2,144,1152]{2,1,0:T(8,128)(2,1)} %get-tuple-element.212), channel_id=1, source_target_pairs={{0,1},{1,0},{2,3},{3,2},{4,5},{5,4},{6,7},{7,6},{8,9},{9,8},{10,11... | collective-permute-start | bytes 1990664 | tf_op jit(solution)/shard_map/ppermute | solution.py:1458
  212.5 38.7 %collective-permute-start.39 = (bf16[2,144,1152]{2,1,0:T(8,128)(2,1)}, bf16[2,144,1152]{2,1,0:T(8,128)(2,1)S(1)}, u32[]{:S(2)}, u32[]{:S(2)}) collective-permute-start(bf16[2,144,1152]{2,1,0:T(8,128)(2,1)} %get-tuple-element.213), channel_id=1, source_target_pairs={{0,4},{1,5},{2,6},{3,7},{4,0},{5,1},{6,2},{7,3},{8,12},{9,13},{10,... | collective-permute-start | bytes 1990664 | tf_op jit(solution)/shard_map/ppermute | solution.py:1458
  213.1 38.1 %collective-permute-start.40 = (bf16[2,144,1152]{2,1,0:T(8,128)(2,1)}, bf16[2,144,1152]{2,1,0:T(8,128)(2,1)S(1)}, u32[]{:S(2)}, u32[]{:S(2)}) collective-permute-start(bf16[2,144,1152]{2,1,0:T(8,128)(2,1)} %get-tuple-element.214), channel_id=1, source_target_pairs={{0,1},{1,0},{2,3},{3,2},{4,5},{5,4},{6,7},{7,6},{8,9},{9,8},{10,11... | collective-permute-start | bytes 1990664 | tf_op jit(solution)/shard_map/ppermute | solution.py:1458
  252.6 27.6 %collective-permute-start.43 = (bf16[2,768,1152]{2,1,0:T(8,128)(2,1)}, bf16[2,768,1152]{2,1,0:T(8,128)(2,1)}, u32[]{:S(2)}, u32[]{:S(2)}) collective-permute-start(bf16[2,768,1152]{2,1,0:T(8,128)(2,1)} %get-tuple-element.224), channel_id=1, source_target_pairs={{0,2},{1,3},{2,0},{3,1},{4,6},{5,7},{6,4},{7,5},{8,10},{9,11},{10,... | collective-permute-start | bytes 10616840 | tf_op jit(solution)/shard_map/ppermute | solution.py:1458
  253.0 27.2 %collective-permute-start.44 = (bf16[768,1152]{1,0:T(8,128)(2,1)}, bf16[768,1152]{1,0:T(8,128)(2,1)S(1)}, u32[]{:S(2)}, u32[]{:S(2)}) collective-permute-start(bf16[768,1152]{1,0:T(8,128)(2,1)} %get-tuple-element.220.grad_any.refs_4_.refs_5_), channel_id=1, source_target_pairs={{0,2},{1,3},{2,0},{3,1},{4,6},{5,7},{6,4},{7,5},{8,10},{9,11},{10,... | collective-permute-start | bytes 5308424 | tf_op jit(solution)/shard_map/ppermute | solution.py:1458
  301.6 117.0 %reduce-scatter.6.cloned.1.call-start = ((), (), s32[]{:S(2)}) async-start(), calls=%async_computation.4 | async-start | bytes 1658880 | tf_op jit(solution)/shard_map/reduce_scatter | solution.py:1497
  302.0 25.1 %collective-permute-start.46 = (bf16[2,144,1152]{2,1,0:T(8,128)(2,1)}, bf16[2,144,1152]{2,1,0:T(8,128)(2,1)S(1)}, u32[]{:S(2)}, u32[]{:S(2)}) collective-permute-start(bf16[2,144,1152]{2,1,0:T(8,128)(2,1)} %get-tuple-element.238), channel_id=1, source_target_pairs={{0,4},{1,5},{2,6},{3,7},{4,0},{5,1},{6,2},{7,3},{8,12},{9,13},{10,... | collective-permute-start | bytes 1990664 | tf_op jit(solution)/shard_map/ppermute | solution.py:1458
  303.2 30.7 %collective-permute-start.48 = (bf16[2,144,1152]{2,1,0:T(8,128)(2,1)}, bf16[2,144,1152]{2,1,0:T(8,128)(2,1)S(1)}, u32[]{:S(2)}, u32[]{:S(2)}) collective-permute-start(bf16[2,144,1152]{2,1,0:T(8,128)(2,1)} %get-tuple-element.240), channel_id=1, source_target_pairs={{0,4},{1,5},{2,6},{3,7},{4,0},{5,1},{6,2},{7,3},{8,12},{9,13},{10,... | collective-permute-start | bytes 1990664 | tf_op jit(solution)/shard_map/ppermute | solution.py:1458
  304.7 29.4 %collective-permute-start.49 = (bf16[2,144,1152]{2,1,0:T(8,128)(2,1)S(1)}, bf16[2,144,1152]{2,1,0:T(8,128)(2,1)S(1)}, u32[]{:S(2)}, u32[]{:S(2)}) collective-permute-start(bf16[2,144,1152]{2,1,0:T(8,128)(2,1)S(1)} %copy-done.60), channel_id=1, source_target_pairs={{0,1},{1,0},{2,3},{3,2},{4,5},{5,4},{6,7},{7,6},{8,9},{9,8},{10,11... | collective-permute-start | bytes 1990664 | tf_op jit(solution)/shard_map/ppermute | solution.py:1458
  337.9 27.8 %collective-permute-start.50 = (bf16[2,144,1152]{2,1,0:T(8,128)(2,1)}, bf16[2,144,1152]{2,1,0:T(8,128)(2,1)}, u32[]{:S(2)}, u32[]{:S(2)}) collective-permute-start(bf16[2,144,1152]{2,1,0:T(8,128)(2,1)} %get-tuple-element.247), channel_id=1, source_target_pairs={{0,4},{1,5},{2,6},{3,7},{4,0},{5,1},{6,2},{7,3},{8,12},{9,13},{10,... | collective-permute-start | bytes 1990664 | tf_op jit(solution)/shard_map/ppermute | solution.py:1458
  339.3 26.4 %collective-permute-start.51 = (bf16[2,144,1152]{2,1,0:T(8,128)(2,1)}, bf16[2,144,1152]{2,1,0:T(8,128)(2,1)}, u32[]{:S(2)}, u32[]{:S(2)}) collective-permute-start(bf16[2,144,1152]{2,1,0:T(8,128)(2,1)} %get-tuple-element.248), channel_id=1, source_target_pairs={{0,1},{1,0},{2,3},{3,2},{4,5},{5,4},{6,7},{7,6},{8,9},{9,8},{10,11... | collective-permute-start | bytes 1990664 | tf_op jit(solution)/shard_map/ppermute | solution.py:1458
  351.9 35.4 %collective-permute-start.53 = (bf16[2,144,1152]{2,1,0:T(8,128)(2,1)}, bf16[2,144,1152]{2,1,0:T(8,128)(2,1)S(1)}, u32[]{:S(2)}, u32[]{:S(2)}) collective-permute-start(bf16[2,144,1152]{2,1,0:T(8,128)(2,1)} %get-tuple-element.270), channel_id=1, source_target_pairs={{0,4},{1,5},{2,6},{3,7},{4,0},{5,1},{6,2},{7,3},{8,12},{9,13},{10,... | collective-permute-start | bytes 1990664 | tf_op jit(solution)/shard_map/ppermute | solution.py:1458
  352.5 34.9 %collective-permute-start.54 = (bf16[2,144,1152]{2,1,0:T(8,128)(2,1)}, bf16[2,144,1152]{2,1,0:T(8,128)(2,1)S(1)}, u32[]{:S(2)}, u32[]{:S(2)}) collective-permute-start(bf16[2,144,1152]{2,1,0:T(8,128)(2,1)} %get-tuple-element.271), channel_id=1, source_target_pairs={{0,1},{1,0},{2,3},{3,2},{4,5},{5,4},{6,7},{7,6},{8,9},{9,8},{10,11... | collective-permute-start | bytes 1990664 | tf_op jit(solution)/shard_map/ppermute | solution.py:1458
  353.9 33.4 %collective-permute-start.55 = (bf16[2,144,1152]{2,1,0:T(8,128)(2,1)}, bf16[2,144,1152]{2,1,0:T(8,128)(2,1)S(1)}, u32[]{:S(2)}, u32[]{:S(2)}) collective-permute-start(bf16[2,144,1152]{2,1,0:T(8,128)(2,1)} %get-tuple-element.272), channel_id=1, source_target_pairs={{0,1},{1,0},{2,3},{3,2},{4,5},{5,4},{6,7},{7,6},{8,9},{9,8},{10,11... | collective-permute-start | bytes 1990664 | tf_op jit(solution)/shard_map/ppermute | solution.py:1458
  388.7 68.1 %reduce-scatter.8.cloned.1.call-start = ((), (), s32[]{:S(2)}) async-start(), calls=%async_computation.5 | async-start | bytes 1658880 | tf_op jit(solution)/shard_map/reduce_scatter | solution.py:1497
  427.0 25.8 %collective-permute-start.68 = (f32[72,1152]{1,0:T(8,128)}, f32[72,1152]{1,0:T(8,128)}, u32[]{:S(2)}, u32[]{:S(2)}) collective-permute-start(f32[72,1152]{1,0:T(8,128)} %constant_dynamic-slice_fusion), channel_id=1, source_target_pairs={{0,2},{1,3},{2,0},{3,1},{4,6},{5,7},{6,4},{7,5},{8,10},{9,11},{10,... | collective-permute-start | bytes 995336 | tf_op jit(solution)/shard_map/ppermute | solution.py:1458
  (104 other events, 675.2 us)
Sparse Core Ops, SparseCore 0:
  19.7 36.7 all-gather.8
  58.6 33.1 all-gather.6
  94.0 98.1 all-gather.10
  301.7 29.4 reduce-scatter.3
  388.8 29.6 reduce-scatter.5
  423.8 32.9 reduce-scatter.7

commit v5 on v4

--- a/solution.py
+++ b/solution.py
@@ -1723,12 +1723,12 @@
     own_active, own_slope = up(1, [other_active])
     normed_two_there = grid.over_core(normed_two)
     near_mixed, far_mixed = grid.over_core(mixed[1]), grid.over_core(mixed[3])
-    own_active, active_there, normed_two_there, near_mixed, far_mixed = fence(
-        [own_active, active_there, normed_two_there, near_mixed, far_mixed]
-    )
+    own_active, active_there, normed_two_there, near_mixed, far_mixed, quads = fence(
+        [own_active, active_there, normed_two_there, near_mixed, far_mixed, quads]
+    )
+    quads_there = grid.over_core(quads)
     fc2_sums = weight_grad(spot, (grad_low, grad_there), (own_active, active_there), depth)
-    fc2_near, quads = fence([fc2_sums[0], quads])
-    quads_there = grid.over_core(quads)
+    fc2_near, quads_there = fence([fc2_sums[0], quads_there])
     down_weights = [
         [(source, 0, 0, at), (source, 0, 1, at + 1)]
         for at in (0, 2)
@@ -1826,16 +1826,14 @@
     )
     beside_first = grid.over_x(beside_lo)
     fc1_total = join(fc1_near, fc1_moved[2:], fc1_second)
-    by_class = [down_weights[i] for i in classes[0] + classes[1]]
-    layer_rows = down_project(
-        spot, other_active, own_active, resid, fc2_shift, by_class, [fc1_total]
-    )
-    *corners, attn_first, beside_first, fc1_total = fence(
-        corners + [attn_first, beside_first, fc1_total], [layer_rows]
-    )
+    *corners, fc1_total = fence(corners + [fc1_total])
     fc1_piece = grid.scatter_depth(fc1_total)
     beside_hi, across_lo = add_pairs(beside_hi, corners[1], across_lo, corners[0])
     moved = [grid.over_x(beside_hi), grid.over_y(across_lo)]
+    by_class = [down_weights[i] for i in classes[0] + classes[1]]
+    layer_rows = down_project(
+        spot, other_active, own_active, resid, fc2_shift, by_class, [beside_hi]
+    )
     by_class = [attn_weights[i] for i in (1, 3, 0, 2)]
     input_grad, sums_one = norm_back(
         spot,
@@ -1844,7 +1842,7 @@
         resid_low,
         gain_one,
         by_class,
-        [beside_hi],
+        [layer_rows],
     )
 
     def column_sum(values):
@@ -1884,7 +1882,9 @@
     length = flat.shape[0]
     lines = -(-length // 1024) * 8
     flat = jnp.pad(flat, (0, lines * 128 - length)).reshape(lines, 128)
-    *moved, flat, fc1_piece = fence(moved + [flat, fc1_piece])
+    *moved, beside_first, attn_first, flat, fc1_piece = fence(
+        moved + [beside_first, attn_first, flat, fc1_piece]
+    )
     total = join(near_sums, [beside_first, attn_first], moved)
     attn_piece = grid.scatter_depth(total)
     (flat, fc1_piece, fc2_piece) = fence([flat, fc1_piece, fc2_piece], [total])

time: 478 us -> 469 us (0.981)
  waiting for transfers between devices: 69.6 us -> 62.5 us
    unnamed x122 -> x116, local copies, waits for them, and re-layouts: 17 us -> 16.5 us
  transfers between devices with their start and end apart: 75 -> 75, of which waited for: 23 -> 22; matrix products, arithmetic and copies ran while one was open for 10% -> 10% of each run, Pallas kernels for 53% -> 54%
where the time goes in v5:
time: 469 us; the launch traced here: 462 us
  Pallas kernels  252 us (54%)
  waiting for transfers between devices  62.5 us (13%)
  starting transfers between devices  54.1 us (12%)
  local copies, waits for them, and re-layouts  40.3 us (9%)
  other arithmetic  30.9 us (7%)
  between operations  22.2 us (5%)
    pallas_call x14, Pallas kernels, call(): pl.pallas_call(kernel, in_specs=list(specs) + [any_spec()] * len(waits),...  227 us
    ppermute x69, starting transfers between devices, move(): return lax.ppermute(values, AXES, pairs)  53.2 us
    ppermute x69, waiting for transfers between devices, move(): return lax.ppermute(values, AXES, pairs)  47 us
    unnamed x116, local copies, waits for them, and re-layouts  16.5 us
    all_gather x3, waiting for transfers between devices, gather_depth(): return lax.all_gather(block, 'dp', axis_index_groups=self.depth_groups())  15.2 us
    pallas_call x3, Pallas kernels, add_square(): pl.pallas_call(square_kernel, in_specs=[vmem_spec()] * 5, out_specs=vmem_...  11.1 us
  transfers between devices with their start and end apart: 75, of which 22 were waited for; matrix products, arithmetic and copies ran while one was open for 10% of the time, Pallas kernels for 54%

profile of v5, /device:TPU:0, one launch (start us, length us, event | category | flops | bytes accessed | tf_op | source)
XLA Modules:
  0.0 462.3 jit_solution(5615092627609852101)
XLA Ops:
  19.9 2.6 collective-permute-start.10
  36.1 3.9 collective-permute-done.3
  43.1 3.1 collective-permute-done.4
  47.9 5.9 %collective-permute-done.5 = bf16[4,2,2,6,72]{4,3,2,1,0:T(8,128)(2,1)S(1)} collective-permute-done((bf16[4,2,2,6,72]{4,3,2,1,0:T(8,128)(2,1)S(1)}, bf16[4,2,2,6,72]{4,3,2,1,0:T(8,128)(2,1)S(1)}, u32[]{:S(2)}, u32[]{:S(2)}) %collective-permute-start.5) | collective-permute-done | bytes 13856 | tf_op jit(solution)/shard_map/ppermute | solution.py:1458
  65.6 2.9 select_select_fusion
  76.7 15.1 %all-gather.7.cloned.1.call-done = bf16[576,1152]{1,0:T(8,128)(2,1)} async-done(((bf16[144,1152]{1,0:T(8,128)(2,1)}), bf16[576,1152]{1,0:T(8,128)(2,1)}) %all-gather.7.cloned.1.call-update) | async-done | bytes 1327120 | tf_op jit(solution)/shard_map/all_gather | solution.py:1494
  101.3 17.2 %heads_forward.2 = (bf16[2,768,896]{2,1,0:T(8,128)(2,1)}, bf16[2,4,768,768]{3,2,1,0:T(8,128)(2,1)}, bf16[768,384]{1,0:T(8,128)(2,1)}, bf16[768,384]{1,0:T(8,128)(2,1)}) custom-call(s32[1]{0:T(128)} %bitcast.4.spot, s32[768,1]{1,0:T(8,128)} %get-tuple-element.170.kind_ref, bf16[768,1152]{1,0:T(8,128)(2,1)} %get-tuple-element.171.x_any.refs_0_, ...), custom_call_target="tpu_custom_call" | custom-call | flops 1024 | bytes 1024 | tf_op jit(solution)/shard_map/heads_forward/pallas_call | solution.py:739
  123.0 17.1 %heads_forward.3 = (bf16[2,768,896]{2,1,0:T(8,128)(2,1)}, bf16[2,4,768,768]{3,2,1,0:T(8,128)(2,1)}, bf16[768,384]{1,0:T(8,128)(2,1)}, bf16[768,384]{1,0:T(8,128)(2,1)}) custom-call(s32[1]{0:T(128)} %bitcast.4.spot, s32[768,1]{1,0:T(8,128)} %get-tuple-element.170.kind_ref, bf16[768,1152]{1,0:T(8,128)(2,1)} %get-tuple-element.171.x_any.refs_0_, ...), custom_call_target="tpu_custom_call" | custom-call | flops 1024 | bytes 1024 | tf_op jit(solution)/shard_map/heads_forward/pallas_call | solution.py:739
  140.1 3.7 collective-permute-done.15.refs_0_
  149.3 9.5 %attn_out.1 = (bf16[768,1152]{1,0:T(8,128)(2,1)}, bf16[768,1152]{1,0:T(8,128)(2,1)}) custom-call(s32[1]{0:T(128)} %bitcast.4.spot, bf16[768,384]{1,0:T(8,128)(2,1)} %get-tuple-element.187.one.refs_1_.refs_5_, bf16[768,384]{1,0:T(8,128)(2,1)} %get-tuple-element.188.two.refs_0_, bf16[768,384]{1,0:T(8,128)(2,1)} %get-tuple-element.189.three.refs_1_.refs_5_, ...), custom_call_target="tpu_custom_call" | custom-call | flops 1024 | bytes 1024 | tf_op jit(solution)/shard_map/attn_out/pallas_call | solution.py:739
  158.8 5.0 %collective-permute-done.25.refs_0_ = bf16[2,144,1152]{2,1,0:T(8,128)(2,1)} collective-permute-done((bf16[2,144,1152]{2,1,0:T(8,128)(2,1)}, bf16[2,144,1152]{2,1,0:T(8,128)(2,1)}, u32[]{:S(2)}, u32[]{:S(2)}) %collective-permute-start.25) | collective-permute-done | bytes 663584 | tf_op jit(solution)/shard_map/ppermute | solution.py:1458
  168.3 11.3 %mlp_up.2 = (bf16[2,768,1152]{2,1,0:T(8,128)(2,1)}, bf16[2,768,1152]{2,1,0:T(8,128)(2,1)}) custom-call(s32[1]{0:T(128)} %bitcast.4.spot, bf16[768,1152]{1,0:T(8,128)(2,1)} %get-tuple-element.192.x_any.refs_0_, f32[2,1,1152]{2,1,0:T(1,128)} %get-tuple-element.193.bias_ref, bf16[4,144,1152]{2,1,0:T(8,128)(2,1)} %collective-permute-done.22.refs_4_.refs_0_.refs_13_, ...), custom_call_target="tpu_custom_call" | custom-call | flops 1024 | bytes 1024 | tf_op jit(solution)/shard_map/mlp_up/pallas_call | solution.py:739
  181.7 11.6 %mlp_up.3 = (bf16[2,768,1152]{2,1,0:T(8,128)(2,1)}, bf16[2,768,1152]{2,1,0:T(8,128)(2,1)}) custom-call(s32[1]{0:T(128)} %bitcast.4.spot, bf16[768,1152]{1,0:T(8,128)(2,1)} %get-tuple-element.192.x_any.refs_0_, f32[2,1,1152]{2,1,0:T(1,128)} %get-tuple-element.197.bias_ref, bf16[4,144,1152]{2,1,0:T(8,128)(2,1)} %get-tuple-element.169.refs_0_.refs_8_, ...), custom_call_target="tpu_custom_call" | custom-call | flops 1024 | bytes 1024 | tf_op jit(solution)/shard_map/mlp_up/pallas_call | solution.py:739
  194.9 14.8 %weight_grad.4 = (bf16[4,144,1152]{2,1,0:T(8,128)(2,1)}, bf16[2,144,1152]{2,1,0:T(8,128)(2,1)}, bf16[2,144,1152]{2,1,0:T(8,128)(2,1)}, bf16[2,144,1152]{2,1,0:T(...) custom-call(s32[1]{0:T(128)} %bitcast.4.spot, ...), custom_call_target="tpu_custom_call" | custom-call | flops 1024 | bytes 1024 | tf_op jit(solution)/shard_map/weight_grad/pallas_call | solution.py:739
  214.0 32.9 %mlp_back.1 = (bf16[2,768,1152]{2,1,0:T(8,128)(2,1)}, bf16[2,768,1152]{2,1,0:T(8,128)(2,1)}, bf16[768,1152]{1,0:T(8,128)(2,1)}, f32[8,1152]{1,0:T(8,128)}, f32[4,1,1152]{2,1,0:T(1,128)}) custom-call(s32[1]{0:T(128)} %bitcast.4.spot, bf16[768,1152]{1,0:T(8,128)(2,1)} %copy-done.4, bf16[2,768,1152]{2,1,0:T(8,128)(2,1)} %get-tuple-element.207.one_any, ...), custom_call_target="tpu_custom_call" | custom-call | flops 1024 | bytes 1024 | tf_op jit(solution)/shard_map/mlp_back/pallas_call | solution.py:739
  248.9 3.0 add_pairs.3
  254.8 21.4 %heads_backward.2 = (bf16[768,896]{1,0:T(8,128)(2,1)}, bf16[768,896]{1,0:T(8,128)(2,1)}, f32[2,1,896]{2,1,0:T(1,128)}) custom-call(s32[1]{0:T(128)} %bitcast.4.spot, bf16[768,1152]{1,0:T(8,128)(2,1)} %get-tuple-element.224.grad_any.refs_4_.refs_5_, bf16[2,768,896]{2,1,0:T(8,128)(2,1)} %get-tuple-element.225.qkv_any, ...), custom_call_target="tpu_custom_call" | custom-call | flops 1024 | bytes 1024 | tf_op jit(solution)/shard_map/heads_backward/pallas_call | solution.py:739
  277.9 3.7 add_square.3.refs_4_.refs_1_
  281.6 14.8 %weight_grad.5 = (bf16[4,144,1152]{2,1,0:T(8,128)(2,1)}, bf16[2,144,1152]{2,1,0:T(8,128)(2,1)}, bf16[2,144,1152]{2,1,0:T(8,128)(2,1)}, bf16[2,144,1152]{2,1,0:T(...) custom-call(s32[1]{0:T(128)} %bitcast.4.spot, ...), custom_call_target="tpu_custom_call" | custom-call | flops 1024 | bytes 1024 | tf_op jit(solution)/shard_map/weight_grad/pallas_call | solution.py:739
  301.9 21.2 %heads_backward.3 = (bf16[768,896]{1,0:T(8,128)(2,1)}, bf16[768,896]{1,0:T(8,128)(2,1)}, f32[2,1,896]{2,1,0:T(1,128)}) custom-call(s32[1]{0:T(128)} %bitcast.4.spot, bf16[768,1152]{1,0:T(8,128)(2,1)} %get-tuple-element.224.grad_any.refs_4_.refs_5_, bf16[2,768,896]{2,1,0:T(8,128)(2,1)} %get-tuple-element.235.qkv_any, ...), custom_call_target="tpu_custom_call" | custom-call | flops 1024 | bytes 1024 | tf_op jit(solution)/shard_map/heads_backward/pallas_call | solution.py:739
  323.2 5.1 %collective-permute-done.48.refs_3_ = bf16[2,144,1152]{2,1,0:T(8,128)(2,1)S(1)} collective-permute-done((bf16[2,144,1152]{2,1,0:T(8,128)(2,1)}, bf16[2,144,1152]{2,1,0:T(8,128)(2,1)S(1)}, u32[]{:S(2)}, u32[]{:S(2)}) %collective-permute-start.48) | collective-permute-done | bytes 663584 | tf_op jit(solution)/shard_map/ppermute | solution.py:1458
  329.1 2.9 add_pairs.4
  333.7 10.9 %weight_grad.6 = (bf16[2,144,1152]{2,1,0:T(8,128)(2,1)}, bf16[2,144,1152]{2,1,0:T(8,128)(2,1)}, bf16[2,144,1152]{2,1,0:T(8,128)(2,1)}, bf16[2,144,1152]{2,1,0:T(8,128)(2,1)}) custom-call(s32[1]{0:T(128)} %bitcast.4.spot, bf16[768,1152]{1,0:T(8,128)(2,1)} %get-tuple-element.171.x_any.refs_0_, bf16[1,768,896]{2,1,0:T(8,128)(2,1)} %bitcast.115, ...), custom_call_target="tpu_custom_call" | custom-call | flops 1024 | bytes 1024 | tf_op jit(solution)/shard_map/weight_grad/pallas_call | solution.py:739
  348.1 11.1 %weight_grad.7 = (bf16[4,144,1152]{2,1,0:T(8,128)(2,1)}, bf16[2,144,1152]{2,1,0:T(8,128)(2,1)}, bf16[2,144,1152]{2,1,0:T(8,128)(2,1)}) custom-call(s32[1]{0:T(128)} %bitcast.4.spot, bf16[768,1152]{1,0:T(8,128)(2,1)} %get-tuple-element.171.x_any.refs_0_, bf16[1,768,896]{2,1,0:T(8,128)(2,1)} %bitcast.116, bf16[768,1152]{1,0:T(8,128)(2,1)} %get-tuple-element.251.refs_2_, ...), custom_call_target="tpu_custom_call" | custom-call | flops 1024 | bytes 1024 | tf_op jit(solution)/shard_map/weight_grad/pallas_call | solution.py:739
  359.2 3.7 add_square.4.refs_2_
  368.0 3.2 add_pairs.5
  374.6 16.4 %mlp_down.1.refs_17_ = bf16[768,1152]{1,0:T(8,128)(2,1)} custom-call(s32[1]{0:T(128)} %bitcast.4.spot, bf16[2,768,1152]{2,1,0:T(8,128)(2,1)} %fence.31.refs_5_.later_any, bf16[2,768,1152]{2,1,0:T(8,128)(2,1)} %get-tuple-element.200.refs_1_.early_any, bf16[768,1152]{1,0:T(8,128)(2,1)} %get-tuple-element.201.resid_any, ...), custom_call_target="tpu_custom_call" | custom-call | flops 1024 | bytes 1024 | tf_op jit(solution)/shard_map/mlp_down/pallas_call | solution.py:739
  391.0 17.2 %norm_one_back.1 = (f32[768,1152]{1,0:T(8,128)}, f32[8,1152]{1,0:T(8,128)}) custom-call(s32[1]{0:T(128)} %bitcast.4.spot, bf16[768,896]{1,0:T(8,128)(2,1)} %get-tuple-element.256.refs_8_.refs_0_, bf16[768,896]{1,0:T(8,128)(2,1)} %get-tuple-element.237.refs_1_, bf16[768,896]{1,0:T(8,128)(2,1)} %get-tuple-element.250.refs_2_, ...), custom_call_target="tpu_custom_call" | custom-call | flops 1024 | bytes 1024 | tf_op jit(solution)/shard_map/norm_one_back/pallas_call | solution.py:739
  411.5 3.7 add_square.5.refs_2_.refs_3_
  431.0 4.5 collective-permute-done.64
  435.6 4.0 slice_select_fusion
  439.6 4.7 %collective-permute-done.65 = f32[112,128]{1,0:T(8,128)S(1)} collective-permute-done((f32[112,128]{1,0:T(8,128)S(1)}, f32[112,128]{1,0:T(8,128)S(1)}, u32[]{:S(2)}, u32[]{:S(2)}) %collective-permute-start.65) | collective-permute-done | bytes 57376 | tf_op jit(solution)/shard_map/ppermute | solution.py:1458
  (414 shorter events, 132.2 us)
Async XLA Ops:
  7.2 51.0 %all-gather.9.cloned.1.call-start = ((), (), s32[]{:S(2)}) async-start(), calls=%async_computation.7 | async-start | bytes 1658880 | tf_op jit(solution)/shard_map/all_gather | solution.py:1494
  19.6 72.3 %all-gather.7.cloned.1.call-start = ((), (), s32[]{:S(2)}) async-start(), calls=%async_computation.6 | async-start | bytes 1658880 | tf_op jit(solution)/shard_map/all_gather | solution.py:1494
  19.9 38.2 %collective-permute-start.10 = (bf16[144,1152]{1,0:T(8,128)(2,1)S(1)}, bf16[144,1152]{1,0:T(8,128)(2,1)S(1)}, u32[]{:S(2)}, u32[]{:S(2)}) collective-permute-start(bf16[144,1152]{1,0:T(8,128)(2,1)S(1)} %pad_maximum_fusion.4.refs_4_), channel_id=1, source_target_pairs={{0,1},{1,0},{2,3},{3,2},{4,5},{5,4},{6,7},{7,6},{8,9},{9,8},{10,11... | collective-permute-start | bytes 995336 | tf_op jit(solution)/shard_map/ppermute | solution.py:1458
  22.5 35.6 %collective-permute-start.11 = (bf16[144,1152]{1,0:T(8,128)(2,1)S(1)}, bf16[144,1152]{1,0:T(8,128)(2,1)S(1)}, u32[]{:S(2)}, u32[]{:S(2)}) collective-permute-start(bf16[144,1152]{1,0:T(8,128)(2,1)S(1)} %pad_maximum_fusion.4.refs_4_), channel_id=1, source_target_pairs={{0,5},{1,4},{2,7},{3,6},{4,1},{5,0},{6,3},{7,2},{8,13},{9,12},{10,... | collective-permute-start | bytes 995336 | tf_op jit(solution)/shard_map/ppermute | solution.py:1458
  23.9 34.2 %collective-permute-start.9 = (bf16[144,1152]{1,0:T(8,128)(2,1)S(1)}, bf16[144,1152]{1,0:T(8,128)(2,1)S(1)}, u32[]{:S(2)}, u32[]{:S(2)}) collective-permute-start(bf16[144,1152]{1,0:T(8,128)(2,1)S(1)} %pad_maximum_fusion.4.refs_4_), channel_id=1, source_target_pairs={{0,4},{1,5},{2,6},{3,7},{4,0},{5,1},{6,2},{7,3},{8,12},{9,13},{10,... | collective-permute-start | bytes 995336 | tf_op jit(solution)/shard_map/ppermute | solution.py:1458
  24.0 34.1 %collective-permute-start.7 = (bf16[26,128]{1,0:T(8,128)(2,1)}, bf16[26,128]{1,0:T(8,128)(2,1)S(1)}, u32[]{:S(2)}, u32[]{:S(2)}) collective-permute-start(bf16[26,128]{1,0:T(8,128)(2,1)} %fence.25), channel_id=1, source_target_pairs={{0,1},{1,0},{2,3},{3,2},{4,5},{5,4},{6,7},{7,6},{8,9},{9,8},{10,11... | collective-permute-start | bytes 19976 | tf_op jit(solution)/shard_map/ppermute | solution.py:1458
  58.0 135.4 %all-gather.11.cloned.1.call-start = ((), (), s32[]{:S(2)}) async-start(), calls=%async_computation.8 | async-start | bytes 6635520 | tf_op jit(solution)/shard_map/all_gather | solution.py:1494
  60.4 31.4 %collective-permute-start.12 = (bf16[4,144,1152]{2,1,0:T(8,128)(2,1)}, bf16[4,144,1152]{2,1,0:T(8,128)(2,1)S(1)}, u32[]{:S(2)}, u32[]{:S(2)}) collective-permute-start(bf16[4,144,1152]{2,1,0:T(8,128)(2,1)} %get-tuple-element.159.refs_0_.refs_4_.refs_12_), channel_id=1, source_target_pairs={{0,4},{1,5},{2,6},{3,7},{4,0},{5,1},{6,2},{7,3},{8,12},{9,13},{10,... | collective-permute-start | bytes 3981320 | tf_op jit(solution)/shard_map/ppermute | solution.py:1458
  62.3 29.6 %collective-permute-start.13 = (bf16[4,144,1152]{2,1,0:T(8,128)(2,1)}, bf16[4,144,1152]{2,1,0:T(8,128)(2,1)}, u32[]{:S(2)}, u32[]{:S(2)}) collective-permute-start(bf16[4,144,1152]{2,1,0:T(8,128)(2,1)} %get-tuple-element.159.refs_0_.refs_4_.refs_12_), channel_id=1, source_target_pairs={{0,1},{1,0},{2,3},{3,2},{4,5},{5,4},{6,7},{7,6},{8,9},{9,8},{10,11... | collective-permute-start | bytes 3981320 | tf_op jit(solution)/shard_map/ppermute | solution.py:1458
  64.0 34.0 %collective-permute-start.20 = (bf16[4,144,1152]{2,1,0:T(8,128)(2,1)}, bf16[4,144,1152]{2,1,0:T(8,128)(2,1)}, u32[]{:S(2)}, u32[]{:S(2)}) collective-permute-start(bf16[4,144,1152]{2,1,0:T(8,128)(2,1)} %get-tuple-element.159.refs_0_.refs_4_.refs_12_), channel_id=1, source_target_pairs={{0,2},{1,3},{2,0},{3,1},{4,6},{5,7},{6,4},{7,5},{8,10},{9,11},{10,... | collective-permute-start | bytes 3981320 | tf_op jit(solution)/shard_map/ppermute | solution.py:1458
  93.5 265.7 %reduce-scatter.4.cloned.1.call-start = ((), (), s32[]{:S(2)}) async-start(), calls=%async_computation.3 | async-start | bytes 1658880 | tf_op jit(solution)/shard_map/reduce_scatter | solution.py:1497
  99.4 44.3 %collective-permute-start.15 = (bf16[4,144,1152]{2,1,0:T(8,128)(2,1)}, bf16[4,144,1152]{2,1,0:T(8,128)(2,1)}, u32[]{:S(2)}, u32[]{:S(2)}) collective-permute-start(bf16[4,144,1152]{2,1,0:T(8,128)(2,1)} %get-tuple-element.169.refs_0_.refs_8_), channel_id=1, source_target_pairs={{0,4},{1,5},{2,6},{3,7},{4,0},{5,1},{6,2},{7,3},{8,12},{9,13},{10,... | collective-permute-start | bytes 3981320 | tf_op jit(solution)/shard_map/ppermute | solution.py:1458
  100.0 43.8 %collective-permute-start.16 = (bf16[4,144,1152]{2,1,0:T(8,128)(2,1)}, bf16[4,144,1152]{2,1,0:T(8,128)(2,1)}, u32[]{:S(2)}, u32[]{:S(2)}) collective-permute-start(bf16[4,144,1152]{2,1,0:T(8,128)(2,1)} %get-tuple-element.169.refs_0_.refs_8_), channel_id=1, source_target_pairs={{0,1},{1,0},{2,3},{3,2},{4,5},{5,4},{6,7},{7,6},{8,9},{9,8},{10,11... | collective-permute-start | bytes 3981320 | tf_op jit(solution)/shard_map/ppermute | solution.py:1458
  121.1 37.8 %collective-permute-start.29 = (bf16[768,1152]{1,0:T(8,128)(2,1)S(1)}, bf16[768,1152]{1,0:T(8,128)(2,1)S(1)}, u32[]{:S(2)}, u32[]{:S(2)}) collective-permute-start(bf16[768,1152]{1,0:T(8,128)(2,1)S(1)} %copy-done.1), channel_id=1, source_target_pairs={{0,2},{1,3},{2,0},{3,1},{4,6},{5,7},{6,4},{7,5},{8,10},{9,11},{10,... | collective-permute-start | bytes 5308424 | tf_op jit(solution)/shard_map/ppermute | solution.py:1458
  209.7 37.2 %collective-permute-start.37 = (bf16[2,144,1152]{2,1,0:T(8,128)(2,1)}, bf16[2,144,1152]{2,1,0:T(8,128)(2,1)S(1)}, u32[]{:S(2)}, u32[]{:S(2)}) collective-permute-start(bf16[2,144,1152]{2,1,0:T(8,128)(2,1)} %get-tuple-element.215), channel_id=1, source_target_pairs={{0,4},{1,5},{2,6},{3,7},{4,0},{5,1},{6,2},{7,3},{8,12},{9,13},{10,... | collective-permute-start | bytes 1990664 | tf_op jit(solution)/shard_map/ppermute | solution.py:1458
  211.4 35.5 %collective-permute-start.38 = (bf16[2,144,1152]{2,1,0:T(8,128)(2,1)}, bf16[2,144,1152]{2,1,0:T(8,128)(2,1)S(1)}, u32[]{:S(2)}, u32[]{:S(2)}) collective-permute-start(bf16[2,144,1152]{2,1,0:T(8,128)(2,1)} %get-tuple-element.216), channel_id=1, source_target_pairs={{0,1},{1,0},{2,3},{3,2},{4,5},{5,4},{6,7},{7,6},{8,9},{9,8},{10,11... | collective-permute-start | bytes 1990664 | tf_op jit(solution)/shard_map/ppermute | solution.py:1458
  212.9 34.0 %collective-permute-start.39 = (bf16[2,144,1152]{2,1,0:T(8,128)(2,1)}, bf16[2,144,1152]{2,1,0:T(8,128)(2,1)S(1)}, u32[]{:S(2)}, u32[]{:S(2)}) collective-permute-start(bf16[2,144,1152]{2,1,0:T(8,128)(2,1)} %get-tuple-element.217), channel_id=1, source_target_pairs={{0,4},{1,5},{2,6},{3,7},{4,0},{5,1},{6,2},{7,3},{8,12},{9,13},{10,... | collective-permute-start | bytes 1990664 | tf_op jit(solution)/shard_map/ppermute | solution.py:1458
  213.5 33.5 %collective-permute-start.40 = (bf16[2,144,1152]{2,1,0:T(8,128)(2,1)}, bf16[2,144,1152]{2,1,0:T(8,128)(2,1)S(1)}, u32[]{:S(2)}, u32[]{:S(2)}) collective-permute-start(bf16[2,144,1152]{2,1,0:T(8,128)(2,1)} %get-tuple-element.218), channel_id=1, source_target_pairs={{0,1},{1,0},{2,3},{3,2},{4,5},{5,4},{6,7},{7,6},{8,9},{9,8},{10,11... | collective-permute-start | bytes 1990664 | tf_op jit(solution)/shard_map/ppermute | solution.py:1458
  248.4 27.9 %collective-permute-start.43 = (bf16[2,768,1152]{2,1,0:T(8,128)(2,1)}, bf16[2,768,1152]{2,1,0:T(8,128)(2,1)}, u32[]{:S(2)}, u32[]{:S(2)}) collective-permute-start(bf16[2,768,1152]{2,1,0:T(8,128)(2,1)} %get-tuple-element.228), channel_id=1, source_target_pairs={{0,2},{1,3},{2,0},{3,1},{4,6},{5,7},{6,4},{7,5},{8,10},{9,11},{10,... | collective-permute-start | bytes 10616840 | tf_op jit(solution)/shard_map/ppermute | solution.py:1458
  248.4 27.8 %collective-permute-start.44 = (bf16[768,1152]{1,0:T(8,128)(2,1)}, bf16[768,1152]{1,0:T(8,128)(2,1)S(1)}, u32[]{:S(2)}, u32[]{:S(2)}) collective-permute-start(bf16[768,1152]{1,0:T(8,128)(2,1)} %get-tuple-element.224.grad_any.refs_4_.refs_5_), channel_id=1, source_target_pairs={{0,2},{1,3},{2,0},{3,1},{4,6},{5,7},{6,4},{7,5},{8,10},{9,11},{10,... | collective-permute-start | bytes 5308424 | tf_op jit(solution)/shard_map/ppermute | solution.py:1458
  296.4 26.7 %collective-permute-start.46 = (bf16[2,144,1152]{2,1,0:T(8,128)(2,1)}, bf16[2,144,1152]{2,1,0:T(8,128)(2,1)S(1)}, u32[]{:S(2)}, u32[]{:S(2)}) collective-permute-start(bf16[2,144,1152]{2,1,0:T(8,128)(2,1)} %get-tuple-element.241), channel_id=1, source_target_pairs={{0,4},{1,5},{2,6},{3,7},{4,0},{5,1},{6,2},{7,3},{8,12},{9,13},{10,... | collective-permute-start | bytes 1990664 | tf_op jit(solution)/shard_map/ppermute | solution.py:1458
  297.0 26.1 %collective-permute-start.47 = (bf16[2,144,1152]{2,1,0:T(8,128)(2,1)}, bf16[2,144,1152]{2,1,0:T(8,128)(2,1)S(1)}, u32[]{:S(2)}, u32[]{:S(2)}) collective-permute-start(bf16[2,144,1152]{2,1,0:T(8,128)(2,1)} %get-tuple-element.242), channel_id=1, source_target_pairs={{0,1},{1,0},{2,3},{3,2},{4,5},{5,4},{6,7},{7,6},{8,9},{9,8},{10,11... | collective-permute-start | bytes 1990664 | tf_op jit(solution)/shard_map/ppermute | solution.py:1458
  297.6 30.6 %collective-permute-start.48 = (bf16[2,144,1152]{2,1,0:T(8,128)(2,1)}, bf16[2,144,1152]{2,1,0:T(8,128)(2,1)S(1)}, u32[]{:S(2)}, u32[]{:S(2)}) collective-permute-start(bf16[2,144,1152]{2,1,0:T(8,128)(2,1)} %get-tuple-element.243), channel_id=1, source_target_pairs={{0,4},{1,5},{2,6},{3,7},{4,0},{5,1},{6,2},{7,3},{8,12},{9,13},{10,... | collective-permute-start | bytes 1990664 | tf_op jit(solution)/shard_map/ppermute | solution.py:1458
  299.1 29.5 %collective-permute-start.49 = (bf16[2,144,1152]{2,1,0:T(8,128)(2,1)}, bf16[2,144,1152]{2,1,0:T(8,128)(2,1)}, u32[]{:S(2)}, u32[]{:S(2)}) collective-permute-start(bf16[2,144,1152]{2,1,0:T(8,128)(2,1)} %get-tuple-element.244), channel_id=1, source_target_pairs={{0,1},{1,0},{2,3},{3,2},{4,5},{5,4},{6,7},{7,6},{8,9},{9,8},{10,11... | collective-permute-start | bytes 1990664 | tf_op jit(solution)/shard_map/ppermute | solution.py:1458
  301.6 108.9 %reduce-scatter.6.cloned.1.call-start = ((), (), s32[]{:S(2)}) async-start(), calls=%async_computation.4 | async-start | bytes 1658880 | tf_op jit(solution)/shard_map/reduce_scatter | solution.py:1497
  332.0 27.2 %collective-permute-start.50 = (bf16[2,144,1152]{2,1,0:T(8,128)(2,1)}, bf16[2,144,1152]{2,1,0:T(8,128)(2,1)}, u32[]{:S(2)}, u32[]{:S(2)}) collective-permute-start(bf16[2,144,1152]{2,1,0:T(8,128)(2,1)} %get-tuple-element.248), channel_id=1, source_target_pairs={{0,4},{1,5},{2,6},{3,7},{4,0},{5,1},{6,2},{7,3},{8,12},{9,13},{10,... | collective-permute-start | bytes 1990664 | tf_op jit(solution)/shard_map/ppermute | solution.py:1458
  365.5 83.2 %reduce-scatter.8.cloned.1.call-start = ((), (), s32[]{:S(2)}) async-start(), calls=%async_computation.5 | async-start | bytes 1658880 | tf_op jit(solution)/shard_map/reduce_scatter | solution.py:1497
  367.4 43.1 %collective-permute-start.58 = (bf16[2,144,1152]{2,1,0:T(8,128)(2,1)}, bf16[2,144,1152]{2,1,0:T(8,128)(2,1)S(1)}, u32[]{:S(2)}, u32[]{:S(2)}) collective-permute-start(bf16[2,144,1152]{2,1,0:T(8,128)(2,1)} %get-tuple-element.281), channel_id=1, source_target_pairs={{0,1},{1,0},{2,3},{3,2},{4,5},{5,4},{6,7},{7,6},{8,9},{9,8},{10,11... | collective-permute-start | bytes 1990664 | tf_op jit(solution)/shard_map/ppermute | solution.py:1458
  371.1 39.3 %collective-permute-start.55 = (bf16[2,144,1152]{2,1,0:T(8,128)(2,1)}, bf16[2,144,1152]{2,1,0:T(8,128)(2,1)S(1)}, u32[]{:S(2)}, u32[]{:S(2)}) collective-permute-start(bf16[2,144,1152]{2,1,0:T(8,128)(2,1)} %get-tuple-element.276.refs_8_), channel_id=1, source_target_pairs={{0,4},{1,5},{2,6},{3,7},{4,0},{5,1},{6,2},{7,3},{8,12},{9,13},{10,... | collective-permute-start | bytes 1990664 | tf_op jit(solution)/shard_map/ppermute | solution.py:1458
  372.0 38.4 %collective-permute-start.56 = (bf16[2,144,1152]{2,1,0:T(8,128)(2,1)}, bf16[2,144,1152]{2,1,0:T(8,128)(2,1)}, u32[]{:S(2)}, u32[]{:S(2)}) collective-permute-start(bf16[2,144,1152]{2,1,0:T(8,128)(2,1)} %get-tuple-element.279), channel_id=1, source_target_pairs={{0,1},{1,0},{2,3},{3,2},{4,5},{5,4},{6,7},{7,6},{8,9},{9,8},{10,11... | collective-permute-start | bytes 1990664 | tf_op jit(solution)/shard_map/ppermute | solution.py:1458
  373.5 37.0 %collective-permute-start.57 = (bf16[2,144,1152]{2,1,0:T(8,128)(2,1)}, bf16[2,144,1152]{2,1,0:T(8,128)(2,1)}, u32[]{:S(2)}, u32[]{:S(2)}) collective-permute-start(bf16[2,144,1152]{2,1,0:T(8,128)(2,1)} %get-tuple-element.280), channel_id=1, source_target_pairs={{0,4},{1,5},{2,6},{3,7},{4,0},{5,1},{6,2},{7,3},{8,12},{9,13},{10,... | collective-permute-start | bytes 1990664 | tf_op jit(solution)/shard_map/ppermute | solution.py:1458
  419.5 26.9 %collective-permute-start.68 = (f32[72,1152]{1,0:T(8,128)}, f32[72,1152]{1,0:T(8,128)}, u32[]{:S(2)}, u32[]{:S(2)}) collective-permute-start(f32[72,1152]{1,0:T(8,128)} %constant_dynamic-slice_fusion), channel_id=1, source_target_pairs={{0,2},{1,3},{2,0},{3,1},{4,6},{5,7},{6,4},{7,5},{8,10},{9,11},{10,... | collective-permute-start | bytes 995336 | tf_op jit(solution)/shard_map/ppermute | solution.py:1458
  (101 other events, 690.0 us)
Sparse Core Ops, SparseCore 0:
  19.7 36.7 all-gather.8
  58.6 33.1 all-gather.6
  94.0 98.1 all-gather.10
  301.8 29.3 reduce-scatter.3
  365.6 29.3 reduce-scatter.5
  416.8 31.8 reduce-scatter.7

commit v6 on v5

--- a/solution.py
+++ b/solution.py
@@ -1507,6 +1507,12 @@
         second = jnp.where(self.c == 0, theirs, mine)
         return jnp.stack([first, second])
 
+    def sum_depth(self, values):
+        terms = [values] + [self.across_z(values, mask) for mask in range(1, self.depth)]
+        while len(terms) > 1:
+            terms = [terms[i] + terms[i + 1] for i in range(0, len(terms), 2)]
+        return terms[0]
+
     def gather_small(self, values):
         count, shard = values.shape
         parts = jnp.zeros((self.depth, 2, 2, count, shard), values.dtype)
@@ -1830,10 +1836,6 @@
     fc1_piece = grid.scatter_depth(fc1_total)
     beside_hi, across_lo = add_pairs(beside_hi, corners[1], across_lo, corners[0])
     moved = [grid.over_x(beside_hi), grid.over_y(across_lo)]
-    by_class = [down_weights[i] for i in classes[0] + classes[1]]
-    layer_rows = down_project(
-        spot, other_active, own_active, resid, fc2_shift, by_class, [beside_hi]
-    )
     by_class = [attn_weights[i] for i in (1, 3, 0, 2)]
     input_grad, sums_one = norm_back(
         spot,
@@ -1842,7 +1844,7 @@
         resid_low,
         gain_one,
         by_class,
-        [layer_rows],
+        [beside_hi],
     )
 
     def column_sum(values):
@@ -1888,20 +1890,22 @@
     total = join(near_sums, [beside_first, attn_first], moved)
     attn_piece = grid.scatter_depth(total)
     (flat, fc1_piece, fc2_piece) = fence([flat, fc1_piece, fc2_piece], [total])
+    by_class = [down_weights[i] for i in classes[0] + classes[1]]
+    layer_rows = down_project(
+        spot, other_active, own_active, resid, fc2_shift, by_class, [total]
+    )
     flat = flat + grid.over_core(flat)
-    flat = flat + grid.over_x(flat)
-    flat = flat + grid.over_y(flat)
-    bit = 1
-    while bit < depth:
-        flat = flat + grid.across_z(flat, bit)
-        bit *= 2
+    moved = [grid.over_x(flat), grid.over_y(flat), grid.over_both(flat)]
+    flat = (flat + moved[0]) + (moved[1] + moved[2])
+    flat = grid.sum_depth(flat)
     flat = flat.reshape(-1)
     fc1_piece = grid.scatter_core(fc1_piece)
     fc2_piece = grid.scatter_core(fc2_piece)
     swap_from = fence([one_row(layer_rows, swap_at), one_row(input_grad, swap_at)], [total])
     returned = [grid.over_y(values) for values in swap_from]
-    layer_output = jnp.where(at_swap, returned[0], layer_rows)[:rows]
-    input_grad = jnp.where(at_swap, returned[1], input_grad)[:rows]
+    kept = [jnp.where(swapped, one, two) for one, two in zip(returned, swap_from)]
+    layer_output = lax.dynamic_update_slice(layer_rows[:rows], kept[0], (swap_at, 0))
+    input_grad = lax.dynamic_update_slice(input_grad[:rows], kept[1], (swap_at, 0))
     attn_piece = grid.scatter_core(attn_piece)
     row_total = flat[: 6 * full_width].reshape(6, full_width)
     row_piece = lax.dynamic_slice_in_dim(row_total, lax.axis_index("dp") * shard, shard, 1)

time: 469 us -> 471 us (level)
  local copies, waits for them, and re-layouts: 40.3 us -> 47.5 us
  other arithmetic: 30.9 us -> 24.8 us
  starting transfers between devices: 54.1 us -> 59.9 us
  waiting for transfers between devices: 62.5 us -> 57.4 us
    ppermute x69 -> x71, starting transfers between devices: 53.2 us -> 58.9 us  [move(): return lax.ppermute(values, AXES, pairs)]
    select_n x2, other arithmetic: 5.48 us -> 0.02 us  [image_shards(): jnp.where(swapped, one, two)]
    ppermute x69 -> x71, waiting for transfers between devices: 47 us -> 42 us  [move(): return lax.ppermute(values, AXES, pairs)]
    unnamed x116 -> x128, local copies, waits for them, and re-layouts: 16.5 us -> 17.6 us
  transfers between devices with their start and end apart: 75 -> 77, of which waited for: 22 -> 23; matrix products, arithmetic and copies ran while one was open for 10% -> 10% of each run, Pallas kernels for 54% -> 54%
where the time goes in v6:
time: 471 us; the launch traced here: 464 us
  Pallas kernels  252 us (54%)
  starting transfers between devices  59.9 us (13%)
  waiting for transfers between devices  57.4 us (12%)
  local copies, waits for them, and re-layouts  47.5 us (10%)
  other arithmetic  24.8 us (5%)
  between operations  22.3 us (5%)
    pallas_call x14, Pallas kernels, call(): pl.pallas_call(kernel, in_specs=list(specs) + [any_spec()] * len(waits),...  227 us
    ppermute x71, starting transfers between devices, move(): return lax.ppermute(values, AXES, pairs)  58.9 us
    ppermute x71, waiting for transfers between devices, move(): return lax.ppermute(values, AXES, pairs)  42 us
    unnamed x128, local copies, waits for them, and re-layouts  17.6 us
    all_gather x3, waiting for transfers between devices, gather_depth(): return lax.all_gather(block, 'dp', axis_index_groups=self.depth_groups())  15.2 us
    pallas_call x3, Pallas kernels, add_square(): pl.pallas_call(square_kernel, in_specs=[vmem_spec()] * 5, out_specs=vmem_...  11 us
  transfers between devices with their start and end apart: 77, of which 23 were waited for; matrix products, arithmetic and copies ran while one was open for 10% of the time, Pallas kernels for 54%

profile of v6, /device:TPU:0, one launch (start us, length us, event | category | flops | bytes accessed | tf_op | source)
XLA Modules:
  0.0 463.9 jit_solution(15585669886060065435)
XLA Ops:
  19.9 2.6 collective-permute-start.10
  36.1 3.9 collective-permute-done.3
  43.1 3.1 collective-permute-done.4
  47.9 5.9 %collective-permute-done.5 = bf16[4,2,2,6,72]{4,3,2,1,0:T(8,128)(2,1)S(1)} collective-permute-done((bf16[4,2,2,6,72]{4,3,2,1,0:T(8,128)(2,1)S(1)}, bf16[4,2,2,6,72]{4,3,2,1,0:T(8,128)(2,1)S(1)}, u32[]{:S(2)}, u32[]{:S(2)}) %collective-permute-start.5) | collective-permute-done | bytes 13856 | tf_op jit(solution)/shard_map/ppermute | solution.py:1458
  65.6 2.9 select_select_fusion
  76.7 15.2 %all-gather.7.cloned.1.call-done = bf16[576,1152]{1,0:T(8,128)(2,1)} async-done(((bf16[144,1152]{1,0:T(8,128)(2,1)}), bf16[576,1152]{1,0:T(8,128)(2,1)}) %all-gather.7.cloned.1.call-update) | async-done | bytes 1327120 | tf_op jit(solution)/shard_map/all_gather | solution.py:1494
  101.3 17.2 %heads_forward.2 = (bf16[2,768,896]{2,1,0:T(8,128)(2,1)}, bf16[2,4,768,768]{3,2,1,0:T(8,128)(2,1)}, bf16[768,384]{1,0:T(8,128)(2,1)}, bf16[768,384]{1,0:T(8,128)(2,1)}) custom-call(s32[1]{0:T(128)} %bitcast.spot, s32[768,1]{1,0:T(8,128)} %get-tuple-element.170.kind_ref, bf16[768,1152]{1,0:T(8,128)(2,1)} %get-tuple-element.171.x_any.refs_0_, ...), custom_call_target="tpu_custom_call" | custom-call | flops 1024 | bytes 1024 | tf_op jit(solution)/shard_map/heads_forward/pallas_call | solution.py:739
  123.0 17.0 %heads_forward.3 = (bf16[2,768,896]{2,1,0:T(8,128)(2,1)}, bf16[2,4,768,768]{3,2,1,0:T(8,128)(2,1)}, bf16[768,384]{1,0:T(8,128)(2,1)}, bf16[768,384]{1,0:T(8,128)(2,1)}) custom-call(s32[1]{0:T(128)} %bitcast.spot, s32[768,1]{1,0:T(8,128)} %get-tuple-element.170.kind_ref, bf16[768,1152]{1,0:T(8,128)(2,1)} %get-tuple-element.171.x_any.refs_0_, ...), custom_call_target="tpu_custom_call" | custom-call | flops 1024 | bytes 1024 | tf_op jit(solution)/shard_map/heads_forward/pallas_call | solution.py:739
  140.1 3.7 collective-permute-done.15.refs_0_
  149.3 9.5 %attn_out.1 = (bf16[768,1152]{1,0:T(8,128)(2,1)}, bf16[768,1152]{1,0:T(8,128)(2,1)}) custom-call(s32[1]{0:T(128)} %bitcast.spot, bf16[768,384]{1,0:T(8,128)(2,1)} %get-tuple-element.187.one.refs_1_.refs_5_, bf16[768,384]{1,0:T(8,128)(2,1)} %get-tuple-element.188.two.refs_0_, bf16[768,384]{1,0:T(8,128)(2,1)} %get-tuple-element.189.three.refs_1_.refs_5_, ...), custom_call_target="tpu_custom_call" | custom-call | flops 1024 | bytes 1024 | tf_op jit(solution)/shard_map/attn_out/pallas_call | solution.py:739
  158.8 5.1 %collective-permute-done.25.refs_0_ = bf16[2,144,1152]{2,1,0:T(8,128)(2,1)} collective-permute-done((bf16[2,144,1152]{2,1,0:T(8,128)(2,1)}, bf16[2,144,1152]{2,1,0:T(8,128)(2,1)}, u32[]{:S(2)}, u32[]{:S(2)}) %collective-permute-start.25) | collective-permute-done | bytes 663584 | tf_op jit(solution)/shard_map/ppermute | solution.py:1458
  168.3 11.2 %mlp_up.2 = (bf16[2,768,1152]{2,1,0:T(8,128)(2,1)}, bf16[2,768,1152]{2,1,0:T(8,128)(2,1)}) custom-call(s32[1]{0:T(128)} %bitcast.spot, bf16[768,1152]{1,0:T(8,128)(2,1)} %get-tuple-element.192.x_any.refs_0_, f32[2,1,1152]{2,1,0:T(1,128)} %get-tuple-element.193.bias_ref, bf16[4,144,1152]{2,1,0:T(8,128)(2,1)} %collective-permute-done.22.refs_4_.refs_0_.refs_13_, ...), custom_call_target="tpu_custom_call" | custom-call | flops 1024 | bytes 1024 | tf_op jit(solution)/shard_map/mlp_up/pallas_call | solution.py:739
  181.6 11.7 %mlp_up.3 = (bf16[2,768,1152]{2,1,0:T(8,128)(2,1)}, bf16[2,768,1152]{2,1,0:T(8,128)(2,1)}) custom-call(s32[1]{0:T(128)} %bitcast.spot, bf16[768,1152]{1,0:T(8,128)(2,1)} %get-tuple-element.192.x_any.refs_0_, f32[2,1,1152]{2,1,0:T(1,128)} %get-tuple-element.197.bias_ref, bf16[4,144,1152]{2,1,0:T(8,128)(2,1)} %get-tuple-element.169.refs_0_.refs_8_, ...), custom_call_target="tpu_custom_call" | custom-call | flops 1024 | bytes 1024 | tf_op jit(solution)/shard_map/mlp_up/pallas_call | solution.py:739
  195.0 14.8 %weight_grad.4 = (bf16[4,144,1152]{2,1,0:T(8,128)(2,1)}, bf16[2,144,1152]{2,1,0:T(8,128)(2,1)}, bf16[2,144,1152]{2,1,0:T(8,128)(2,1)}, bf16[2,144,1152]{2,1,0:T(...) custom-call(s32[1]{0:T(128)} %bitcast.spot, ...), custom_call_target="tpu_custom_call" | custom-call | flops 1024 | bytes 1024 | tf_op jit(solution)/shard_map/weight_grad/pallas_call | solution.py:739
  214.1 32.9 %mlp_back.1 = (bf16[2,768,1152]{2,1,0:T(8,128)(2,1)}, bf16[2,768,1152]{2,1,0:T(8,128)(2,1)}, bf16[768,1152]{1,0:T(8,128)(2,1)}, f32[8,1152]{1,0:T(8,128)}, f32[4,1,1152]{2,1,0:T(1,128)}) custom-call(s32[1]{0:T(128)} %bitcast.spot, bf16[768,1152]{1,0:T(8,128)(2,1)} %copy-done.4, bf16[2,768,1152]{2,1,0:T(8,128)(2,1)} %get-tuple-element.207.one_any, ...), custom_call_target="tpu_custom_call" | custom-call | flops 1024 | bytes 1024 | tf_op jit(solution)/shard_map/mlp_back/pallas_call | solution.py:739
  249.0 3.0 add_pairs.3
  254.9 21.3 %heads_backward.2 = (bf16[768,896]{1,0:T(8,128)(2,1)}, bf16[768,896]{1,0:T(8,128)(2,1)}, f32[2,1,896]{2,1,0:T(1,128)}) custom-call(s32[1]{0:T(128)} %bitcast.spot, bf16[768,1152]{1,0:T(8,128)(2,1)} %get-tuple-element.216.grad_any.refs_4_.refs_5_, bf16[2,768,896]{2,1,0:T(8,128)(2,1)} %get-tuple-element.225.qkv_any, ...), custom_call_target="tpu_custom_call" | custom-call | flops 1024 | bytes 1024 | tf_op jit(solution)/shard_map/heads_backward/pallas_call | solution.py:739
  277.9 3.7 add_square.3.refs_4_.refs_1_
  281.6 14.8 %weight_grad.5 = (bf16[4,144,1152]{2,1,0:T(8,128)(2,1)}, bf16[2,144,1152]{2,1,0:T(8,128)(2,1)}, bf16[2,144,1152]{2,1,0:T(8,128)(2,1)}, bf16[2,144,1152]{2,1,0:T(...) custom-call(s32[1]{0:T(128)} %bitcast.spot, ...), custom_call_target="tpu_custom_call" | custom-call | flops 1024 | bytes 1024 | tf_op jit(solution)/shard_map/weight_grad/pallas_call | solution.py:739
  301.9 21.2 %heads_backward.3 = (bf16[768,896]{1,0:T(8,128)(2,1)}, bf16[768,896]{1,0:T(8,128)(2,1)}, f32[2,1,896]{2,1,0:T(1,128)}) custom-call(s32[1]{0:T(128)} %bitcast.spot, bf16[768,1152]{1,0:T(8,128)(2,1)} %get-tuple-element.216.grad_any.refs_4_.refs_5_, bf16[2,768,896]{2,1,0:T(8,128)(2,1)} %get-tuple-element.217.qkv_any, ...), custom_call_target="tpu_custom_call" | custom-call | flops 1024 | bytes 1024 | tf_op jit(solution)/shard_map/heads_backward/pallas_call | solution.py:739
  323.2 5.0 %collective-permute-done.48.refs_3_ = bf16[2,144,1152]{2,1,0:T(8,128)(2,1)S(1)} collective-permute-done((bf16[2,144,1152]{2,1,0:T(8,128)(2,1)}, bf16[2,144,1152]{2,1,0:T(8,128)(2,1)S(1)}, u32[]{:S(2)}, u32[]{:S(2)}) %collective-permute-start.48) | collective-permute-done | bytes 663584 | tf_op jit(solution)/shard_map/ppermute | solution.py:1458
  329.1 2.9 add_pairs.4
  333.6 10.9 %weight_grad.6 = (bf16[2,144,1152]{2,1,0:T(8,128)(2,1)}, bf16[2,144,1152]{2,1,0:T(8,128)(2,1)}, bf16[2,144,1152]{2,1,0:T(8,128)(2,1)}, bf16[2,144,1152]{2,1,0:T(8,128)(2,1)}) custom-call(s32[1]{0:T(128)} %bitcast.spot, bf16[768,1152]{1,0:T(8,128)(2,1)} %get-tuple-element.171.x_any.refs_0_, bf16[1,768,896]{2,1,0:T(8,128)(2,1)} %bitcast.114, ...), custom_call_target="tpu_custom_call" | custom-call | flops 1024 | bytes 1024 | tf_op jit(solution)/shard_map/weight_grad/pallas_call | solution.py:739
  348.0 11.1 %weight_grad.7 = (bf16[4,144,1152]{2,1,0:T(8,128)(2,1)}, bf16[2,144,1152]{2,1,0:T(8,128)(2,1)}, bf16[2,144,1152]{2,1,0:T(8,128)(2,1)}) custom-call(s32[1]{0:T(128)} %bitcast.spot, bf16[768,1152]{1,0:T(8,128)(2,1)} %get-tuple-element.171.x_any.refs_0_, bf16[1,768,896]{2,1,0:T(8,128)(2,1)} %bitcast.115, bf16[768,1152]{1,0:T(8,128)(2,1)} %get-tuple-element.240.refs_2_, ...), custom_call_target="tpu_custom_call" | custom-call | flops 1024 | bytes 1024 | tf_op jit(solution)/shard_map/weight_grad/pallas_call | solution.py:739
  359.2 3.7 add_square.4.refs_2_
  367.9 3.1 add_pairs.5
  374.6 16.9 %norm_one_back.1 = (f32[768,1152]{1,0:T(8,128)}, f32[8,1152]{1,0:T(8,128)}) custom-call(s32[1]{0:T(128)} %bitcast.spot, bf16[768,896]{1,0:T(8,128)(2,1)} %get-tuple-element.250.refs_8_.refs_0_, bf16[768,896]{1,0:T(8,128)(2,1)} %get-tuple-element.229.refs_1_, bf16[768,896]{1,0:T(8,128)(2,1)} %get-tuple-element.239.refs_2_, ...), custom_call_target="tpu_custom_call" | custom-call | flops 1024 | bytes 1024 | tf_op jit(solution)/shard_map/norm_one_back/pallas_call | solution.py:739
  391.4 3.9 slice.295
  398.4 2.9 collective-permute-done.57.refs_2_
  402.2 3.7 add_square.5.refs_8_.refs_2_.refs_3_
  405.9 16.6 %mlp_down.1 = bf16[768,1152]{1,0:T(8,128)(2,1)} custom-call(s32[1]{0:T(128)} %bitcast.spot, bf16[2,768,1152]{2,1,0:T(8,128)(2,1)} %fence.31.refs_5_.later_any, bf16[2,768,1152]{2,1,0:T(8,128)(2,1)} %get-tuple-element.200.refs_1_.early_any, bf16[768,1152]{1,0:T(8,128)(2,1)} %get-tuple-element.201.resid_any, f32[1,1152]{1,0:T(1,128)} %get-tuple-element.360.shift_ref, ...), custom_call_target="tpu_custom_call" | custom-call | flops 1024 | bytes 1024 | tf_op jit(solution)/shard_map/mlp_down/pallas_call | solution.py:739
  438.3 2.5 collective-permute-start.67
  (431 shorter events, 137.7 us)
Async XLA Ops:
  7.2 51.0 %all-gather.9.cloned.1.call-start = ((), (), s32[]{:S(2)}) async-start(), calls=%async_computation.7 | async-start | bytes 1658880 | tf_op jit(solution)/shard_map/all_gather | solution.py:1494
  19.6 72.3 %all-gather.7.cloned.1.call-start = ((), (), s32[]{:S(2)}) async-start(), calls=%async_computation.6 | async-start | bytes 1658880 | tf_op jit(solution)/shard_map/all_gather | solution.py:1494
  19.9 38.2 %collective-permute-start.10 = (bf16[144,1152]{1,0:T(8,128)(2,1)S(1)}, bf16[144,1152]{1,0:T(8,128)(2,1)S(1)}, u32[]{:S(2)}, u32[]{:S(2)}) collective-permute-start(bf16[144,1152]{1,0:T(8,128)(2,1)S(1)} %pad_maximum_fusion.4.refs_4_), channel_id=1, source_target_pairs={{0,1},{1,0},{2,3},{3,2},{4,5},{5,4},{6,7},{7,6},{8,9},{9,8},{10,11... | collective-permute-start | bytes 995336 | tf_op jit(solution)/shard_map/ppermute | solution.py:1458
  22.5 35.6 %collective-permute-start.11 = (bf16[144,1152]{1,0:T(8,128)(2,1)S(1)}, bf16[144,1152]{1,0:T(8,128)(2,1)S(1)}, u32[]{:S(2)}, u32[]{:S(2)}) collective-permute-start(bf16[144,1152]{1,0:T(8,128)(2,1)S(1)} %pad_maximum_fusion.4.refs_4_), channel_id=1, source_target_pairs={{0,5},{1,4},{2,7},{3,6},{4,1},{5,0},{6,3},{7,2},{8,13},{9,12},{10,... | collective-permute-start | bytes 995336 | tf_op jit(solution)/shard_map/ppermute | solution.py:1458
  23.9 34.2 %collective-permute-start.9 = (bf16[144,1152]{1,0:T(8,128)(2,1)S(1)}, bf16[144,1152]{1,0:T(8,128)(2,1)S(1)}, u32[]{:S(2)}, u32[]{:S(2)}) collective-permute-start(bf16[144,1152]{1,0:T(8,128)(2,1)S(1)} %pad_maximum_fusion.4.refs_4_), channel_id=1, source_target_pairs={{0,4},{1,5},{2,6},{3,7},{4,0},{5,1},{6,2},{7,3},{8,12},{9,13},{10,... | collective-permute-start | bytes 995336 | tf_op jit(solution)/shard_map/ppermute | solution.py:1458
  24.0 34.1 %collective-permute-start.7 = (bf16[26,128]{1,0:T(8,128)(2,1)}, bf16[26,128]{1,0:T(8,128)(2,1)S(1)}, u32[]{:S(2)}, u32[]{:S(2)}) collective-permute-start(bf16[26,128]{1,0:T(8,128)(2,1)} %fence.25), channel_id=1, source_target_pairs={{0,1},{1,0},{2,3},{3,2},{4,5},{5,4},{6,7},{7,6},{8,9},{9,8},{10,11... | collective-permute-start | bytes 19976 | tf_op jit(solution)/shard_map/ppermute | solution.py:1458
  58.0 135.4 %all-gather.11.cloned.1.call-start = ((), (), s32[]{:S(2)}) async-start(), calls=%async_computation.8 | async-start | bytes 6635520 | tf_op jit(solution)/shard_map/all_gather | solution.py:1494
  60.4 31.4 %collective-permute-start.12 = (bf16[4,144,1152]{2,1,0:T(8,128)(2,1)}, bf16[4,144,1152]{2,1,0:T(8,128)(2,1)S(1)}, u32[]{:S(2)}, u32[]{:S(2)}) collective-permute-start(bf16[4,144,1152]{2,1,0:T(8,128)(2,1)} %get-tuple-element.158.refs_0_.refs_4_.refs_12_), channel_id=1, source_target_pairs={{0,4},{1,5},{2,6},{3,7},{4,0},{5,1},{6,2},{7,3},{8,12},{9,13},{10,... | collective-permute-start | bytes 3981320 | tf_op jit(solution)/shard_map/ppermute | solution.py:1458
  62.3 29.6 %collective-permute-start.13 = (bf16[4,144,1152]{2,1,0:T(8,128)(2,1)}, bf16[4,144,1152]{2,1,0:T(8,128)(2,1)}, u32[]{:S(2)}, u32[]{:S(2)}) collective-permute-start(bf16[4,144,1152]{2,1,0:T(8,128)(2,1)} %get-tuple-element.158.refs_0_.refs_4_.refs_12_), channel_id=1, source_target_pairs={{0,1},{1,0},{2,3},{3,2},{4,5},{5,4},{6,7},{7,6},{8,9},{9,8},{10,11... | collective-permute-start | bytes 3981320 | tf_op jit(solution)/shard_map/ppermute | solution.py:1458
  64.0 34.0 %collective-permute-start.20 = (bf16[4,144,1152]{2,1,0:T(8,128)(2,1)}, bf16[4,144,1152]{2,1,0:T(8,128)(2,1)}, u32[]{:S(2)}, u32[]{:S(2)}) collective-permute-start(bf16[4,144,1152]{2,1,0:T(8,128)(2,1)} %get-tuple-element.158.refs_0_.refs_4_.refs_12_), channel_id=1, source_target_pairs={{0,2},{1,3},{2,0},{3,1},{4,6},{5,7},{6,4},{7,5},{8,10},{9,11},{10,... | collective-permute-start | bytes 3981320 | tf_op jit(solution)/shard_map/ppermute | solution.py:1458
  93.5 265.7 %reduce-scatter.4.cloned.1.call-start = ((), (), s32[]{:S(2)}) async-start(), calls=%async_computation.3 | async-start | bytes 1658880 | tf_op jit(solution)/shard_map/reduce_scatter | solution.py:1497
  99.4 44.3 %collective-permute-start.15 = (bf16[4,144,1152]{2,1,0:T(8,128)(2,1)}, bf16[4,144,1152]{2,1,0:T(8,128)(2,1)}, u32[]{:S(2)}, u32[]{:S(2)}) collective-permute-start(bf16[4,144,1152]{2,1,0:T(8,128)(2,1)} %get-tuple-element.169.refs_0_.refs_8_), channel_id=1, source_target_pairs={{0,4},{1,5},{2,6},{3,7},{4,0},{5,1},{6,2},{7,3},{8,12},{9,13},{10,... | collective-permute-start | bytes 3981320 | tf_op jit(solution)/shard_map/ppermute | solution.py:1458
  100.0 43.8 %collective-permute-start.16 = (bf16[4,144,1152]{2,1,0:T(8,128)(2,1)}, bf16[4,144,1152]{2,1,0:T(8,128)(2,1)}, u32[]{:S(2)}, u32[]{:S(2)}) collective-permute-start(bf16[4,144,1152]{2,1,0:T(8,128)(2,1)} %get-tuple-element.169.refs_0_.refs_8_), channel_id=1, source_target_pairs={{0,1},{1,0},{2,3},{3,2},{4,5},{5,4},{6,7},{7,6},{8,9},{9,8},{10,11... | collective-permute-start | bytes 3981320 | tf_op jit(solution)/shard_map/ppermute | solution.py:1458
  121.1 37.7 %collective-permute-start.29 = (bf16[768,1152]{1,0:T(8,128)(2,1)S(1)}, bf16[768,1152]{1,0:T(8,128)(2,1)S(1)}, u32[]{:S(2)}, u32[]{:S(2)}) collective-permute-start(bf16[768,1152]{1,0:T(8,128)(2,1)S(1)} %copy-done.1), channel_id=1, source_target_pairs={{0,2},{1,3},{2,0},{3,1},{4,6},{5,7},{6,4},{7,5},{8,10},{9,11},{10,... | collective-permute-start | bytes 5308424 | tf_op jit(solution)/shard_map/ppermute | solution.py:1458
  209.8 37.2 %collective-permute-start.37 = (bf16[2,144,1152]{2,1,0:T(8,128)(2,1)}, bf16[2,144,1152]{2,1,0:T(8,128)(2,1)S(1)}, u32[]{:S(2)}, u32[]{:S(2)}) collective-permute-start(bf16[2,144,1152]{2,1,0:T(8,128)(2,1)} %get-tuple-element.212), channel_id=1, source_target_pairs={{0,4},{1,5},{2,6},{3,7},{4,0},{5,1},{6,2},{7,3},{8,12},{9,13},{10,... | collective-permute-start | bytes 1990664 | tf_op jit(solution)/shard_map/ppermute | solution.py:1458
  211.5 35.5 %collective-permute-start.38 = (bf16[2,144,1152]{2,1,0:T(8,128)(2,1)}, bf16[2,144,1152]{2,1,0:T(8,128)(2,1)S(1)}, u32[]{:S(2)}, u32[]{:S(2)}) collective-permute-start(bf16[2,144,1152]{2,1,0:T(8,128)(2,1)} %get-tuple-element.213), channel_id=1, source_target_pairs={{0,1},{1,0},{2,3},{3,2},{4,5},{5,4},{6,7},{7,6},{8,9},{9,8},{10,11... | collective-permute-start | bytes 1990664 | tf_op jit(solution)/shard_map/ppermute | solution.py:1458
  213.0 34.1 %collective-permute-start.39 = (bf16[2,144,1152]{2,1,0:T(8,128)(2,1)}, bf16[2,144,1152]{2,1,0:T(8,128)(2,1)S(1)}, u32[]{:S(2)}, u32[]{:S(2)}) collective-permute-start(bf16[2,144,1152]{2,1,0:T(8,128)(2,1)} %get-tuple-element.214), channel_id=1, source_target_pairs={{0,4},{1,5},{2,6},{3,7},{4,0},{5,1},{6,2},{7,3},{8,12},{9,13},{10,... | collective-permute-start | bytes 1990664 | tf_op jit(solution)/shard_map/ppermute | solution.py:1458
  213.5 33.5 %collective-permute-start.40 = (bf16[2,144,1152]{2,1,0:T(8,128)(2,1)}, bf16[2,144,1152]{2,1,0:T(8,128)(2,1)S(1)}, u32[]{:S(2)}, u32[]{:S(2)}) collective-permute-start(bf16[2,144,1152]{2,1,0:T(8,128)(2,1)} %get-tuple-element.215), channel_id=1, source_target_pairs={{0,1},{1,0},{2,3},{3,2},{4,5},{5,4},{6,7},{7,6},{8,9},{9,8},{10,11... | collective-permute-start | bytes 1990664 | tf_op jit(solution)/shard_map/ppermute | solution.py:1458
  248.5 27.8 %collective-permute-start.43 = (bf16[2,768,1152]{2,1,0:T(8,128)(2,1)}, bf16[2,768,1152]{2,1,0:T(8,128)(2,1)}, u32[]{:S(2)}, u32[]{:S(2)}) collective-permute-start(bf16[2,768,1152]{2,1,0:T(8,128)(2,1)} %get-tuple-element.228), channel_id=1, source_target_pairs={{0,2},{1,3},{2,0},{3,1},{4,6},{5,7},{6,4},{7,5},{8,10},{9,11},{10,... | collective-permute-start | bytes 10616840 | tf_op jit(solution)/shard_map/ppermute | solution.py:1458
  248.5 27.8 %collective-permute-start.44 = (bf16[768,1152]{1,0:T(8,128)(2,1)}, bf16[768,1152]{1,0:T(8,128)(2,1)S(1)}, u32[]{:S(2)}, u32[]{:S(2)}) collective-permute-start(bf16[768,1152]{1,0:T(8,128)(2,1)} %get-tuple-element.216.grad_any.refs_4_.refs_5_), channel_id=1, source_target_pairs={{0,2},{1,3},{2,0},{3,1},{4,6},{5,7},{6,4},{7,5},{8,10},{9,11},{10,... | collective-permute-start | bytes 5308424 | tf_op jit(solution)/shard_map/ppermute | solution.py:1458
  296.4 26.7 %collective-permute-start.46 = (bf16[2,144,1152]{2,1,0:T(8,128)(2,1)}, bf16[2,144,1152]{2,1,0:T(8,128)(2,1)S(1)}, u32[]{:S(2)}, u32[]{:S(2)}) collective-permute-start(bf16[2,144,1152]{2,1,0:T(8,128)(2,1)} %get-tuple-element.246), channel_id=1, source_target_pairs={{0,4},{1,5},{2,6},{3,7},{4,0},{5,1},{6,2},{7,3},{8,12},{9,13},{10,... | collective-permute-start | bytes 1990664 | tf_op jit(solution)/shard_map/ppermute | solution.py:1458
  297.0 26.1 %collective-permute-start.47 = (bf16[2,144,1152]{2,1,0:T(8,128)(2,1)}, bf16[2,144,1152]{2,1,0:T(8,128)(2,1)S(1)}, u32[]{:S(2)}, u32[]{:S(2)}) collective-permute-start(bf16[2,144,1152]{2,1,0:T(8,128)(2,1)} %get-tuple-element.247), channel_id=1, source_target_pairs={{0,1},{1,0},{2,3},{3,2},{4,5},{5,4},{6,7},{7,6},{8,9},{9,8},{10,11... | collective-permute-start | bytes 1990664 | tf_op jit(solution)/shard_map/ppermute | solution.py:1458
  297.6 30.6 %collective-permute-start.48 = (bf16[2,144,1152]{2,1,0:T(8,128)(2,1)}, bf16[2,144,1152]{2,1,0:T(8,128)(2,1)S(1)}, u32[]{:S(2)}, u32[]{:S(2)}) collective-permute-start(bf16[2,144,1152]{2,1,0:T(8,128)(2,1)} %get-tuple-element.248), channel_id=1, source_target_pairs={{0,4},{1,5},{2,6},{3,7},{4,0},{5,1},{6,2},{7,3},{8,12},{9,13},{10,... | collective-permute-start | bytes 1990664 | tf_op jit(solution)/shard_map/ppermute | solution.py:1458
  299.0 29.6 %collective-permute-start.49 = (bf16[2,144,1152]{2,1,0:T(8,128)(2,1)}, bf16[2,144,1152]{2,1,0:T(8,128)(2,1)}, u32[]{:S(2)}, u32[]{:S(2)}) collective-permute-start(bf16[2,144,1152]{2,1,0:T(8,128)(2,1)} %get-tuple-element.249), channel_id=1, source_target_pairs={{0,1},{1,0},{2,3},{3,2},{4,5},{5,4},{6,7},{7,6},{8,9},{9,8},{10,11... | collective-permute-start | bytes 1990664 | tf_op jit(solution)/shard_map/ppermute | solution.py:1458
  301.6 99.7 %reduce-scatter.6.cloned.1.call-start = ((), (), s32[]{:S(2)}) async-start(), calls=%async_computation.4 | async-start | bytes 1658880 | tf_op jit(solution)/shard_map/reduce_scatter | solution.py:1497
  331.9 27.2 %collective-permute-start.51 = (bf16[2,144,1152]{2,1,0:T(8,128)(2,1)}, bf16[2,144,1152]{2,1,0:T(8,128)(2,1)}, u32[]{:S(2)}, u32[]{:S(2)}) collective-permute-start(bf16[2,144,1152]{2,1,0:T(8,128)(2,1)} %get-tuple-element.263), channel_id=1, source_target_pairs={{0,4},{1,5},{2,6},{3,7},{4,0},{5,1},{6,2},{7,3},{8,12},{9,13},{10,... | collective-permute-start | bytes 1990664 | tf_op jit(solution)/shard_map/ppermute | solution.py:1458
  333.1 26.1 %collective-permute-start.52 = (bf16[2,144,1152]{2,1,0:T(8,128)(2,1)}, bf16[2,144,1152]{2,1,0:T(8,128)(2,1)}, u32[]{:S(2)}, u32[]{:S(2)}) collective-permute-start(bf16[2,144,1152]{2,1,0:T(8,128)(2,1)} %get-tuple-element.264), channel_id=1, source_target_pairs={{0,1},{1,0},{2,3},{3,2},{4,5},{5,4},{6,7},{7,6},{8,9},{9,8},{10,11... | collective-permute-start | bytes 1990664 | tf_op jit(solution)/shard_map/ppermute | solution.py:1458
  365.4 84.8 %reduce-scatter.8.cloned.1.call-start = ((), (), s32[]{:S(2)}) async-start(), calls=%async_computation.5 | async-start | bytes 1658880 | tf_op jit(solution)/shard_map/reduce_scatter | solution.py:1497
  367.3 31.0 %collective-permute-start.58 = (bf16[2,144,1152]{2,1,0:T(8,128)(2,1)}, bf16[2,144,1152]{2,1,0:T(8,128)(2,1)S(1)}, u32[]{:S(2)}, u32[]{:S(2)}) collective-permute-start(bf16[2,144,1152]{2,1,0:T(8,128)(2,1)} %get-tuple-element.280), channel_id=1, source_target_pairs={{0,1},{1,0},{2,3},{3,2},{4,5},{5,4},{6,7},{7,6},{8,9},{9,8},{10,11... | collective-permute-start | bytes 1990664 | tf_op jit(solution)/shard_map/ppermute | solution.py:1458
  371.0 27.3 %collective-permute-start.55 = (bf16[2,144,1152]{2,1,0:T(8,128)(2,1)}, bf16[2,144,1152]{2,1,0:T(8,128)(2,1)S(1)}, u32[]{:S(2)}, u32[]{:S(2)}) collective-permute-start(bf16[2,144,1152]{2,1,0:T(8,128)(2,1)} %get-tuple-element.277.refs_17_), channel_id=1, source_target_pairs={{0,4},{1,5},{2,6},{3,7},{4,0},{5,1},{6,2},{7,3},{8,12},{9,13},{10,... | collective-permute-start | bytes 1990664 | tf_op jit(solution)/shard_map/ppermute | solution.py:1458
  371.9 26.4 %collective-permute-start.56 = (bf16[2,144,1152]{2,1,0:T(8,128)(2,1)}, bf16[2,144,1152]{2,1,0:T(8,128)(2,1)S(1)}, u32[]{:S(2)}, u32[]{:S(2)}) collective-permute-start(bf16[2,144,1152]{2,1,0:T(8,128)(2,1)} %get-tuple-element.278), channel_id=1, source_target_pairs={{0,1},{1,0},{2,3},{3,2},{4,5},{5,4},{6,7},{7,6},{8,9},{9,8},{10,11... | collective-permute-start | bytes 1990664 | tf_op jit(solution)/shard_map/ppermute | solution.py:1458
  373.4 27.9 %collective-permute-start.57 = (bf16[2,144,1152]{2,1,0:T(8,128)(2,1)S(1)}, bf16[2,144,1152]{2,1,0:T(8,128)(2,1)S(1)}, u32[]{:S(2)}, u32[]{:S(2)}) collective-permute-start(bf16[2,144,1152]{2,1,0:T(8,128)(2,1)S(1)} %copy-done.44), channel_id=1, source_target_pairs={{0,4},{1,5},{2,6},{3,7},{4,0},{5,1},{6,2},{7,3},{8,12},{9,13},{10,... | collective-permute-start | bytes 1990664 | tf_op jit(solution)/shard_map/ppermute | solution.py:1458
  (110 other events, 708.0 us)
Sparse Core Ops, SparseCore 0:
  19.7 36.7 all-gather.8
  58.6 33.1 all-gather.6
  94.0 98.1 all-gather.10
  301.7 29.3 reduce-scatter.3
  365.5 29.3 reduce-scatter.5
  406.0 30.4 reduce-scatter.7
